TPU v7x, 32 devices: a whole 2x2x4 slice. The times are simulated.
32 devices in a mesh: grp: 2 (over x), sfc: 16 (over z, y, core).
Axes of the slice: x: 2, y: 2, z: 4, core: 2. Of those that a mesh axis runs over, the one named last changes fastest.
Arguments:
- charges: bfloat16 [512, 8, 256], P(('grp', 'sfc')), parts along dimension 0, may hold values from -6 to 6
- self_blocks: bfloat16 [512, 256, 256], P(('grp', 'sfc')), parts along dimension 0, may hold values from -0.375 to 0.375
- near_blocks: bfloat16 [1024, 256, 256], P(('grp', 'sfc')), parts along dimension 0, may hold values from -0.375 to 0.375
- near_pairs: int32 [1024, 2], P(('grp', 'sfc')), parts along dimension 0, may hold values from 0 to 255, as said below
- bases: bfloat16 [512, 64, 256], P(('grp', 'sfc')), parts along dimension 0, may hold values from -0.375 to 0.375
- transfers: bfloat16 [512, 64, 64], P(('grp', 'sfc')), parts along dimension 0, may hold values from -0.75 to 0.75
- parent_of: int32 [512], P(('grp', 'sfc')), parts along dimension 0, may hold values from 0 to 127, as said below
- far_pairs: int32 [4096, 2], P(('grp', 'sfc')), parts along dimension 0, may hold values from -1 to 255, as said below
- far_coupling: bfloat16 [4096, 64, 64], P(('grp', 'sfc')), parts along dimension 0, may hold values from -0.75 to 0.75
- par_pairs: int32 [1024, 2], P(('grp', 'sfc')), parts along dimension 0, may hold values from 0 to 127, as said below
- par_coupling: bfloat16 [1024, 64, 64], P(('grp', 'sfc')), parts along dimension 0, may hold values from -0.75 to 0.75
Outputs:
- potentials: float32 [512, 8, 256], P(('grp', 'sfc')), parts along dimension 0
There are 2 independent parts, one for each index of `grp`. A program takes and returns all parts, laid end to end along the dimension named above; each array names one. Nothing has to cross between parts.
Inputs may be any that keep to these rules, and one draw needn't show every extreme that they name: `near_pairs`: slot s lies on device d = s // 32; column 0 is a leaf of device d (leaves d * 16 to (d + 1) * 16 - 1), column 1 a different leaf of device d or of device d + 1; on the last device only of device d. `parent_of`: leaves of device d have parents of device d (parents d * 8 to (d + 1) * 8 - 1), non-decreasing along the leaves; every parent has at least one child. `far_pairs`: the 128 slots of device d form 16 buckets of 8 slots; column 0 is always a leaf of device d; in bucket k a live slot has column 1 a leaf of device k (different from column 0 when k = d), an empty slot has -1; live slots come first in a bucket. At most 8 live slots a bucket, and every device has a full bucket. `par_pairs`: pair s lies on device d = s // 32; column 0 is a parent of device d, column 1 any other parent.
All inputs are finite; a program needn't handle non-finite values.
Results may differ from a plain program's by a relative error of at most 0.004.
Values may be sent and summed in bfloat16 or wider, within the bound.
No kernel may reach another device: no remote copies, remote signals or barrier semaphores. Data moves between devices by JAX's collectives and lax.ppermute only.
A program may use at most 128 MiB of HBM per device.

v0:
```python
import jax
import jax.numpy as jnp
from jax import lax
from jax.sharding import PartitionSpec as P


def passed_along(value, axis, steps):
    count = lax.axis_size(axis)
    leading, last = (max(0, -steps), min(count, count - steps))
    return lax.ppermute(value, axis, [(source, source + steps) for source in range(leading, last)])


def one_hot_rows(targets, target_count, values):
    column = jnp.arange(target_count, dtype=jnp.int32)
    selector = (column[:, None] == targets[None, :]).astype(jnp.float32)
    return jnp.dot(selector, values, precision=lax.Precision.HIGHEST)


def make_picker(wanted):

    def picker(running, shard_rows, offset_row):
        row_count = shard_rows.shape[0]
        inside = (wanted >= 0) & (wanted < row_count)
        fetched = jnp.take(shard_rows, jnp.clip(wanted, 0, row_count - 1), axis=0).astype(
            jnp.float32
        )
        return jnp.where(inside[:, None], fetched, 0.0)

    return picker


def make_bucket_picker(wanted):
    whole_picker = make_picker(wanted)

    def picker(running, shard_rows, offset_row):
        return whole_picker(running, shard_rows, offset_row)

    return picker


def make_terms(targets, contributions):

    def terms(offset_row, row_count):
        inside = (targets >= 0) & (targets >= 0) & (targets < row_count)
        segment_ids = jnp.where(inside, targets, row_count)
        summed = jax.ops.segment_sum(contributions, segment_ids, num_segments=row_count + 1)
        return summed[:row_count]

    return terms


def make_bucket_terms(targets, contributions):
    whole_terms = make_terms(targets, contributions)

    def terms(offset_row, row_count):
        return whole_terms(offset_row, row_count)

    return terms


def on_device(
    charges,
    self_blocks,
    near_blocks,
    near_pairs,
    bases,
    transfers,
    parent_of,
    far_pairs,
    far_coupling,
    par_pairs,
    par_coupling,
):
    leaf_count, rhs_count, panel_count = charges.shape
    rank = bases.shape[1]
    parent_count = leaf_count // 2
    width = rhs_count * rank
    position = lax.axis_index("sfc")
    first_leaf = position * leaf_count
    first_parent = position * parent_count
    moments = jnp.einsum("lkp,lrp->lrk", bases, charges, preferred_element_type=jnp.float32).astype(
        jnp.bfloat16
    )
    child_terms = jnp.einsum("lkj,lrj->lrk", transfers, moments, preferred_element_type=jnp.float32)
    parent_local = parent_of - first_parent
    parent_moments = (
        one_hot_rows(parent_local, parent_count, child_terms.reshape(leaf_count, width))
        .astype(jnp.bfloat16)
        .reshape(parent_count, rhs_count, rank)
    )
    following = passed_along(charges, "sfc", -1)
    extended = jnp.concatenate([charges, following], axis=0)
    near_owner = near_pairs[:, 0] - first_leaf
    near_partner = near_pairs[:, 1] - first_leaf
    near_count = near_pairs.shape[0]
    forward_near = jnp.einsum(
        "spq,srq->srp",
        near_blocks,
        jnp.take(extended, near_partner, axis=0),
        preferred_element_type=jnp.float32,
    )
    backward_near = jnp.einsum(
        "spq,srp->srq",
        near_blocks,
        jnp.take(charges, near_owner, axis=0),
        preferred_element_type=jnp.float32,
    )
    near_sums = one_hot_rows(near_owner, 2 * leaf_count, forward_near.reshape(near_count, -1))
    near_sums = near_sums + one_hot_rows(
        near_partner, 2 * leaf_count, backward_near.reshape(near_count, -1)
    )
    near_sums = near_sums.reshape(2 * leaf_count, rhs_count, panel_count)
    returned_near = passed_along(near_sums[leaf_count:], "sfc", 1)
    self_terms = jnp.einsum(
        "lpq,lrq->lrp", self_blocks, charges, preferred_element_type=jnp.float32
    )
    pair_total = par_pairs.shape[0]
    par_owner = par_pairs[:, 0] - first_parent
    par_partner = par_pairs[:, 1]
    parent_flat = parent_moments.reshape(parent_count, width)
    partner_parents = make_picker(par_partner)(
        jnp.zeros((pair_total, width), jnp.float32),
        lax.all_gather(parent_flat, "sfc", axis=0, tiled=True),
        jnp.int32(0),
    )
    partner_parents = partner_parents.astype(jnp.bfloat16).reshape(pair_total, rhs_count, rank)
    forward_par = jnp.einsum(
        "skj,srj->srk", par_coupling, partner_parents, preferred_element_type=jnp.float32
    )
    owner_parents = jnp.take(parent_moments, par_owner, axis=0)
    backward_par = jnp.einsum(
        "sjk,srj->srk", par_coupling, owner_parents, preferred_element_type=jnp.float32
    )
    parent_own = one_hot_rows(par_owner, parent_count, forward_par.reshape(pair_total, width))
    parent_back = lax.psum_scatter(
        make_terms(par_partner, backward_par.reshape(pair_total, width))(
            jnp.int32(0), parent_count * lax.axis_size("sfc")
        ),
        "sfc",
        scatter_dimension=0,
        tiled=True,
    )
    parent_locals = (
        (parent_own + parent_back).astype(jnp.bfloat16).reshape(parent_count, rhs_count, rank)
    )
    downward = jnp.einsum(
        "ljk,lrj->lrk",
        transfers,
        jnp.take(parent_locals, parent_local, axis=0),
        preferred_element_type=jnp.float32,
    )
    slot_count = far_pairs.shape[0]
    far_owner = far_pairs[:, 0] - first_leaf
    far_partner = far_pairs[:, 1]
    is_live = (far_partner >= 0)[:, None, None]
    owner_moments = jnp.take(moments, far_owner, axis=0)
    moments_flat = moments.reshape(leaf_count, width)
    backward_far = jnp.where(
        is_live,
        jnp.einsum("sjk,srj->srk", far_coupling, owner_moments, preferred_element_type=jnp.float32),
        0.0,
    )
    picker = make_bucket_picker(far_partner)
    partner_moments = picker(
        jnp.zeros((slot_count, width), jnp.float32),
        lax.all_gather(moments_flat, "sfc", axis=0, tiled=True),
        jnp.int32(0),
    )
    partner_moments = partner_moments.astype(jnp.bfloat16).reshape(slot_count, rhs_count, rank)
    terms = make_bucket_terms(far_partner, backward_far.reshape(slot_count, width))
    far_back = lax.psum_scatter(
        terms(jnp.int32(0), leaf_count * lax.axis_size("sfc")),
        "sfc",
        scatter_dimension=0,
        tiled=True,
    )
    forward_far = jnp.where(
        is_live,
        jnp.einsum(
            "skj,srj->srk", far_coupling, partner_moments, preferred_element_type=jnp.float32
        ),
        0.0,
    )
    far_own = one_hot_rows(far_owner, leaf_count, forward_far.reshape(slot_count, width))
    leaf_locals = (far_own + far_back).reshape(leaf_count, rhs_count, rank)
    locals_all = (leaf_locals + downward).astype(jnp.bfloat16)
    potentials = jnp.einsum("lkp,lrk->lrp", bases, locals_all, preferred_element_type=jnp.float32)
    return potentials + self_terms + near_sums[:leaf_count] + returned_near


def solution(mesh):
    placed = (
        P(("grp", "sfc"), None, None),
        P(("grp", "sfc"), None, None),
        P(("grp", "sfc"), None, None),
        P(("grp", "sfc"), None),
        P(("grp", "sfc"), None, None),
        P(("grp", "sfc"), None, None),
        P(("grp", "sfc")),
        P(("grp", "sfc"), None),
        P(("grp", "sfc"), None, None),
        P(("grp", "sfc"), None),
        P(("grp", "sfc"), None, None),
    )
    return jax.shard_map(
        on_device,
        mesh=mesh,
        in_specs=placed,
        out_specs=P(("grp", "sfc"), None, None),
        check_vma=False,
    )
```

profile of v0, /device:TPU:0, one launch (start us, length us, event | category | flops | bytes accessed | tf_op | source)
XLA Modules:
  0.0 145.8 jit_solution(4989152166957759216)
XLA Ops:
  6.5 1.6 %collective-permute-start = (bf16[16,8,256]{2,1,0:T(8,128)(2,1)}, bf16[16,8,256]{2,1,0:T(8,128)(2,1)}, u32[]{:S(2)}, u32[]{:S(2)}) collective-permute-start(bf16[16,8,256]{2,1,0:T(8,128)(2,1)} %param.11), channel_id=1, source_target_pairs={{1,0},{2,1},{3,2},{4,3},{5,4},{6,5},{7,6},{8,7},{9,8},{10,9},{11,1... | collective-permute-start | bytes 196616 | tf_op jit(solution)/shard_map/ppermute | solution.py:10
  8.1 1.3 fusion.66
  9.4 1.2 and_bitcast_fusion.4
  10.6 1.3 convolution_convert_fusion
  11.9 0.7 compare_and_fusion
  12.6 1.2 fusion.70
  13.8 0.1 reshape.129
  13.9 0.1 convolution_convert_fusion.1
  14.1 0.6 gather_fusion.3
  14.7 1.3 fusion.25
  16.1 0.1 reshape.204
  16.2 1.0 scatter_custom_fusion.1
  17.1 0.7 slice.63
  18.0 0.7 gather_fusion.1
  18.7 3.8 %copy.16 = bf16[128,64,64]{2,1,0:T(8,128)(2,1)} copy(bf16[128,64,64]{0,2,1:T(8,128)(2,1)S(1)} %copy-done.4) | data formatting | bytes 2097152 | tf_op args[8]
  22.5 2.3 %convolution_select_fusion = f32[128,8,64]{2,1,0:T(8,128)S(1)} fusion(bf16[128,64,64]{2,1,0:T(8,128)(2,1)} %copy.16, bf16[128,8,64]{2,1,0:T(8,128)(2,1)S(1)} %gather_fusion.1, pred[128]{0:T(512)(128)(4,1)S(1)} %get-tuple-element.21, pred[128]{0:T(512)(128)(4,1)S(1)} %get-tuple-element.23), kind=kOutput, calls=%fused_computation.10 | convolution fusion | flops 8519680 | bytes 1442048 | tf_op jit(solution)/shard_map/sjk,srj->srk/dot_general | solution.py:160
  24.8 0.2 copy.19
  25.0 0.1 copy.20
  25.2 1.4 scatter_custom_fusion
  26.6 0.8 slice.62
  27.5 0.1 reshape.125
  27.6 24.1 %all_gather.7 = bf16[128,512]{1,0:T(8,128)(2,1)S(1)} all-gather(bf16[8,512]{1,0:T(8,128)(2,1)S(1)} %convolution_convert_fusion.1), channel_id=1, replica_groups=mesh['grp'=2,'sfc'=16] {'sfc'}, dimensions={0}, use_global_device_ids=true | all-gather | bytes 139264 | tf_op jit(solution)/shard_map/all_gather | solution.py:123
  51.7 18.2 %all_gather.6 = bf16[256,512]{1,0:T(8,128)(2,1)S(1)} all-gather(bf16[16,512]{1,0:T(8,128)(2,1)S(1)} %reshape.125), channel_id=1, replica_groups=mesh['grp'=2,'sfc'=16] {'sfc'}, dimensions={0}, use_global_device_ids=true | all-gather | bytes 278528 | tf_op jit(solution)/shard_map/all_gather | solution.py:166
  69.9 0.8 gather_fusion
  70.7 0.1 copy.14
  70.9 0.2 copy.15
  71.1 3.7 %convolution_select_fusion.1 = f32[128,8,64]{2,1,0:T(8,128)} fusion(bf16[128,64,64]{2,1,0:T(8,128)(2,1)} %copy.16, bf16[128,8,64]{2,1,0:T(8,128)(2,1)S(1)} %copy.15, pred[128]{0:T(512)(128)(4,1)S(1)} %get-tuple-element.22, pred[128]{0:T(512)(128)(4,1)S(1)} %get-tuple-element.20, pred[128]{0:T(512)(128)(4,1)S(1)} %get-tuple-element.23), kind=kOutput, calls=%fused_computation.11 | convolution fusion | flops 8716288 | bytes 1442176 | tf_op jit(solution)/shard_map/skj,srj->srk/dot_general | solution.py:179
  74.8 1.2 copy.17
  76.0 0.6 gather_fusion.2
  76.7 0.1 gather.36
  76.8 0.4 fusion.22
  77.2 0.1 reshape.130
  77.4 0.6 gather_fusion.6
  77.9 2.9 %fusion.14 = f32[32,8,256]{2,1,0:T(8,128)S(1)} fusion(bf16[32,256,256]{2,1,0:T(8,128)(2,1)} %param.13, bf16[32,8,256]{2,1,0:T(8,128)(2,1)S(1)} %gather_fusion.6, pred[32]{0:T(512)(128)(4,1)S(1)} %get-tuple-element.28), kind=kOutput, calls=%fused_computation.34 | convolution fusion | flops 33619968 | bytes 4587552 | tf_op jit(solution)/shard_map/spq,srp->srq/dot_general | solution.py:102
  80.8 0.8 copy.22
  81.6 0.6 fusion.71
  82.3 0.9 pad_maximum_fusion
  83.2 0.6 gather_fusion.5
  83.7 3.4 %fusion.16 = f32[32,8,256]{2,1,0:T(8,128)S(1)} fusion(bf16[32,256,256]{2,1,0:T(8,128)(2,1)} %param.13, bf16[32,8,256]{2,1,0:T(8,128)(2,1)S(1)} %gather_fusion.5, pred[32]{0:T(512)(128)(4,1)S(1)} %get-tuple-element.29), kind=kOutput, calls=%fused_computation.36 | convolution fusion | flops 33619968 | bytes 4587552 | tf_op jit(solution)/shard_map/spq,srq->srp/dot_general | solution.py:96
  87.3 0.3 fusion.40
  87.6 0.3 convolution_add_fusion
  87.9 0.7 copy.24
  88.6 2.9 %collective-permute-start.1 = (f32[16,8,256]{2,1,0:T(8,128)}, f32[16,8,256]{2,1,0:T(8,128)}, u32[]{:S(2)}, u32[]{:S(2)}) collective-permute-start(f32[16,8,256]{2,1,0:T(8,128)} %bitcast.31), channel_id=1, source_target_pairs={{0,1},{1,2},{2,3},{3,4},{4,5},{5,6},{6,7},{7,8},{8,9},{9,10},{10,1... | collective-permute-start | bytes 393224 | tf_op jit(solution)/shard_map/ppermute | solution.py:10
  91.5 0.9 fusion.3
  92.5 0.6 gather_fusion.4
  93.1 42.8 %reduce-scatter.3.cloned.1.call-done = f32[16,512]{1,0:T(8,128)} async-done(((f32[256,512]{1,0:T(8,128)}), f32[16,512]{1,0:T(8,128)}) %reduce-scatter.3.cloned.1.call-update) | async-done | bytes 32784 | tf_op jit(solution)/shard_map/reduce_scatter | solution.py:171
  135.9 1.0 convolution_add_fusion.3
  137.0 1.9 %fusion.1 = f32[16,8,256]{2,1,0:T(8,128)} fusion(f32[16,8,256]{2,1,0:T(8,128)} %collective-permute-done.1, f32[16,8,256]{2,1,0:T(8,128)S(1)} %bitcast.78, f32[16,8,256]{2,1,0:T(8,128)S(1)} %fusion.71, bf16[16,64,256]{2,1,0:T(8,128)(2,1)S(1)} %copy-done.1, f32[16,8,64]{2,1,0:T(8,128)S(1)} %reshape.128, bf16[16,64,64]{2,1,0:T(8,128)(2,1)S(1)} %copy-done.5, ...), kind=kOutput, calls=%fused_computation.14 | convolution fusion | flops 5365760 | bytes 1228816 | tf_op jit(solution)/shard_map/lkp,lrk->lrp/dot_general | solution.py:187
  (45 shorter events, 0.7 us)
Async XLA Ops:
  6.5 75.1 %copy-start = (bf16[16,256,256]{2,1,0:T(8,128)(2,1)S(1)}, bf16[16,256,256]{2,1,0:T(8,128)(2,1)}, u32[]{:S(2)}) copy-start(bf16[16,256,256]{2,1,0:T(8,128)(2,1)} %param.12) | copy-start | bytes 6291460
  6.5 11.4 %copy-start.7 = (s32[128,2]{0,1:T(2,128)S(1)}, s32[128,2]{0,1:T(2,128)}, u32[]{:S(2)}) copy-start(s32[128,2]{0,1:T(2,128)} %param.18) | copy-start | bytes 3076
  6.5 12.2 %copy-start.4 = (bf16[128,64,64]{0,2,1:T(8,128)(2,1)S(1)}, bf16[128,64,64]{0,2,1:T(8,128)(2,1)}, u32[]{:S(2)}) copy-start(bf16[128,64,64]{0,2,1:T(8,128)(2,1)} %param.19) | copy-start | bytes 3145732
  6.5 85.0 %reduce-scatter.5.cloned.1.call-start = ((), (), s32[]{:S(2)}) async-start(), calls=%async_computation.3 | async-start | bytes 278528 | tf_op jit(solution)/shard_map/reduce_scatter | solution.py:135
  6.5 75.7 %collective-permute-start = (bf16[16,8,256]{2,1,0:T(8,128)(2,1)}, bf16[16,8,256]{2,1,0:T(8,128)(2,1)}, u32[]{:S(2)}, u32[]{:S(2)}) collective-permute-start(bf16[16,8,256]{2,1,0:T(8,128)(2,1)} %param.11), channel_id=1, source_target_pairs={{1,0},{2,1},{3,2},{4,3},{5,4},{6,5},{7,6},{8,7},{9,8},{10,9},{11,1... | collective-permute-start | bytes 196616 | tf_op jit(solution)/shard_map/ppermute | solution.py:10
  17.9 118.0 %reduce-scatter.3.cloned.1.call-start = ((), (), s32[]{:S(2)}) async-start(), calls=%async_computation.2 | async-start | bytes 557056 | tf_op jit(solution)/shard_map/reduce_scatter | solution.py:171
  24.8 26.9 %copy-start.8 = (s32[32,2]{0,1:T(2,128)S(1)}, s32[32,2]{0,1:T(2,128)}, u32[]{:S(2)}) copy-start(s32[32,2]{0,1:T(2,128)} %param.14) | copy-start | bytes 772
  71.1 5.7 %copy-start.2 = (bf16[32,64,64]{2,1,0:T(8,128)(2,1)S(1)}, bf16[32,64,64]{2,1,0:T(8,128)(2,1)}, u32[]{:S(2)}) copy-start(bf16[32,64,64]{2,1,0:T(8,128)(2,1)} %param.21) | copy-start | bytes 786436
  71.1 5.7 %copy-start.9 = (pred[32]{0:T(512)(128)(4,1)S(1)}, pred[32]{0:T(512)(128)(4,1)}, u32[]{:S(2)}) copy-start(pred[32]{0:T(512)(128)(4,1)} %get-tuple-element.15) | copy-start | bytes 100
  71.1 6.3 %copy-start.3 = (bf16[16,8,256]{2,1,0:T(8,128)(2,1)S(1)}, bf16[16,8,256]{2,1,0:T(8,128)(2,1)}, u32[]{:S(2)}) copy-start(bf16[16,8,256]{2,1,0:T(8,128)(2,1)} %param.11) | copy-start | bytes 196612
  83.7 3.8 %copy-start.6 = (f32[4,8,8,256]{3,1,2,0:T(8,128)S(1)}, f32[4,8,8,256]{3,1,2,0:T(8,128)}, u32[]{:S(2)}) copy-start(f32[4,8,8,256]{3,1,2,0:T(8,128)} %copy.22) | copy-start | bytes 786436
  87.2 49.8 %copy-start.1 = (bf16[16,64,256]{2,1,0:T(8,128)(2,1)S(1)}, bf16[16,64,256]{2,1,0:T(8,128)(2,1)}, u32[]{:S(2)}) copy-start(bf16[16,64,256]{2,1,0:T(8,128)(2,1)} %param.15) | copy-start | bytes 1572868
  87.2 49.8 %copy-start.5 = (bf16[16,64,64]{2,1,0:T(8,128)(2,1)S(1)}, bf16[16,64,64]{2,1,0:T(8,128)(2,1)}, u32[]{:S(2)}) copy-start(bf16[16,64,64]{2,1,0:T(8,128)(2,1)} %param.16) | copy-start | bytes 393220
  88.6 48.5 %collective-permute-start.1 = (f32[16,8,256]{2,1,0:T(8,128)}, f32[16,8,256]{2,1,0:T(8,128)}, u32[]{:S(2)}, u32[]{:S(2)}) collective-permute-start(f32[16,8,256]{2,1,0:T(8,128)} %bitcast.31), channel_id=1, source_target_pairs={{0,1},{1,2},{2,3},{3,4},{4,5},{5,6},{6,7},{7,8},{8,9},{9,10},{10,1... | collective-permute-start | bytes 393224 | tf_op jit(solution)/shard_map/ppermute | solution.py:10
Sparse Core Ops, SparseCore 0:
  18.0 59.4 reduce-scatter.4
  81.0 54.8 reduce-scatter.2
where the time goes:
time: 146 us
  waiting for transfers between devices  42.9 us (29%)
  blocking collectives  42.3 us (29%)
  matrix products  21.6 us (15%)
  local copies, waits for them, and re-layouts  14.2 us (10%)
  between operations  13.7 us (9%)
  other arithmetic  6.53 us (4%)
  starting transfers between devices  4.5 us (3%)
    reduce_scatter x1, waiting for transfers between devices, on_device(): lax.psum_scatter(terms(jnp.int32(0), leaf_count * lax.axis_size('sfc')),...  42.8 us
    all_gather x1, blocking collectives, on_device(): lax.all_gather(parent_flat, 'sfc', axis=0, tiled=True)  24.1 us
    all_gather x1, blocking collectives, on_device(): lax.all_gather(moments_flat, 'sfc', axis=0, tiled=True)  18.2 us
    unnamed x25, local copies, waits for them, and re-layouts  5.48 us
    ppermute x2, starting transfers between devices, passed_along(): lax.ppermute(value, axis, [(source, source + steps) for source in range(l...  4.46 us
    dot_general x1, matrix products, on_device(): jnp.einsum('skj,srj->srk', far_coupling, partner_moments, preferred_eleme...  3.7 us
    dot_general x1, matrix products, on_device(): jnp.einsum('spq,srq->srp', near_blocks, jnp.take(extended, near_partner,...  3.44 us
  transfers between devices with their start and end apart: 4, of which 1 were waited for; matrix products, arithmetic and copies ran while one was open for 28% of the time, Pallas kernels for 0%

commit v1 on v0

v1 whole, which is shorter than its diff:
```python
import functools

import jax
import jax.numpy as jnp
from jax import lax
from jax.experimental import pallas as pl
from jax.experimental.pallas import tpu as pltpu
from jax.sharding import PartitionSpec as P

F32 = jnp.float32
BF16 = jnp.bfloat16
LANES = 128


def dot_nn(a, b):
    return lax.dot_general(a, b, (((1,), (0,)), ((), ())), preferred_element_type=F32)


def dot_nt(a, b):
    return lax.dot_general(a, b, (((1,), (1,)), ((), ())), preferred_element_type=F32)


def dot_tn(a, b):
    return lax.dot_general(a, b, (((0,), (0,)), ((), ())), preferred_element_type=F32)


def split2(x):
    high = x.astype(BF16)
    return high, (x - high.astype(F32)).astype(BF16)


def iota(shape, axis):
    return lax.broadcasted_iota(jnp.int32, shape, axis)


def one_hot(condition):
    return jnp.where(condition, 1.0, 0.0).astype(BF16)


def rows_to_lanes(ref, count, rhs):
    return jnp.concatenate([ref[pl.ds(r, count, stride=rhs), :] for r in range(rhs)], axis=1)


def lanes_to_rows(ref, value, rhs):
    count, width = value.shape
    rank = width // rhs
    for r in range(rhs):
        ref[pl.ds(r, count, stride=rhs), :] = value[:, r * rank : (r + 1) * rank]


def pre_kernel(
    par_smem,
    charges,
    bases,
    transfers,
    parent_of,
    far_pairs,
    far_c,
    par_pairs,
    par_c,
    send,
    mo,
    ch,
    pm3,
    pb,
    a_ref,
    ob,
):
    leaves, rhs, _ = charges.shape
    rank = bases.shape[1]
    width = rhs * rank
    slots = far_c.shape[2]
    pairs = par_c.shape[0]
    parents = leaves // 2
    rows = send.shape[0]

    for l in range(leaves):
        m = dot_nt(charges[l], bases[l]).astype(BF16)
        mo[l * rhs : (l + 1) * rhs, :] = m.astype(F32)
        ch[l * rhs : (l + 1) * rhs, :] = dot_nt(m, transfers[l])
    m2 = rows_to_lanes(mo, leaves, rhs)
    high, low = split2(rows_to_lanes(ch, leaves, rhs))
    par_hot = one_hot(parent_of[...] % parents == iota((parents, leaves), 0))
    pm = (dot_nn(par_hot, high) + dot_nn(par_hot, low)).astype(BF16).astype(F32)
    lanes_to_rows(pm3, pm, rhs)
    shared = jnp.concatenate([m2[:parents], m2[parents:], pm], axis=1)
    shared = jnp.concatenate([shared, shared], axis=0).astype(BF16)
    at = 2 * width + LANES
    for p in range(rows // (2 * parents)):
        send[p * 2 * parents : (p + 1) * 2 * parents, at : at + 3 * width] = shared

    owner_hot = one_hot(far_pairs[0:1, :] % leaves == iota((leaves, slots), 0))
    a_ref[...] = dot_tn(m2.astype(BF16), owner_hot)
    half = rank // 2
    for sb in range(slots // LANES):
        lanes = slice(sb * LANES, (sb + 1) * LANES)
        for jh in range(2):

            def body(k8, acc):
                rows_a = [
                    a_ref[pl.ds(pl.multiple_of(r * rank + k8 * 8, 8), 8), lanes]
                    for r in range(rhs)
                ]
                for i in range(8):
                    c = far_c[k8 * 8 + i, jh * half : (jh + 1) * half, lanes].astype(F32)
                    acc = tuple(acc[r] + c * rows_a[r][i : i + 1, :] for r in range(rhs))
                return acc

            acc = lax.fori_loop(
                0, rank // 8, body, tuple(jnp.zeros((half, LANES), F32) for _ in range(rhs))
            )
            for r in range(rhs):
                first = r * rank + jh * half
                ob[first : first + half, lanes] = acc[r].astype(BF16)
    partner = far_pairs[1:2, :]
    local = jnp.where(partner >= 0, partner % leaves, -1).astype(F32)
    ob[width : width + LANES, :] = jnp.broadcast_to(local, (LANES, slots)).astype(BF16)
    unit = one_hot(iota((LANES, LANES), 0) == iota((LANES, LANES), 1))
    for sb in range(slots // LANES):
        lanes = slice(sb * LANES, (sb + 1) * LANES)
        send[lanes, 0 : width + LANES] = dot_nt(unit, ob[:, lanes]).astype(BF16)

    for s in range(pairs):
        q = par_smem[0, s] % parents
        x = pm3[pl.ds(pl.multiple_of(q * rhs, rhs), rhs), :].astype(BF16)
        pb[s * rhs : (s + 1) * rhs, :] = dot_nn(x, par_c[s])
    high, low = split2(rows_to_lanes(pb, pairs, rhs))
    hot = one_hot(par_pairs[1:2, :] == iota((rows, pairs), 0))
    at = width + LANES
    send[:, at : at + width] = (dot_nn(hot, high) + dot_nn(hot, low)).astype(BF16)


def near_kernel(pairs, charges, following, self_blocks, near_blocks, own, away, ext, out):
    leaves = charges.shape[0]
    step = pl.program_id(0)
    selves, nears = self_blocks.shape[0], near_blocks.shape[0]

    @pl.when(step == 0)
    def _():
        ext[0:leaves] = charges[...]
        ext[leaves:] = following[...]
        out[...] = jnp.zeros_like(out)

    for i in range(selves):
        l = step * selves + i
        out[l] += dot_nt(ext[l], self_blocks[i])
    for i in range(nears):
        s = step * nears + i
        a, b = pairs[0, s], pairs[1, s]
        first = (a // leaves) * leaves
        a, b = a - first, b - first
        out[a] += dot_nt(ext[b], near_blocks[i])
        out[b] += dot_nn(ext[a], near_blocks[i])

    @pl.when(step == pl.num_programs(0) - 1)
    def _():
        own[...] = out[0:leaves]
        away[...] = out[leaves:].astype(BF16)


def post_kernel(
    got,
    bases,
    transfers,
    parent_of,
    far_pairs,
    far_c,
    par_pairs,
    par_c,
    near_own,
    near_back,
    out,
    b_ref,
    fw,
    g_ref,
    pf,
    lf,
    pg,
):
    leaves, rank, _ = bases.shape
    slots = far_c.shape[2]
    pairs = par_c.shape[0]
    parents = leaves // 2
    rows = got.shape[0]
    rhs = b_ref.shape[0] // rank
    width = rhs * rank
    at_par = width + LANES
    at_mom = at_par + width

    row_id = iota((rows, slots), 0)
    base_leaf = row_id // parents * leaves + row_id % parents
    partner = far_pairs[1:2, :]
    total = None
    for h in range(2):
        hot = one_hot(partner == base_leaf + h * parents)
        part = dot_tn(got[:, at_mom + h * width : at_mom + (h + 1) * width], hot)
        total = part if total is None else total + part
    b_ref[...] = total

    hot = one_hot(par_pairs[1:2, :] == iota((rows, pairs), 0))
    picked = dot_tn(hot, got[:, at_mom + 2 * width : at_mom + 3 * width])
    lanes_to_rows(g_ref, picked, rhs)
    for s in range(pairs):
        x = g_ref[s * rhs : (s + 1) * rhs, :].astype(BF16)
        pf[s * rhs : (s + 1) * rhs, :] = dot_nt(x, par_c[s])
    high, low = split2(rows_to_lanes(pf, pairs, rhs))
    hot = one_hot(par_pairs[0:1, :] % parents == iota((parents, pairs), 0))
    fold = one_hot(iota((parents, rows), 1) % parents == iota((parents, rows), 0))
    locals_p = dot_nn(hot, high) + dot_nn(hot, low) + dot_nn(fold, got[:, at_par : at_par + width])
    hot = one_hot(parent_of[...] % parents == iota((parents, leaves), 0))
    lanes_to_rows(pg, dot_tn(hot, locals_p.astype(BF16)), rhs)

    for sb in range(slots // LANES):
        lanes = slice(sb * LANES, (sb + 1) * LANES)

        def body(k8, carry):
            for r in range(rhs):
                b = b_ref[r * rank : (r + 1) * rank, lanes]
                sums = [
                    jnp.sum(far_c[k8 * 8 + i, :, lanes].astype(F32) * b, axis=0, keepdims=True)
                    for i in range(8)
                ]
                fw[pl.ds(pl.multiple_of(r * rank + k8 * 8, 8), 8), lanes] = jnp.concatenate(
                    sums, axis=0
                )
            return carry

        lax.fori_loop(0, rank // 8, body, 0)

    hot = one_hot(far_pairs[0:1, :] % leaves == iota((leaves, slots), 0))
    high, low = split2(fw[...])
    leaf = dot_nt(hot, high) + dot_nt(hot, low)
    index = got[:, width : width + LANES].astype(F32)[:, :leaves].astype(jnp.int32)
    hot = one_hot(index == iota((rows, leaves), 1))
    leaf = leaf + dot_tn(hot, got[:, 0:width])
    lanes_to_rows(lf, leaf, rhs)

    for l in range(leaves):
        at = slice(l * rhs, (l + 1) * rhs)
        down = dot_nn(pg[at, :].astype(BF16), transfers[l])
        mine = (lf[at, :] + down).astype(BF16)
        out[l] = dot_nn(mine, bases[l]) + near_own[l] + near_back[l].astype(F32)


def passed_along(value, axis, steps):
    count = lax.axis_size(axis)
    leading, last = (max(0, -steps), min(count, count - steps))
    return lax.ppermute(value, axis, [(source, source + steps) for source in range(leading, last)])


def on_device(
    charges,
    self_blocks,
    near_blocks,
    near_pairs,
    bases,
    transfers,
    parent_of,
    far_pairs,
    far_coupling,
    par_pairs,
    par_coupling,
):
    leaves, rhs, panels = charges.shape
    rank = bases.shape[1]
    width = rhs * rank
    slots = far_coupling.shape[0]
    pairs = par_coupling.shape[0]
    parents = leaves // 2
    devices = lax.axis_size("sfc")
    rows = devices * parents
    columns = 5 * width + LANES
    vmem = pl.BlockSpec(memory_space=pltpu.VMEM)
    smem = pl.BlockSpec(memory_space=pltpu.SMEM)
    params = pltpu.CompilerParams(vmem_limit_bytes=48 * 1024 * 1024)

    following = passed_along(charges, "sfc", -1)
    far_pairs = far_pairs.T
    par_pairs = par_pairs.T
    near_pairs = near_pairs.T
    far_c = jnp.transpose(far_coupling, (1, 2, 0))
    parent_of = parent_of.reshape(1, leaves)

    send = pl.pallas_call(
        pre_kernel,
        out_shape=jax.ShapeDtypeStruct((rows, columns), BF16),
        in_specs=[smem] + [vmem] * 8,
        out_specs=vmem,
        scratch_shapes=[
            pltpu.VMEM((leaves * rhs, rank), F32),
            pltpu.VMEM((leaves * rhs, rank), F32),
            pltpu.VMEM((parents * rhs, rank), F32),
            pltpu.VMEM((pairs * rhs, rank), F32),
            pltpu.VMEM((width, slots), F32),
            pltpu.VMEM((width + LANES, slots), BF16),
        ],
        compiler_params=params,
        name="upward",
    )(par_pairs, charges, bases, transfers, parent_of, far_pairs, far_c, par_pairs, par_coupling)
    got = lax.all_to_all(send, "sfc", split_axis=0, concat_axis=0, tiled=True)

    steps = 8
    selves, nears = leaves // steps, near_blocks.shape[0] // steps
    whole = lambda *shape: pl.BlockSpec(shape, lambda i: (0,) * len(shape))
    near_own, near_away = pl.pallas_call(
        near_kernel,
        grid=(steps,),
        out_shape=[
            jax.ShapeDtypeStruct((leaves, rhs, panels), F32),
            jax.ShapeDtypeStruct((leaves, rhs, panels), BF16),
        ],
        in_specs=[
            smem,
            whole(leaves, rhs, panels),
            whole(leaves, rhs, panels),
            pl.BlockSpec((selves, panels, panels), lambda i: (i, 0, 0)),
            pl.BlockSpec((nears, panels, panels), lambda i: (i, 0, 0)),
        ],
        out_specs=[whole(leaves, rhs, panels)] * 2,
        scratch_shapes=[
            pltpu.VMEM((2 * leaves, rhs, panels), BF16),
            pltpu.VMEM((2 * leaves, rhs, panels), F32),
        ],
        compiler_params=params,
        name="near",
    )(near_pairs, charges, following, self_blocks, near_blocks)
    near_back = passed_along(near_away, "sfc", 1)

    return pl.pallas_call(
        post_kernel,
        out_shape=jax.ShapeDtypeStruct((leaves, rhs, panels), F32),
        in_specs=[vmem] * 10,
        out_specs=vmem,
        scratch_shapes=[
            pltpu.VMEM((width, slots), F32),
            pltpu.VMEM((width, slots), F32),
            pltpu.VMEM((pairs * rhs, rank), F32),
            pltpu.VMEM((pairs * rhs, rank), F32),
            pltpu.VMEM((leaves * rhs, rank), F32),
            pltpu.VMEM((leaves * rhs, rank), F32),
        ],
        compiler_params=params,
        name="downward",
    )(
        got,
        bases,
        transfers,
        parent_of,
        far_pairs,
        far_c,
        par_pairs,
        par_coupling,
        near_own,
        near_back,
    )


def solution(mesh):
    split = ("grp", "sfc")
    cube, flat = P(split, None, None), P(split, None)
    placed = (cube, cube, cube, flat, cube, cube, P(split), flat, cube, flat, cube)
    return jax.shard_map(
        on_device, mesh=mesh, in_specs=placed, out_specs=cube, check_vma=False
    )
```

time: 146 us -> 53.7 us (0.37)
  the two profiles are of different devices: /device:TPU:0 before, /device:TPU:16 now
where the time goes in v1:
time: 53.7 us; the launch traced here: 53 us
  waiting for transfers between devices  17.9 us (33%)
  Pallas kernels  15 us (28%)
  starting transfers between devices  11.4 us (21%)
  local copies, waits for them, and re-layouts  8.75 us (16%)
    ppermute x2, waiting for transfers between devices, passed_along(): lax.ppermute(value, axis, [(source, source + steps) for source in range(l...  17.8 us
    unnamed x36, local copies, waits for them, and re-layouts  8.75 us
    pallas_call x1, Pallas kernels, on_device(): pl.pallas_call(near_kernel, grid=(steps,), out_shape=[jax.ShapeDtypeStruc...  6.37 us
    all_to_all x1, starting transfers between devices, on_device(): got = lax.all_to_all(send, 'sfc', split_axis=0, concat_axis=0, tiled=True)  6.33 us
    ppermute x2, starting transfers between devices, passed_along(): lax.ppermute(value, axis, [(source, source + steps) for source in range(l...  5.04 us
    pallas_call x1, Pallas kernels, on_device(): pl.pallas_call(post_kernel, out_shape=jax.ShapeDtypeStruct((leaves, rhs,...  4.41 us
    pallas_call x1, Pallas kernels, on_device(): pl.pallas_call(pre_kernel, out_shape=jax.ShapeDtypeStruct((rows, columns)...  4.17 us
  transfers between devices with their start and end apart: 3, of which 2 were waited for; matrix products, arithmetic and copies ran while one was open for 0% of the time, Pallas kernels for 12%

profile of v1, /device:TPU:16, one launch (start us, length us, event | category | flops | bytes accessed | tf_op | source)
XLA Modules:
  0.0 53.0 jit_solution(4730191797145534917)
XLA Ops:
  0.0 0.0 copy-start.17
  0.0 0.0 copy-start
  0.0 1.2 %copy-done = bf16[128,64,64]{0,2,1:T(8,128)(2,1)S(1)} copy-done((bf16[128,64,64]{0,2,1:T(8,128)(2,1)S(1)}, bf16[128,64,64]{0,2,1:T(8,128)(2,1)}, u32[]{:S(2)}) %copy-start) | copy-done | bytes 1048600
  1.2 0.0 copy-start.3
  1.2 1.0 %copy-done.3 = bf16[16,64,256]{2,1,0:T(8,128)(2,1)S(1)} copy-done((bf16[16,64,256]{2,1,0:T(8,128)(2,1)S(1)}, bf16[16,64,256]{2,1,0:T(8,128)(2,1)}, u32[]{:S(2)}) %copy-start.3) | copy-done | bytes 524312
  2.3 0.0 copy-start.5
  2.3 1.0 %copy-done.5 = bf16[32,64,64]{2,1,0:T(8,128)(2,1)S(1)} copy-done((bf16[32,64,64]{2,1,0:T(8,128)(2,1)S(1)}, bf16[32,64,64]{2,1,0:T(8,128)(2,1)}, u32[]{:S(2)}) %copy-start.5) | copy-done | bytes 262168
  3.3 0.0 copy-start.7
  3.3 0.9 %copy-done.7 = bf16[16,64,64]{2,1,0:T(8,128)(2,1)S(1)} copy-done((bf16[16,64,64]{2,1,0:T(8,128)(2,1)S(1)}, bf16[16,64,64]{2,1,0:T(8,128)(2,1)}, u32[]{:S(2)}) %copy-start.7) | copy-done | bytes 131096
  4.3 0.0 copy-start.9
  4.3 0.8 %copy-done.9 = bf16[16,8,256]{2,1,0:T(8,128)(2,1)S(1)} copy-done((bf16[16,8,256]{2,1,0:T(8,128)(2,1)S(1)}, bf16[16,8,256]{2,1,0:T(8,128)(2,1)}, u32[]{:S(2)}) %copy-start.9) | copy-done | bytes 65560
  5.1 0.0 copy-start.11
  5.1 0.7 %copy-done.11 = s32[32,2]{0,1:T(2,128)S(1)} copy-done((s32[32,2]{0,1:T(2,128)S(1)}, s32[32,2]{0,1:T(2,128)}, u32[]{:S(2)}) %copy-start.11) | copy-done | bytes 280
  5.8 0.0 copy-start.13
  5.8 0.7 %copy-done.13 = s32[128,2]{0,1:T(2,128)S(1)} copy-done((s32[128,2]{0,1:T(2,128)S(1)}, s32[128,2]{0,1:T(2,128)}, u32[]{:S(2)}) %copy-start.13) | copy-done | bytes 1048
  6.5 0.0 copy-start.15
  6.5 0.7 %copy-done.15 = s32[16]{0:T(128)S(1)} copy-done((s32[16]{0:T(128)S(1)}, s32[16]{0:T(128)}, u32[]{:S(2)}) %copy-start.15) | copy-done | bytes 88
  7.1 0.0 copy-start.10
  7.1 0.0 copy-start.4
  7.1 0.0 copy-start.6
  7.1 4.2 %upward.1 = bf16[128,2688]{1,0:T(8,128)(2,1)} custom-call(s32[2,32]{1,0:T(2,128)S(1)} %bitcast.10, bf16[16,8,256]{2,1,0:T(8,128)(2,1)S(1)} %copy-done.9, bf16[16,64,256]{2,1,0:T(8,128)(2,1)S(1)} %copy-done.3, bf16[16,64,64]{2,1,0:T(8,128)(2,1)S(1)} %copy-done.7, s32[1,16]{1,0:T(1,128)S(1)} %bitcast.15, s32[2,128]{1,0:T(2,128)S(1)} %bitcast.13, ...), custom_call_target="tpu_custom_call" | custom-call | tf_op jit(solution)/shard_map/upward/pallas_call | solution.py:284
  11.3 0.0 copy-start.1
  11.3 0.0 copy-start.8
  11.3 0.0 copy-start.12
  11.3 0.0 copy-start.14
  11.3 0.0 copy-start.16
  11.3 6.3 %all-to-all-start = ((bf16[16,8,2688]{2,1,0:T(8,128)(2,1)}), bf16[16,8,2688]{2,1,0:T(8,128)(2,1)S(1)}, u32[]{:S(2)}, u32[]{:S(2)}) async-start(bf16[16,8,2688]{2,1,0:T(8,128)(2,1)} %bitcast.4), calls=%async_computation | async-start | bytes 1376256 | tf_op jit(solution)/shard_map/all_to_all | solution.py:300
  17.7 0.0 copy-done.10
  17.7 3.1 %collective-permute-start = (bf16[16,8,256]{2,1,0:T(8,128)(2,1)S(1)}, bf16[16,8,256]{2,1,0:T(8,128)(2,1)S(1)}, u32[]{:S(2)}, u32[]{:S(2)}) collective-permute-start(bf16[16,8,256]{2,1,0:T(8,128)(2,1)S(1)} %copy-done.10), channel_id=1, source_target_pairs={{1,0},{2,1},{3,2},{4,3},{5,4},{6,5},{7,6},{8,7},{9,8},{10,9},{11,1... | collective-permute-start | bytes 196616 | tf_op jit(solution)/shard_map/ppermute | solution.py:248
  20.8 13.1 %collective-permute-done.following = bf16[16,8,256]{2,1,0:T(8,128)(2,1)S(1)} collective-permute-done((bf16[16,8,256]{2,1,0:T(8,128)(2,1)S(1)}, bf16[16,8,256]{2,1,0:T(8,128)(2,1)S(1)}, u32[]{:S(2)}, u32[]{:S(2)}) %collective-permute-start) | collective-permute-done | bytes 65568 | tf_op jit(solution)/shard_map/ppermute | solution.py:248
  33.9 0.0 copy-done.17
  33.9 0.0 copy-start.2
  33.9 1.6 %copy-done.2 = bf16[16,256,256]{2,1,0:T(8,128)(2,1)S(1)} copy-done((bf16[16,256,256]{2,1,0:T(8,128)(2,1)S(1)}, bf16[16,256,256]{2,1,0:T(8,128)(2,1)}, u32[]{:S(2)}) %copy-start.2) | copy-done | bytes 2097176
  35.5 6.4 %near.1 = (f32[16,8,256]{2,1,0:T(8,128)S(1)}, bf16[16,8,256]{2,1,0:T(8,128)(2,1)S(1)}) custom-call(s32[2,32]{1,0:T(2,128)S(1)} %bitcast.17, bf16[16,8,256]{2,1,0:T(8,128)(2,1)S(1)} %copy-done.10, bf16[16,8,256]{2,1,0:T(8,128)(2,1)S(1)} %collective-permute-done.following, bf16[16,256,256]{2,1,0:T(8,128)(2,1)S(1)} %copy-done.2, bf16[32,256,256]{2,1,0:T(8,128)(2,1)} %near_blocks.1), custom_call_target="tpu_custom_call" | custom-call | tf_op jit(solution)/shard_map/near/pallas_call | solution.py:305
  41.9 1.9 %collective-permute-start.1 = (bf16[16,8,256]{2,1,0:T(8,128)(2,1)S(1)}, bf16[16,8,256]{2,1,0:T(8,128)(2,1)S(1)}, u32[]{:S(2)}, u32[]{:S(2)}) collective-permute-start(bf16[16,8,256]{2,1,0:T(8,128)(2,1)S(1)} %get-tuple-element.8), channel_id=1, source_target_pairs={{0,1},{1,2},{2,3},{3,4},{4,5},{5,6},{6,7},{7,8},{8,9},{9,10},{10,1... | collective-permute-start | bytes 196616 | tf_op jit(solution)/shard_map/ppermute | solution.py:248
  43.8 4.7 %collective-permute-done.1.near_back = bf16[16,8,256]{2,1,0:T(8,128)(2,1)S(1)} collective-permute-done((bf16[16,8,256]{2,1,0:T(8,128)(2,1)S(1)}, bf16[16,8,256]{2,1,0:T(8,128)(2,1)S(1)}, u32[]{:S(2)}, u32[]{:S(2)}) %collective-permute-start.1) | collective-permute-done | bytes 65568 | tf_op jit(solution)/shard_map/ppermute | solution.py:248
  48.5 0.0 all-to-all-done
  48.6 0.0 copy-done.4
  48.6 0.0 copy-done.6
  48.6 0.0 copy-done.1
  48.6 0.0 copy-done.8
  48.6 0.0 copy-done.12
  48.6 0.0 copy-done.14
  48.6 0.0 copy-done.16
  48.6 4.4 %downward.1 = f32[16,8,256]{2,1,0:T(8,128)} custom-call(bf16[128,2688]{1,0:T(8,128)(2,1)S(1)} %bitcast.9, bf16[16,64,256]{2,1,0:T(8,128)(2,1)S(1)} %copy-done.4, bf16[16,64,64]{2,1,0:T(8,128)(2,1)S(1)} %copy-done.8, s32[1,16]{1,0:T(1,128)S(1)} %bitcast.16, s32[2,128]{1,0:T(2,128)S(1)} %bitcast.14, bf16[64,64,128]{2,1,0:T(8,128)(2,1)S(1)} %bitcast.8, ...), custom_call_target="tpu_custom_call" | custom-call | tf_op jit(solution)/shard_map/downward/pallas_call | solution.py:329
Async XLA Ops:
  0.0 33.9 %copy-start.17 = (s32[32,2]{0,1:T(2,128)S(1)}, s32[32,2]{0,1:T(2,128)}, u32[]{:S(2)}) copy-start(s32[32,2]{0,1:T(2,128)} %param.14) | copy-start | bytes 772
  0.0 1.2 %copy-start = (bf16[128,64,64]{0,2,1:T(8,128)(2,1)S(1)}, bf16[128,64,64]{0,2,1:T(8,128)(2,1)}, u32[]{:S(2)}) copy-start(bf16[128,64,64]{0,2,1:T(8,128)(2,1)} %param.19) | copy-start | bytes 3145732
  1.2 1.0 %copy-start.3 = (bf16[16,64,256]{2,1,0:T(8,128)(2,1)S(1)}, bf16[16,64,256]{2,1,0:T(8,128)(2,1)}, u32[]{:S(2)}) copy-start(bf16[16,64,256]{2,1,0:T(8,128)(2,1)} %bases.3) | copy-start | bytes 1572868
  2.3 1.0 %copy-start.5 = (bf16[32,64,64]{2,1,0:T(8,128)(2,1)S(1)}, bf16[32,64,64]{2,1,0:T(8,128)(2,1)}, u32[]{:S(2)}) copy-start(bf16[32,64,64]{2,1,0:T(8,128)(2,1)} %par_c.3) | copy-start | bytes 786436
  3.3 0.9 %copy-start.7 = (bf16[16,64,64]{2,1,0:T(8,128)(2,1)S(1)}, bf16[16,64,64]{2,1,0:T(8,128)(2,1)}, u32[]{:S(2)}) copy-start(bf16[16,64,64]{2,1,0:T(8,128)(2,1)} %transfers.3) | copy-start | bytes 393220
  4.3 0.8 %copy-start.9 = (bf16[16,8,256]{2,1,0:T(8,128)(2,1)S(1)}, bf16[16,8,256]{2,1,0:T(8,128)(2,1)}, u32[]{:S(2)}) copy-start(bf16[16,8,256]{2,1,0:T(8,128)(2,1)} %charges.3) | copy-start | bytes 196612
  5.1 0.7 %copy-start.11 = (s32[32,2]{0,1:T(2,128)S(1)}, s32[32,2]{0,1:T(2,128)}, u32[]{:S(2)}) copy-start(s32[32,2]{0,1:T(2,128)} %param.20) | copy-start | bytes 772
  5.8 0.7 %copy-start.13 = (s32[128,2]{0,1:T(2,128)S(1)}, s32[128,2]{0,1:T(2,128)}, u32[]{:S(2)}) copy-start(s32[128,2]{0,1:T(2,128)} %param.18) | copy-start | bytes 3076
  6.5 0.7 %copy-start.15 = (s32[16]{0:T(128)S(1)}, s32[16]{0:T(128)}, u32[]{:S(2)}) copy-start(s32[16]{0:T(128)} %param.17) | copy-start | bytes 196
  7.1 10.5 %copy-start.10 = (bf16[16,8,256]{2,1,0:T(8,128)(2,1)S(1)}, bf16[16,8,256]{2,1,0:T(8,128)(2,1)}, u32[]{:S(2)}) copy-start(bf16[16,8,256]{2,1,0:T(8,128)(2,1)} %charges.3) | copy-start | bytes 196612
  7.1 41.4 %copy-start.4 = (bf16[16,64,256]{2,1,0:T(8,128)(2,1)S(1)}, bf16[16,64,256]{2,1,0:T(8,128)(2,1)}, u32[]{:S(2)}) copy-start(bf16[16,64,256]{2,1,0:T(8,128)(2,1)} %bases.3) | copy-start | bytes 1572868
  7.1 41.4 %copy-start.6 = (bf16[32,64,64]{2,1,0:T(8,128)(2,1)S(1)}, bf16[32,64,64]{2,1,0:T(8,128)(2,1)}, u32[]{:S(2)}) copy-start(bf16[32,64,64]{2,1,0:T(8,128)(2,1)} %par_c.3) | copy-start | bytes 786436
  11.3 37.3 %copy-start.1 = (bf16[128,64,64]{0,2,1:T(8,128)(2,1)S(1)}, bf16[128,64,64]{0,2,1:T(8,128)(2,1)}, u32[]{:S(2)}) copy-start(bf16[128,64,64]{0,2,1:T(8,128)(2,1)} %param.19) | copy-start | bytes 3145732
  11.3 37.3 %copy-start.8 = (bf16[16,64,64]{2,1,0:T(8,128)(2,1)S(1)}, bf16[16,64,64]{2,1,0:T(8,128)(2,1)}, u32[]{:S(2)}) copy-start(bf16[16,64,64]{2,1,0:T(8,128)(2,1)} %transfers.3) | copy-start | bytes 393220
  11.3 37.3 %copy-start.12 = (s32[32,2]{0,1:T(2,128)S(1)}, s32[32,2]{0,1:T(2,128)}, u32[]{:S(2)}) copy-start(s32[32,2]{0,1:T(2,128)} %param.20) | copy-start | bytes 772
  11.3 37.3 %copy-start.14 = (s32[128,2]{0,1:T(2,128)S(1)}, s32[128,2]{0,1:T(2,128)}, u32[]{:S(2)}) copy-start(s32[128,2]{0,1:T(2,128)} %param.18) | copy-start | bytes 3076
  11.3 37.3 %copy-start.16 = (s32[16]{0:T(128)S(1)}, s32[16]{0:T(128)}, u32[]{:S(2)}) copy-start(s32[16]{0:T(128)} %param.17) | copy-start | bytes 196
  11.3 37.2 %all-to-all-start = ((bf16[16,8,2688]{2,1,0:T(8,128)(2,1)}), bf16[16,8,2688]{2,1,0:T(8,128)(2,1)S(1)}, u32[]{:S(2)}, u32[]{:S(2)}) async-start(bf16[16,8,2688]{2,1,0:T(8,128)(2,1)} %bitcast.4), calls=%async_computation | async-start | bytes 1376256 | tf_op jit(solution)/shard_map/all_to_all | solution.py:300
  17.7 16.2 %collective-permute-start = (bf16[16,8,256]{2,1,0:T(8,128)(2,1)S(1)}, bf16[16,8,256]{2,1,0:T(8,128)(2,1)S(1)}, u32[]{:S(2)}, u32[]{:S(2)}) collective-permute-start(bf16[16,8,256]{2,1,0:T(8,128)(2,1)S(1)} %copy-done.10), channel_id=1, source_target_pairs={{1,0},{2,1},{3,2},{4,3},{5,4},{6,5},{7,6},{8,7},{9,8},{10,9},{11,1... | collective-permute-start | bytes 196616 | tf_op jit(solution)/shard_map/ppermute | solution.py:248
  33.9 1.6 %copy-start.2 = (bf16[16,256,256]{2,1,0:T(8,128)(2,1)S(1)}, bf16[16,256,256]{2,1,0:T(8,128)(2,1)}, u32[]{:S(2)}) copy-start(bf16[16,256,256]{2,1,0:T(8,128)(2,1)} %self_blocks.1) | copy-start | bytes 6291460
  41.9 6.7 %collective-permute-start.1 = (bf16[16,8,256]{2,1,0:T(8,128)(2,1)S(1)}, bf16[16,8,256]{2,1,0:T(8,128)(2,1)S(1)}, u32[]{:S(2)}, u32[]{:S(2)}) collective-permute-start(bf16[16,8,256]{2,1,0:T(8,128)(2,1)S(1)} %get-tuple-element.8), channel_id=1, source_target_pairs={{0,1},{1,2},{2,3},{3,4},{4,5},{5,6},{6,7},{7,8},{8,9},{9,10},{10,1... | collective-permute-start | bytes 196616 | tf_op jit(solution)/shard_map/ppermute | solution.py:248

commit v2 on v1

--- a/solution.py
+++ b/solution.py
@@ -48,8 +48,23 @@
         ref[pl.ds(r, count, stride=rhs), :] = value[:, r * rank : (r + 1) * rank]
 
 
+def fetch(pairs, sems):
+    copies = [pltpu.make_async_copy(src, dst, sems.at[i]) for i, (src, dst) in enumerate(pairs)]
+    for copy in copies:
+        copy.start()
+    return copies
+
+
 def pre_kernel(
-    par_smem,
+    charges_h,
+    bases_h,
+    transfers_h,
+    parent_of_h,
+    far_pairs_h,
+    far_c_h,
+    par_pairs_h,
+    par_c_h,
+    send,
     charges,
     bases,
     transfers,
@@ -58,7 +73,8 @@
     far_c,
     par_pairs,
     par_c,
-    send,
+    par_smem,
+    sems,
     mo,
     ch,
     pm3,
@@ -73,11 +89,29 @@
     pairs = par_c.shape[0]
     parents = leaves // 2
     rows = send.shape[0]
+    copies = fetch(
+        [
+            (charges_h, charges),
+            (bases_h, bases),
+            (transfers_h, transfers),
+            (parent_of_h, parent_of),
+            (far_pairs_h, far_pairs),
+            (par_pairs_h, par_pairs),
+            (par_pairs_h, par_smem),
+            (far_c_h, far_c),
+            (par_c_h, par_c),
+        ],
+        sems,
+    )
+    for copy in copies[:3]:
+        copy.wait()
 
     for l in range(leaves):
         m = dot_nt(charges[l], bases[l]).astype(BF16)
         mo[l * rhs : (l + 1) * rhs, :] = m.astype(F32)
         ch[l * rhs : (l + 1) * rhs, :] = dot_nt(m, transfers[l])
+    for copy in copies[3:]:
+        copy.wait()
     m2 = rows_to_lanes(mo, leaves, rhs)
     high, low = split2(rows_to_lanes(ch, leaves, rhs))
     par_hot = one_hot(parent_of[...] % parents == iota((parents, leaves), 0))
@@ -141,16 +175,15 @@
         ext[leaves:] = following[...]
         out[...] = jnp.zeros_like(out)
 
-    for i in range(selves):
-        l = step * selves + i
-        out[l] += dot_nt(ext[l], self_blocks[i])
+    terms = [(step * selves + i, dot_nt(ext[step * selves + i], self_blocks[i])) for i in range(selves)]
     for i in range(nears):
-        s = step * nears + i
-        a, b = pairs[0, s], pairs[1, s]
+        a, b = pairs[0, step * nears + i], pairs[1, step * nears + i]
         first = (a // leaves) * leaves
         a, b = a - first, b - first
-        out[a] += dot_nt(ext[b], near_blocks[i])
-        out[b] += dot_nn(ext[a], near_blocks[i])
+        terms.append((a, dot_nt(ext[b], near_blocks[i])))
+        terms.append((b, dot_nn(ext[a], near_blocks[i])))
+    for at, term in terms:
+        out[at] += term
 
     @pl.when(step == pl.num_programs(0) - 1)
     def _():
@@ -159,7 +192,17 @@
 
 
 def post_kernel(
+    bases_h,
+    transfers_h,
+    parent_of_h,
+    far_pairs_h,
+    far_c_h,
+    par_pairs_h,
+    par_c_h,
     got,
+    near_own,
+    near_back,
+    out,
     bases,
     transfers,
     parent_of,
@@ -167,9 +210,7 @@
     far_c,
     par_pairs,
     par_c,
-    near_own,
-    near_back,
-    out,
+    sems,
     b_ref,
     fw,
     g_ref,
@@ -186,6 +227,20 @@
     width = rhs * rank
     at_par = width + LANES
     at_mom = at_par + width
+    copies = fetch(
+        [
+            (far_pairs_h, far_pairs),
+            (par_pairs_h, par_pairs),
+            (parent_of_h, parent_of),
+            (par_c_h, par_c),
+            (far_c_h, far_c),
+            (transfers_h, transfers),
+            (bases_h, bases),
+        ],
+        sems,
+    )
+    for copy in copies:
+        copy.wait()
 
     row_id = iota((rows, slots), 0)
     base_leaf = row_id // parents * leaves + row_id % parents
@@ -272,7 +327,8 @@
     columns = 5 * width + LANES
     vmem = pl.BlockSpec(memory_space=pltpu.VMEM)
     smem = pl.BlockSpec(memory_space=pltpu.SMEM)
-    params = pltpu.CompilerParams(vmem_limit_bytes=48 * 1024 * 1024)
+    hbm = pl.BlockSpec(memory_space=pltpu.HBM)
+    params = pltpu.CompilerParams(vmem_limit_bytes=60 * 1024 * 1024)
 
     following = passed_along(charges, "sfc", -1)
     far_pairs = far_pairs.T
@@ -281,12 +337,25 @@
     far_c = jnp.transpose(far_coupling, (1, 2, 0))
     parent_of = parent_of.reshape(1, leaves)
 
+    def like(value, memory=pltpu.VMEM):
+        return memory(value.shape, value.dtype)
+
     send = pl.pallas_call(
         pre_kernel,
         out_shape=jax.ShapeDtypeStruct((rows, columns), BF16),
-        in_specs=[smem] + [vmem] * 8,
+        in_specs=[hbm] * 8,
         out_specs=vmem,
         scratch_shapes=[
+            like(charges),
+            like(bases),
+            like(transfers),
+            like(parent_of),
+            like(far_pairs),
+            like(far_c),
+            like(par_pairs),
+            like(par_coupling),
+            like(par_pairs, pltpu.SMEM),
+            pltpu.SemaphoreType.DMA((9,)),
             pltpu.VMEM((leaves * rhs, rank), F32),
             pltpu.VMEM((leaves * rhs, rank), F32),
             pltpu.VMEM((parents * rhs, rank), F32),
@@ -296,7 +365,7 @@
         ],
         compiler_params=params,
         name="upward",
-    )(par_pairs, charges, bases, transfers, parent_of, far_pairs, far_c, par_pairs, par_coupling)
+    )(charges, bases, transfers, parent_of, far_pairs, far_c, par_pairs, par_coupling)
     got = lax.all_to_all(send, "sfc", split_axis=0, concat_axis=0, tiled=True)
 
     steps = 8
@@ -329,9 +398,17 @@
     return pl.pallas_call(
         post_kernel,
         out_shape=jax.ShapeDtypeStruct((leaves, rhs, panels), F32),
-        in_specs=[vmem] * 10,
+        in_specs=[hbm] * 7 + [vmem] * 3,
         out_specs=vmem,
         scratch_shapes=[
+            like(bases),
+            like(transfers),
+            like(parent_of),
+            like(far_pairs),
+            like(far_c),
+            like(par_pairs),
+            like(par_coupling),
+            pltpu.SemaphoreType.DMA((7,)),
             pltpu.VMEM((width, slots), F32),
             pltpu.VMEM((width, slots), F32),
             pltpu.VMEM((pairs * rhs, rank), F32),
@@ -342,7 +419,6 @@
         compiler_params=params,
         name="downward",
     )(
-        got,
         bases,
         transfers,
         parent_of,
@@ -350,6 +426,7 @@
         far_c,
         par_pairs,
         par_coupling,
+        got,
         near_own,
         near_back,
     )

time: 53.7 us -> 50.6 us (0.942)
  the two profiles are of different devices: /device:TPU:16 before, /device:TPU:18 now
where the time goes in v2:
time: 50.6 us; the launch traced here: 50.2 us
  Pallas kernels  19.4 us (38%)
  waiting for transfers between devices  18 us (36%)
  starting transfers between devices  11.2 us (22%)
  local copies, waits for them, and re-layouts  1.51 us (3%)
    ppermute x2, waiting for transfers between devices, passed_along(): lax.ppermute(value, axis, [(source, source + steps) for source in range(l...  18 us
    pallas_call x1, Pallas kernels, on_device(): pl.pallas_call(near_kernel, grid=(steps,), out_shape=[jax.ShapeDtypeStruc...  7.44 us
    pallas_call x1, Pallas kernels, on_device(): pl.pallas_call(post_kernel, out_shape=jax.ShapeDtypeStruct((leaves, rhs,...  7.03 us
    all_to_all x1, starting transfers between devices, on_device(): got = lax.all_to_all(send, 'sfc', split_axis=0, concat_axis=0, tiled=True)  6.2 us
    ppermute x2, starting transfers between devices, passed_along(): lax.ppermute(value, axis, [(source, source + steps) for source in range(l...  5.03 us
    pallas_call x1, Pallas kernels, on_device(): pl.pallas_call(pre_kernel, out_shape=jax.ShapeDtypeStruct((rows, columns)...  4.9 us
    unnamed x8, local copies, waits for them, and re-layouts  1.51 us
  transfers between devices with their start and end apart: 3, of which 2 were waited for; matrix products, arithmetic and copies ran while one was open for 0% of the time, Pallas kernels for 15%

profile of v2, /device:TPU:18, one launch (start us, length us, event | category | flops | bytes accessed | tf_op | source)
XLA Modules:
  0.0 50.2 jit_solution(11186492179820537232)
XLA Ops:
  0.0 0.0 copy-start.1
  0.0 4.9 %upward.1 = bf16[128,2688]{1,0:T(8,128)(2,1)} custom-call(bf16[16,8,256]{2,1,0:T(8,128)(2,1)} %charges.1, bf16[16,64,256]{2,1,0:T(8,128)(2,1)} %bases_h.3, bf16[16,64,64]{2,1,0:T(8,128)(2,1)} %transfers_h.3, s32[1,16]{1,0:T(1,128)} %bitcast.15, s32[2,128]{1,0:T(2,128)} %bitcast.11, bf16[64,64,128]{2,1,0:T(8,128)(2,1)} %bitcast.7, s32[2,32]{1,0:T(2,128)} %bitcast.13, ...), custom_call_target="tpu_custom_call" | custom-call | tf_op jit(solution)/shard_map/upward/pallas_call | solution.py:343
  4.9 6.2 %all-to-all-start = ((bf16[16,8,2688]{2,1,0:T(8,128)(2,1)}), bf16[16,8,2688]{2,1,0:T(8,128)(2,1)S(1)}, u32[]{:S(2)}, u32[]{:S(2)}) async-start(bf16[16,8,2688]{2,1,0:T(8,128)(2,1)} %bitcast.10), calls=%async_computation | async-start | bytes 1376256 | tf_op jit(solution)/shard_map/all_to_all | solution.py:369
  11.1 0.0 copy-done.1
  11.1 3.1 %collective-permute-start = (bf16[16,8,256]{2,1,0:T(8,128)(2,1)S(1)}, bf16[16,8,256]{2,1,0:T(8,128)(2,1)S(1)}, u32[]{:S(2)}, u32[]{:S(2)}) collective-permute-start(bf16[16,8,256]{2,1,0:T(8,128)(2,1)S(1)} %copy-done.1), channel_id=1, source_target_pairs={{1,0},{2,1},{3,2},{4,3},{5,4},{6,5},{7,6},{8,7},{9,8},{10,9},{11,1... | collective-permute-start | bytes 196616 | tf_op jit(solution)/shard_map/ppermute | solution.py:303
  14.2 13.1 %collective-permute-done.following = bf16[16,8,256]{2,1,0:T(8,128)(2,1)S(1)} collective-permute-done((bf16[16,8,256]{2,1,0:T(8,128)(2,1)S(1)}, bf16[16,8,256]{2,1,0:T(8,128)(2,1)S(1)}, u32[]{:S(2)}, u32[]{:S(2)}) %collective-permute-start) | collective-permute-done | bytes 65568 | tf_op jit(solution)/shard_map/ppermute | solution.py:303
  27.3 0.0 copy-start.2
  27.4 0.6 %copy-done.2 = bf16[16,8,256]{2,1,0:T(8,128)(2,1)} copy-done((bf16[16,8,256]{2,1,0:T(8,128)(2,1)}, bf16[16,8,256]{2,1,0:T(8,128)(2,1)S(1)}, u32[]{:S(2)}) %copy-start.2) | copy-done | bytes 65560
  28.0 7.4 %near.1 = (f32[16,8,256]{2,1,0:T(8,128)}, bf16[16,8,256]{2,1,0:T(8,128)(2,1)}) custom-call(s32[2,32]{1,0:T(2,128)} %bitcast.17, bf16[16,8,256]{2,1,0:T(8,128)(2,1)} %charges.1, bf16[16,8,256]{2,1,0:T(8,128)(2,1)} %copy-done.2, bf16[16,256,256]{2,1,0:T(8,128)(2,1)} %self_blocks.1, bf16[32,256,256]{2,1,0:T(8,128)(2,1)} %near_blocks.1), custom_call_target="tpu_custom_call" | custom-call | tf_op jit(solution)/shard_map/near/pallas_call | solution.py:374
  35.4 1.9 %collective-permute-start.1 = (bf16[16,8,256]{2,1,0:T(8,128)(2,1)}, bf16[16,8,256]{2,1,0:T(8,128)(2,1)S(1)}, u32[]{:S(2)}, u32[]{:S(2)}) collective-permute-start(bf16[16,8,256]{2,1,0:T(8,128)(2,1)} %get-tuple-element.8), channel_id=1, source_target_pairs={{0,1},{1,2},{2,3},{3,4},{4,5},{5,6},{6,7},{7,8},{8,9},{9,10},{10,1... | collective-permute-start | bytes 196616 | tf_op jit(solution)/shard_map/ppermute | solution.py:303
  37.3 4.9 %collective-permute-done.1.near_back = bf16[16,8,256]{2,1,0:T(8,128)(2,1)S(1)} collective-permute-done((bf16[16,8,256]{2,1,0:T(8,128)(2,1)}, bf16[16,8,256]{2,1,0:T(8,128)(2,1)S(1)}, u32[]{:S(2)}, u32[]{:S(2)}) %collective-permute-start.1) | collective-permute-done | bytes 65568 | tf_op jit(solution)/shard_map/ppermute | solution.py:303
  42.3 0.0 copy-start.3
  42.3 0.0 all-to-all-done
  42.3 0.0 copy-start
  42.3 0.6 %copy-done.3 = bf16[16,8,256]{2,1,0:T(8,128)(2,1)} copy-done((bf16[16,8,256]{2,1,0:T(8,128)(2,1)}, bf16[16,8,256]{2,1,0:T(8,128)(2,1)S(1)}, u32[]{:S(2)}) %copy-start.3) | copy-done | bytes 65560
  42.9 0.2 copy-done
  43.2 7.0 %downward.1 = f32[16,8,256]{2,1,0:T(8,128)} custom-call(bf16[16,64,256]{2,1,0:T(8,128)(2,1)} %bases_h.3, bf16[16,64,64]{2,1,0:T(8,128)(2,1)} %transfers_h.3, s32[1,16]{1,0:T(1,128)} %bitcast.16, s32[2,128]{1,0:T(2,128)} %bitcast.12, bf16[64,64,128]{2,1,0:T(8,128)(2,1)} %bitcast.8, s32[2,32]{1,0:T(2,128)} %bitcast.14, bf16[32,64,64]{2,1,0:T(8,128)(2,1)} %par_c_h.3, ...), custom_call_target="tpu_custom_call" | custom-call | tf_op jit(solution)/shard_map/downward/pallas_call | solution.py:398
Async XLA Ops:
  0.0 11.1 %copy-start.1 = (bf16[16,8,256]{2,1,0:T(8,128)(2,1)S(1)}, bf16[16,8,256]{2,1,0:T(8,128)(2,1)}, u32[]{:S(2)}) copy-start(bf16[16,8,256]{2,1,0:T(8,128)(2,1)} %charges.1) | copy-start | bytes 196612
  4.9 37.4 %all-to-all-start = ((bf16[16,8,2688]{2,1,0:T(8,128)(2,1)}), bf16[16,8,2688]{2,1,0:T(8,128)(2,1)S(1)}, u32[]{:S(2)}, u32[]{:S(2)}) async-start(bf16[16,8,2688]{2,1,0:T(8,128)(2,1)} %bitcast.10), calls=%async_computation | async-start | bytes 1376256 | tf_op jit(solution)/shard_map/all_to_all | solution.py:369
  11.1 16.2 %collective-permute-start = (bf16[16,8,256]{2,1,0:T(8,128)(2,1)S(1)}, bf16[16,8,256]{2,1,0:T(8,128)(2,1)S(1)}, u32[]{:S(2)}, u32[]{:S(2)}) collective-permute-start(bf16[16,8,256]{2,1,0:T(8,128)(2,1)S(1)} %copy-done.1), channel_id=1, source_target_pairs={{1,0},{2,1},{3,2},{4,3},{5,4},{6,5},{7,6},{8,7},{9,8},{10,9},{11,1... | collective-permute-start | bytes 196616 | tf_op jit(solution)/shard_map/ppermute | solution.py:303
  27.3 0.6 %copy-start.2 = (bf16[16,8,256]{2,1,0:T(8,128)(2,1)}, bf16[16,8,256]{2,1,0:T(8,128)(2,1)S(1)}, u32[]{:S(2)}) copy-start(bf16[16,8,256]{2,1,0:T(8,128)(2,1)S(1)} %collective-permute-done.following) | copy-start | bytes 196612
  35.4 6.9 %collective-permute-start.1 = (bf16[16,8,256]{2,1,0:T(8,128)(2,1)}, bf16[16,8,256]{2,1,0:T(8,128)(2,1)S(1)}, u32[]{:S(2)}, u32[]{:S(2)}) collective-permute-start(bf16[16,8,256]{2,1,0:T(8,128)(2,1)} %get-tuple-element.8), channel_id=1, source_target_pairs={{0,1},{1,2},{2,3},{3,4},{4,5},{5,6},{6,7},{7,8},{8,9},{9,10},{10,1... | collective-permute-start | bytes 196616 | tf_op jit(solution)/shard_map/ppermute | solution.py:303
  42.3 0.6 %copy-start.3 = (bf16[16,8,256]{2,1,0:T(8,128)(2,1)}, bf16[16,8,256]{2,1,0:T(8,128)(2,1)S(1)}, u32[]{:S(2)}) copy-start(bf16[16,8,256]{2,1,0:T(8,128)(2,1)S(1)} %collective-permute-done.1.near_back) | copy-start | bytes 196612
  42.3 0.9 %copy-start = (bf16[16,8,2688]{2,1,0:T(8,128)(2,1)}, bf16[16,8,2688]{2,1,0:T(8,128)(2,1)S(1)}, u32[]{:S(2)}) copy-start(bf16[16,8,2688]{2,1,0:T(8,128)(2,1)S(1)} %all-to-all-done) | copy-start | bytes 2064388

commit v3 on v2

--- a/solution.py
+++ b/solution.py
@@ -64,7 +64,12 @@
     far_c_h,
     par_pairs_h,
     par_c_h,
+    near_pairs_h,
+    near_h,
+    following_h,
     send,
+    back_own,
+    back_away,
     charges,
     bases,
     transfers,
@@ -74,6 +79,9 @@
     par_pairs,
     par_c,
     par_smem,
+    near_smem,
+    near_v,
+    back,
     sems,
     mo,
     ch,
@@ -100,6 +108,8 @@
             (par_pairs_h, par_smem),
             (far_c_h, far_c),
             (par_c_h, par_c),
+            (near_pairs_h, near_smem),
+            (near_h, near_v),
         ],
         sems,
     )
@@ -110,7 +120,7 @@
         m = dot_nt(charges[l], bases[l]).astype(BF16)
         mo[l * rhs : (l + 1) * rhs, :] = m.astype(F32)
         ch[l * rhs : (l + 1) * rhs, :] = dot_nt(m, transfers[l])
-    for copy in copies[3:]:
+    for copy in copies[3:-1]:
         copy.wait()
     m2 = rows_to_lanes(mo, leaves, rhs)
     high, low = split2(rows_to_lanes(ch, leaves, rhs))
@@ -125,12 +135,23 @@
 
     owner_hot = one_hot(far_pairs[0:1, :] % leaves == iota((leaves, slots), 0))
     a_ref[...] = dot_tn(m2.astype(BF16), owner_hot)
+    copies[-1].wait()
+    back[...] = jnp.zeros_like(back)
     half = rank // 2
+    trips = (slots // LANES) * 2 * (rank // 8)
+    nears = near_v.shape[0] // trips
     for sb in range(slots // LANES):
         lanes = slice(sb * LANES, (sb + 1) * LANES)
         for jh in range(2):
+            first_pair = (sb * 2 + jh) * (rank // 8) * nears
 
             def body(k8, acc):
+                terms = []
+                for i in range(nears):
+                    s = first_pair + k8 * nears + i
+                    a, b = near_smem[0, s], near_smem[1, s]
+                    first = (a // leaves) * leaves
+                    terms.append((b - first, dot_nn(charges[a - first], near_v[s])))
                 rows_a = [
                     a_ref[pl.ds(pl.multiple_of(r * rank + k8 * 8, 8), 8), lanes]
                     for r in range(rhs)
@@ -138,6 +159,8 @@
                 for i in range(8):
                     c = far_c[k8 * 8 + i, jh * half : (jh + 1) * half, lanes].astype(F32)
                     acc = tuple(acc[r] + c * rows_a[r][i : i + 1, :] for r in range(rhs))
+                for at, term in terms:
+                    back[at] += term
                 return acc
 
             acc = lax.fori_loop(
@@ -146,6 +169,12 @@
             for r in range(rhs):
                 first = r * rank + jh * half
                 ob[first : first + half, lanes] = acc[r].astype(BF16)
+    for s in range(nears * trips, near_v.shape[0]):
+        a, b = near_smem[0, s], near_smem[1, s]
+        first = (a // leaves) * leaves
+        back[b - first] += dot_nn(charges[a - first], near_v[s])
+    back_own[...] = back[0:leaves]
+    back_away[...] = back[leaves:].astype(BF16)
     partner = far_pairs[1:2, :]
     local = jnp.where(partner >= 0, partner % leaves, -1).astype(F32)
     ob[width : width + LANES, :] = jnp.broadcast_to(local, (LANES, slots)).astype(BF16)
@@ -164,7 +193,7 @@
     send[:, at : at + width] = (dot_nn(hot, high) + dot_nn(hot, low)).astype(BF16)
 
 
-def near_kernel(pairs, charges, following, self_blocks, near_blocks, own, away, ext, out):
+def near_kernel(pairs, charges, following, self_blocks, near_blocks, own, ext):
     leaves = charges.shape[0]
     step = pl.program_id(0)
     selves, nears = self_blocks.shape[0], near_blocks.shape[0]
@@ -173,22 +202,18 @@
     def _():
         ext[0:leaves] = charges[...]
         ext[leaves:] = following[...]
-        out[...] = jnp.zeros_like(out)
-
-    terms = [(step * selves + i, dot_nt(ext[step * selves + i], self_blocks[i])) for i in range(selves)]
+        own[...] = jnp.zeros_like(own)
+
+    terms = []
+    for i in range(selves):
+        l = step * selves + i
+        terms.append((l, dot_nt(ext[l], self_blocks[i])))
     for i in range(nears):
         a, b = pairs[0, step * nears + i], pairs[1, step * nears + i]
         first = (a // leaves) * leaves
-        a, b = a - first, b - first
-        terms.append((a, dot_nt(ext[b], near_blocks[i])))
-        terms.append((b, dot_nn(ext[a], near_blocks[i])))
+        terms.append((a - first, dot_nt(ext[b - first], near_blocks[i])))
     for at, term in terms:
-        out[at] += term
-
-    @pl.when(step == pl.num_programs(0) - 1)
-    def _():
-        own[...] = out[0:leaves]
-        away[...] = out[leaves:].astype(BF16)
+        own[at] += term
 
 
 def post_kernel(
@@ -199,9 +224,10 @@
     far_c_h,
     par_pairs_h,
     par_c_h,
-    got,
-    near_own,
-    near_back,
+    got_h,
+    near_own_h,
+    back_own_h,
+    near_back_h,
     out,
     bases,
     transfers,
@@ -210,6 +236,10 @@
     far_c,
     par_pairs,
     par_c,
+    got,
+    near_own,
+    back_own,
+    near_back,
     sems,
     b_ref,
     fw,
@@ -231,15 +261,19 @@
         [
             (far_pairs_h, far_pairs),
             (par_pairs_h, par_pairs),
+            (got_h, got),
             (parent_of_h, parent_of),
             (par_c_h, par_c),
             (far_c_h, far_c),
             (transfers_h, transfers),
             (bases_h, bases),
+            (near_own_h, near_own),
+            (back_own_h, back_own),
+            (near_back_h, near_back),
         ],
         sems,
     )
-    for copy in copies:
+    for copy in copies[:6]:
         copy.wait()
 
     row_id = iota((rows, slots), 0)
@@ -290,11 +324,14 @@
     leaf = leaf + dot_tn(hot, got[:, 0:width])
     lanes_to_rows(lf, leaf, rhs)
 
+    for copy in copies[6:]:
+        copy.wait()
     for l in range(leaves):
         at = slice(l * rhs, (l + 1) * rhs)
         down = dot_nn(pg[at, :].astype(BF16), transfers[l])
         mine = (lf[at, :] + down).astype(BF16)
-        out[l] = dot_nn(mine, bases[l]) + near_own[l] + near_back[l].astype(F32)
+        near = near_own[l] + back_own[l] + near_back[l].astype(F32)
+        out[l] = dot_nn(mine, bases[l]) + near
 
 
 def passed_along(value, axis, steps):
@@ -340,11 +377,15 @@
     def like(value, memory=pltpu.VMEM):
         return memory(value.shape, value.dtype)
 
-    send = pl.pallas_call(
+    send, back_own, back_away = pl.pallas_call(
         pre_kernel,
-        out_shape=jax.ShapeDtypeStruct((rows, columns), BF16),
-        in_specs=[hbm] * 8,
-        out_specs=vmem,
+        out_shape=[
+            jax.ShapeDtypeStruct((rows, columns), BF16),
+            jax.ShapeDtypeStruct((leaves, rhs, panels), F32),
+            jax.ShapeDtypeStruct((leaves, rhs, panels), BF16),
+        ],
+        in_specs=[hbm] * 11,
+        out_specs=[vmem] * 3,
         scratch_shapes=[
             like(charges),
             like(bases),
@@ -355,7 +396,10 @@
             like(par_pairs),
             like(par_coupling),
             like(par_pairs, pltpu.SMEM),
-            pltpu.SemaphoreType.DMA((9,)),
+            like(near_pairs, pltpu.SMEM),
+            like(near_blocks),
+            pltpu.VMEM((2 * leaves, rhs, panels), F32),
+            pltpu.SemaphoreType.DMA((11,)),
             pltpu.VMEM((leaves * rhs, rank), F32),
             pltpu.VMEM((leaves * rhs, rank), F32),
             pltpu.VMEM((parents * rhs, rank), F32),
@@ -365,19 +409,29 @@
         ],
         compiler_params=params,
         name="upward",
-    )(charges, bases, transfers, parent_of, far_pairs, far_c, par_pairs, par_coupling)
+    )(
+        charges,
+        bases,
+        transfers,
+        parent_of,
+        far_pairs,
+        far_c,
+        par_pairs,
+        par_coupling,
+        near_pairs,
+        near_blocks,
+        following,
+    )
+    near_back = passed_along(back_away, "sfc", 1)
     got = lax.all_to_all(send, "sfc", split_axis=0, concat_axis=0, tiled=True)
 
     steps = 8
     selves, nears = leaves // steps, near_blocks.shape[0] // steps
     whole = lambda *shape: pl.BlockSpec(shape, lambda i: (0,) * len(shape))
-    near_own, near_away = pl.pallas_call(
+    near_own = pl.pallas_call(
         near_kernel,
         grid=(steps,),
-        out_shape=[
-            jax.ShapeDtypeStruct((leaves, rhs, panels), F32),
-            jax.ShapeDtypeStruct((leaves, rhs, panels), BF16),
-        ],
+        out_shape=jax.ShapeDtypeStruct((leaves, rhs, panels), F32),
         in_specs=[
             smem,
             whole(leaves, rhs, panels),
@@ -385,20 +439,16 @@
             pl.BlockSpec((selves, panels, panels), lambda i: (i, 0, 0)),
             pl.BlockSpec((nears, panels, panels), lambda i: (i, 0, 0)),
         ],
-        out_specs=[whole(leaves, rhs, panels)] * 2,
-        scratch_shapes=[
-            pltpu.VMEM((2 * leaves, rhs, panels), BF16),
-            pltpu.VMEM((2 * leaves, rhs, panels), F32),
-        ],
+        out_specs=whole(leaves, rhs, panels),
+        scratch_shapes=[pltpu.VMEM((2 * leaves, rhs, panels), BF16)],
         compiler_params=params,
         name="near",
     )(near_pairs, charges, following, self_blocks, near_blocks)
-    near_back = passed_along(near_away, "sfc", 1)
 
     return pl.pallas_call(
         post_kernel,
         out_shape=jax.ShapeDtypeStruct((leaves, rhs, panels), F32),
-        in_specs=[hbm] * 7 + [vmem] * 3,
+        in_specs=[hbm] * 11,
         out_specs=vmem,
         scratch_shapes=[
             like(bases),
@@ -408,7 +458,11 @@
             like(far_c),
             like(par_pairs),
             like(par_coupling),
-            pltpu.SemaphoreType.DMA((7,)),
+            like(got),
+            like(near_own),
+            like(back_own),
+            like(near_back),
+            pltpu.SemaphoreType.DMA((11,)),
             pltpu.VMEM((width, slots), F32),
             pltpu.VMEM((width, slots), F32),
             pltpu.VMEM((pairs * rhs, rank), F32),
@@ -428,6 +482,7 @@
         par_coupling,
         got,
         near_own,
+        back_own,
         near_back,
     )
 

time: 50.6 us -> 45.3 us (0.90)
  the two profiles are of different devices: /device:TPU:18 before, /device:TPU:0 now
where the time goes in v3:
time: 45.3 us; the launch traced here: 44.9 us
  Pallas kernels  20.8 us (46%)
  starting transfers between devices  12.8 us (28%)
  waiting for transfers between devices  9.85 us (22%)
  local copies, waits for them, and re-layouts  1.47 us (3%)
    all_to_all x1, starting transfers between devices, on_device(): got = lax.all_to_all(send, 'sfc', split_axis=0, concat_axis=0, tiled=True)  9.17 us
    all_to_all x1, waiting for transfers between devices, on_device(): got = lax.all_to_all(send, 'sfc', split_axis=0, concat_axis=0, tiled=True)  7.79 us
    pallas_call x1, Pallas kernels, on_device(): pl.pallas_call(pre_kernel, out_shape=[jax.ShapeDtypeStruct((rows, columns...  7.77 us
    pallas_call x1, Pallas kernels, on_device(): pl.pallas_call(near_kernel, grid=(steps,), out_shape=jax.ShapeDtypeStruct...  7.02 us
    pallas_call x1, Pallas kernels, on_device(): pl.pallas_call(post_kernel, out_shape=jax.ShapeDtypeStruct((leaves, rhs,...  6.02 us
    ppermute x2, starting transfers between devices, passed_along(): lax.ppermute(value, axis, [(source, source + steps) for source in range(l...  3.58 us
    ppermute x2, waiting for transfers between devices, passed_along(): lax.ppermute(value, axis, [(source, source + steps) for source in range(l...  2.06 us
    unnamed x6, local copies, waits for them, and re-layouts  1.47 us
  transfers between devices with their start and end apart: 3, of which 2 were waited for; matrix products, arithmetic and copies ran while one was open for 0% of the time, Pallas kernels for 16%

profile of v3, /device:TPU:0, one launch (start us, length us, event | category | flops | bytes accessed | tf_op | source)
XLA Modules:
  0.0 44.9 jit_solution(9624243282329902028)
XLA Ops:
  0.0 1.3 %collective-permute-start = (bf16[16,8,256]{2,1,0:T(8,128)(2,1)}, bf16[16,8,256]{2,1,0:T(8,128)(2,1)S(1)}, u32[]{:S(2)}, u32[]{:S(2)}) collective-permute-start(bf16[16,8,256]{2,1,0:T(8,128)(2,1)} %charges.1), channel_id=1, source_target_pairs={{1,0},{2,1},{3,2},{4,3},{5,4},{6,5},{7,6},{8,7},{9,8},{10,9},{11,1... | collective-permute-start | bytes 196616 | tf_op jit(solution)/shard_map/ppermute | solution.py:340
  1.3 2.1 %collective-permute-done.following_h.following = bf16[16,8,256]{2,1,0:T(8,128)(2,1)S(1)} collective-permute-done((bf16[16,8,256]{2,1,0:T(8,128)(2,1)}, bf16[16,8,256]{2,1,0:T(8,128)(2,1)S(1)}, u32[]{:S(2)}, u32[]{:S(2)}) %collective-permute-start) | collective-permute-done | bytes 65568 | tf_op jit(solution)/shard_map/ppermute | solution.py:340
  3.4 0.0 copy-start.1
  3.4 0.6 %copy-done.1 = bf16[16,8,256]{2,1,0:T(8,128)(2,1)} copy-done((bf16[16,8,256]{2,1,0:T(8,128)(2,1)}, bf16[16,8,256]{2,1,0:T(8,128)(2,1)S(1)}, u32[]{:S(2)}) %copy-start.1) | copy-done | bytes 65560
  4.0 7.8 %upward.1 = (bf16[128,2688]{1,0:T(8,128)(2,1)}, f32[16,8,256]{2,1,0:T(8,128)}, bf16[16,8,256]{2,1,0:T(8,128)(2,1)}) custom-call(bf16[16,8,256]{2,1,0:T(8,128)(2,1)} %charges.1, bf16[16,64,256]{2,1,0:T(8,128)(2,1)} %bases_h.3, bf16[16,64,64]{2,1,0:T(8,128)(2,1)} %transfers_h.3, s32[1,16]{1,0:T(1,128)} %bitcast.17, s32[2,128]{1,0:T(2,128)} %bitcast.11, ...), custom_call_target="tpu_custom_call" | custom-call | tf_op jit(solution)/shard_map/upward/pallas_call | solution.py:380
  11.8 9.2 %all-to-all-start = ((bf16[16,8,2688]{2,1,0:T(8,128)(2,1)}), bf16[16,8,2688]{2,1,0:T(8,128)(2,1)S(1)}, u32[]{:S(2)}, u32[]{:S(2)}) async-start(bf16[16,8,2688]{2,1,0:T(8,128)(2,1)} %bitcast.10), calls=%async_computation | async-start | bytes 1376256 | tf_op jit(solution)/shard_map/all_to_all | solution.py:426
  20.9 2.3 %collective-permute-start.1 = (bf16[16,8,256]{2,1,0:T(8,128)(2,1)}, bf16[16,8,256]{2,1,0:T(8,128)(2,1)S(1)}, u32[]{:S(2)}, u32[]{:S(2)}) collective-permute-start(bf16[16,8,256]{2,1,0:T(8,128)(2,1)} %get-tuple-element.10), channel_id=1, source_target_pairs={{0,1},{1,2},{2,3},{3,4},{4,5},{5,6},{6,7},{7,8},{8,9},{9,10},{10,1... | collective-permute-start | bytes 196616 | tf_op jit(solution)/shard_map/ppermute | solution.py:340
  23.2 7.0 %near.1.near_own_h = f32[16,8,256]{2,1,0:T(8,128)} custom-call(s32[2,32]{1,0:T(2,128)} %bitcast.16, bf16[16,8,256]{2,1,0:T(8,128)(2,1)} %charges.1, bf16[16,8,256]{2,1,0:T(8,128)(2,1)} %copy-done.1, bf16[16,256,256]{2,1,0:T(8,128)(2,1)} %self_blocks.1, bf16[32,256,256]{2,1,0:T(8,128)(2,1)} %near_blocks.1), custom_call_target="tpu_custom_call" | custom-call | tf_op jit(solution)/shard_map/near/pallas_call | solution.py:431
  30.3 0.0 collective-permute-done.1.near_back_h
  30.3 0.0 copy-start.2
  30.3 7.8 %all-to-all-done = bf16[16,8,2688]{2,1,0:T(8,128)(2,1)S(1)} async-done(((bf16[16,8,2688]{2,1,0:T(8,128)(2,1)}), bf16[16,8,2688]{2,1,0:T(8,128)(2,1)S(1)}, u32[]{:S(2)}, u32[]{:S(2)}) %all-to-all-start) | async-done | bytes 688160 | tf_op jit(solution)/shard_map/all_to_all | solution.py:426
  38.1 0.0 copy-start
  38.1 0.0 copy-done.2
  38.1 0.8 %copy-done = bf16[16,8,2688]{2,1,0:T(8,128)(2,1)} copy-done((bf16[16,8,2688]{2,1,0:T(8,128)(2,1)}, bf16[16,8,2688]{2,1,0:T(8,128)(2,1)S(1)}, u32[]{:S(2)}) %copy-start) | copy-done | bytes 688152
  38.9 6.0 %downward.1 = f32[16,8,256]{2,1,0:T(8,128)} custom-call(bf16[16,64,256]{2,1,0:T(8,128)(2,1)} %bases_h.3, bf16[16,64,64]{2,1,0:T(8,128)(2,1)} %transfers_h.3, s32[1,16]{1,0:T(1,128)} %bitcast.18, s32[2,128]{1,0:T(2,128)} %bitcast.12, bf16[64,64,128]{2,1,0:T(8,128)(2,1)} %bitcast.8, s32[2,32]{1,0:T(2,128)} %bitcast.14, bf16[32,64,64]{2,1,0:T(8,128)(2,1)} %par_c_h.3, ...), custom_call_target="tpu_custom_call" | custom-call | tf_op jit(solution)/shard_map/downward/pallas_call | solution.py:448
Async XLA Ops:
  0.0 3.3 %collective-permute-start = (bf16[16,8,256]{2,1,0:T(8,128)(2,1)}, bf16[16,8,256]{2,1,0:T(8,128)(2,1)S(1)}, u32[]{:S(2)}, u32[]{:S(2)}) collective-permute-start(bf16[16,8,256]{2,1,0:T(8,128)(2,1)} %charges.1), channel_id=1, source_target_pairs={{1,0},{2,1},{3,2},{4,3},{5,4},{6,5},{7,6},{8,7},{9,8},{10,9},{11,1... | collective-permute-start | bytes 196616 | tf_op jit(solution)/shard_map/ppermute | solution.py:340
  3.4 0.6 %copy-start.1 = (bf16[16,8,256]{2,1,0:T(8,128)(2,1)}, bf16[16,8,256]{2,1,0:T(8,128)(2,1)S(1)}, u32[]{:S(2)}) copy-start(bf16[16,8,256]{2,1,0:T(8,128)(2,1)S(1)} %collective-permute-done.following_h.following) | copy-start | bytes 196612
  11.8 26.3 %all-to-all-start = ((bf16[16,8,2688]{2,1,0:T(8,128)(2,1)}), bf16[16,8,2688]{2,1,0:T(8,128)(2,1)S(1)}, u32[]{:S(2)}, u32[]{:S(2)}) async-start(bf16[16,8,2688]{2,1,0:T(8,128)(2,1)} %bitcast.10), calls=%async_computation | async-start | bytes 1376256 | tf_op jit(solution)/shard_map/all_to_all | solution.py:426
  20.9 9.3 %collective-permute-start.1 = (bf16[16,8,256]{2,1,0:T(8,128)(2,1)}, bf16[16,8,256]{2,1,0:T(8,128)(2,1)S(1)}, u32[]{:S(2)}, u32[]{:S(2)}) collective-permute-start(bf16[16,8,256]{2,1,0:T(8,128)(2,1)} %get-tuple-element.10), channel_id=1, source_target_pairs={{0,1},{1,2},{2,3},{3,4},{4,5},{5,6},{6,7},{7,8},{8,9},{9,10},{10,1... | collective-permute-start | bytes 196616 | tf_op jit(solution)/shard_map/ppermute | solution.py:340
  30.3 7.8 %copy-start.2 = (bf16[16,8,256]{2,1,0:T(8,128)(2,1)}, bf16[16,8,256]{2,1,0:T(8,128)(2,1)S(1)}, u32[]{:S(2)}) copy-start(bf16[16,8,256]{2,1,0:T(8,128)(2,1)S(1)} %collective-permute-done.1.near_back_h) | copy-start | bytes 196612
  38.1 0.8 %copy-start = (bf16[16,8,2688]{2,1,0:T(8,128)(2,1)}, bf16[16,8,2688]{2,1,0:T(8,128)(2,1)S(1)}, u32[]{:S(2)}) copy-start(bf16[16,8,2688]{2,1,0:T(8,128)(2,1)S(1)} %all-to-all-done) | copy-start | bytes 2064388

commit v4 on v3

--- a/solution.py
+++ b/solution.py
@@ -55,11 +55,50 @@
     return copies
 
 
-def pre_kernel(
+def moment_kernel(
     charges_h,
     bases_h,
     transfers_h,
     parent_of_h,
+    shared,
+    charges,
+    bases,
+    transfers,
+    parent_of,
+    sems,
+    mo,
+    ch,
+):
+    leaves, rhs, _ = charges.shape
+    parents = leaves // 2
+    copies = fetch(
+        [
+            (charges_h, charges),
+            (bases_h, bases),
+            (transfers_h, transfers),
+            (parent_of_h, parent_of),
+        ],
+        sems,
+    )
+    for copy in copies:
+        copy.wait()
+    for l in range(leaves):
+        m = dot_nt(charges[l], bases[l]).astype(BF16)
+        mo[l * rhs : (l + 1) * rhs, :] = m.astype(F32)
+        ch[l * rhs : (l + 1) * rhs, :] = dot_nt(m, transfers[l])
+    m2 = rows_to_lanes(mo, leaves, rhs)
+    high, low = split2(rows_to_lanes(ch, leaves, rhs))
+    par_hot = one_hot(parent_of[...] % parents == iota((parents, leaves), 0))
+    pm = dot_nn(par_hot, high) + dot_nn(par_hot, low)
+    block = jnp.concatenate([m2[:parents], m2[parents:], pm], axis=1)
+    block = jnp.concatenate([block, block], axis=0).astype(BF16)
+    for p in range(shared.shape[0] // (2 * parents)):
+        shared[p * 2 * parents : (p + 1) * 2 * parents, :] = block
+
+
+def back_kernel(
+    charges_h,
+    shared_h,
     far_pairs_h,
     far_c_h,
     par_pairs_h,
@@ -71,9 +110,7 @@
     back_own,
     back_away,
     charges,
-    bases,
-    transfers,
-    parent_of,
+    mine,
     far_pairs,
     far_c,
     par_pairs,
@@ -83,15 +120,13 @@
     near_v,
     back,
     sems,
-    mo,
-    ch,
     pm3,
     pb,
     a_ref,
     ob,
 ):
     leaves, rhs, _ = charges.shape
-    rank = bases.shape[1]
+    rank = far_c.shape[0]
     width = rhs * rank
     slots = far_c.shape[2]
     pairs = par_c.shape[0]
@@ -99,42 +134,34 @@
     rows = send.shape[0]
     copies = fetch(
         [
-            (charges_h, charges),
-            (bases_h, bases),
-            (transfers_h, transfers),
-            (parent_of_h, parent_of),
+            (shared_h.at[0 : 2 * parents], mine),
             (far_pairs_h, far_pairs),
             (par_pairs_h, par_pairs),
             (par_pairs_h, par_smem),
+            (near_pairs_h, near_smem),
+            (charges_h, charges),
             (far_c_h, far_c),
             (par_c_h, par_c),
-            (near_pairs_h, near_smem),
             (near_h, near_v),
         ],
         sems,
     )
-    for copy in copies[:3]:
+    for copy in copies[:-1]:
         copy.wait()
-
-    for l in range(leaves):
-        m = dot_nt(charges[l], bases[l]).astype(BF16)
-        mo[l * rhs : (l + 1) * rhs, :] = m.astype(F32)
-        ch[l * rhs : (l + 1) * rhs, :] = dot_nt(m, transfers[l])
-    for copy in copies[3:-1]:
-        copy.wait()
-    m2 = rows_to_lanes(mo, leaves, rhs)
-    high, low = split2(rows_to_lanes(ch, leaves, rhs))
-    par_hot = one_hot(parent_of[...] % parents == iota((parents, leaves), 0))
-    pm = (dot_nn(par_hot, high) + dot_nn(par_hot, low)).astype(BF16).astype(F32)
-    lanes_to_rows(pm3, pm, rhs)
-    shared = jnp.concatenate([m2[:parents], m2[parents:], pm], axis=1)
-    shared = jnp.concatenate([shared, shared], axis=0).astype(BF16)
-    at = 2 * width + LANES
-    for p in range(rows // (2 * parents)):
-        send[p * 2 * parents : (p + 1) * 2 * parents, at : at + 3 * width] = shared
+    m2 = jnp.concatenate([mine[:parents, 0:width], mine[:parents, width : 2 * width]], axis=0)
+    lanes_to_rows(pm3, mine[:parents, 2 * width :].astype(F32), rhs)
 
     owner_hot = one_hot(far_pairs[0:1, :] % leaves == iota((leaves, slots), 0))
-    a_ref[...] = dot_tn(m2.astype(BF16), owner_hot)
+    a_ref[...] = dot_tn(m2, owner_hot)
+    for s in range(pairs):
+        q = par_smem[0, s] % parents
+        x = pm3[pl.ds(pl.multiple_of(q * rhs, rhs), rhs), :].astype(BF16)
+        pb[s * rhs : (s + 1) * rhs, :] = dot_nn(x, par_c[s])
+    high, low = split2(rows_to_lanes(pb, pairs, rhs))
+    hot = one_hot(par_pairs[1:2, :] == iota((rows, pairs), 0))
+    at = width + LANES
+    send[:, at : at + width] = (dot_nn(hot, high) + dot_nn(hot, low)).astype(BF16)
+
     copies[-1].wait()
     back[...] = jnp.zeros_like(back)
     half = rank // 2
@@ -183,15 +210,6 @@
         lanes = slice(sb * LANES, (sb + 1) * LANES)
         send[lanes, 0 : width + LANES] = dot_nt(unit, ob[:, lanes]).astype(BF16)
 
-    for s in range(pairs):
-        q = par_smem[0, s] % parents
-        x = pm3[pl.ds(pl.multiple_of(q * rhs, rhs), rhs), :].astype(BF16)
-        pb[s * rhs : (s + 1) * rhs, :] = dot_nn(x, par_c[s])
-    high, low = split2(rows_to_lanes(pb, pairs, rhs))
-    hot = one_hot(par_pairs[1:2, :] == iota((rows, pairs), 0))
-    at = width + LANES
-    send[:, at : at + width] = (dot_nn(hot, high) + dot_nn(hot, low)).astype(BF16)
-
 
 def near_kernel(pairs, charges, following, self_blocks, near_blocks, own, ext):
     leaves = charges.shape[0]
@@ -224,6 +242,8 @@
     far_c_h,
     par_pairs_h,
     par_c_h,
+    mom_h,
+    mom2_h,
     got_h,
     near_own_h,
     back_own_h,
@@ -236,6 +256,7 @@
     far_c,
     par_pairs,
     par_c,
+    mom,
     got,
     near_own,
     back_own,
@@ -256,11 +277,12 @@
     rhs = b_ref.shape[0] // rank
     width = rhs * rank
     at_par = width + LANES
-    at_mom = at_par + width
     copies = fetch(
         [
             (far_pairs_h, far_pairs),
             (par_pairs_h, par_pairs),
+            (mom_h, mom.at[0 : rows // 2]),
+            (mom2_h, mom.at[rows // 2 :]),
             (got_h, got),
             (parent_of_h, parent_of),
             (par_c_h, par_c),
@@ -273,21 +295,29 @@
         ],
         sems,
     )
-    for copy in copies[:6]:
+    for copy in copies[:8]:
         copy.wait()
 
+    parity = far_pairs[0:1, 0:1] // leaves % 2
+
+    def source(row):
+        chip = row // parents
+        own = chip < rows // parents // 2
+        return jnp.where(own, 2 * chip + parity, 2 * chip - rows // parents + 1 - parity)
+
     row_id = iota((rows, slots), 0)
-    base_leaf = row_id // parents * leaves + row_id % parents
+    base_leaf = source(row_id) * leaves + row_id % parents
     partner = far_pairs[1:2, :]
     total = None
     for h in range(2):
         hot = one_hot(partner == base_leaf + h * parents)
-        part = dot_tn(got[:, at_mom + h * width : at_mom + (h + 1) * width], hot)
+        part = dot_tn(mom[:, h * width : (h + 1) * width], hot)
         total = part if total is None else total + part
     b_ref[...] = total
 
-    hot = one_hot(par_pairs[1:2, :] == iota((rows, pairs), 0))
-    picked = dot_tn(hot, got[:, at_mom + 2 * width : at_mom + 3 * width])
+    row_id = iota((rows, pairs), 0)
+    hot = one_hot(par_pairs[1:2, :] == source(row_id) * parents + row_id % parents)
+    picked = dot_tn(hot, mom[:, 2 * width :])
     lanes_to_rows(g_ref, picked, rhs)
     for s in range(pairs):
         x = g_ref[s * rhs : (s + 1) * rhs, :].astype(BF16)
@@ -324,7 +354,7 @@
     leaf = leaf + dot_tn(hot, got[:, 0:width])
     lanes_to_rows(lf, leaf, rhs)
 
-    for copy in copies[6:]:
+    for copy in copies[8:]:
         copy.wait()
     for l in range(leaves):
         at = slice(l * rhs, (l + 1) * rhs)
@@ -361,11 +391,14 @@
     parents = leaves // 2
     devices = lax.axis_size("sfc")
     rows = devices * parents
-    columns = 5 * width + LANES
+    columns = 2 * width + LANES
     vmem = pl.BlockSpec(memory_space=pltpu.VMEM)
     smem = pl.BlockSpec(memory_space=pltpu.SMEM)
     hbm = pl.BlockSpec(memory_space=pltpu.HBM)
     params = pltpu.CompilerParams(vmem_limit_bytes=60 * 1024 * 1024)
+
+    def cost(moved):
+        return pl.CostEstimate(flops=4 * moved, bytes_accessed=moved, transcendentals=0)
 
     following = passed_along(charges, "sfc", -1)
     far_pairs = far_pairs.T
@@ -377,20 +410,42 @@
     def like(value, memory=pltpu.VMEM):
         return memory(value.shape, value.dtype)
 
-    send, back_own, back_away = pl.pallas_call(
-        pre_kernel,
-        out_shape=[
-            jax.ShapeDtypeStruct((rows, columns), BF16),
-            jax.ShapeDtypeStruct((leaves, rhs, panels), F32),
-            jax.ShapeDtypeStruct((leaves, rhs, panels), BF16),
-        ],
-        in_specs=[hbm] * 11,
-        out_specs=[vmem] * 3,
+    shared = pl.pallas_call(
+        moment_kernel,
+        out_shape=jax.ShapeDtypeStruct((rows // 2, 3 * width), BF16),
+        in_specs=[hbm] * 4,
+        out_specs=vmem,
         scratch_shapes=[
             like(charges),
             like(bases),
             like(transfers),
             like(parent_of),
+            pltpu.SemaphoreType.DMA((4,)),
+            pltpu.VMEM((leaves * rhs, rank), F32),
+            pltpu.VMEM((leaves * rhs, rank), F32),
+        ],
+        compiler_params=params,
+        cost_estimate=cost(4_000_000),
+        name="moments",
+    )(charges, bases, transfers, parent_of)
+    same_core = [list(range(core, devices, 2)) for core in range(2)]
+    mom = lax.all_to_all(
+        shared, "sfc", split_axis=0, concat_axis=0, tiled=True, axis_index_groups=same_core
+    )
+    mom2 = lax.ppermute(mom, "sfc", [(i, i ^ 1) for i in range(devices)])
+
+    send, back_own, back_away = pl.pallas_call(
+        back_kernel,
+        out_shape=[
+            jax.ShapeDtypeStruct((rows, columns), BF16),
+            jax.ShapeDtypeStruct((leaves, rhs, panels), F32),
+            jax.ShapeDtypeStruct((leaves, rhs, panels), BF16),
+        ],
+        in_specs=[hbm] * 9,
+        out_specs=[vmem] * 3,
+        scratch_shapes=[
+            like(charges),
+            pltpu.VMEM((2 * parents, 3 * width), BF16),
             like(far_pairs),
             like(far_c),
             like(par_pairs),
@@ -399,21 +454,18 @@
             like(near_pairs, pltpu.SMEM),
             like(near_blocks),
             pltpu.VMEM((2 * leaves, rhs, panels), F32),
-            pltpu.SemaphoreType.DMA((11,)),
-            pltpu.VMEM((leaves * rhs, rank), F32),
-            pltpu.VMEM((leaves * rhs, rank), F32),
+            pltpu.SemaphoreType.DMA((9,)),
             pltpu.VMEM((parents * rhs, rank), F32),
             pltpu.VMEM((pairs * rhs, rank), F32),
             pltpu.VMEM((width, slots), F32),
             pltpu.VMEM((width + LANES, slots), BF16),
         ],
         compiler_params=params,
-        name="upward",
+        cost_estimate=cost(12_000_000),
+        name="transposed",
     )(
         charges,
-        bases,
-        transfers,
-        parent_of,
+        shared,
         far_pairs,
         far_c,
         par_pairs,
@@ -442,13 +494,14 @@
         out_specs=whole(leaves, rhs, panels),
         scratch_shapes=[pltpu.VMEM((2 * leaves, rhs, panels), BF16)],
         compiler_params=params,
+        cost_estimate=cost(20_000_000),
         name="near",
     )(near_pairs, charges, following, self_blocks, near_blocks)
 
     return pl.pallas_call(
         post_kernel,
         out_shape=jax.ShapeDtypeStruct((leaves, rhs, panels), F32),
-        in_specs=[hbm] * 11,
+        in_specs=[hbm] * 13,
         out_specs=vmem,
         scratch_shapes=[
             like(bases),
@@ -458,11 +511,12 @@
             like(far_c),
             like(par_pairs),
             like(par_coupling),
+            pltpu.VMEM((rows, 3 * width), BF16),
             like(got),
             like(near_own),
             like(back_own),
             like(near_back),
-            pltpu.SemaphoreType.DMA((11,)),
+            pltpu.SemaphoreType.DMA((13,)),
             pltpu.VMEM((width, slots), F32),
             pltpu.VMEM((width, slots), F32),
             pltpu.VMEM((pairs * rhs, rank), F32),
@@ -480,6 +534,8 @@
         far_c,
         par_pairs,
         par_coupling,
+        mom,
+        mom2,
         got,
         near_own,
         back_own,

time: 45.3 us -> 46.4 us (1.024)
  waiting for transfers between devices: 9.85 us -> 3.12 us
  starting transfers between devices: 12.8 us -> 18.5 us
  Pallas kernels: 20.8 us -> 22.7 us
    all_to_all x0 -> x1, starting transfers between devices: none -> 7.29 us  [on_device(): lax.all_to_all(shared, 'sfc', split_axis=0, concat_axis=0, tiled=True, ax...]
    all_to_all x1, waiting for transfers between devices: 7.79 us -> 1.06 us  [on_device(): got = lax.all_to_all(send, 'sfc', split_axis=0, concat_axis=0, tiled=True)]
    pallas_call x1 -> x2, Pallas kernels: 7.77 us -> 9.55 us  [the longest x1 6.98 us: on_device(): pl.pallas_call(back_kernel, out_shape=[jax.ShapeDtypeStruct((rows, column...]
    all_to_all x1, starting transfers between devices: 9.17 us -> 7.43 us  [on_device(): got = lax.all_to_all(send, 'sfc', split_axis=0, concat_axis=0, tiled=True)]
    unnamed x6 -> x10, local copies, waits for them, and re-layouts: 1.47 us -> 1.35 us
  transfers between devices with their start and end apart: 3 -> 5, of which waited for: 2 -> 2; matrix products, arithmetic and copies ran while one was open for 0% -> 0% of each run, Pallas kernels for 16% -> 31%
where the time goes in v4:
time: 46.4 us; the launch traced here: 45.8 us
  Pallas kernels  22.7 us (49%)
  starting transfers between devices  18.5 us (40%)
  waiting for transfers between devices  3.12 us (7%)
  local copies, waits for them, and re-layouts  1.35 us (3%)
    all_to_all x1, starting transfers between devices, on_device(): got = lax.all_to_all(send, 'sfc', split_axis=0, concat_axis=0, tiled=True)  7.43 us
    all_to_all x1, starting transfers between devices, on_device(): lax.all_to_all(shared, 'sfc', split_axis=0, concat_axis=0, tiled=True, ax...  7.29 us
    pallas_call x1, Pallas kernels, on_device(): pl.pallas_call(near_kernel, grid=(steps,), out_shape=jax.ShapeDtypeStruct...  7.01 us
    pallas_call x1, Pallas kernels, on_device(): pl.pallas_call(back_kernel, out_shape=[jax.ShapeDtypeStruct((rows, column...  6.98 us
    pallas_call x1, Pallas kernels, on_device(): pl.pallas_call(post_kernel, out_shape=jax.ShapeDtypeStruct((leaves, rhs,...  6.16 us
    ppermute x2, starting transfers between devices, passed_along(): lax.ppermute(value, axis, [(source, source + steps) for source in range(l...  3.34 us
    pallas_call x1, Pallas kernels, on_device(): pl.pallas_call(moment_kernel, out_shape=jax.ShapeDtypeStruct((rows // 2,...  2.57 us
    ppermute x2, waiting for transfers between devices, passed_along(): lax.ppermute(value, axis, [(source, source + steps) for source in range(l...  2.06 us
  transfers between devices with their start and end apart: 5, of which 2 were waited for; matrix products, arithmetic and copies ran while one was open for 0% of the time, Pallas kernels for 31%

profile of v4, /device:TPU:0, one launch (start us, length us, event | category | flops | bytes accessed | tf_op | source)
XLA Modules:
  0.0 45.8 jit_solution(9845469437465164859)
XLA Ops:
  0.0 2.6 %moments.1.shared_h = bf16[64,1536]{1,0:T(8,128)(2,1)} custom-call(bf16[16,8,256]{2,1,0:T(8,128)(2,1)} %charges.1, bf16[16,64,256]{2,1,0:T(8,128)(2,1)} %bases_h.3, bf16[16,64,64]{2,1,0:T(8,128)(2,1)} %transfers_h.3, s32[1,16]{1,0:T(1,128)} %bitcast.22), custom_call_target="tpu_custom_call" | custom-call | flops 16000000 | bytes 4000000 | tf_op jit(solution)/shard_map/moments/pallas_call | solution.py:413
  2.6 7.3 %all-to-all-start = ((bf16[8,8,1536]{2,1,0:T(8,128)(2,1)}), bf16[8,8,1536]{2,1,0:T(8,128)(2,1)S(1)}, u32[]{:S(2)}, u32[]{:S(2)}) async-start(bf16[8,8,1536]{2,1,0:T(8,128)(2,1)} %bitcast.11), calls=%async_computation | async-start | bytes 393216 | tf_op jit(solution)/shard_map/all_to_all | solution.py:432
  9.9 1.3 %collective-permute-start.1 = (bf16[16,8,256]{2,1,0:T(8,128)(2,1)}, bf16[16,8,256]{2,1,0:T(8,128)(2,1)S(1)}, u32[]{:S(2)}, u32[]{:S(2)}) collective-permute-start(bf16[16,8,256]{2,1,0:T(8,128)(2,1)} %charges.1), channel_id=1, source_target_pairs={{1,0},{2,1},{3,2},{4,3},{5,4},{6,5},{7,6},{8,7},{9,8},{10,9},{11,1... | collective-permute-start | bytes 196616 | tf_op jit(solution)/shard_map/ppermute | solution.py:370
  11.2 2.1 %collective-permute-done.1.following_h.following = bf16[16,8,256]{2,1,0:T(8,128)(2,1)S(1)} collective-permute-done((bf16[16,8,256]{2,1,0:T(8,128)(2,1)}, bf16[16,8,256]{2,1,0:T(8,128)(2,1)S(1)}, u32[]{:S(2)}, u32[]{:S(2)}) %collective-permute-start.1) | collective-permute-done | bytes 65568 | tf_op jit(solution)/shard_map/ppermute | solution.py:370
  13.2 0.0 copy-start.2
  13.2 0.6 %copy-done.2 = bf16[16,8,256]{2,1,0:T(8,128)(2,1)} copy-done((bf16[16,8,256]{2,1,0:T(8,128)(2,1)}, bf16[16,8,256]{2,1,0:T(8,128)(2,1)S(1)}, u32[]{:S(2)}) %copy-start.2) | copy-done | bytes 65560
  13.9 7.0 %transposed.1 = (bf16[128,1152]{1,0:T(8,128)(2,1)}, f32[16,8,256]{2,1,0:T(8,128)}, bf16[16,8,256]{2,1,0:T(8,128)(2,1)}) custom-call(bf16[16,8,256]{2,1,0:T(8,128)(2,1)} %charges.1, bf16[64,1536]{1,0:T(8,128)(2,1)} %moments.1.shared_h, s32[2,128]{1,0:T(2,128)} %bitcast.16, bf16[64,64,128]{2,1,0:T(8,128)(2,1)} %bitcast.9, s32[2,32]{1,0:T(2,128)} %bitcast.18, ...), custom_call_target="tpu_custom_call" | custom-call | flops 48000000 | bytes 12000000 | tf_op jit(solution)/shard_map/transposed/pallas_call | solution.py:437
  20.8 0.0 all-to-all-done
  20.8 0.0 copy-start.1
  20.9 7.4 %all-to-all-start.1 = ((bf16[16,8,1152]{2,1,0:T(8,128)(2,1)}), bf16[16,8,1152]{2,1,0:T(8,128)(2,1)S(1)}, u32[]{:S(2)}, u32[]{:S(2)}) async-start(bf16[16,8,1152]{2,1,0:T(8,128)(2,1)} %bitcast.15), calls=%async_computation.1 | async-start | bytes 589824 | tf_op jit(solution)/shard_map/all_to_all | solution.py:478
  28.3 0.4 collective-permute-start
  28.7 2.1 %collective-permute-start.2 = (bf16[16,8,256]{2,1,0:T(8,128)(2,1)}, bf16[16,8,256]{2,1,0:T(8,128)(2,1)S(1)}, u32[]{:S(2)}, u32[]{:S(2)}) collective-permute-start(bf16[16,8,256]{2,1,0:T(8,128)(2,1)} %get-tuple-element.10), channel_id=1, source_target_pairs={{0,1},{1,2},{2,3},{3,4},{4,5},{5,6},{6,7},{7,8},{8,9},{9,10},{10,1... | collective-permute-start | bytes 196616 | tf_op jit(solution)/shard_map/ppermute | solution.py:370
  30.8 7.0 %near.1.near_own_h = f32[16,8,256]{2,1,0:T(8,128)} custom-call(s32[2,32]{1,0:T(2,128)} %bitcast.21, bf16[16,8,256]{2,1,0:T(8,128)(2,1)} %charges.1, bf16[16,8,256]{2,1,0:T(8,128)(2,1)} %copy-done.2, bf16[16,256,256]{2,1,0:T(8,128)(2,1)} %self_blocks.1, bf16[32,256,256]{2,1,0:T(8,128)(2,1)} %near_blocks.1), custom_call_target="tpu_custom_call" | custom-call | flops 80000000 | bytes 20000000 | tf_op jit(solution)/shard_map/near/pallas_call | solution.py:483
  37.8 0.0 collective-permute-done.2.near_back_h
  37.8 0.0 copy-start.4
  37.8 0.0 collective-permute-done.mom2_h
  37.8 0.0 copy-start.3
  37.8 1.1 %all-to-all-done.1 = bf16[16,8,1152]{2,1,0:T(8,128)(2,1)S(1)} async-done(((bf16[16,8,1152]{2,1,0:T(8,128)(2,1)}), bf16[16,8,1152]{2,1,0:T(8,128)(2,1)S(1)}, u32[]{:S(2)}, u32[]{:S(2)}) %all-to-all-start.1) | async-done | bytes 294944 | tf_op jit(solution)/shard_map/all_to_all | solution.py:478
  38.9 0.0 copy-start
  38.9 0.0 copy-done.1
  38.9 0.0 copy-done.4
  38.9 0.0 copy-done.3
  38.9 0.7 %copy-done = bf16[16,8,1152]{2,1,0:T(8,128)(2,1)} copy-done((bf16[16,8,1152]{2,1,0:T(8,128)(2,1)}, bf16[16,8,1152]{2,1,0:T(8,128)(2,1)S(1)}, u32[]{:S(2)}) %copy-start) | copy-done | bytes 294936
  39.6 6.2 %downward.1 = f32[16,8,256]{2,1,0:T(8,128)} custom-call(bf16[16,64,256]{2,1,0:T(8,128)(2,1)} %bases_h.3, bf16[16,64,64]{2,1,0:T(8,128)(2,1)} %transfers_h.3, s32[1,16]{1,0:T(1,128)} %bitcast.23, s32[2,128]{1,0:T(2,128)} %bitcast.17, bf16[64,64,128]{2,1,0:T(8,128)(2,1)} %bitcast.10, s32[2,32]{1,0:T(2,128)} %bitcast.19, bf16[32,64,64]{2,1,0:T(8,128)(2,1)} %par_c_h.3, ...), custom_call_target="tpu_custom_call" | custom-call | tf_op jit(solution)/shard_map/downward/pallas_call | solution.py:501
Async XLA Ops:
  2.6 18.3 %all-to-all-start = ((bf16[8,8,1536]{2,1,0:T(8,128)(2,1)}), bf16[8,8,1536]{2,1,0:T(8,128)(2,1)S(1)}, u32[]{:S(2)}, u32[]{:S(2)}) async-start(bf16[8,8,1536]{2,1,0:T(8,128)(2,1)} %bitcast.11), calls=%async_computation | async-start | bytes 393216 | tf_op jit(solution)/shard_map/all_to_all | solution.py:432
  9.9 3.3 %collective-permute-start.1 = (bf16[16,8,256]{2,1,0:T(8,128)(2,1)}, bf16[16,8,256]{2,1,0:T(8,128)(2,1)S(1)}, u32[]{:S(2)}, u32[]{:S(2)}) collective-permute-start(bf16[16,8,256]{2,1,0:T(8,128)(2,1)} %charges.1), channel_id=1, source_target_pairs={{1,0},{2,1},{3,2},{4,3},{5,4},{6,5},{7,6},{8,7},{9,8},{10,9},{11,1... | collective-permute-start | bytes 196616 | tf_op jit(solution)/shard_map/ppermute | solution.py:370
  13.2 0.6 %copy-start.2 = (bf16[16,8,256]{2,1,0:T(8,128)(2,1)}, bf16[16,8,256]{2,1,0:T(8,128)(2,1)S(1)}, u32[]{:S(2)}) copy-start(bf16[16,8,256]{2,1,0:T(8,128)(2,1)S(1)} %collective-permute-done.1.following_h.following) | copy-start | bytes 196612
  20.8 18.0 %copy-start.1 = (bf16[8,8,1536]{2,1,0:T(8,128)(2,1)}, bf16[8,8,1536]{2,1,0:T(8,128)(2,1)S(1)}, u32[]{:S(2)}) copy-start(bf16[8,8,1536]{2,1,0:T(8,128)(2,1)S(1)} %all-to-all-done) | copy-start | bytes 589828
  20.9 18.0 %all-to-all-start.1 = ((bf16[16,8,1152]{2,1,0:T(8,128)(2,1)}), bf16[16,8,1152]{2,1,0:T(8,128)(2,1)S(1)}, u32[]{:S(2)}, u32[]{:S(2)}) async-start(bf16[16,8,1152]{2,1,0:T(8,128)(2,1)} %bitcast.15), calls=%async_computation.1 | async-start | bytes 589824 | tf_op jit(solution)/shard_map/all_to_all | solution.py:478
  28.3 9.5 %collective-permute-start = (bf16[64,1536]{1,0:T(8,128)(2,1)S(1)}, bf16[64,1536]{1,0:T(8,128)(2,1)S(1)}, u32[]{:S(2)}, u32[]{:S(2)}) collective-permute-start(bf16[64,1536]{1,0:T(8,128)(2,1)S(1)} %bitcast.13), channel_id=1, source_target_pairs={{0,1},{1,0},{2,3},{3,2},{4,5},{5,4},{6,7},{7,6},{8,9},{9,8},{10,11... | collective-permute-start | bytes 589832 | tf_op jit(solution)/shard_map/ppermute | solution.py:435
  28.7 9.1 %collective-permute-start.2 = (bf16[16,8,256]{2,1,0:T(8,128)(2,1)}, bf16[16,8,256]{2,1,0:T(8,128)(2,1)S(1)}, u32[]{:S(2)}, u32[]{:S(2)}) collective-permute-start(bf16[16,8,256]{2,1,0:T(8,128)(2,1)} %get-tuple-element.10), channel_id=1, source_target_pairs={{0,1},{1,2},{2,3},{3,4},{4,5},{5,6},{6,7},{7,8},{8,9},{9,10},{10,1... | collective-permute-start | bytes 196616 | tf_op jit(solution)/shard_map/ppermute | solution.py:370
  37.8 1.1 %copy-start.4 = (bf16[16,8,256]{2,1,0:T(8,128)(2,1)}, bf16[16,8,256]{2,1,0:T(8,128)(2,1)S(1)}, u32[]{:S(2)}) copy-start(bf16[16,8,256]{2,1,0:T(8,128)(2,1)S(1)} %collective-permute-done.2.near_back_h) | copy-start | bytes 196612
  37.8 1.1 %copy-start.3 = (bf16[64,1536]{1,0:T(8,128)(2,1)}, bf16[64,1536]{1,0:T(8,128)(2,1)S(1)}, u32[]{:S(2)}) copy-start(bf16[64,1536]{1,0:T(8,128)(2,1)S(1)} %collective-permute-done.mom2_h) | copy-start | bytes 589828
  38.9 0.7 %copy-start = (bf16[16,8,1152]{2,1,0:T(8,128)(2,1)}, bf16[16,8,1152]{2,1,0:T(8,128)(2,1)S(1)}, u32[]{:S(2)}) copy-start(bf16[16,8,1152]{2,1,0:T(8,128)(2,1)S(1)} %all-to-all-done.1) | copy-start | bytes 884740

commit v5 on v2

--- a/solution.py
+++ b/solution.py
@@ -118,10 +118,11 @@
     pm = (dot_nn(par_hot, high) + dot_nn(par_hot, low)).astype(BF16).astype(F32)
     lanes_to_rows(pm3, pm, rhs)
     shared = jnp.concatenate([m2[:parents], m2[parents:], pm], axis=1)
-    shared = jnp.concatenate([shared, shared], axis=0).astype(BF16)
+    half = 3 * width // 2
+    shared = jnp.concatenate([shared[:, :half], shared[:, half:]], axis=0).astype(BF16)
     at = 2 * width + LANES
     for p in range(rows // (2 * parents)):
-        send[p * 2 * parents : (p + 1) * 2 * parents, at : at + 3 * width] = shared
+        send[p * 2 * parents : (p + 1) * 2 * parents, at : at + half] = shared
 
     owner_hot = one_hot(far_pairs[0:1, :] % leaves == iota((leaves, slots), 0))
     a_ref[...] = dot_tn(m2.astype(BF16), owner_hot)
@@ -192,17 +193,9 @@
 
 
 def post_kernel(
-    bases_h,
-    transfers_h,
-    parent_of_h,
-    far_pairs_h,
-    far_c_h,
-    par_pairs_h,
-    par_c_h,
+    core_smem,
+    mom2,
     got,
-    near_own,
-    near_back,
-    out,
     bases,
     transfers,
     parent_of,
@@ -210,7 +203,9 @@
     far_c,
     par_pairs,
     par_c,
-    sems,
+    near_own,
+    near_back,
+    out,
     b_ref,
     fw,
     g_ref,
@@ -227,33 +222,23 @@
     width = rhs * rank
     at_par = width + LANES
     at_mom = at_par + width
-    copies = fetch(
-        [
-            (far_pairs_h, far_pairs),
-            (par_pairs_h, par_pairs),
-            (parent_of_h, parent_of),
-            (par_c_h, par_c),
-            (far_c_h, far_c),
-            (transfers_h, transfers),
-            (bases_h, bases),
-        ],
-        sems,
+    core = core_smem[0, 0] // leaves % 2
+    mom = got[:, at_mom:]
+    shared = jnp.concatenate(
+        [jnp.where(core == 0, mom, mom2[...]), jnp.where(core == 0, mom2[...], mom)], axis=1
     )
-    for copy in copies:
-        copy.wait()
-
     row_id = iota((rows, slots), 0)
     base_leaf = row_id // parents * leaves + row_id % parents
     partner = far_pairs[1:2, :]
     total = None
     for h in range(2):
         hot = one_hot(partner == base_leaf + h * parents)
-        part = dot_tn(got[:, at_mom + h * width : at_mom + (h + 1) * width], hot)
+        part = dot_tn(shared[:, h * width : (h + 1) * width], hot)
         total = part if total is None else total + part
     b_ref[...] = total
 
     hot = one_hot(par_pairs[1:2, :] == iota((rows, pairs), 0))
-    picked = dot_tn(hot, got[:, at_mom + 2 * width : at_mom + 3 * width])
+    picked = dot_tn(hot, shared[:, 2 * width :])
     lanes_to_rows(g_ref, picked, rhs)
     for s in range(pairs):
         x = g_ref[s * rhs : (s + 1) * rhs, :].astype(BF16)
@@ -294,7 +279,20 @@
         at = slice(l * rhs, (l + 1) * rhs)
         down = dot_nn(pg[at, :].astype(BF16), transfers[l])
         mine = (lf[at, :] + down).astype(BF16)
-        out[l] = dot_nn(mine, bases[l]) + near_own[l] + near_back[l].astype(F32)
+        near = near_own[l] + near_back[l].astype(F32)
+        out[l] = dot_nn(mine, bases[l]) + near
+
+
+def after(value, earlier):
+    anywhere = pl.BlockSpec(memory_space=pl.ANY)
+    return pl.pallas_call(
+        lambda value, earlier, same: None,
+        out_shape=jax.ShapeDtypeStruct(value.shape, value.dtype),
+        in_specs=[anywhere] * 2,
+        out_specs=anywhere,
+        input_output_aliases={0: 0},
+        name="after",
+    )(value, earlier)
 
 
 def passed_along(value, axis, steps):
@@ -324,11 +322,15 @@
     parents = leaves // 2
     devices = lax.axis_size("sfc")
     rows = devices * parents
-    columns = 5 * width + LANES
+    columns = 2 * width + LANES + 3 * width // 2
     vmem = pl.BlockSpec(memory_space=pltpu.VMEM)
     smem = pl.BlockSpec(memory_space=pltpu.SMEM)
     hbm = pl.BlockSpec(memory_space=pltpu.HBM)
     params = pltpu.CompilerParams(vmem_limit_bytes=60 * 1024 * 1024)
+    late = pltpu.CompilerParams(vmem_limit_bytes=48 * 1024 * 1024)
+
+    def cost(moved):
+        return pl.CostEstimate(flops=4 * moved, bytes_accessed=moved, transcendentals=0)
 
     following = passed_along(charges, "sfc", -1)
     far_pairs = far_pairs.T
@@ -364,10 +366,11 @@
             pltpu.VMEM((width + LANES, slots), BF16),
         ],
         compiler_params=params,
+        cost_estimate=cost(10_000_000),
         name="upward",
     )(charges, bases, transfers, parent_of, far_pairs, far_c, par_pairs, par_coupling)
+    send = after(send, following)
     got = lax.all_to_all(send, "sfc", split_axis=0, concat_axis=0, tiled=True)
-
     steps = 8
     selves, nears = leaves // steps, near_blocks.shape[0] // steps
     whole = lambda *shape: pl.BlockSpec(shape, lambda i: (0,) * len(shape))
@@ -390,25 +393,23 @@
             pltpu.VMEM((2 * leaves, rhs, panels), BF16),
             pltpu.VMEM((2 * leaves, rhs, panels), F32),
         ],
-        compiler_params=params,
+        compiler_params=late,
+        cost_estimate=cost(20_000_000),
         name="near",
     )(near_pairs, charges, following, self_blocks, near_blocks)
     near_back = passed_along(near_away, "sfc", 1)
 
+    got = after(got, near_back)
+    mom2 = lax.ppermute(
+        got[:, 2 * width + LANES :], "sfc", [(i, i ^ 1) for i in range(devices)]
+    )
+
     return pl.pallas_call(
         post_kernel,
         out_shape=jax.ShapeDtypeStruct((leaves, rhs, panels), F32),
-        in_specs=[hbm] * 7 + [vmem] * 3,
+        in_specs=[smem] + [vmem] * 11,
         out_specs=vmem,
         scratch_shapes=[
-            like(bases),
-            like(transfers),
-            like(parent_of),
-            like(far_pairs),
-            like(far_c),
-            like(par_pairs),
-            like(par_coupling),
-            pltpu.SemaphoreType.DMA((7,)),
             pltpu.VMEM((width, slots), F32),
             pltpu.VMEM((width, slots), F32),
             pltpu.VMEM((pairs * rhs, rank), F32),
@@ -416,9 +417,12 @@
             pltpu.VMEM((leaves * rhs, rank), F32),
             pltpu.VMEM((leaves * rhs, rank), F32),
         ],
-        compiler_params=params,
+        compiler_params=late,
         name="downward",
     )(
+        far_pairs,
+        mom2,
+        got,
         bases,
         transfers,
         parent_of,
@@ -426,7 +430,6 @@
         far_c,
         par_pairs,
         par_coupling,
-        got,
         near_own,
         near_back,
     )

time: 50.6 us -> 40.6 us (0.80)
  the two profiles are of different devices: /device:TPU:18 before, /device:TPU:11 now
where the time goes in v5:
time: 40.6 us; the launch traced here: 39.9 us
  Pallas kernels  16.3 us (40%)
  starting transfers between devices  14.5 us (36%)
  local copies, waits for them, and re-layouts  6.69 us (16%)
  waiting for transfers between devices  2.39 us (6%)
    pallas_call x1, Pallas kernels, on_device(): pl.pallas_call(near_kernel, grid=(steps,), out_shape=[jax.ShapeDtypeStruc...  6.48 us
    all_to_all x1, starting transfers between devices, on_device(): got = lax.all_to_all(send, 'sfc', split_axis=0, concat_axis=0, tiled=True)  6.18 us
    ppermute x2, starting transfers between devices, passed_along(): lax.ppermute(value, axis, [(source, source + steps) for source in range(l...  6.04 us
    unnamed x32, local copies, waits for them, and re-layouts  5.75 us
    pallas_call x1, Pallas kernels, on_device(): pl.pallas_call(post_kernel, out_shape=jax.ShapeDtypeStruct((leaves, rhs,...  4.98 us
    pallas_call x1, Pallas kernels, on_device(): pl.pallas_call(pre_kernel, out_shape=jax.ShapeDtypeStruct((rows, columns)...  4.8 us
    ppermute x1, starting transfers between devices, on_device(): lax.ppermute(got[:, 2 * width + LANES:], 'sfc', [(i, i ^ 1) for i in rang...  2.26 us
    ppermute x2, waiting for transfers between devices, passed_along(): lax.ppermute(value, axis, [(source, source + steps) for source in range(l...  1.31 us
  transfers between devices with their start and end apart: 4, of which 2 were waited for; matrix products, arithmetic and copies ran while one was open for 0% of the time, Pallas kernels for 28%

profile of v5, /device:TPU:11, one launch (start us, length us, event | category | flops | bytes accessed | tf_op | source)
XLA Modules:
  0.0 39.9 jit_solution(1305657612246556411)
XLA Ops:
  0.0 0.0 copy-start.7
  0.0 0.0 copy-start.15
  0.0 2.7 %collective-permute-start = (bf16[16,8,256]{2,1,0:T(8,128)(2,1)}, bf16[16,8,256]{2,1,0:T(8,128)(2,1)S(1)}, u32[]{:S(2)}, u32[]{:S(2)}) collective-permute-start(bf16[16,8,256]{2,1,0:T(8,128)(2,1)} %charges.1), channel_id=1, source_target_pairs={{1,0},{2,1},{3,2},{4,3},{5,4},{6,5},{7,6},{8,7},{9,8},{10,9},{11,1... | collective-permute-start | bytes 196616 | tf_op jit(solution)/shard_map/ppermute | solution.py:301
  2.7 4.8 %upward.1.value = bf16[128,1920]{1,0:T(8,128)(2,1)} custom-call(bf16[16,8,256]{2,1,0:T(8,128)(2,1)} %charges.1, bf16[16,64,256]{2,1,0:T(8,128)(2,1)} %bases.1, bf16[16,64,64]{2,1,0:T(8,128)(2,1)} %transfers.1, s32[1,16]{1,0:T(1,128)} %bitcast.15, s32[2,128]{1,0:T(2,128)} %bitcast.10, bf16[64,64,128]{2,1,0:T(8,128)(2,1)} %bitcast.8, s32[2,32]{1,0:T(2,128)} %bitcast.13, ...), custom_call_target="tpu_custom_call" | custom-call | flops 40000000 | bytes 10000000 | tf_op jit(solution)/shard_map/upward/pallas_call | solution.py:345
  7.5 0.0 collective-permute-done.earlier.following
  7.5 0.0 copy-start.8
  7.5 0.6 %copy-done.8 = bf16[16,8,256]{2,1,0:T(8,128)(2,1)} copy-done((bf16[16,8,256]{2,1,0:T(8,128)(2,1)}, bf16[16,8,256]{2,1,0:T(8,128)(2,1)S(1)}, u32[]{:S(2)}) %copy-start.8) | copy-done | bytes 65560
  8.2 0.0 copy-start.12
  8.2 0.0 copy-start.14
  8.2 0.0 copy-start.2
  8.2 6.2 %all-to-all-start = ((bf16[16,8,1920]{2,1,0:T(8,128)(2,1)}), bf16[16,8,1920]{2,1,0:T(8,128)(2,1)S(1)}, u32[]{:S(2)}, u32[]{:S(2)}) async-start(bf16[16,8,1920]{2,1,0:T(8,128)(2,1)} %bitcast.18), calls=%async_computation | async-start | bytes 983040 | tf_op jit(solution)/shard_map/all_to_all | solution.py:373
  14.4 0.0 copy-done.7
  14.4 0.0 copy-done.15
  14.4 0.0 copy-start.3
  14.4 1.6 %copy-done.3 = bf16[16,256,256]{2,1,0:T(8,128)(2,1)S(1)} copy-done((bf16[16,256,256]{2,1,0:T(8,128)(2,1)S(1)}, bf16[16,256,256]{2,1,0:T(8,128)(2,1)}, u32[]{:S(2)}) %copy-start.3) | copy-done | bytes 2097176
  16.0 0.0 copy-start.9
  16.0 0.8 %copy-done.9 = bf16[16,8,256]{2,1,0:T(8,128)(2,1)S(1)} copy-done((bf16[16,8,256]{2,1,0:T(8,128)(2,1)S(1)}, bf16[16,8,256]{2,1,0:T(8,128)(2,1)}, u32[]{:S(2)}) %copy-start.9) | copy-done | bytes 65560
  16.8 0.0 copy-start.4
  16.8 0.0 copy-start.5
  16.8 0.0 copy-start.6
  16.8 0.0 copy-start.13
  16.8 6.5 %near.1 = (f32[16,8,256]{2,1,0:T(8,128)S(1)}, bf16[16,8,256]{2,1,0:T(8,128)(2,1)S(1)}) custom-call(s32[2,32]{1,0:T(2,128)S(1)} %bitcast.17, bf16[16,8,256]{2,1,0:T(8,128)(2,1)S(1)} %copy-done.7, bf16[16,8,256]{2,1,0:T(8,128)(2,1)S(1)} %copy-done.9, bf16[16,256,256]{2,1,0:T(8,128)(2,1)S(1)} %copy-done.3, bf16[32,256,256]{2,1,0:T(8,128)(2,1)} %near_blocks.1), custom_call_target="tpu_custom_call" | custom-call | flops 80000000 | bytes 20000000 | tf_op jit(solution)/shard_map/near/pallas_call | solution.py:377
  23.3 3.3 %collective-permute-start.1 = (bf16[16,8,256]{2,1,0:T(8,128)(2,1)S(1)}, bf16[16,8,256]{2,1,0:T(8,128)(2,1)S(1)}, u32[]{:S(2)}, u32[]{:S(2)}) collective-permute-start(bf16[16,8,256]{2,1,0:T(8,128)(2,1)S(1)} %get-tuple-element.7), channel_id=1, source_target_pairs={{0,1},{1,2},{2,3},{3,4},{4,5},{5,6},{6,7},{7,8},{8,9},{9,10},{10,1... | collective-permute-start | bytes 196616 | tf_op jit(solution)/shard_map/ppermute | solution.py:301
  26.7 1.3 %collective-permute-done.1.earlier.near_back = bf16[16,8,256]{2,1,0:T(8,128)(2,1)S(1)} collective-permute-done((bf16[16,8,256]{2,1,0:T(8,128)(2,1)S(1)}, bf16[16,8,256]{2,1,0:T(8,128)(2,1)S(1)}, u32[]{:S(2)}, u32[]{:S(2)}) %collective-permute-start.1) | collective-permute-done | bytes 65568 | tf_op jit(solution)/shard_map/ppermute | solution.py:301
  28.0 0.0 copy-start.10
  28.0 0.0 all-to-all-done
  28.0 0.0 copy-start
  28.0 0.6 %copy-done.10 = bf16[16,8,256]{2,1,0:T(8,128)(2,1)} copy-done((bf16[16,8,256]{2,1,0:T(8,128)(2,1)}, bf16[16,8,256]{2,1,0:T(8,128)(2,1)S(1)}, u32[]{:S(2)}) %copy-start.10) | copy-done | bytes 65560
  28.6 0.2 copy-done
  28.8 0.9 %slice.4 = bf16[128,768]{1,0:T(8,128)(2,1)S(1)} slice(bf16[128,1920]{1,0:T(8,128)(2,1)} %after.3.got), slice={[0:128], [1152:1920]} | slice | bytes 393216 | tf_op jit(solution)/shard_map/slice | solution.py:404
  29.7 2.3 %collective-permute-start.2 = (bf16[128,768]{1,0:T(8,128)(2,1)S(1)}, bf16[128,768]{1,0:T(8,128)(2,1)S(1)}, u32[]{:S(2)}, u32[]{:S(2)}) collective-permute-start(bf16[128,768]{1,0:T(8,128)(2,1)S(1)} %slice.4), channel_id=1, source_target_pairs={{0,1},{1,0},{2,3},{3,2},{4,5},{5,4},{6,7},{7,6},{8,9},{9,8},{10,11... | collective-permute-start | bytes 589832 | tf_op jit(solution)/shard_map/ppermute | solution.py:403
  32.0 1.1 %collective-permute-done.2.mom2 = bf16[128,768]{1,0:T(8,128)(2,1)S(1)} collective-permute-done((bf16[128,768]{1,0:T(8,128)(2,1)S(1)}, bf16[128,768]{1,0:T(8,128)(2,1)S(1)}, u32[]{:S(2)}, u32[]{:S(2)}) %collective-permute-start.2) | collective-permute-done | bytes 196640 | tf_op jit(solution)/shard_map/ppermute | solution.py:403
  33.0 0.0 copy-done.12
  33.0 0.0 copy-done.14
  33.1 0.0 copy-done.2
  33.1 0.0 copy-done.4
  33.1 0.0 copy-done.5
  33.1 0.0 copy-done.6
  33.1 0.0 copy-done.13
  33.1 0.0 copy-start.1
  33.1 1.0 %copy-done.1 = bf16[128,1920]{1,0:T(8,128)(2,1)S(1)} copy-done((bf16[128,1920]{1,0:T(8,128)(2,1)S(1)}, bf16[128,1920]{1,0:T(8,128)(2,1)}, u32[]{:S(2)}) %copy-start.1) | copy-done | bytes 491544
  34.1 0.0 copy-start.11
  34.1 0.8 %copy-done.11 = bf16[16,8,256]{2,1,0:T(8,128)(2,1)S(1)} copy-done((bf16[16,8,256]{2,1,0:T(8,128)(2,1)S(1)}, bf16[16,8,256]{2,1,0:T(8,128)(2,1)}, u32[]{:S(2)}) %copy-start.11) | copy-done | bytes 65560
  35.0 5.0 %downward.1 = f32[16,8,256]{2,1,0:T(8,128)} custom-call(s32[2,128]{1,0:T(2,128)S(1)} %bitcast.11, bf16[128,768]{1,0:T(8,128)(2,1)S(1)} %collective-permute-done.2.mom2, bf16[128,1920]{1,0:T(8,128)(2,1)S(1)} %copy-done.1, bf16[16,64,256]{2,1,0:T(8,128)(2,1)S(1)} %copy-done.4, bf16[16,64,64]{2,1,0:T(8,128)(2,1)S(1)} %copy-done.6, s32[1,16]{1,0:T(1,128)S(1)} %bitcast.16, ...), custom_call_target="tpu_custom_call" | custom-call | tf_op jit(solution)/shard_map/downward/pallas_call | solution.py:407
  (2 shorter events, 0.0 us)
Async XLA Ops:
  0.0 14.4 %copy-start.7 = (bf16[16,8,256]{2,1,0:T(8,128)(2,1)S(1)}, bf16[16,8,256]{2,1,0:T(8,128)(2,1)}, u32[]{:S(2)}) copy-start(bf16[16,8,256]{2,1,0:T(8,128)(2,1)} %charges.1) | copy-start | bytes 196612
  0.0 14.4 %copy-start.15 = (s32[32,2]{0,1:T(2,128)S(1)}, s32[32,2]{0,1:T(2,128)}, u32[]{:S(2)}) copy-start(s32[32,2]{0,1:T(2,128)} %param.14) | copy-start | bytes 772
  0.0 7.5 %collective-permute-start = (bf16[16,8,256]{2,1,0:T(8,128)(2,1)}, bf16[16,8,256]{2,1,0:T(8,128)(2,1)S(1)}, u32[]{:S(2)}, u32[]{:S(2)}) collective-permute-start(bf16[16,8,256]{2,1,0:T(8,128)(2,1)} %charges.1), channel_id=1, source_target_pairs={{1,0},{2,1},{3,2},{4,3},{5,4},{6,5},{7,6},{8,7},{9,8},{10,9},{11,1... | collective-permute-start | bytes 196616 | tf_op jit(solution)/shard_map/ppermute | solution.py:301
  7.5 0.6 %copy-start.8 = (bf16[16,8,256]{2,1,0:T(8,128)(2,1)}, bf16[16,8,256]{2,1,0:T(8,128)(2,1)S(1)}, u32[]{:S(2)}) copy-start(bf16[16,8,256]{2,1,0:T(8,128)(2,1)S(1)} %collective-permute-done.earlier.following) | copy-start | bytes 196612
  8.2 24.9 %copy-start.12 = (s32[128,2]{0,1:T(2,128)S(1)}, s32[128,2]{0,1:T(2,128)}, u32[]{:S(2)}) copy-start(s32[128,2]{0,1:T(2,128)} %param.18) | copy-start | bytes 3076
  8.2 24.9 %copy-start.14 = (s32[16]{0:T(128)S(1)}, s32[16]{0:T(128)}, u32[]{:S(2)}) copy-start(s32[16]{0:T(128)} %param.17) | copy-start | bytes 196
  8.2 24.9 %copy-start.2 = (bf16[128,64,64]{0,2,1:T(8,128)(2,1)S(1)}, bf16[128,64,64]{0,2,1:T(8,128)(2,1)}, u32[]{:S(2)}) copy-start(bf16[128,64,64]{0,2,1:T(8,128)(2,1)} %param.19) | copy-start | bytes 3145732
  8.2 19.8 %all-to-all-start = ((bf16[16,8,1920]{2,1,0:T(8,128)(2,1)}), bf16[16,8,1920]{2,1,0:T(8,128)(2,1)S(1)}, u32[]{:S(2)}, u32[]{:S(2)}) async-start(bf16[16,8,1920]{2,1,0:T(8,128)(2,1)} %bitcast.18), calls=%async_computation | async-start | bytes 983040 | tf_op jit(solution)/shard_map/all_to_all | solution.py:373
  14.4 1.6 %copy-start.3 = (bf16[16,256,256]{2,1,0:T(8,128)(2,1)S(1)}, bf16[16,256,256]{2,1,0:T(8,128)(2,1)}, u32[]{:S(2)}) copy-start(bf16[16,256,256]{2,1,0:T(8,128)(2,1)} %self_blocks.1) | copy-start | bytes 6291460
  16.0 0.8 %copy-start.9 = (bf16[16,8,256]{2,1,0:T(8,128)(2,1)S(1)}, bf16[16,8,256]{2,1,0:T(8,128)(2,1)}, u32[]{:S(2)}) copy-start(bf16[16,8,256]{2,1,0:T(8,128)(2,1)} %copy-done.8) | copy-start | bytes 196612
  16.8 16.2 %copy-start.4 = (bf16[16,64,256]{2,1,0:T(8,128)(2,1)S(1)}, bf16[16,64,256]{2,1,0:T(8,128)(2,1)}, u32[]{:S(2)}) copy-start(bf16[16,64,256]{2,1,0:T(8,128)(2,1)} %bases.1) | copy-start | bytes 1572868
  16.8 16.3 %copy-start.5 = (bf16[32,64,64]{2,1,0:T(8,128)(2,1)S(1)}, bf16[32,64,64]{2,1,0:T(8,128)(2,1)}, u32[]{:S(2)}) copy-start(bf16[32,64,64]{2,1,0:T(8,128)(2,1)} %par_c.1) | copy-start | bytes 786436
  16.8 16.3 %copy-start.6 = (bf16[16,64,64]{2,1,0:T(8,128)(2,1)S(1)}, bf16[16,64,64]{2,1,0:T(8,128)(2,1)}, u32[]{:S(2)}) copy-start(bf16[16,64,64]{2,1,0:T(8,128)(2,1)} %transfers.1) | copy-start | bytes 393220
  16.8 16.3 %copy-start.13 = (s32[32,2]{0,1:T(2,128)S(1)}, s32[32,2]{0,1:T(2,128)}, u32[]{:S(2)}) copy-start(s32[32,2]{0,1:T(2,128)} %param.20) | copy-start | bytes 772
  23.3 4.7 %collective-permute-start.1 = (bf16[16,8,256]{2,1,0:T(8,128)(2,1)S(1)}, bf16[16,8,256]{2,1,0:T(8,128)(2,1)S(1)}, u32[]{:S(2)}, u32[]{:S(2)}) collective-permute-start(bf16[16,8,256]{2,1,0:T(8,128)(2,1)S(1)} %get-tuple-element.7), channel_id=1, source_target_pairs={{0,1},{1,2},{2,3},{3,4},{4,5},{5,6},{6,7},{7,8},{8,9},{9,10},{10,1... | collective-permute-start | bytes 196616 | tf_op jit(solution)/shard_map/ppermute | solution.py:301
  28.0 0.6 %copy-start.10 = (bf16[16,8,256]{2,1,0:T(8,128)(2,1)}, bf16[16,8,256]{2,1,0:T(8,128)(2,1)S(1)}, u32[]{:S(2)}) copy-start(bf16[16,8,256]{2,1,0:T(8,128)(2,1)S(1)} %collective-permute-done.1.earlier.near_back) | copy-start | bytes 196612
  28.0 0.8 %copy-start = (bf16[16,8,1920]{2,1,0:T(8,128)(2,1)}, bf16[16,8,1920]{2,1,0:T(8,128)(2,1)S(1)}, u32[]{:S(2)}) copy-start(bf16[16,8,1920]{2,1,0:T(8,128)(2,1)S(1)} %all-to-all-done) | copy-start | bytes 1474564
  29.7 3.3 %collective-permute-start.2 = (bf16[128,768]{1,0:T(8,128)(2,1)S(1)}, bf16[128,768]{1,0:T(8,128)(2,1)S(1)}, u32[]{:S(2)}, u32[]{:S(2)}) collective-permute-start(bf16[128,768]{1,0:T(8,128)(2,1)S(1)} %slice.4), channel_id=1, source_target_pairs={{0,1},{1,0},{2,3},{3,2},{4,5},{5,4},{6,7},{7,6},{8,9},{9,8},{10,11... | collective-permute-start | bytes 589832 | tf_op jit(solution)/shard_map/ppermute | solution.py:403
  33.1 1.0 %copy-start.1 = (bf16[128,1920]{1,0:T(8,128)(2,1)S(1)}, bf16[128,1920]{1,0:T(8,128)(2,1)}, u32[]{:S(2)}) copy-start(bf16[128,1920]{1,0:T(8,128)(2,1)} %after.3.got) | copy-start | bytes 1474564
  34.1 0.8 %copy-start.11 = (bf16[16,8,256]{2,1,0:T(8,128)(2,1)S(1)}, bf16[16,8,256]{2,1,0:T(8,128)(2,1)}, u32[]{:S(2)}) copy-start(bf16[16,8,256]{2,1,0:T(8,128)(2,1)} %copy-done.10) | copy-start | bytes 196612

commit v6 on v5

--- a/solution.py
+++ b/solution.py
@@ -291,6 +291,7 @@
         in_specs=[anywhere] * 2,
         out_specs=anywhere,
         input_output_aliases={0: 0},
+        compiler_params=pltpu.CompilerParams(vmem_limit_bytes=1024 * 1024),
         name="after",
     )(value, earlier)
 
@@ -393,7 +394,7 @@
             pltpu.VMEM((2 * leaves, rhs, panels), BF16),
             pltpu.VMEM((2 * leaves, rhs, panels), F32),
         ],
-        compiler_params=late,
+        compiler_params=pltpu.CompilerParams(vmem_limit_bytes=52 * 1024 * 1024),
         cost_estimate=cost(20_000_000),
         name="near",
     )(near_pairs, charges, following, self_blocks, near_blocks)

time: 40.6 us -> 37.2 us (0.916)
  the two profiles are of different devices: /device:TPU:11 before, /device:TPU:0 now
where the time goes in v6:
time: 37.2 us; the launch traced here: 36.7 us
  Pallas kernels  16.5 us (44%)
  starting transfers between devices  12.2 us (33%)
  waiting for transfers between devices  5.99 us (16%)
  local copies, waits for them, and re-layouts  1.86 us (5%)
    all_to_all x1, starting transfers between devices, on_device(): got = lax.all_to_all(send, 'sfc', split_axis=0, concat_axis=0, tiled=True)  8.26 us
    pallas_call x1, Pallas kernels, on_device(): pl.pallas_call(near_kernel, grid=(steps,), out_shape=[jax.ShapeDtypeStruc...  6.77 us
    pallas_call x1, Pallas kernels, on_device(): pl.pallas_call(post_kernel, out_shape=jax.ShapeDtypeStruct((leaves, rhs,...  4.96 us
    pallas_call x1, Pallas kernels, on_device(): pl.pallas_call(pre_kernel, out_shape=jax.ShapeDtypeStruct((rows, columns)...  4.8 us
    all_to_all x1, waiting for transfers between devices, on_device(): got = lax.all_to_all(send, 'sfc', split_axis=0, concat_axis=0, tiled=True)  3.78 us
    ppermute x2, starting transfers between devices, passed_along(): lax.ppermute(value, axis, [(source, source + steps) for source in range(l...  3.72 us
    unnamed x22, local copies, waits for them, and re-layouts  1.84 us
    ppermute x1, waiting for transfers between devices, on_device(): lax.ppermute(got[:, 2 * width + LANES:], 'sfc', [(i, i ^ 1) for i in rang...  1.33 us
  transfers between devices with their start and end apart: 4, of which 3 were waited for; matrix products, arithmetic and copies ran while one was open for 0% of the time, Pallas kernels for 32%

profile of v6, /device:TPU:0, one launch (start us, length us, event | category | flops | bytes accessed | tf_op | source)
XLA Modules:
  0.0 36.7 jit_solution(7257461961784330173)
XLA Ops:
  0.0 0.0 copy-start.6
  0.0 0.0 copy-start.10
  0.0 1.4 %collective-permute-start = (bf16[16,8,256]{2,1,0:T(8,128)(2,1)}, bf16[16,8,256]{2,1,0:T(8,128)(2,1)S(1)}, u32[]{:S(2)}, u32[]{:S(2)}) collective-permute-start(bf16[16,8,256]{2,1,0:T(8,128)(2,1)} %charges.1), channel_id=1, source_target_pairs={{1,0},{2,1},{3,2},{4,3},{5,4},{6,5},{7,6},{8,7},{9,8},{10,9},{11,1... | collective-permute-start | bytes 196616 | tf_op jit(solution)/shard_map/ppermute | solution.py:302
  1.4 4.8 %upward.1.value = bf16[128,1920]{1,0:T(8,128)(2,1)} custom-call(bf16[16,8,256]{2,1,0:T(8,128)(2,1)} %charges.1, bf16[16,64,256]{2,1,0:T(8,128)(2,1)} %bases.1, bf16[16,64,64]{2,1,0:T(8,128)(2,1)} %transfers.1, s32[1,16]{1,0:T(1,128)} %bitcast.16, s32[2,128]{1,0:T(2,128)} %bitcast.11, bf16[64,64,128]{2,1,0:T(8,128)(2,1)} %bitcast.9, s32[2,32]{1,0:T(2,128)} %bitcast.14, ...), custom_call_target="tpu_custom_call" | custom-call | flops 40000000 | bytes 10000000 | tf_op jit(solution)/shard_map/upward/pallas_call | solution.py:346
  6.2 0.0 collective-permute-done.earlier.following
  6.2 0.0 copy-start
  6.3 1.0 %copy-done = bf16[128,1920]{1,0:T(8,128)(2,1)S(1)} copy-done((bf16[128,1920]{1,0:T(8,128)(2,1)S(1)}, bf16[128,1920]{1,0:T(8,128)(2,1)}, u32[]{:S(2)}) %copy-start) | copy-done | bytes 491544
  7.3 0.0 copy-start.1
  7.3 0.8 %copy-done.1 = bf16[128,1920]{1,0:T(8,128)(2,1)} copy-done((bf16[128,1920]{1,0:T(8,128)(2,1)}, bf16[128,1920]{1,0:T(8,128)(2,1)S(1)}, u32[]{:S(2)}) %copy-start.1) | copy-done | bytes 491544
  8.1 0.0 copy-start.2
  8.1 0.0 copy-start.3
  8.1 0.0 copy-start.4
  8.1 0.0 copy-start.5
  8.1 0.0 copy-start.7
  8.1 0.0 copy-start.8
  8.1 0.0 copy-start.9
  8.1 8.3 %all-to-all-start = ((bf16[16,8,1920]{2,1,0:T(8,128)(2,1)}), bf16[16,8,1920]{2,1,0:T(8,128)(2,1)S(1)}, u32[]{:S(2)}, u32[]{:S(2)}) async-start(bf16[16,8,1920]{2,1,0:T(8,128)(2,1)} %bitcast.8), calls=%async_computation | async-start | bytes 983040 | tf_op jit(solution)/shard_map/all_to_all | solution.py:374
  16.4 0.0 copy-done.6
  16.4 0.0 copy-done.10
  16.4 6.8 %near.1 = (f32[16,8,256]{2,1,0:T(8,128)S(1)}, bf16[16,8,256]{2,1,0:T(8,128)(2,1)S(1)}) custom-call(s32[2,32]{1,0:T(2,128)S(1)} %bitcast.18, bf16[16,8,256]{2,1,0:T(8,128)(2,1)S(1)} %copy-done.6, bf16[16,8,256]{2,1,0:T(8,128)(2,1)S(1)} %collective-permute-done.earlier.following, bf16[16,256,256]{2,1,0:T(8,128)(2,1)} %self_blocks.1, ...), custom_call_target="tpu_custom_call" | custom-call | flops 80000000 | bytes 20000000 | tf_op jit(solution)/shard_map/near/pallas_call | solution.py:378
  23.2 2.3 %collective-permute-start.1 = (bf16[16,8,256]{2,1,0:T(8,128)(2,1)S(1)}, bf16[16,8,256]{2,1,0:T(8,128)(2,1)S(1)}, u32[]{:S(2)}, u32[]{:S(2)}) collective-permute-start(bf16[16,8,256]{2,1,0:T(8,128)(2,1)S(1)} %get-tuple-element.7), channel_id=1, source_target_pairs={{0,1},{1,2},{2,3},{3,4},{4,5},{5,6},{6,7},{7,8},{8,9},{9,10},{10,1... | collective-permute-start | bytes 196616 | tf_op jit(solution)/shard_map/ppermute | solution.py:302
  25.5 0.9 %collective-permute-done.1.earlier.near_back = bf16[16,8,256]{2,1,0:T(8,128)(2,1)S(1)} collective-permute-done((bf16[16,8,256]{2,1,0:T(8,128)(2,1)S(1)}, bf16[16,8,256]{2,1,0:T(8,128)(2,1)S(1)}, u32[]{:S(2)}, u32[]{:S(2)}) %collective-permute-start.1) | collective-permute-done | bytes 65568 | tf_op jit(solution)/shard_map/ppermute | solution.py:302
  26.4 3.8 %all-to-all-done = bf16[16,8,1920]{2,1,0:T(8,128)(2,1)S(1)} async-done(((bf16[16,8,1920]{2,1,0:T(8,128)(2,1)}), bf16[16,8,1920]{2,1,0:T(8,128)(2,1)S(1)}, u32[]{:S(2)}, u32[]{:S(2)}) %all-to-all-start) | async-done | bytes 491552 | tf_op jit(solution)/shard_map/all_to_all | solution.py:374
  30.2 0.2 collective-permute-start.2
  30.3 1.3 %collective-permute-done.2.mom2 = bf16[128,768]{1,0:T(8,128)(2,1)S(1)} collective-permute-done((bf16[128,768]{1,0:T(8,128)(2,1)S(1)}, bf16[128,768]{1,0:T(8,128)(2,1)S(1)}, u32[]{:S(2)}, u32[]{:S(2)}) %collective-permute-start.2) | collective-permute-done | bytes 196640 | tf_op jit(solution)/shard_map/ppermute | solution.py:404
  31.7 0.0 copy-done.2
  31.7 0.0 copy-done.3
  31.7 0.0 copy-done.4
  31.7 0.0 copy-done.5
  31.7 0.0 copy-done.7
  31.7 0.0 copy-done.8
  31.7 0.0 copy-done.9
  31.7 5.0 %downward.1 = f32[16,8,256]{2,1,0:T(8,128)} custom-call(s32[2,128]{1,0:T(2,128)S(1)} %bitcast.12, bf16[128,768]{1,0:T(8,128)(2,1)S(1)} %collective-permute-done.2.mom2, bf16[128,1920]{1,0:T(8,128)(2,1)S(1)} %after.3.got, bf16[16,64,256]{2,1,0:T(8,128)(2,1)S(1)} %copy-done.3, bf16[16,64,64]{2,1,0:T(8,128)(2,1)S(1)} %copy-done.5, s32[1,16]{1,0:T(1,128)S(1)} %bitcast.17, ...), custom_call_target="tpu_custom_call" | custom-call | tf_op jit(solution)/shard_map/downward/pallas_call | solution.py:408
  (3 shorter events, 0.0 us)
Async XLA Ops:
  0.0 16.4 %copy-start.6 = (bf16[16,8,256]{2,1,0:T(8,128)(2,1)S(1)}, bf16[16,8,256]{2,1,0:T(8,128)(2,1)}, u32[]{:S(2)}) copy-start(bf16[16,8,256]{2,1,0:T(8,128)(2,1)} %charges.1) | copy-start | bytes 196612
  0.0 16.4 %copy-start.10 = (s32[32,2]{0,1:T(2,128)S(1)}, s32[32,2]{0,1:T(2,128)}, u32[]{:S(2)}) copy-start(s32[32,2]{0,1:T(2,128)} %param.14) | copy-start | bytes 772
  0.0 6.2 %collective-permute-start = (bf16[16,8,256]{2,1,0:T(8,128)(2,1)}, bf16[16,8,256]{2,1,0:T(8,128)(2,1)S(1)}, u32[]{:S(2)}, u32[]{:S(2)}) collective-permute-start(bf16[16,8,256]{2,1,0:T(8,128)(2,1)} %charges.1), channel_id=1, source_target_pairs={{1,0},{2,1},{3,2},{4,3},{5,4},{6,5},{7,6},{8,7},{9,8},{10,9},{11,1... | collective-permute-start | bytes 196616 | tf_op jit(solution)/shard_map/ppermute | solution.py:302
  6.2 1.0 %copy-start = (bf16[128,1920]{1,0:T(8,128)(2,1)S(1)}, bf16[128,1920]{1,0:T(8,128)(2,1)}, u32[]{:S(2)}) copy-start(bf16[128,1920]{1,0:T(8,128)(2,1)} %upward.1.value) | copy-start | bytes 1474564
  7.3 0.8 %copy-start.1 = (bf16[128,1920]{1,0:T(8,128)(2,1)}, bf16[128,1920]{1,0:T(8,128)(2,1)S(1)}, u32[]{:S(2)}) copy-start(bf16[128,1920]{1,0:T(8,128)(2,1)S(1)} %after.2) | copy-start | bytes 1474564
  8.1 23.6 %copy-start.2 = (bf16[128,64,64]{0,2,1:T(8,128)(2,1)S(1)}, bf16[128,64,64]{0,2,1:T(8,128)(2,1)}, u32[]{:S(2)}) copy-start(bf16[128,64,64]{0,2,1:T(8,128)(2,1)} %param.19) | copy-start | bytes 3145732
  8.1 23.6 %copy-start.3 = (bf16[16,64,256]{2,1,0:T(8,128)(2,1)S(1)}, bf16[16,64,256]{2,1,0:T(8,128)(2,1)}, u32[]{:S(2)}) copy-start(bf16[16,64,256]{2,1,0:T(8,128)(2,1)} %bases.1) | copy-start | bytes 1572868
  8.1 23.6 %copy-start.4 = (bf16[32,64,64]{2,1,0:T(8,128)(2,1)S(1)}, bf16[32,64,64]{2,1,0:T(8,128)(2,1)}, u32[]{:S(2)}) copy-start(bf16[32,64,64]{2,1,0:T(8,128)(2,1)} %par_c.1) | copy-start | bytes 786436
  8.1 23.6 %copy-start.5 = (bf16[16,64,64]{2,1,0:T(8,128)(2,1)S(1)}, bf16[16,64,64]{2,1,0:T(8,128)(2,1)}, u32[]{:S(2)}) copy-start(bf16[16,64,64]{2,1,0:T(8,128)(2,1)} %transfers.1) | copy-start | bytes 393220
  8.1 23.6 %copy-start.7 = (s32[128,2]{0,1:T(2,128)S(1)}, s32[128,2]{0,1:T(2,128)}, u32[]{:S(2)}) copy-start(s32[128,2]{0,1:T(2,128)} %param.18) | copy-start | bytes 3076
  8.1 23.6 %copy-start.8 = (s32[32,2]{0,1:T(2,128)S(1)}, s32[32,2]{0,1:T(2,128)}, u32[]{:S(2)}) copy-start(s32[32,2]{0,1:T(2,128)} %param.20) | copy-start | bytes 772
  8.1 23.6 %copy-start.9 = (s32[16]{0:T(128)S(1)}, s32[16]{0:T(128)}, u32[]{:S(2)}) copy-start(s32[16]{0:T(128)} %param.17) | copy-start | bytes 196
  8.1 22.0 %all-to-all-start = ((bf16[16,8,1920]{2,1,0:T(8,128)(2,1)}), bf16[16,8,1920]{2,1,0:T(8,128)(2,1)S(1)}, u32[]{:S(2)}, u32[]{:S(2)}) async-start(bf16[16,8,1920]{2,1,0:T(8,128)(2,1)} %bitcast.8), calls=%async_computation | async-start | bytes 983040 | tf_op jit(solution)/shard_map/all_to_all | solution.py:374
  23.2 3.2 %collective-permute-start.1 = (bf16[16,8,256]{2,1,0:T(8,128)(2,1)S(1)}, bf16[16,8,256]{2,1,0:T(8,128)(2,1)S(1)}, u32[]{:S(2)}, u32[]{:S(2)}) collective-permute-start(bf16[16,8,256]{2,1,0:T(8,128)(2,1)S(1)} %get-tuple-element.7), channel_id=1, source_target_pairs={{0,1},{1,2},{2,3},{3,4},{4,5},{5,6},{6,7},{7,8},{8,9},{9,10},{10,1... | collective-permute-start | bytes 196616 | tf_op jit(solution)/shard_map/ppermute | solution.py:302
  30.2 1.5 %collective-permute-start.2 = (bf16[128,768]{1,0:T(8,128)(2,1)S(1)}, bf16[128,768]{1,0:T(8,128)(2,1)S(1)}, u32[]{:S(2)}, u32[]{:S(2)}) collective-permute-start(bf16[128,768]{1,0:T(8,128)(2,1)S(1)} %slice.4), channel_id=1, source_target_pairs={{0,1},{1,0},{2,3},{3,2},{4,5},{5,4},{6,7},{7,6},{8,9},{9,8},{10,11... | collective-permute-start | bytes 589832 | tf_op jit(solution)/shard_map/ppermute | solution.py:404

commit v7 on v6

--- a/solution.py
+++ b/solution.py
@@ -46,6 +46,26 @@
     rank = width // rhs
     for r in range(rhs):
         ref[pl.ds(r, count, stride=rhs), :] = value[:, r * rank : (r + 1) * rank]
+
+
+def row_sums(parts):
+    row = iota(parts[0].shape, 0)
+    for step in (4, 2, 1):
+        upper = row % (2 * step) >= step
+        merged = []
+        for a, b in zip(parts[:step], parts[step:]):
+            swapped = jnp.where(upper, a, b)
+            if step == 4:
+                moved = pltpu.roll(swapped, 4, axis=0)
+            else:
+                moved = jnp.where(
+                    upper,
+                    pltpu.roll(swapped, step, axis=0),
+                    pltpu.roll(swapped, 8 - step, axis=0),
+                )
+            merged.append(jnp.where(upper, b, a) + moved)
+        parts = merged
+    return parts[0]
 
 
 def fetch(pairs, sems):
@@ -127,11 +147,18 @@
     owner_hot = one_hot(far_pairs[0:1, :] % leaves == iota((leaves, slots), 0))
     a_ref[...] = dot_tn(m2.astype(BF16), owner_hot)
     half = rank // 2
+    each = max(1, pairs // (slots // LANES * 2 * (rank // 8)))
     for sb in range(slots // LANES):
         lanes = slice(sb * LANES, (sb + 1) * LANES)
         for jh in range(2):
+            first_pair = (sb * 2 + jh) * (rank // 8) * each
 
             def body(k8, acc):
+                for i in range(each if first_pair < pairs else 0):
+                    s = first_pair + k8 * each + i
+                    q = par_smem[0, s] % parents
+                    x = pm3[pl.ds(pl.multiple_of(q * rhs, rhs), rhs), :].astype(BF16)
+                    pb[pl.ds(pl.multiple_of(s * rhs, rhs), rhs), :] = dot_nn(x, par_c[s])
                 rows_a = [
                     a_ref[pl.ds(pl.multiple_of(r * rank + k8 * 8, 8), 8), lanes]
                     for r in range(rhs)
@@ -155,10 +182,6 @@
         lanes = slice(sb * LANES, (sb + 1) * LANES)
         send[lanes, 0 : width + LANES] = dot_nt(unit, ob[:, lanes]).astype(BF16)
 
-    for s in range(pairs):
-        q = par_smem[0, s] % parents
-        x = pm3[pl.ds(pl.multiple_of(q * rhs, rhs), rhs), :].astype(BF16)
-        pb[s * rhs : (s + 1) * rhs, :] = dot_nn(x, par_c[s])
     high, low = split2(rows_to_lanes(pb, pairs, rhs))
     hot = one_hot(par_pairs[1:2, :] == iota((rows, pairs), 0))
     at = width + LANES
@@ -212,6 +235,7 @@
     pf,
     lf,
     pg,
+    dn,
 ):
     leaves, rank, _ = bases.shape
     slots = far_c.shape[2]
@@ -238,11 +262,35 @@
     b_ref[...] = total
 
     hot = one_hot(par_pairs[1:2, :] == iota((rows, pairs), 0))
-    picked = dot_tn(hot, shared[:, 2 * width :])
-    lanes_to_rows(g_ref, picked, rhs)
-    for s in range(pairs):
-        x = g_ref[s * rhs : (s + 1) * rhs, :].astype(BF16)
-        pf[s * rhs : (s + 1) * rhs, :] = dot_nt(x, par_c[s])
+    lanes_to_rows(g_ref, dot_tn(hot, shared[:, 2 * width :]), rhs)
+
+    def couple(k8, sb):
+        lanes = slice(sb * LANES, (sb + 1) * LANES)
+        parts = [[] for _ in range(rhs)]
+        for i in range(8):
+            c = far_c[k8 * 8 + i, :, lanes].astype(F32)
+            for r in range(rhs):
+                prod = c * b_ref[r * rank : (r + 1) * rank, lanes]
+                parts[r].append(sum(prod[j * 8 : (j + 1) * 8] for j in range(rank // 8)))
+        for r in range(rhs):
+            fw[pl.ds(pl.multiple_of(r * rank + k8 * 8, 8), 8), lanes] = row_sums(parts[r])
+
+    blocks = slots // LANES
+    trips = rank // 16
+    each = max(1, pairs // (blocks * trips))
+    for sb in range(blocks):
+        first_pair = sb * trips * each
+
+        def body(k8, carry):
+            for i in range(each if first_pair < pairs else 0):
+                s = first_pair + k8 * each + i
+                at = pl.ds(pl.multiple_of(s * rhs, rhs), rhs)
+                pf[at, :] = dot_nt(g_ref[at, :].astype(BF16), par_c[s])
+            couple(k8, sb)
+            return carry
+
+        lax.fori_loop(0, trips, body, 0)
+
     high, low = split2(rows_to_lanes(pf, pairs, rhs))
     hot = one_hot(par_pairs[0:1, :] % parents == iota((parents, pairs), 0))
     fold = one_hot(iota((parents, rows), 1) % parents == iota((parents, rows), 0))
@@ -250,22 +298,19 @@
     hot = one_hot(parent_of[...] % parents == iota((parents, leaves), 0))
     lanes_to_rows(pg, dot_tn(hot, locals_p.astype(BF16)), rhs)
 
-    for sb in range(slots // LANES):
-        lanes = slice(sb * LANES, (sb + 1) * LANES)
+    each = max(1, leaves // (blocks * trips))
+    for sb in range(blocks):
+        first_leaf = sb * trips * each
 
         def body(k8, carry):
-            for r in range(rhs):
-                b = b_ref[r * rank : (r + 1) * rank, lanes]
-                sums = [
-                    jnp.sum(far_c[k8 * 8 + i, :, lanes].astype(F32) * b, axis=0, keepdims=True)
-                    for i in range(8)
-                ]
-                fw[pl.ds(pl.multiple_of(r * rank + k8 * 8, 8), 8), lanes] = jnp.concatenate(
-                    sums, axis=0
-                )
+            for i in range(each if first_leaf < leaves else 0):
+                l = first_leaf + k8 * each + i
+                at = pl.ds(pl.multiple_of(l * rhs, rhs), rhs)
+                dn[at, :] = dot_nn(pg[at, :].astype(BF16), transfers[l])
+            couple(trips + k8, sb)
             return carry
 
-        lax.fori_loop(0, rank // 8, body, 0)
+        lax.fori_loop(0, trips, body, 0)
 
     hot = one_hot(far_pairs[0:1, :] % leaves == iota((leaves, slots), 0))
     high, low = split2(fw[...])
@@ -277,13 +322,12 @@
 
     for l in range(leaves):
         at = slice(l * rhs, (l + 1) * rhs)
-        down = dot_nn(pg[at, :].astype(BF16), transfers[l])
-        mine = (lf[at, :] + down).astype(BF16)
+        mine = (lf[at, :] + dn[at, :]).astype(BF16)
         near = near_own[l] + near_back[l].astype(F32)
         out[l] = dot_nn(mine, bases[l]) + near
 
 
-def after(value, earlier):
+def after(value, earlier, vmem_limit):
     anywhere = pl.BlockSpec(memory_space=pl.ANY)
     return pl.pallas_call(
         lambda value, earlier, same: None,
@@ -291,7 +335,7 @@
         in_specs=[anywhere] * 2,
         out_specs=anywhere,
         input_output_aliases={0: 0},
-        compiler_params=pltpu.CompilerParams(vmem_limit_bytes=1024 * 1024),
+        compiler_params=pltpu.CompilerParams(vmem_limit_bytes=vmem_limit),
         name="after",
     )(value, earlier)
 
@@ -370,7 +414,7 @@
         cost_estimate=cost(10_000_000),
         name="upward",
     )(charges, bases, transfers, parent_of, far_pairs, far_c, par_pairs, par_coupling)
-    send = after(send, following)
+    send = after(send, following, 107 << 19)
     got = lax.all_to_all(send, "sfc", split_axis=0, concat_axis=0, tiled=True)
     steps = 8
     selves, nears = leaves // steps, near_blocks.shape[0] // steps
@@ -400,7 +444,7 @@
     )(near_pairs, charges, following, self_blocks, near_blocks)
     near_back = passed_along(near_away, "sfc", 1)
 
-    got = after(got, near_back)
+    got = after(got, near_back, 1 << 20)
     mom2 = lax.ppermute(
         got[:, 2 * width + LANES :], "sfc", [(i, i ^ 1) for i in range(devices)]
     )
@@ -415,6 +459,7 @@
             pltpu.VMEM((width, slots), F32),
             pltpu.VMEM((pairs * rhs, rank), F32),
             pltpu.VMEM((pairs * rhs, rank), F32),
+            pltpu.VMEM((leaves * rhs, rank), F32),
             pltpu.VMEM((leaves * rhs, rank), F32),
             pltpu.VMEM((leaves * rhs, rank), F32),
         ],

time: 37.2 us -> 36.9 us (level)
  local copies, waits for them, and re-layouts: 1.86 us -> 0.07 us
  Pallas kernels: 16.5 us -> 18.1 us
    unnamed x22 -> x18, local copies, waits for them, and re-layouts: 1.84 us -> 0.05 us
    pallas_call x1, Pallas kernels: 4.8 us -> 6.29 us  [on_device(): pl.pallas_call(pre_kernel, out_shape=jax.ShapeDtypeStruct((rows, columns)...]
  transfers between devices with their start and end apart: 4 -> 4, of which waited for: 3 -> 3; matrix products, arithmetic and copies ran while one was open for 0% -> 0% of each run, Pallas kernels for 32% -> 36%
where the time goes in v7:
time: 36.9 us; the launch traced here: 36.5 us
  Pallas kernels  18.1 us (49%)
  starting transfers between devices  12.2 us (33%)
  waiting for transfers between devices  5.99 us (16%)
    all_to_all x1, starting transfers between devices, on_device(): got = lax.all_to_all(send, 'sfc', split_axis=0, concat_axis=0, tiled=True)  8.26 us
    pallas_call x1, Pallas kernels, on_device(): pl.pallas_call(near_kernel, grid=(steps,), out_shape=[jax.ShapeDtypeStruc...  6.77 us
    pallas_call x1, Pallas kernels, on_device(): pl.pallas_call(pre_kernel, out_shape=jax.ShapeDtypeStruct((rows, columns)...  6.29 us
    pallas_call x1, Pallas kernels, on_device(): pl.pallas_call(post_kernel, out_shape=jax.ShapeDtypeStruct((leaves, rhs,...  5.05 us
    all_to_all x1, waiting for transfers between devices, on_device(): got = lax.all_to_all(send, 'sfc', split_axis=0, concat_axis=0, tiled=True)  3.78 us
    ppermute x2, starting transfers between devices, passed_along(): lax.ppermute(value, axis, [(source, source + steps) for source in range(l...  3.73 us
    ppermute x1, waiting for transfers between devices, on_device(): lax.ppermute(got[:, 2 * width + LANES:], 'sfc', [(i, i ^ 1) for i in rang...  1.33 us
    ppermute x2, waiting for transfers between devices, passed_along(): lax.ppermute(value, axis, [(source, source + steps) for source in range(l...  0.88 us
  transfers between devices with their start and end apart: 4, of which 3 were waited for; matrix products, arithmetic and copies ran while one was open for 0% of the time, Pallas kernels for 36%

profile of v7, /device:TPU:0, one launch (start us, length us, event | category | flops | bytes accessed | tf_op | source)
XLA Modules:
  0.0 36.5 jit_solution(5198780196542437469)
XLA Ops:
  0.0 0.0 copy-start.4
  0.0 0.0 copy-start.8
  0.0 1.4 %collective-permute-start = (bf16[16,8,256]{2,1,0:T(8,128)(2,1)}, bf16[16,8,256]{2,1,0:T(8,128)(2,1)S(1)}, u32[]{:S(2)}, u32[]{:S(2)}) collective-permute-start(bf16[16,8,256]{2,1,0:T(8,128)(2,1)} %charges.1), channel_id=1, source_target_pairs={{1,0},{2,1},{3,2},{4,3},{5,4},{6,5},{7,6},{8,7},{9,8},{10,9},{11,1... | collective-permute-start | bytes 196616 | tf_op jit(solution)/shard_map/ppermute | solution.py:346
  1.4 6.3 %upward.1.value = bf16[128,1920]{1,0:T(8,128)(2,1)} custom-call(bf16[16,8,256]{2,1,0:T(8,128)(2,1)} %charges.1, bf16[16,64,256]{2,1,0:T(8,128)(2,1)} %bases.1, bf16[16,64,64]{2,1,0:T(8,128)(2,1)} %transfers.1, s32[1,16]{1,0:T(1,128)} %bitcast.15, s32[2,128]{1,0:T(2,128)} %bitcast.10, bf16[64,64,128]{2,1,0:T(8,128)(2,1)} %bitcast.8, s32[2,32]{1,0:T(2,128)} %bitcast.13, ...), custom_call_target="tpu_custom_call" | custom-call | flops 40000000 | bytes 10000000 | tf_op jit(solution)/shard_map/upward/pallas_call | solution.py:390
  7.7 0.0 collective-permute-done.earlier.following
  7.7 0.0 copy-start
  7.8 0.0 copy-start.1
  7.8 0.0 copy-start.2
  7.8 0.0 copy-start.3
  7.8 0.0 copy-start.5
  7.8 0.0 copy-start.6
  7.8 0.0 copy-start.7
  7.8 8.3 %all-to-all-start = ((bf16[16,8,1920]{2,1,0:T(8,128)(2,1)}), bf16[16,8,1920]{2,1,0:T(8,128)(2,1)S(1)}, u32[]{:S(2)}, u32[]{:S(2)}) async-start(bf16[16,8,1920]{2,1,0:T(8,128)(2,1)} %bitcast.18), calls=%async_computation | async-start | bytes 983040 | tf_op jit(solution)/shard_map/all_to_all | solution.py:418
  16.1 0.0 copy-done.4
  16.1 0.0 copy-done.8
  16.1 6.8 %near.1 = (f32[16,8,256]{2,1,0:T(8,128)S(1)}, bf16[16,8,256]{2,1,0:T(8,128)(2,1)S(1)}) custom-call(s32[2,32]{1,0:T(2,128)S(1)} %bitcast.17, bf16[16,8,256]{2,1,0:T(8,128)(2,1)S(1)} %copy-done.4, bf16[16,8,256]{2,1,0:T(8,128)(2,1)S(1)} %collective-permute-done.earlier.following, bf16[16,256,256]{2,1,0:T(8,128)(2,1)} %self_blocks.1, ...), custom_call_target="tpu_custom_call" | custom-call | flops 80000000 | bytes 20000000 | tf_op jit(solution)/shard_map/near/pallas_call | solution.py:422
  22.9 2.3 %collective-permute-start.1 = (bf16[16,8,256]{2,1,0:T(8,128)(2,1)S(1)}, bf16[16,8,256]{2,1,0:T(8,128)(2,1)S(1)}, u32[]{:S(2)}, u32[]{:S(2)}) collective-permute-start(bf16[16,8,256]{2,1,0:T(8,128)(2,1)S(1)} %get-tuple-element.7), channel_id=1, source_target_pairs={{0,1},{1,2},{2,3},{3,4},{4,5},{5,6},{6,7},{7,8},{8,9},{9,10},{10,1... | collective-permute-start | bytes 196616 | tf_op jit(solution)/shard_map/ppermute | solution.py:346
  25.2 0.9 %collective-permute-done.1.earlier.near_back = bf16[16,8,256]{2,1,0:T(8,128)(2,1)S(1)} collective-permute-done((bf16[16,8,256]{2,1,0:T(8,128)(2,1)S(1)}, bf16[16,8,256]{2,1,0:T(8,128)(2,1)S(1)}, u32[]{:S(2)}, u32[]{:S(2)}) %collective-permute-start.1) | collective-permute-done | bytes 65568 | tf_op jit(solution)/shard_map/ppermute | solution.py:346
  26.1 3.8 %all-to-all-done = bf16[16,8,1920]{2,1,0:T(8,128)(2,1)S(1)} async-done(((bf16[16,8,1920]{2,1,0:T(8,128)(2,1)}), bf16[16,8,1920]{2,1,0:T(8,128)(2,1)S(1)}, u32[]{:S(2)}, u32[]{:S(2)}) %all-to-all-start) | async-done | bytes 491552 | tf_op jit(solution)/shard_map/all_to_all | solution.py:418
  29.9 0.2 collective-permute-start.2
  30.1 1.3 %collective-permute-done.2.mom2 = bf16[128,768]{1,0:T(8,128)(2,1)S(1)} collective-permute-done((bf16[128,768]{1,0:T(8,128)(2,1)S(1)}, bf16[128,768]{1,0:T(8,128)(2,1)S(1)}, u32[]{:S(2)}, u32[]{:S(2)}) %collective-permute-start.2) | collective-permute-done | bytes 196640 | tf_op jit(solution)/shard_map/ppermute | solution.py:448
  31.4 0.0 copy-done
  31.4 0.0 copy-done.1
  31.4 0.0 copy-done.2
  31.4 0.0 copy-done.3
  31.4 0.0 copy-done.5
  31.4 0.0 copy-done.6
  31.4 0.0 copy-done.7
  31.5 5.0 %downward.1 = f32[16,8,256]{2,1,0:T(8,128)} custom-call(s32[2,128]{1,0:T(2,128)S(1)} %bitcast.11, bf16[128,768]{1,0:T(8,128)(2,1)S(1)} %collective-permute-done.2.mom2, bf16[128,1920]{1,0:T(8,128)(2,1)S(1)} %after.3.got, bf16[16,64,256]{2,1,0:T(8,128)(2,1)S(1)} %copy-done.1, bf16[16,64,64]{2,1,0:T(8,128)(2,1)S(1)} %copy-done.3, s32[1,16]{1,0:T(1,128)S(1)} %bitcast.16, ...), custom_call_target="tpu_custom_call" | custom-call | tf_op jit(solution)/shard_map/downward/pallas_call | solution.py:452
  (3 shorter events, 0.0 us)
Async XLA Ops:
  0.0 16.1 %copy-start.4 = (bf16[16,8,256]{2,1,0:T(8,128)(2,1)S(1)}, bf16[16,8,256]{2,1,0:T(8,128)(2,1)}, u32[]{:S(2)}) copy-start(bf16[16,8,256]{2,1,0:T(8,128)(2,1)} %charges.1) | copy-start | bytes 196612
  0.0 16.1 %copy-start.8 = (s32[32,2]{0,1:T(2,128)S(1)}, s32[32,2]{0,1:T(2,128)}, u32[]{:S(2)}) copy-start(s32[32,2]{0,1:T(2,128)} %param.14) | copy-start | bytes 772
  0.0 7.7 %collective-permute-start = (bf16[16,8,256]{2,1,0:T(8,128)(2,1)}, bf16[16,8,256]{2,1,0:T(8,128)(2,1)S(1)}, u32[]{:S(2)}, u32[]{:S(2)}) collective-permute-start(bf16[16,8,256]{2,1,0:T(8,128)(2,1)} %charges.1), channel_id=1, source_target_pairs={{1,0},{2,1},{3,2},{4,3},{5,4},{6,5},{7,6},{8,7},{9,8},{10,9},{11,1... | collective-permute-start | bytes 196616 | tf_op jit(solution)/shard_map/ppermute | solution.py:346
  7.7 23.7 %copy-start = (bf16[128,64,64]{0,2,1:T(8,128)(2,1)S(1)}, bf16[128,64,64]{0,2,1:T(8,128)(2,1)}, u32[]{:S(2)}) copy-start(bf16[128,64,64]{0,2,1:T(8,128)(2,1)} %param.19) | copy-start | bytes 3145732
  7.8 23.7 %copy-start.1 = (bf16[16,64,256]{2,1,0:T(8,128)(2,1)S(1)}, bf16[16,64,256]{2,1,0:T(8,128)(2,1)}, u32[]{:S(2)}) copy-start(bf16[16,64,256]{2,1,0:T(8,128)(2,1)} %bases.1) | copy-start | bytes 1572868
  7.8 23.6 %copy-start.2 = (bf16[32,64,64]{2,1,0:T(8,128)(2,1)S(1)}, bf16[32,64,64]{2,1,0:T(8,128)(2,1)}, u32[]{:S(2)}) copy-start(bf16[32,64,64]{2,1,0:T(8,128)(2,1)} %par_c.1) | copy-start | bytes 786436
  7.8 23.6 %copy-start.3 = (bf16[16,64,64]{2,1,0:T(8,128)(2,1)S(1)}, bf16[16,64,64]{2,1,0:T(8,128)(2,1)}, u32[]{:S(2)}) copy-start(bf16[16,64,64]{2,1,0:T(8,128)(2,1)} %transfers.1) | copy-start | bytes 393220
  7.8 23.6 %copy-start.5 = (s32[128,2]{0,1:T(2,128)S(1)}, s32[128,2]{0,1:T(2,128)}, u32[]{:S(2)}) copy-start(s32[128,2]{0,1:T(2,128)} %param.18) | copy-start | bytes 3076
  7.8 23.6 %copy-start.6 = (s32[32,2]{0,1:T(2,128)S(1)}, s32[32,2]{0,1:T(2,128)}, u32[]{:S(2)}) copy-start(s32[32,2]{0,1:T(2,128)} %param.20) | copy-start | bytes 772
  7.8 23.6 %copy-start.7 = (s32[16]{0:T(128)S(1)}, s32[16]{0:T(128)}, u32[]{:S(2)}) copy-start(s32[16]{0:T(128)} %param.17) | copy-start | bytes 196
  7.8 22.0 %all-to-all-start = ((bf16[16,8,1920]{2,1,0:T(8,128)(2,1)}), bf16[16,8,1920]{2,1,0:T(8,128)(2,1)S(1)}, u32[]{:S(2)}, u32[]{:S(2)}) async-start(bf16[16,8,1920]{2,1,0:T(8,128)(2,1)} %bitcast.18), calls=%async_computation | async-start | bytes 983040 | tf_op jit(solution)/shard_map/all_to_all | solution.py:418
  22.9 3.2 %collective-permute-start.1 = (bf16[16,8,256]{2,1,0:T(8,128)(2,1)S(1)}, bf16[16,8,256]{2,1,0:T(8,128)(2,1)S(1)}, u32[]{:S(2)}, u32[]{:S(2)}) collective-permute-start(bf16[16,8,256]{2,1,0:T(8,128)(2,1)S(1)} %get-tuple-element.7), channel_id=1, source_target_pairs={{0,1},{1,2},{2,3},{3,4},{4,5},{5,6},{6,7},{7,8},{8,9},{9,10},{10,1... | collective-permute-start | bytes 196616 | tf_op jit(solution)/shard_map/ppermute | solution.py:346
  29.9 1.5 %collective-permute-start.2 = (bf16[128,768]{1,0:T(8,128)(2,1)S(1)}, bf16[128,768]{1,0:T(8,128)(2,1)S(1)}, u32[]{:S(2)}, u32[]{:S(2)}) collective-permute-start(bf16[128,768]{1,0:T(8,128)(2,1)S(1)} %slice.4), channel_id=1, source_target_pairs={{0,1},{1,0},{2,3},{3,2},{4,5},{5,4},{6,7},{7,6},{8,9},{9,8},{10,11... | collective-permute-start | bytes 589832 | tf_op jit(solution)/shard_map/ppermute | solution.py:448

commit v8 on v7

--- a/solution.py
+++ b/solution.py
@@ -146,19 +146,16 @@
 
     owner_hot = one_hot(far_pairs[0:1, :] % leaves == iota((leaves, slots), 0))
     a_ref[...] = dot_tn(m2.astype(BF16), owner_hot)
+    for s in range(pairs):
+        q = par_smem[0, s] % parents
+        x = pm3[pl.ds(pl.multiple_of(q * rhs, rhs), rhs), :].astype(BF16)
+        pb[s * rhs : (s + 1) * rhs, :] = dot_nn(x, par_c[s])
     half = rank // 2
-    each = max(1, pairs // (slots // LANES * 2 * (rank // 8)))
     for sb in range(slots // LANES):
         lanes = slice(sb * LANES, (sb + 1) * LANES)
         for jh in range(2):
-            first_pair = (sb * 2 + jh) * (rank // 8) * each
 
             def body(k8, acc):
-                for i in range(each if first_pair < pairs else 0):
-                    s = first_pair + k8 * each + i
-                    q = par_smem[0, s] % parents
-                    x = pm3[pl.ds(pl.multiple_of(q * rhs, rhs), rhs), :].astype(BF16)
-                    pb[pl.ds(pl.multiple_of(s * rhs, rhs), rhs), :] = dot_nn(x, par_c[s])
                 rows_a = [
                     a_ref[pl.ds(pl.multiple_of(r * rank + k8 * 8, 8), 8), lanes]
                     for r in range(rhs)
@@ -168,9 +165,8 @@
                     acc = tuple(acc[r] + c * rows_a[r][i : i + 1, :] for r in range(rhs))
                 return acc
 
-            acc = lax.fori_loop(
-                0, rank // 8, body, tuple(jnp.zeros((half, LANES), F32) for _ in range(rhs))
-            )
+            acc = tuple(jnp.zeros((half, LANES), F32) for _ in range(rhs))
+            acc = lax.fori_loop(0, rank // 8, body, acc, unroll=4)
             for r in range(rhs):
                 first = r * rank + jh * half
                 ob[first : first + half, lanes] = acc[r].astype(BF16)
@@ -275,22 +271,9 @@
         for r in range(rhs):
             fw[pl.ds(pl.multiple_of(r * rank + k8 * 8, 8), 8), lanes] = row_sums(parts[r])
 
-    blocks = slots // LANES
-    trips = rank // 16
-    each = max(1, pairs // (blocks * trips))
-    for sb in range(blocks):
-        first_pair = sb * trips * each
-
-        def body(k8, carry):
-            for i in range(each if first_pair < pairs else 0):
-                s = first_pair + k8 * each + i
-                at = pl.ds(pl.multiple_of(s * rhs, rhs), rhs)
-                pf[at, :] = dot_nt(g_ref[at, :].astype(BF16), par_c[s])
-            couple(k8, sb)
-            return carry
-
-        lax.fori_loop(0, trips, body, 0)
-
+    for s in range(pairs):
+        at = slice(s * rhs, (s + 1) * rhs)
+        pf[at, :] = dot_nt(g_ref[at, :].astype(BF16), par_c[s])
     high, low = split2(rows_to_lanes(pf, pairs, rhs))
     hot = one_hot(par_pairs[0:1, :] % parents == iota((parents, pairs), 0))
     fold = one_hot(iota((parents, rows), 1) % parents == iota((parents, rows), 0))
@@ -298,19 +281,17 @@
     hot = one_hot(parent_of[...] % parents == iota((parents, leaves), 0))
     lanes_to_rows(pg, dot_tn(hot, locals_p.astype(BF16)), rhs)
 
-    each = max(1, leaves // (blocks * trips))
-    for sb in range(blocks):
-        first_leaf = sb * trips * each
+    for l in range(leaves):
+        at = slice(l * rhs, (l + 1) * rhs)
+        dn[at, :] = dot_nn(pg[at, :].astype(BF16), transfers[l])
+
+    for sb in range(slots // LANES):
 
         def body(k8, carry):
-            for i in range(each if first_leaf < leaves else 0):
-                l = first_leaf + k8 * each + i
-                at = pl.ds(pl.multiple_of(l * rhs, rhs), rhs)
-                dn[at, :] = dot_nn(pg[at, :].astype(BF16), transfers[l])
-            couple(trips + k8, sb)
+            couple(k8, sb)
             return carry
 
-        lax.fori_loop(0, trips, body, 0)
+        lax.fori_loop(0, rank // 8, body, 0, unroll=4)
 
     hot = one_hot(far_pairs[0:1, :] % leaves == iota((leaves, slots), 0))
     high, low = split2(fw[...])

time: 36.9 us -> 34.6 us (0.938)
  Pallas kernels: 18.1 us -> 15.8 us
    pallas_call x1, Pallas kernels: 6.29 us -> 4.64 us  [on_device(): pl.pallas_call(pre_kernel, out_shape=jax.ShapeDtypeStruct((rows, columns)...]
    pallas_call x1, Pallas kernels: 5.05 us -> 4.41 us  [on_device(): pl.pallas_call(post_kernel, out_shape=jax.ShapeDtypeStruct((leaves, rhs,...]
  transfers between devices with their start and end apart: 4 -> 4, of which waited for: 3 -> 3; matrix products, arithmetic and copies ran while one was open for 0% -> 0% of each run, Pallas kernels for 36% -> 33%
where the time goes in v8:
time: 34.6 us; the launch traced here: 34.2 us
  Pallas kernels  15.8 us (46%)
  starting transfers between devices  12.2 us (35%)
  waiting for transfers between devices  5.99 us (17%)
    all_to_all x1, starting transfers between devices, on_device(): got = lax.all_to_all(send, 'sfc', split_axis=0, concat_axis=0, tiled=True)  8.26 us
    pallas_call x1, Pallas kernels, on_device(): pl.pallas_call(near_kernel, grid=(steps,), out_shape=[jax.ShapeDtypeStruc...  6.77 us
    pallas_call x1, Pallas kernels, on_device(): pl.pallas_call(pre_kernel, out_shape=jax.ShapeDtypeStruct((rows, columns)...  4.64 us
    pallas_call x1, Pallas kernels, on_device(): pl.pallas_call(post_kernel, out_shape=jax.ShapeDtypeStruct((leaves, rhs,...  4.41 us
    all_to_all x1, waiting for transfers between devices, on_device(): got = lax.all_to_all(send, 'sfc', split_axis=0, concat_axis=0, tiled=True)  3.78 us
    ppermute x2, starting transfers between devices, passed_along(): lax.ppermute(value, axis, [(source, source + steps) for source in range(l...  3.72 us
    ppermute x1, waiting for transfers between devices, on_device(): lax.ppermute(got[:, 2 * width + LANES:], 'sfc', [(i, i ^ 1) for i in rang...  1.33 us
    ppermute x2, waiting for transfers between devices, passed_along(): lax.ppermute(value, axis, [(source, source + steps) for source in range(l...  0.88 us
  transfers between devices with their start and end apart: 4, of which 3 were waited for; matrix products, arithmetic and copies ran while one was open for 0% of the time, Pallas kernels for 33%

profile of v8, /device:TPU:0, one launch (start us, length us, event | category | flops | bytes accessed | tf_op | source)
XLA Modules:
  0.0 34.2 jit_solution(3395071170867482451)
XLA Ops:
  0.0 0.0 copy-start.4
  0.0 0.0 copy-start.8
  0.0 1.4 %collective-permute-start = (bf16[16,8,256]{2,1,0:T(8,128)(2,1)}, bf16[16,8,256]{2,1,0:T(8,128)(2,1)S(1)}, u32[]{:S(2)}, u32[]{:S(2)}) collective-permute-start(bf16[16,8,256]{2,1,0:T(8,128)(2,1)} %charges.1), channel_id=1, source_target_pairs={{1,0},{2,1},{3,2},{4,3},{5,4},{6,5},{7,6},{8,7},{9,8},{10,9},{11,1... | collective-permute-start | bytes 196616 | tf_op jit(solution)/shard_map/ppermute | solution.py:327
  1.4 4.6 %upward.1.value = bf16[128,1920]{1,0:T(8,128)(2,1)} custom-call(bf16[16,8,256]{2,1,0:T(8,128)(2,1)} %charges.1, bf16[16,64,256]{2,1,0:T(8,128)(2,1)} %bases.1, bf16[16,64,64]{2,1,0:T(8,128)(2,1)} %transfers.1, s32[1,16]{1,0:T(1,128)} %bitcast.15, s32[2,128]{1,0:T(2,128)} %bitcast.10, bf16[64,64,128]{2,1,0:T(8,128)(2,1)} %bitcast.8, s32[2,32]{1,0:T(2,128)} %bitcast.13, ...), custom_call_target="tpu_custom_call" | custom-call | flops 40000000 | bytes 10000000 | tf_op jit(solution)/shard_map/upward/pallas_call | solution.py:371
  6.1 0.0 collective-permute-done.earlier.following
  6.1 0.0 copy-start
  6.1 0.0 copy-start.1
  6.1 0.0 copy-start.2
  6.1 0.0 copy-start.3
  6.1 0.0 copy-start.5
  6.2 0.0 copy-start.6
  6.2 0.0 copy-start.7
  6.2 8.3 %all-to-all-start = ((bf16[16,8,1920]{2,1,0:T(8,128)(2,1)}), bf16[16,8,1920]{2,1,0:T(8,128)(2,1)S(1)}, u32[]{:S(2)}, u32[]{:S(2)}) async-start(bf16[16,8,1920]{2,1,0:T(8,128)(2,1)} %bitcast.18), calls=%async_computation | async-start | bytes 983040 | tf_op jit(solution)/shard_map/all_to_all | solution.py:399
  14.4 0.0 copy-done.4
  14.5 0.0 copy-done.8
  14.5 6.8 %near.1 = (f32[16,8,256]{2,1,0:T(8,128)S(1)}, bf16[16,8,256]{2,1,0:T(8,128)(2,1)S(1)}) custom-call(s32[2,32]{1,0:T(2,128)S(1)} %bitcast.17, bf16[16,8,256]{2,1,0:T(8,128)(2,1)S(1)} %copy-done.4, bf16[16,8,256]{2,1,0:T(8,128)(2,1)S(1)} %collective-permute-done.earlier.following, bf16[16,256,256]{2,1,0:T(8,128)(2,1)} %self_blocks.1, ...), custom_call_target="tpu_custom_call" | custom-call | flops 80000000 | bytes 20000000 | tf_op jit(solution)/shard_map/near/pallas_call | solution.py:403
  21.2 2.3 %collective-permute-start.1 = (bf16[16,8,256]{2,1,0:T(8,128)(2,1)S(1)}, bf16[16,8,256]{2,1,0:T(8,128)(2,1)S(1)}, u32[]{:S(2)}, u32[]{:S(2)}) collective-permute-start(bf16[16,8,256]{2,1,0:T(8,128)(2,1)S(1)} %get-tuple-element.7), channel_id=1, source_target_pairs={{0,1},{1,2},{2,3},{3,4},{4,5},{5,6},{6,7},{7,8},{8,9},{9,10},{10,1... | collective-permute-start | bytes 196616 | tf_op jit(solution)/shard_map/ppermute | solution.py:327
  23.6 0.9 %collective-permute-done.1.earlier.near_back = bf16[16,8,256]{2,1,0:T(8,128)(2,1)S(1)} collective-permute-done((bf16[16,8,256]{2,1,0:T(8,128)(2,1)S(1)}, bf16[16,8,256]{2,1,0:T(8,128)(2,1)S(1)}, u32[]{:S(2)}, u32[]{:S(2)}) %collective-permute-start.1) | collective-permute-done | bytes 65568 | tf_op jit(solution)/shard_map/ppermute | solution.py:327
  24.4 3.8 %all-to-all-done = bf16[16,8,1920]{2,1,0:T(8,128)(2,1)S(1)} async-done(((bf16[16,8,1920]{2,1,0:T(8,128)(2,1)}), bf16[16,8,1920]{2,1,0:T(8,128)(2,1)S(1)}, u32[]{:S(2)}, u32[]{:S(2)}) %all-to-all-start) | async-done | bytes 491552 | tf_op jit(solution)/shard_map/all_to_all | solution.py:399
  28.2 0.2 collective-permute-start.2
  28.4 1.3 %collective-permute-done.2.mom2 = bf16[128,768]{1,0:T(8,128)(2,1)S(1)} collective-permute-done((bf16[128,768]{1,0:T(8,128)(2,1)S(1)}, bf16[128,768]{1,0:T(8,128)(2,1)S(1)}, u32[]{:S(2)}, u32[]{:S(2)}) %collective-permute-start.2) | collective-permute-done | bytes 196640 | tf_op jit(solution)/shard_map/ppermute | solution.py:429
  29.7 0.0 copy-done
  29.7 0.0 copy-done.1
  29.8 0.0 copy-done.2
  29.8 0.0 copy-done.3
  29.8 0.0 copy-done.5
  29.8 0.0 copy-done.6
  29.8 0.0 copy-done.7
  29.8 4.4 %downward.1 = f32[16,8,256]{2,1,0:T(8,128)} custom-call(s32[2,128]{1,0:T(2,128)S(1)} %bitcast.11, bf16[128,768]{1,0:T(8,128)(2,1)S(1)} %collective-permute-done.2.mom2, bf16[128,1920]{1,0:T(8,128)(2,1)S(1)} %after.3.got, bf16[16,64,256]{2,1,0:T(8,128)(2,1)S(1)} %copy-done.1, bf16[16,64,64]{2,1,0:T(8,128)(2,1)S(1)} %copy-done.3, s32[1,16]{1,0:T(1,128)S(1)} %bitcast.16, ...), custom_call_target="tpu_custom_call" | custom-call | tf_op jit(solution)/shard_map/downward/pallas_call | solution.py:433
  (3 shorter events, 0.0 us)
Async XLA Ops:
  0.0 14.4 %copy-start.4 = (bf16[16,8,256]{2,1,0:T(8,128)(2,1)S(1)}, bf16[16,8,256]{2,1,0:T(8,128)(2,1)}, u32[]{:S(2)}) copy-start(bf16[16,8,256]{2,1,0:T(8,128)(2,1)} %charges.1) | copy-start | bytes 196612
  0.0 14.4 %copy-start.8 = (s32[32,2]{0,1:T(2,128)S(1)}, s32[32,2]{0,1:T(2,128)}, u32[]{:S(2)}) copy-start(s32[32,2]{0,1:T(2,128)} %param.14) | copy-start | bytes 772
  0.0 6.1 %collective-permute-start = (bf16[16,8,256]{2,1,0:T(8,128)(2,1)}, bf16[16,8,256]{2,1,0:T(8,128)(2,1)S(1)}, u32[]{:S(2)}, u32[]{:S(2)}) collective-permute-start(bf16[16,8,256]{2,1,0:T(8,128)(2,1)} %charges.1), channel_id=1, source_target_pairs={{1,0},{2,1},{3,2},{4,3},{5,4},{6,5},{7,6},{8,7},{9,8},{10,9},{11,1... | collective-permute-start | bytes 196616 | tf_op jit(solution)/shard_map/ppermute | solution.py:327
  6.1 23.7 %copy-start = (bf16[128,64,64]{0,2,1:T(8,128)(2,1)S(1)}, bf16[128,64,64]{0,2,1:T(8,128)(2,1)}, u32[]{:S(2)}) copy-start(bf16[128,64,64]{0,2,1:T(8,128)(2,1)} %param.19) | copy-start | bytes 3145732
  6.1 23.6 %copy-start.1 = (bf16[16,64,256]{2,1,0:T(8,128)(2,1)S(1)}, bf16[16,64,256]{2,1,0:T(8,128)(2,1)}, u32[]{:S(2)}) copy-start(bf16[16,64,256]{2,1,0:T(8,128)(2,1)} %bases.1) | copy-start | bytes 1572868
  6.1 23.6 %copy-start.2 = (bf16[32,64,64]{2,1,0:T(8,128)(2,1)S(1)}, bf16[32,64,64]{2,1,0:T(8,128)(2,1)}, u32[]{:S(2)}) copy-start(bf16[32,64,64]{2,1,0:T(8,128)(2,1)} %par_c.1) | copy-start | bytes 786436
  6.1 23.6 %copy-start.3 = (bf16[16,64,64]{2,1,0:T(8,128)(2,1)S(1)}, bf16[16,64,64]{2,1,0:T(8,128)(2,1)}, u32[]{:S(2)}) copy-start(bf16[16,64,64]{2,1,0:T(8,128)(2,1)} %transfers.1) | copy-start | bytes 393220
  6.1 23.6 %copy-start.5 = (s32[128,2]{0,1:T(2,128)S(1)}, s32[128,2]{0,1:T(2,128)}, u32[]{:S(2)}) copy-start(s32[128,2]{0,1:T(2,128)} %param.18) | copy-start | bytes 3076
  6.2 23.6 %copy-start.6 = (s32[32,2]{0,1:T(2,128)S(1)}, s32[32,2]{0,1:T(2,128)}, u32[]{:S(2)}) copy-start(s32[32,2]{0,1:T(2,128)} %param.20) | copy-start | bytes 772
  6.2 23.6 %copy-start.7 = (s32[16]{0:T(128)S(1)}, s32[16]{0:T(128)}, u32[]{:S(2)}) copy-start(s32[16]{0:T(128)} %param.17) | copy-start | bytes 196
  6.2 22.0 %all-to-all-start = ((bf16[16,8,1920]{2,1,0:T(8,128)(2,1)}), bf16[16,8,1920]{2,1,0:T(8,128)(2,1)S(1)}, u32[]{:S(2)}, u32[]{:S(2)}) async-start(bf16[16,8,1920]{2,1,0:T(8,128)(2,1)} %bitcast.18), calls=%async_computation | async-start | bytes 983040 | tf_op jit(solution)/shard_map/all_to_all | solution.py:399
  21.2 3.2 %collective-permute-start.1 = (bf16[16,8,256]{2,1,0:T(8,128)(2,1)S(1)}, bf16[16,8,256]{2,1,0:T(8,128)(2,1)S(1)}, u32[]{:S(2)}, u32[]{:S(2)}) collective-permute-start(bf16[16,8,256]{2,1,0:T(8,128)(2,1)S(1)} %get-tuple-element.7), channel_id=1, source_target_pairs={{0,1},{1,2},{2,3},{3,4},{4,5},{5,6},{6,7},{7,8},{8,9},{9,10},{10,1... | collective-permute-start | bytes 196616 | tf_op jit(solution)/shard_map/ppermute | solution.py:327
  28.2 1.5 %collective-permute-start.2 = (bf16[128,768]{1,0:T(8,128)(2,1)S(1)}, bf16[128,768]{1,0:T(8,128)(2,1)S(1)}, u32[]{:S(2)}, u32[]{:S(2)}) collective-permute-start(bf16[128,768]{1,0:T(8,128)(2,1)S(1)} %slice.4), channel_id=1, source_target_pairs={{0,1},{1,0},{2,3},{3,2},{4,5},{5,4},{6,7},{7,6},{8,9},{9,8},{10,11... | collective-permute-start | bytes 589832 | tf_op jit(solution)/shard_map/ppermute | solution.py:429

commit v9 on v8

--- a/solution.py
+++ b/solution.py
@@ -184,31 +184,42 @@
     send[:, at : at + width] = (dot_nn(hot, high) + dot_nn(hot, low)).astype(BF16)
 
 
-def near_kernel(pairs, charges, following, self_blocks, near_blocks, own, away, ext, out):
-    leaves = charges.shape[0]
+def near_kernel(pairs, charges, following, self_blocks, near_blocks, own, away, ct, acc, back):
+    leaves, rhs, panels = charges.shape
     step = pl.program_id(0)
     selves, nears = self_blocks.shape[0], near_blocks.shape[0]
 
     @pl.when(step == 0)
     def _():
-        ext[0:leaves] = charges[...]
-        ext[leaves:] = following[...]
-        out[...] = jnp.zeros_like(out)
-
-    terms = [(step * selves + i, dot_nt(ext[step * selves + i], self_blocks[i])) for i in range(selves)]
+        ct[0] = charges[...].astype(F32).reshape(leaves * rhs, panels).T
+        ct[1] = following[...].astype(F32).reshape(leaves * rhs, panels).T
+        acc[...] = jnp.zeros_like(acc)
+        back[...] = jnp.zeros_like(back)
+
+    column_leaf = iota((panels, leaves * rhs), 1) // rhs
+    total = None
+    for i in range(selves):
+        placed = jnp.where(column_leaf == step * selves + i, ct[0], 0.0).astype(BF16)
+        term = dot_nn(self_blocks[i], placed)
+        total = term if total is None else total + term
+    terms = []
     for i in range(nears):
         a, b = pairs[0, step * nears + i], pairs[1, step * nears + i]
         first = (a // leaves) * leaves
         a, b = a - first, b - first
-        terms.append((a, dot_nt(ext[b], near_blocks[i])))
-        terms.append((b, dot_nn(ext[a], near_blocks[i])))
+        shift = (a - b + 2 * leaves) % leaves * rhs
+        turned = pltpu.roll(ct[b // leaves], shift, axis=1)
+        placed = jnp.where(column_leaf == a, turned, 0.0).astype(BF16)
+        total = total + dot_nn(near_blocks[i], placed)
+        terms.append((b, dot_nn(charges[a], near_blocks[i])))
+    acc[...] += total
     for at, term in terms:
-        out[at] += term
+        back[at] += term
 
     @pl.when(step == pl.num_programs(0) - 1)
     def _():
-        own[...] = out[0:leaves]
-        away[...] = out[leaves:].astype(BF16)
+        own[...] = acc[...].T.reshape(leaves, rhs, panels) + back[0:leaves]
+        away[...] = back[leaves:].astype(BF16)
 
 
 def post_kernel(
@@ -416,7 +427,8 @@
         ],
         out_specs=[whole(leaves, rhs, panels)] * 2,
         scratch_shapes=[
-            pltpu.VMEM((2 * leaves, rhs, panels), BF16),
+            pltpu.VMEM((2, panels, leaves * rhs), F32),
+            pltpu.VMEM((panels, leaves * rhs), F32),
             pltpu.VMEM((2 * leaves, rhs, panels), F32),
         ],
         compiler_params=pltpu.CompilerParams(vmem_limit_bytes=52 * 1024 * 1024),

time: 34.6 us -> 34.6 us (level)
  Pallas kernels: 15.8 us -> 16.3 us
  waiting for transfers between devices: 5.99 us -> 5.5 us
    all_to_all x1, waiting for transfers between devices: 3.78 us -> 3.28 us  [on_device(): got = lax.all_to_all(send, 'sfc', split_axis=0, concat_axis=0, tiled=True)]
    pallas_call x1, Pallas kernels: 6.77 us -> 7.26 us  [on_device(): pl.pallas_call(near_kernel, grid=(steps,), out_shape=[jax.ShapeDtypeStruc...]
  transfers between devices with their start and end apart: 4 -> 4, of which waited for: 3 -> 3; matrix products, arithmetic and copies ran while one was open for 0% -> 0% of each run, Pallas kernels for 33% -> 35%
where the time goes in v9:
time: 34.6 us; the launch traced here: 34.2 us
  Pallas kernels  16.3 us (47%)
  starting transfers between devices  12.2 us (35%)
  waiting for transfers between devices  5.5 us (16%)
    all_to_all x1, starting transfers between devices, on_device(): got = lax.all_to_all(send, 'sfc', split_axis=0, concat_axis=0, tiled=True)  8.26 us
    pallas_call x1, Pallas kernels, on_device(): pl.pallas_call(near_kernel, grid=(steps,), out_shape=[jax.ShapeDtypeStruc...  7.26 us
    pallas_call x1, Pallas kernels, on_device(): pl.pallas_call(pre_kernel, out_shape=jax.ShapeDtypeStruct((rows, columns)...  4.64 us
    pallas_call x1, Pallas kernels, on_device(): pl.pallas_call(post_kernel, out_shape=jax.ShapeDtypeStruct((leaves, rhs,...  4.41 us
    ppermute x2, starting transfers between devices, passed_along(): lax.ppermute(value, axis, [(source, source + steps) for source in range(l...  3.73 us
    all_to_all x1, waiting for transfers between devices, on_device(): got = lax.all_to_all(send, 'sfc', split_axis=0, concat_axis=0, tiled=True)  3.28 us
    ppermute x1, waiting for transfers between devices, on_device(): lax.ppermute(got[:, 2 * width + LANES:], 'sfc', [(i, i ^ 1) for i in rang...  1.33 us
    ppermute x2, waiting for transfers between devices, passed_along(): lax.ppermute(value, axis, [(source, source + steps) for source in range(l...  0.88 us
  transfers between devices with their start and end apart: 4, of which 3 were waited for; matrix products, arithmetic and copies ran while one was open for 0% of the time, Pallas kernels for 35%

profile of v9, /device:TPU:0, one launch (start us, length us, event | category | flops | bytes accessed | tf_op | source)
XLA Modules:
  0.0 34.2 jit_solution(12800011424267981481)
XLA Ops:
  0.0 0.0 copy-start.4
  0.0 0.0 copy-start.8
  0.0 1.4 %collective-permute-start = (bf16[16,8,256]{2,1,0:T(8,128)(2,1)}, bf16[16,8,256]{2,1,0:T(8,128)(2,1)S(1)}, u32[]{:S(2)}, u32[]{:S(2)}) collective-permute-start(bf16[16,8,256]{2,1,0:T(8,128)(2,1)} %charges.1), channel_id=1, source_target_pairs={{1,0},{2,1},{3,2},{4,3},{5,4},{6,5},{7,6},{8,7},{9,8},{10,9},{11,1... | collective-permute-start | bytes 196616 | tf_op jit(solution)/shard_map/ppermute | solution.py:338
  1.4 4.6 %upward.1.value = bf16[128,1920]{1,0:T(8,128)(2,1)} custom-call(bf16[16,8,256]{2,1,0:T(8,128)(2,1)} %charges.1, bf16[16,64,256]{2,1,0:T(8,128)(2,1)} %bases.1, bf16[16,64,64]{2,1,0:T(8,128)(2,1)} %transfers.1, s32[1,16]{1,0:T(1,128)} %bitcast.15, s32[2,128]{1,0:T(2,128)} %bitcast.10, bf16[64,64,128]{2,1,0:T(8,128)(2,1)} %bitcast.8, s32[2,32]{1,0:T(2,128)} %bitcast.13, ...), custom_call_target="tpu_custom_call" | custom-call | flops 40000000 | bytes 10000000 | tf_op jit(solution)/shard_map/upward/pallas_call | solution.py:382
  6.1 0.0 collective-permute-done.earlier.following
  6.1 0.0 copy-start
  6.1 0.0 copy-start.1
  6.1 0.0 copy-start.2
  6.1 0.0 copy-start.3
  6.1 0.0 copy-start.5
  6.2 0.0 copy-start.6
  6.2 0.0 copy-start.7
  6.2 8.3 %all-to-all-start = ((bf16[16,8,1920]{2,1,0:T(8,128)(2,1)}), bf16[16,8,1920]{2,1,0:T(8,128)(2,1)S(1)}, u32[]{:S(2)}, u32[]{:S(2)}) async-start(bf16[16,8,1920]{2,1,0:T(8,128)(2,1)} %bitcast.18), calls=%async_computation | async-start | bytes 983040 | tf_op jit(solution)/shard_map/all_to_all | solution.py:410
  14.4 0.0 copy-done.4
  14.5 0.0 copy-done.8
  14.5 7.3 %near.1 = (f32[16,8,256]{2,1,0:T(8,128)S(1)}, bf16[16,8,256]{2,1,0:T(8,128)(2,1)S(1)}) custom-call(s32[2,32]{1,0:T(2,128)S(1)} %bitcast.17, bf16[16,8,256]{2,1,0:T(8,128)(2,1)S(1)} %copy-done.4, bf16[16,8,256]{2,1,0:T(8,128)(2,1)S(1)} %collective-permute-done.earlier.following, bf16[16,256,256]{2,1,0:T(8,128)(2,1)} %self_blocks.1, ...), custom_call_target="tpu_custom_call" | custom-call | flops 80000000 | bytes 20000000 | tf_op jit(solution)/shard_map/near/pallas_call | solution.py:414
  21.7 2.3 %collective-permute-start.1 = (bf16[16,8,256]{2,1,0:T(8,128)(2,1)S(1)}, bf16[16,8,256]{2,1,0:T(8,128)(2,1)S(1)}, u32[]{:S(2)}, u32[]{:S(2)}) collective-permute-start(bf16[16,8,256]{2,1,0:T(8,128)(2,1)S(1)} %get-tuple-element.7), channel_id=1, source_target_pairs={{0,1},{1,2},{2,3},{3,4},{4,5},{5,6},{6,7},{7,8},{8,9},{9,10},{10,1... | collective-permute-start | bytes 196616 | tf_op jit(solution)/shard_map/ppermute | solution.py:338
  24.1 0.9 %collective-permute-done.1.earlier.near_back = bf16[16,8,256]{2,1,0:T(8,128)(2,1)S(1)} collective-permute-done((bf16[16,8,256]{2,1,0:T(8,128)(2,1)S(1)}, bf16[16,8,256]{2,1,0:T(8,128)(2,1)S(1)}, u32[]{:S(2)}, u32[]{:S(2)}) %collective-permute-start.1) | collective-permute-done | bytes 65568 | tf_op jit(solution)/shard_map/ppermute | solution.py:338
  24.9 3.3 %all-to-all-done = bf16[16,8,1920]{2,1,0:T(8,128)(2,1)S(1)} async-done(((bf16[16,8,1920]{2,1,0:T(8,128)(2,1)}), bf16[16,8,1920]{2,1,0:T(8,128)(2,1)S(1)}, u32[]{:S(2)}, u32[]{:S(2)}) %all-to-all-start) | async-done | bytes 491552 | tf_op jit(solution)/shard_map/all_to_all | solution.py:410
  28.2 0.2 collective-permute-start.2
  28.4 1.3 %collective-permute-done.2.mom2 = bf16[128,768]{1,0:T(8,128)(2,1)S(1)} collective-permute-done((bf16[128,768]{1,0:T(8,128)(2,1)S(1)}, bf16[128,768]{1,0:T(8,128)(2,1)S(1)}, u32[]{:S(2)}, u32[]{:S(2)}) %collective-permute-start.2) | collective-permute-done | bytes 196640 | tf_op jit(solution)/shard_map/ppermute | solution.py:441
  29.7 0.0 copy-done
  29.7 0.0 copy-done.1
  29.8 0.0 copy-done.2
  29.8 0.0 copy-done.3
  29.8 0.0 copy-done.5
  29.8 0.0 copy-done.6
  29.8 0.0 copy-done.7
  29.8 4.4 %downward.1 = f32[16,8,256]{2,1,0:T(8,128)} custom-call(s32[2,128]{1,0:T(2,128)S(1)} %bitcast.11, bf16[128,768]{1,0:T(8,128)(2,1)S(1)} %collective-permute-done.2.mom2, bf16[128,1920]{1,0:T(8,128)(2,1)S(1)} %after.3.got, bf16[16,64,256]{2,1,0:T(8,128)(2,1)S(1)} %copy-done.1, bf16[16,64,64]{2,1,0:T(8,128)(2,1)S(1)} %copy-done.3, s32[1,16]{1,0:T(1,128)S(1)} %bitcast.16, ...), custom_call_target="tpu_custom_call" | custom-call | tf_op jit(solution)/shard_map/downward/pallas_call | solution.py:445
  (3 shorter events, 0.0 us)
Async XLA Ops:
  0.0 14.4 %copy-start.4 = (bf16[16,8,256]{2,1,0:T(8,128)(2,1)S(1)}, bf16[16,8,256]{2,1,0:T(8,128)(2,1)}, u32[]{:S(2)}) copy-start(bf16[16,8,256]{2,1,0:T(8,128)(2,1)} %charges.1) | copy-start | bytes 196612
  0.0 14.4 %copy-start.8 = (s32[32,2]{0,1:T(2,128)S(1)}, s32[32,2]{0,1:T(2,128)}, u32[]{:S(2)}) copy-start(s32[32,2]{0,1:T(2,128)} %param.14) | copy-start | bytes 772
  0.0 6.1 %collective-permute-start = (bf16[16,8,256]{2,1,0:T(8,128)(2,1)}, bf16[16,8,256]{2,1,0:T(8,128)(2,1)S(1)}, u32[]{:S(2)}, u32[]{:S(2)}) collective-permute-start(bf16[16,8,256]{2,1,0:T(8,128)(2,1)} %charges.1), channel_id=1, source_target_pairs={{1,0},{2,1},{3,2},{4,3},{5,4},{6,5},{7,6},{8,7},{9,8},{10,9},{11,1... | collective-permute-start | bytes 196616 | tf_op jit(solution)/shard_map/ppermute | solution.py:338
  6.1 23.7 %copy-start = (bf16[128,64,64]{0,2,1:T(8,128)(2,1)S(1)}, bf16[128,64,64]{0,2,1:T(8,128)(2,1)}, u32[]{:S(2)}) copy-start(bf16[128,64,64]{0,2,1:T(8,128)(2,1)} %param.19) | copy-start | bytes 3145732
  6.1 23.6 %copy-start.1 = (bf16[16,64,256]{2,1,0:T(8,128)(2,1)S(1)}, bf16[16,64,256]{2,1,0:T(8,128)(2,1)}, u32[]{:S(2)}) copy-start(bf16[16,64,256]{2,1,0:T(8,128)(2,1)} %bases.1) | copy-start | bytes 1572868
  6.1 23.6 %copy-start.2 = (bf16[32,64,64]{2,1,0:T(8,128)(2,1)S(1)}, bf16[32,64,64]{2,1,0:T(8,128)(2,1)}, u32[]{:S(2)}) copy-start(bf16[32,64,64]{2,1,0:T(8,128)(2,1)} %par_c.1) | copy-start | bytes 786436
  6.1 23.6 %copy-start.3 = (bf16[16,64,64]{2,1,0:T(8,128)(2,1)S(1)}, bf16[16,64,64]{2,1,0:T(8,128)(2,1)}, u32[]{:S(2)}) copy-start(bf16[16,64,64]{2,1,0:T(8,128)(2,1)} %transfers.1) | copy-start | bytes 393220
  6.1 23.6 %copy-start.5 = (s32[128,2]{0,1:T(2,128)S(1)}, s32[128,2]{0,1:T(2,128)}, u32[]{:S(2)}) copy-start(s32[128,2]{0,1:T(2,128)} %param.18) | copy-start | bytes 3076
  6.2 23.6 %copy-start.6 = (s32[32,2]{0,1:T(2,128)S(1)}, s32[32,2]{0,1:T(2,128)}, u32[]{:S(2)}) copy-start(s32[32,2]{0,1:T(2,128)} %param.20) | copy-start | bytes 772
  6.2 23.6 %copy-start.7 = (s32[16]{0:T(128)S(1)}, s32[16]{0:T(128)}, u32[]{:S(2)}) copy-start(s32[16]{0:T(128)} %param.17) | copy-start | bytes 196
  6.2 22.0 %all-to-all-start = ((bf16[16,8,1920]{2,1,0:T(8,128)(2,1)}), bf16[16,8,1920]{2,1,0:T(8,128)(2,1)S(1)}, u32[]{:S(2)}, u32[]{:S(2)}) async-start(bf16[16,8,1920]{2,1,0:T(8,128)(2,1)} %bitcast.18), calls=%async_computation | async-start | bytes 983040 | tf_op jit(solution)/shard_map/all_to_all | solution.py:410
  21.7 3.2 %collective-permute-start.1 = (bf16[16,8,256]{2,1,0:T(8,128)(2,1)S(1)}, bf16[16,8,256]{2,1,0:T(8,128)(2,1)S(1)}, u32[]{:S(2)}, u32[]{:S(2)}) collective-permute-start(bf16[16,8,256]{2,1,0:T(8,128)(2,1)S(1)} %get-tuple-element.7), channel_id=1, source_target_pairs={{0,1},{1,2},{2,3},{3,4},{4,5},{5,6},{6,7},{7,8},{8,9},{9,10},{10,1... | collective-permute-start | bytes 196616 | tf_op jit(solution)/shard_map/ppermute | solution.py:338
  28.2 1.5 %collective-permute-start.2 = (bf16[128,768]{1,0:T(8,128)(2,1)S(1)}, bf16[128,768]{1,0:T(8,128)(2,1)S(1)}, u32[]{:S(2)}, u32[]{:S(2)}) collective-permute-start(bf16[128,768]{1,0:T(8,128)(2,1)S(1)} %slice.4), channel_id=1, source_target_pairs={{0,1},{1,0},{2,3},{3,2},{4,5},{5,4},{6,7},{7,6},{8,9},{9,8},{10,11... | collective-permute-start | bytes 589832 | tf_op jit(solution)/shard_map/ppermute | solution.py:441

commit v10 on v8

--- a/solution.py
+++ b/solution.py
@@ -397,7 +397,7 @@
     )(charges, bases, transfers, parent_of, far_pairs, far_c, par_pairs, par_coupling)
     send = after(send, following, 107 << 19)
     got = lax.all_to_all(send, "sfc", split_axis=0, concat_axis=0, tiled=True)
-    steps = 8
+    steps = 4
     selves, nears = leaves // steps, near_blocks.shape[0] // steps
     whole = lambda *shape: pl.BlockSpec(shape, lambda i: (0,) * len(shape))
     near_own, near_away = pl.pallas_call(

time: 34.6 us -> 34.6 us (level)
  waiting for transfers between devices: 5.99 us -> 7.74 us
  Pallas kernels: 15.8 us -> 14.1 us
    pallas_call x1, Pallas kernels: 6.77 us -> 5.02 us  [on_device(): pl.pallas_call(near_kernel, grid=(steps,), out_shape=[jax.ShapeDtypeStruc...]
    all_to_all x1, waiting for transfers between devices: 3.78 us -> 5.53 us  [on_device(): got = lax.all_to_all(send, 'sfc', split_axis=0, concat_axis=0, tiled=True)]
  transfers between devices with their start and end apart: 4 -> 4, of which waited for: 3 -> 3; matrix products, arithmetic and copies ran while one was open for 0% -> 0% of each run, Pallas kernels for 33% -> 28%
where the time goes in v10:
time: 34.6 us; the launch traced here: 34.2 us
  Pallas kernels  14.1 us (41%)
  starting transfers between devices  12.2 us (35%)
  waiting for transfers between devices  7.74 us (22%)
    all_to_all x1, starting transfers between devices, on_device(): got = lax.all_to_all(send, 'sfc', split_axis=0, concat_axis=0, tiled=True)  8.26 us
    all_to_all x1, waiting for transfers between devices, on_device(): got = lax.all_to_all(send, 'sfc', split_axis=0, concat_axis=0, tiled=True)  5.53 us
    pallas_call x1, Pallas kernels, on_device(): pl.pallas_call(near_kernel, grid=(steps,), out_shape=[jax.ShapeDtypeStruc...  5.02 us
    pallas_call x1, Pallas kernels, on_device(): pl.pallas_call(pre_kernel, out_shape=jax.ShapeDtypeStruct((rows, columns)...  4.64 us
    pallas_call x1, Pallas kernels, on_device(): pl.pallas_call(post_kernel, out_shape=jax.ShapeDtypeStruct((leaves, rhs,...  4.41 us
    ppermute x2, starting transfers between devices, passed_along(): lax.ppermute(value, axis, [(source, source + steps) for source in range(l...  3.72 us
    ppermute x1, waiting for transfers between devices, on_device(): lax.ppermute(got[:, 2 * width + LANES:], 'sfc', [(i, i ^ 1) for i in rang...  1.33 us
    ppermute x2, waiting for transfers between devices, passed_along(): lax.ppermute(value, axis, [(source, source + steps) for source in range(l...  0.88 us
  transfers between devices with their start and end apart: 4, of which 3 were waited for; matrix products, arithmetic and copies ran while one was open for 0% of the time, Pallas kernels for 28%

profile of v10, /device:TPU:0, one launch (start us, length us, event | category | flops | bytes accessed | tf_op | source)
XLA Modules:
  0.0 34.2 jit_solution(18325285641579167868)
XLA Ops:
  0.0 0.0 copy-start.4
  0.0 0.0 copy-start.8
  0.0 1.4 %collective-permute-start = (bf16[16,8,256]{2,1,0:T(8,128)(2,1)}, bf16[16,8,256]{2,1,0:T(8,128)(2,1)S(1)}, u32[]{:S(2)}, u32[]{:S(2)}) collective-permute-start(bf16[16,8,256]{2,1,0:T(8,128)(2,1)} %charges.1), channel_id=1, source_target_pairs={{1,0},{2,1},{3,2},{4,3},{5,4},{6,5},{7,6},{8,7},{9,8},{10,9},{11,1... | collective-permute-start | bytes 196616 | tf_op jit(solution)/shard_map/ppermute | solution.py:327
  1.4 4.6 %upward.1.value = bf16[128,1920]{1,0:T(8,128)(2,1)} custom-call(bf16[16,8,256]{2,1,0:T(8,128)(2,1)} %charges.1, bf16[16,64,256]{2,1,0:T(8,128)(2,1)} %bases.1, bf16[16,64,64]{2,1,0:T(8,128)(2,1)} %transfers.1, s32[1,16]{1,0:T(1,128)} %bitcast.15, s32[2,128]{1,0:T(2,128)} %bitcast.10, bf16[64,64,128]{2,1,0:T(8,128)(2,1)} %bitcast.8, s32[2,32]{1,0:T(2,128)} %bitcast.13, ...), custom_call_target="tpu_custom_call" | custom-call | flops 40000000 | bytes 10000000 | tf_op jit(solution)/shard_map/upward/pallas_call | solution.py:371
  6.1 0.0 collective-permute-done.earlier.following
  6.1 0.0 copy-start
  6.1 0.0 copy-start.1
  6.1 0.0 copy-start.2
  6.1 0.0 copy-start.3
  6.1 0.0 copy-start.5
  6.2 0.0 copy-start.6
  6.2 0.0 copy-start.7
  6.2 8.3 %all-to-all-start = ((bf16[16,8,1920]{2,1,0:T(8,128)(2,1)}), bf16[16,8,1920]{2,1,0:T(8,128)(2,1)S(1)}, u32[]{:S(2)}, u32[]{:S(2)}) async-start(bf16[16,8,1920]{2,1,0:T(8,128)(2,1)} %bitcast.18), calls=%async_computation | async-start | bytes 983040 | tf_op jit(solution)/shard_map/all_to_all | solution.py:399
  14.4 0.0 copy-done.4
  14.5 0.0 copy-done.8
  14.5 5.0 %near.1 = (f32[16,8,256]{2,1,0:T(8,128)S(1)}, bf16[16,8,256]{2,1,0:T(8,128)(2,1)S(1)}) custom-call(s32[2,32]{1,0:T(2,128)S(1)} %bitcast.17, bf16[16,8,256]{2,1,0:T(8,128)(2,1)S(1)} %copy-done.4, bf16[16,8,256]{2,1,0:T(8,128)(2,1)S(1)} %collective-permute-done.earlier.following, bf16[16,256,256]{2,1,0:T(8,128)(2,1)} %self_blocks.1, ...), custom_call_target="tpu_custom_call" | custom-call | flops 80000000 | bytes 20000000 | tf_op jit(solution)/shard_map/near/pallas_call | solution.py:403
  19.5 2.3 %collective-permute-start.1 = (bf16[16,8,256]{2,1,0:T(8,128)(2,1)S(1)}, bf16[16,8,256]{2,1,0:T(8,128)(2,1)S(1)}, u32[]{:S(2)}, u32[]{:S(2)}) collective-permute-start(bf16[16,8,256]{2,1,0:T(8,128)(2,1)S(1)} %get-tuple-element.7), channel_id=1, source_target_pairs={{0,1},{1,2},{2,3},{3,4},{4,5},{5,6},{6,7},{7,8},{8,9},{9,10},{10,1... | collective-permute-start | bytes 196616 | tf_op jit(solution)/shard_map/ppermute | solution.py:327
  21.8 0.9 %collective-permute-done.1.earlier.near_back = bf16[16,8,256]{2,1,0:T(8,128)(2,1)S(1)} collective-permute-done((bf16[16,8,256]{2,1,0:T(8,128)(2,1)S(1)}, bf16[16,8,256]{2,1,0:T(8,128)(2,1)S(1)}, u32[]{:S(2)}, u32[]{:S(2)}) %collective-permute-start.1) | collective-permute-done | bytes 65568 | tf_op jit(solution)/shard_map/ppermute | solution.py:327
  22.7 5.5 %all-to-all-done = bf16[16,8,1920]{2,1,0:T(8,128)(2,1)S(1)} async-done(((bf16[16,8,1920]{2,1,0:T(8,128)(2,1)}), bf16[16,8,1920]{2,1,0:T(8,128)(2,1)S(1)}, u32[]{:S(2)}, u32[]{:S(2)}) %all-to-all-start) | async-done | bytes 491552 | tf_op jit(solution)/shard_map/all_to_all | solution.py:399
  28.2 0.2 collective-permute-start.2
  28.4 1.3 %collective-permute-done.2.mom2 = bf16[128,768]{1,0:T(8,128)(2,1)S(1)} collective-permute-done((bf16[128,768]{1,0:T(8,128)(2,1)S(1)}, bf16[128,768]{1,0:T(8,128)(2,1)S(1)}, u32[]{:S(2)}, u32[]{:S(2)}) %collective-permute-start.2) | collective-permute-done | bytes 196640 | tf_op jit(solution)/shard_map/ppermute | solution.py:429
  29.7 0.0 copy-done
  29.7 0.0 copy-done.1
  29.8 0.0 copy-done.2
  29.8 0.0 copy-done.3
  29.8 0.0 copy-done.5
  29.8 0.0 copy-done.6
  29.8 0.0 copy-done.7
  29.8 4.4 %downward.1 = f32[16,8,256]{2,1,0:T(8,128)} custom-call(s32[2,128]{1,0:T(2,128)S(1)} %bitcast.11, bf16[128,768]{1,0:T(8,128)(2,1)S(1)} %collective-permute-done.2.mom2, bf16[128,1920]{1,0:T(8,128)(2,1)S(1)} %after.3.got, bf16[16,64,256]{2,1,0:T(8,128)(2,1)S(1)} %copy-done.1, bf16[16,64,64]{2,1,0:T(8,128)(2,1)S(1)} %copy-done.3, s32[1,16]{1,0:T(1,128)S(1)} %bitcast.16, ...), custom_call_target="tpu_custom_call" | custom-call | tf_op jit(solution)/shard_map/downward/pallas_call | solution.py:433
  (3 shorter events, 0.0 us)
Async XLA Ops:
  0.0 14.4 %copy-start.4 = (bf16[16,8,256]{2,1,0:T(8,128)(2,1)S(1)}, bf16[16,8,256]{2,1,0:T(8,128)(2,1)}, u32[]{:S(2)}) copy-start(bf16[16,8,256]{2,1,0:T(8,128)(2,1)} %charges.1) | copy-start | bytes 196612
  0.0 14.4 %copy-start.8 = (s32[32,2]{0,1:T(2,128)S(1)}, s32[32,2]{0,1:T(2,128)}, u32[]{:S(2)}) copy-start(s32[32,2]{0,1:T(2,128)} %param.14) | copy-start | bytes 772
  0.0 6.1 %collective-permute-start = (bf16[16,8,256]{2,1,0:T(8,128)(2,1)}, bf16[16,8,256]{2,1,0:T(8,128)(2,1)S(1)}, u32[]{:S(2)}, u32[]{:S(2)}) collective-permute-start(bf16[16,8,256]{2,1,0:T(8,128)(2,1)} %charges.1), channel_id=1, source_target_pairs={{1,0},{2,1},{3,2},{4,3},{5,4},{6,5},{7,6},{8,7},{9,8},{10,9},{11,1... | collective-permute-start | bytes 196616 | tf_op jit(solution)/shard_map/ppermute | solution.py:327
  6.1 23.7 %copy-start = (bf16[128,64,64]{0,2,1:T(8,128)(2,1)S(1)}, bf16[128,64,64]{0,2,1:T(8,128)(2,1)}, u32[]{:S(2)}) copy-start(bf16[128,64,64]{0,2,1:T(8,128)(2,1)} %param.19) | copy-start | bytes 3145732
  6.1 23.6 %copy-start.1 = (bf16[16,64,256]{2,1,0:T(8,128)(2,1)S(1)}, bf16[16,64,256]{2,1,0:T(8,128)(2,1)}, u32[]{:S(2)}) copy-start(bf16[16,64,256]{2,1,0:T(8,128)(2,1)} %bases.1) | copy-start | bytes 1572868
  6.1 23.6 %copy-start.2 = (bf16[32,64,64]{2,1,0:T(8,128)(2,1)S(1)}, bf16[32,64,64]{2,1,0:T(8,128)(2,1)}, u32[]{:S(2)}) copy-start(bf16[32,64,64]{2,1,0:T(8,128)(2,1)} %par_c.1) | copy-start | bytes 786436
  6.1 23.6 %copy-start.3 = (bf16[16,64,64]{2,1,0:T(8,128)(2,1)S(1)}, bf16[16,64,64]{2,1,0:T(8,128)(2,1)}, u32[]{:S(2)}) copy-start(bf16[16,64,64]{2,1,0:T(8,128)(2,1)} %transfers.1) | copy-start | bytes 393220
  6.1 23.6 %copy-start.5 = (s32[128,2]{0,1:T(2,128)S(1)}, s32[128,2]{0,1:T(2,128)}, u32[]{:S(2)}) copy-start(s32[128,2]{0,1:T(2,128)} %param.18) | copy-start | bytes 3076
  6.2 23.6 %copy-start.6 = (s32[32,2]{0,1:T(2,128)S(1)}, s32[32,2]{0,1:T(2,128)}, u32[]{:S(2)}) copy-start(s32[32,2]{0,1:T(2,128)} %param.20) | copy-start | bytes 772
  6.2 23.6 %copy-start.7 = (s32[16]{0:T(128)S(1)}, s32[16]{0:T(128)}, u32[]{:S(2)}) copy-start(s32[16]{0:T(128)} %param.17) | copy-start | bytes 196
  6.2 22.0 %all-to-all-start = ((bf16[16,8,1920]{2,1,0:T(8,128)(2,1)}), bf16[16,8,1920]{2,1,0:T(8,128)(2,1)S(1)}, u32[]{:S(2)}, u32[]{:S(2)}) async-start(bf16[16,8,1920]{2,1,0:T(8,128)(2,1)} %bitcast.18), calls=%async_computation | async-start | bytes 983040 | tf_op jit(solution)/shard_map/all_to_all | solution.py:399
  19.5 3.2 %collective-permute-start.1 = (bf16[16,8,256]{2,1,0:T(8,128)(2,1)S(1)}, bf16[16,8,256]{2,1,0:T(8,128)(2,1)S(1)}, u32[]{:S(2)}, u32[]{:S(2)}) collective-permute-start(bf16[16,8,256]{2,1,0:T(8,128)(2,1)S(1)} %get-tuple-element.7), channel_id=1, source_target_pairs={{0,1},{1,2},{2,3},{3,4},{4,5},{5,6},{6,7},{7,8},{8,9},{9,10},{10,1... | collective-permute-start | bytes 196616 | tf_op jit(solution)/shard_map/ppermute | solution.py:327
  28.2 1.5 %collective-permute-start.2 = (bf16[128,768]{1,0:T(8,128)(2,1)S(1)}, bf16[128,768]{1,0:T(8,128)(2,1)S(1)}, u32[]{:S(2)}, u32[]{:S(2)}) collective-permute-start(bf16[128,768]{1,0:T(8,128)(2,1)S(1)} %slice.4), channel_id=1, source_target_pairs={{0,1},{1,0},{2,3},{3,2},{4,5},{5,4},{6,7},{7,6},{8,9},{9,8},{10,11... | collective-permute-start | bytes 589832 | tf_op jit(solution)/shard_map/ppermute | solution.py:429

commit v11 on v10

--- a/solution.py
+++ b/solution.py
@@ -166,7 +166,7 @@
                 return acc
 
             acc = tuple(jnp.zeros((half, LANES), F32) for _ in range(rhs))
-            acc = lax.fori_loop(0, rank // 8, body, acc, unroll=4)
+            acc = lax.fori_loop(0, rank // 8, body, acc, unroll=8)
             for r in range(rhs):
                 first = r * rank + jh * half
                 ob[first : first + half, lanes] = acc[r].astype(BF16)
@@ -291,7 +291,7 @@
             couple(k8, sb)
             return carry
 
-        lax.fori_loop(0, rank // 8, body, 0, unroll=4)
+        lax.fori_loop(0, rank // 8, body, 0, unroll=8)
 
     hot = one_hot(far_pairs[0:1, :] % leaves == iota((leaves, slots), 0))
     high, low = split2(fw[...])

time: 34.6 us -> 33.8 us (0.977)
  Pallas kernels: 14.1 us -> 13.3 us
    pallas_call x1, Pallas kernels: 4.41 us -> 3.53 us  [on_device(): pl.pallas_call(post_kernel, out_shape=jax.ShapeDtypeStruct((leaves, rhs,...]
  transfers between devices with their start and end apart: 4 -> 4, of which waited for: 3 -> 3; matrix products, arithmetic and copies ran while one was open for 0% -> 0% of each run, Pallas kernels for 28% -> 29%
where the time goes in v11:
time: 33.8 us; the launch traced here: 33.4 us
  Pallas kernels  13.3 us (39%)
  starting transfers between devices  12.2 us (36%)
  waiting for transfers between devices  7.74 us (23%)
    all_to_all x1, starting transfers between devices, on_device(): got = lax.all_to_all(send, 'sfc', split_axis=0, concat_axis=0, tiled=True)  8.26 us
    all_to_all x1, waiting for transfers between devices, on_device(): got = lax.all_to_all(send, 'sfc', split_axis=0, concat_axis=0, tiled=True)  5.53 us
    pallas_call x1, Pallas kernels, on_device(): pl.pallas_call(near_kernel, grid=(steps,), out_shape=[jax.ShapeDtypeStruc...  5.02 us
    pallas_call x1, Pallas kernels, on_device(): pl.pallas_call(pre_kernel, out_shape=jax.ShapeDtypeStruct((rows, columns)...  4.73 us
    ppermute x2, starting transfers between devices, passed_along(): lax.ppermute(value, axis, [(source, source + steps) for source in range(l...  3.72 us
    pallas_call x1, Pallas kernels, on_device(): pl.pallas_call(post_kernel, out_shape=jax.ShapeDtypeStruct((leaves, rhs,...  3.53 us
    ppermute x1, waiting for transfers between devices, on_device(): lax.ppermute(got[:, 2 * width + LANES:], 'sfc', [(i, i ^ 1) for i in rang...  1.33 us
    ppermute x2, waiting for transfers between devices, passed_along(): lax.ppermute(value, axis, [(source, source + steps) for source in range(l...  0.88 us
  transfers between devices with their start and end apart: 4, of which 3 were waited for; matrix products, arithmetic and copies ran while one was open for 0% of the time, Pallas kernels for 29%

profile of v11, /device:TPU:0, one launch (start us, length us, event | category | flops | bytes accessed | tf_op | source)
XLA Modules:
  0.0 33.4 jit_solution(503565189175078251)
XLA Ops:
  0.0 0.0 copy-start.4
  0.0 0.0 copy-start.8
  0.0 1.4 %collective-permute-start = (bf16[16,8,256]{2,1,0:T(8,128)(2,1)}, bf16[16,8,256]{2,1,0:T(8,128)(2,1)S(1)}, u32[]{:S(2)}, u32[]{:S(2)}) collective-permute-start(bf16[16,8,256]{2,1,0:T(8,128)(2,1)} %charges.1), channel_id=1, source_target_pairs={{1,0},{2,1},{3,2},{4,3},{5,4},{6,5},{7,6},{8,7},{9,8},{10,9},{11,1... | collective-permute-start | bytes 196616 | tf_op jit(solution)/shard_map/ppermute | solution.py:327
  1.4 4.7 %upward.1.value = bf16[128,1920]{1,0:T(8,128)(2,1)} custom-call(bf16[16,8,256]{2,1,0:T(8,128)(2,1)} %charges.1, bf16[16,64,256]{2,1,0:T(8,128)(2,1)} %bases.1, bf16[16,64,64]{2,1,0:T(8,128)(2,1)} %transfers.1, s32[1,16]{1,0:T(1,128)} %bitcast.15, s32[2,128]{1,0:T(2,128)} %bitcast.10, bf16[64,64,128]{2,1,0:T(8,128)(2,1)} %bitcast.8, s32[2,32]{1,0:T(2,128)} %bitcast.13, ...), custom_call_target="tpu_custom_call" | custom-call | flops 40000000 | bytes 10000000 | tf_op jit(solution)/shard_map/upward/pallas_call | solution.py:371
  6.2 0.0 collective-permute-done.earlier.following
  6.2 0.0 copy-start
  6.2 0.0 copy-start.1
  6.2 0.0 copy-start.2
  6.2 0.0 copy-start.3
  6.2 0.0 copy-start.5
  6.2 0.0 copy-start.6
  6.3 0.0 copy-start.7
  6.3 8.3 %all-to-all-start = ((bf16[16,8,1920]{2,1,0:T(8,128)(2,1)}), bf16[16,8,1920]{2,1,0:T(8,128)(2,1)S(1)}, u32[]{:S(2)}, u32[]{:S(2)}) async-start(bf16[16,8,1920]{2,1,0:T(8,128)(2,1)} %bitcast.18), calls=%async_computation | async-start | bytes 983040 | tf_op jit(solution)/shard_map/all_to_all | solution.py:399
  14.5 0.0 copy-done.4
  14.5 0.0 copy-done.8
  14.6 5.0 %near.1 = (f32[16,8,256]{2,1,0:T(8,128)S(1)}, bf16[16,8,256]{2,1,0:T(8,128)(2,1)S(1)}) custom-call(s32[2,32]{1,0:T(2,128)S(1)} %bitcast.17, bf16[16,8,256]{2,1,0:T(8,128)(2,1)S(1)} %copy-done.4, bf16[16,8,256]{2,1,0:T(8,128)(2,1)S(1)} %collective-permute-done.earlier.following, bf16[16,256,256]{2,1,0:T(8,128)(2,1)} %self_blocks.1, ...), custom_call_target="tpu_custom_call" | custom-call | flops 80000000 | bytes 20000000 | tf_op jit(solution)/shard_map/near/pallas_call | solution.py:403
  19.6 2.3 %collective-permute-start.1 = (bf16[16,8,256]{2,1,0:T(8,128)(2,1)S(1)}, bf16[16,8,256]{2,1,0:T(8,128)(2,1)S(1)}, u32[]{:S(2)}, u32[]{:S(2)}) collective-permute-start(bf16[16,8,256]{2,1,0:T(8,128)(2,1)S(1)} %get-tuple-element.7), channel_id=1, source_target_pairs={{0,1},{1,2},{2,3},{3,4},{4,5},{5,6},{6,7},{7,8},{8,9},{9,10},{10,1... | collective-permute-start | bytes 196616 | tf_op jit(solution)/shard_map/ppermute | solution.py:327
  21.9 0.9 %collective-permute-done.1.earlier.near_back = bf16[16,8,256]{2,1,0:T(8,128)(2,1)S(1)} collective-permute-done((bf16[16,8,256]{2,1,0:T(8,128)(2,1)S(1)}, bf16[16,8,256]{2,1,0:T(8,128)(2,1)S(1)}, u32[]{:S(2)}, u32[]{:S(2)}) %collective-permute-start.1) | collective-permute-done | bytes 65568 | tf_op jit(solution)/shard_map/ppermute | solution.py:327
  22.8 5.5 %all-to-all-done = bf16[16,8,1920]{2,1,0:T(8,128)(2,1)S(1)} async-done(((bf16[16,8,1920]{2,1,0:T(8,128)(2,1)}), bf16[16,8,1920]{2,1,0:T(8,128)(2,1)S(1)}, u32[]{:S(2)}, u32[]{:S(2)}) %all-to-all-start) | async-done | bytes 491552 | tf_op jit(solution)/shard_map/all_to_all | solution.py:399
  28.3 0.2 collective-permute-start.2
  28.5 1.3 %collective-permute-done.2.mom2 = bf16[128,768]{1,0:T(8,128)(2,1)S(1)} collective-permute-done((bf16[128,768]{1,0:T(8,128)(2,1)S(1)}, bf16[128,768]{1,0:T(8,128)(2,1)S(1)}, u32[]{:S(2)}, u32[]{:S(2)}) %collective-permute-start.2) | collective-permute-done | bytes 196640 | tf_op jit(solution)/shard_map/ppermute | solution.py:429
  29.8 0.0 copy-done
  29.8 0.0 copy-done.1
  29.8 0.0 copy-done.2
  29.8 0.0 copy-done.3
  29.9 0.0 copy-done.5
  29.9 0.0 copy-done.6
  29.9 0.0 copy-done.7
  29.9 3.5 %downward.1 = f32[16,8,256]{2,1,0:T(8,128)} custom-call(s32[2,128]{1,0:T(2,128)S(1)} %bitcast.11, bf16[128,768]{1,0:T(8,128)(2,1)S(1)} %collective-permute-done.2.mom2, bf16[128,1920]{1,0:T(8,128)(2,1)S(1)} %after.3.got, bf16[16,64,256]{2,1,0:T(8,128)(2,1)S(1)} %copy-done.1, bf16[16,64,64]{2,1,0:T(8,128)(2,1)S(1)} %copy-done.3, s32[1,16]{1,0:T(1,128)S(1)} %bitcast.16, ...), custom_call_target="tpu_custom_call" | custom-call | tf_op jit(solution)/shard_map/downward/pallas_call | solution.py:433
  (3 shorter events, 0.0 us)
Async XLA Ops:
  0.0 14.5 %copy-start.4 = (bf16[16,8,256]{2,1,0:T(8,128)(2,1)S(1)}, bf16[16,8,256]{2,1,0:T(8,128)(2,1)}, u32[]{:S(2)}) copy-start(bf16[16,8,256]{2,1,0:T(8,128)(2,1)} %charges.1) | copy-start | bytes 196612
  0.0 14.5 %copy-start.8 = (s32[32,2]{0,1:T(2,128)S(1)}, s32[32,2]{0,1:T(2,128)}, u32[]{:S(2)}) copy-start(s32[32,2]{0,1:T(2,128)} %param.14) | copy-start | bytes 772
  0.0 6.2 %collective-permute-start = (bf16[16,8,256]{2,1,0:T(8,128)(2,1)}, bf16[16,8,256]{2,1,0:T(8,128)(2,1)S(1)}, u32[]{:S(2)}, u32[]{:S(2)}) collective-permute-start(bf16[16,8,256]{2,1,0:T(8,128)(2,1)} %charges.1), channel_id=1, source_target_pairs={{1,0},{2,1},{3,2},{4,3},{5,4},{6,5},{7,6},{8,7},{9,8},{10,9},{11,1... | collective-permute-start | bytes 196616 | tf_op jit(solution)/shard_map/ppermute | solution.py:327
  6.2 23.7 %copy-start = (bf16[128,64,64]{0,2,1:T(8,128)(2,1)S(1)}, bf16[128,64,64]{0,2,1:T(8,128)(2,1)}, u32[]{:S(2)}) copy-start(bf16[128,64,64]{0,2,1:T(8,128)(2,1)} %param.19) | copy-start | bytes 3145732
  6.2 23.6 %copy-start.1 = (bf16[16,64,256]{2,1,0:T(8,128)(2,1)S(1)}, bf16[16,64,256]{2,1,0:T(8,128)(2,1)}, u32[]{:S(2)}) copy-start(bf16[16,64,256]{2,1,0:T(8,128)(2,1)} %bases.1) | copy-start | bytes 1572868
  6.2 23.6 %copy-start.2 = (bf16[32,64,64]{2,1,0:T(8,128)(2,1)S(1)}, bf16[32,64,64]{2,1,0:T(8,128)(2,1)}, u32[]{:S(2)}) copy-start(bf16[32,64,64]{2,1,0:T(8,128)(2,1)} %par_c.1) | copy-start | bytes 786436
  6.2 23.6 %copy-start.3 = (bf16[16,64,64]{2,1,0:T(8,128)(2,1)S(1)}, bf16[16,64,64]{2,1,0:T(8,128)(2,1)}, u32[]{:S(2)}) copy-start(bf16[16,64,64]{2,1,0:T(8,128)(2,1)} %transfers.1) | copy-start | bytes 393220
  6.2 23.6 %copy-start.5 = (s32[128,2]{0,1:T(2,128)S(1)}, s32[128,2]{0,1:T(2,128)}, u32[]{:S(2)}) copy-start(s32[128,2]{0,1:T(2,128)} %param.18) | copy-start | bytes 3076
  6.2 23.6 %copy-start.6 = (s32[32,2]{0,1:T(2,128)S(1)}, s32[32,2]{0,1:T(2,128)}, u32[]{:S(2)}) copy-start(s32[32,2]{0,1:T(2,128)} %param.20) | copy-start | bytes 772
  6.3 23.6 %copy-start.7 = (s32[16]{0:T(128)S(1)}, s32[16]{0:T(128)}, u32[]{:S(2)}) copy-start(s32[16]{0:T(128)} %param.17) | copy-start | bytes 196
  6.3 22.0 %all-to-all-start = ((bf16[16,8,1920]{2,1,0:T(8,128)(2,1)}), bf16[16,8,1920]{2,1,0:T(8,128)(2,1)S(1)}, u32[]{:S(2)}, u32[]{:S(2)}) async-start(bf16[16,8,1920]{2,1,0:T(8,128)(2,1)} %bitcast.18), calls=%async_computation | async-start | bytes 983040 | tf_op jit(solution)/shard_map/all_to_all | solution.py:399
  19.6 3.2 %collective-permute-start.1 = (bf16[16,8,256]{2,1,0:T(8,128)(2,1)S(1)}, bf16[16,8,256]{2,1,0:T(8,128)(2,1)S(1)}, u32[]{:S(2)}, u32[]{:S(2)}) collective-permute-start(bf16[16,8,256]{2,1,0:T(8,128)(2,1)S(1)} %get-tuple-element.7), channel_id=1, source_target_pairs={{0,1},{1,2},{2,3},{3,4},{4,5},{5,6},{6,7},{7,8},{8,9},{9,10},{10,1... | collective-permute-start | bytes 196616 | tf_op jit(solution)/shard_map/ppermute | solution.py:327
  28.3 1.5 %collective-permute-start.2 = (bf16[128,768]{1,0:T(8,128)(2,1)S(1)}, bf16[128,768]{1,0:T(8,128)(2,1)S(1)}, u32[]{:S(2)}, u32[]{:S(2)}) collective-permute-start(bf16[128,768]{1,0:T(8,128)(2,1)S(1)} %slice.4), channel_id=1, source_target_pairs={{0,1},{1,0},{2,3},{3,2},{4,5},{5,4},{6,7},{7,6},{8,9},{9,8},{10,11... | collective-permute-start | bytes 589832 | tf_op jit(solution)/shard_map/ppermute | solution.py:429

commit v12 on v11

--- a/solution.py
+++ b/solution.py
@@ -100,7 +100,6 @@
     pm3,
     pb,
     a_ref,
-    ob,
 ):
     leaves, rhs, _ = charges.shape
     rank = bases.shape[1]
@@ -123,13 +122,21 @@
         ],
         sems,
     )
-    for copy in copies[:3]:
+    def own_blocks(big):
+        lane_leaf = iota((rank, leaves * rhs), 1) // rhs
+        kept = big[0:rank]
+        for l in range(1, leaves):
+            kept = jnp.where(lane_leaf == l, big[l * rank : (l + 1) * rank], kept)
+        return kept
+
+    for copy in copies[:2]:
         copy.wait()
-
-    for l in range(leaves):
-        m = dot_nt(charges[l], bases[l]).astype(BF16)
-        mo[l * rhs : (l + 1) * rhs, :] = m.astype(F32)
-        ch[l * rhs : (l + 1) * rhs, :] = dot_nt(m, transfers[l])
+    panels = charges.shape[2]
+    flat = charges[...].astype(F32).reshape(leaves * rhs, panels).astype(BF16)
+    mt = own_blocks(dot_nt(bases[...].reshape(leaves * rank, panels), flat)).astype(BF16)
+    mo[...] = mt.astype(F32).T
+    copies[2].wait()
+    ch[...] = own_blocks(dot_nn(transfers[...].reshape(leaves * rank, rank), mt)).T
     for copy in copies[3:]:
         copy.wait()
     m2 = rows_to_lanes(mo, leaves, rhs)
@@ -150,33 +157,31 @@
         q = par_smem[0, s] % parents
         x = pm3[pl.ds(pl.multiple_of(q * rhs, rhs), rhs), :].astype(BF16)
         pb[s * rhs : (s + 1) * rhs, :] = dot_nn(x, par_c[s])
-    half = rank // 2
+    partner = far_pairs[1:2, :]
+    local = jnp.where(partner >= 0, partner % leaves, -1).astype(F32)
+    unit = one_hot(iota((LANES, LANES), 0) == iota((LANES, LANES), 1))
+    some = rhs // 2
     for sb in range(slots // LANES):
         lanes = slice(sb * LANES, (sb + 1) * LANES)
-        for jh in range(2):
+        for rh in range(2):
 
             def body(k8, acc):
                 rows_a = [
-                    a_ref[pl.ds(pl.multiple_of(r * rank + k8 * 8, 8), 8), lanes]
-                    for r in range(rhs)
+                    a_ref[pl.ds(pl.multiple_of((rh * some + r) * rank + k8 * 8, 8), 8), lanes]
+                    for r in range(some)
                 ]
                 for i in range(8):
-                    c = far_c[k8 * 8 + i, jh * half : (jh + 1) * half, lanes].astype(F32)
-                    acc = tuple(acc[r] + c * rows_a[r][i : i + 1, :] for r in range(rhs))
+                    c = far_c[k8 * 8 + i, :, lanes].astype(F32)
+                    acc = tuple(acc[r] + c * rows_a[r][i : i + 1, :] for r in range(some))
                 return acc
 
-            acc = tuple(jnp.zeros((half, LANES), F32) for _ in range(rhs))
+            acc = tuple(jnp.zeros((rank, LANES), F32) for _ in range(some))
             acc = lax.fori_loop(0, rank // 8, body, acc, unroll=8)
-            for r in range(rhs):
-                first = r * rank + jh * half
-                ob[first : first + half, lanes] = acc[r].astype(BF16)
-    partner = far_pairs[1:2, :]
-    local = jnp.where(partner >= 0, partner % leaves, -1).astype(F32)
-    ob[width : width + LANES, :] = jnp.broadcast_to(local, (LANES, slots)).astype(BF16)
-    unit = one_hot(iota((LANES, LANES), 0) == iota((LANES, LANES), 1))
-    for sb in range(slots // LANES):
-        lanes = slice(sb * LANES, (sb + 1) * LANES)
-        send[lanes, 0 : width + LANES] = dot_nt(unit, ob[:, lanes]).astype(BF16)
+            part = jnp.concatenate(acc, axis=0).astype(BF16)
+            at = rh * some * rank
+            send[lanes, at : at + some * rank] = dot_nt(unit, part).astype(BF16)
+        index = jnp.broadcast_to(local[:, lanes], (LANES, LANES)).astype(BF16)
+        send[lanes, width : width + LANES] = dot_nt(unit, index).astype(BF16)
 
     high, low = split2(rows_to_lanes(pb, pairs, rhs))
     hot = one_hot(par_pairs[1:2, :] == iota((rows, pairs), 0))
@@ -389,7 +394,6 @@
             pltpu.VMEM((parents * rhs, rank), F32),
             pltpu.VMEM((pairs * rhs, rank), F32),
             pltpu.VMEM((width, slots), F32),
-            pltpu.VMEM((width + LANES, slots), BF16),
         ],
         compiler_params=params,
         cost_estimate=cost(10_000_000),

time: 33.8 us -> 33.8 us (level)
  no operation moved by 1% of the time
where the time goes in v12:
time: 33.8 us; the launch traced here: 33.5 us
  Pallas kernels  13.3 us (39%)
  starting transfers between devices  12.2 us (36%)
  waiting for transfers between devices  7.73 us (23%)
    all_to_all x1, starting transfers between devices, on_device(): got = lax.all_to_all(send, 'sfc', split_axis=0, concat_axis=0, tiled=True)  8.26 us
    all_to_all x1, waiting for transfers between devices, on_device(): got = lax.all_to_all(send, 'sfc', split_axis=0, concat_axis=0, tiled=True)  5.52 us
    pallas_call x1, Pallas kernels, on_device(): pl.pallas_call(near_kernel, grid=(steps,), out_shape=[jax.ShapeDtypeStruc...  5.02 us
    pallas_call x1, Pallas kernels, on_device(): pl.pallas_call(pre_kernel, out_shape=jax.ShapeDtypeStruct((rows, columns)...  4.79 us
    ppermute x2, starting transfers between devices, passed_along(): lax.ppermute(value, axis, [(source, source + steps) for source in range(l...  3.73 us
    pallas_call x1, Pallas kernels, on_device(): pl.pallas_call(post_kernel, out_shape=jax.ShapeDtypeStruct((leaves, rhs,...  3.53 us
    ppermute x1, waiting for transfers between devices, on_device(): lax.ppermute(got[:, 2 * width + LANES:], 'sfc', [(i, i ^ 1) for i in rang...  1.33 us
    ppermute x2, waiting for transfers between devices, passed_along(): lax.ppermute(value, axis, [(source, source + steps) for source in range(l...  0.88 us
  transfers between devices with their start and end apart: 4, of which 3 were waited for; matrix products, arithmetic and copies ran while one was open for 0% of the time, Pallas kernels for 29%

profile of v12, /device:TPU:0, one launch (start us, length us, event | category | flops | bytes accessed | tf_op | source)
XLA Modules:
  0.0 33.5 jit_solution(11513573949860395905)
XLA Ops:
  0.0 0.0 copy-start.4
  0.0 0.0 copy-start.8
  0.0 1.4 %collective-permute-start = (bf16[16,8,256]{2,1,0:T(8,128)(2,1)}, bf16[16,8,256]{2,1,0:T(8,128)(2,1)S(1)}, u32[]{:S(2)}, u32[]{:S(2)}) collective-permute-start(bf16[16,8,256]{2,1,0:T(8,128)(2,1)} %charges.1), channel_id=1, source_target_pairs={{1,0},{2,1},{3,2},{4,3},{5,4},{6,5},{7,6},{8,7},{9,8},{10,9},{11,1... | collective-permute-start | bytes 196616 | tf_op jit(solution)/shard_map/ppermute | solution.py:332
  1.4 4.8 %upward.1.value = bf16[128,1920]{1,0:T(8,128)(2,1)} custom-call(bf16[16,8,256]{2,1,0:T(8,128)(2,1)} %charges.1, bf16[16,64,256]{2,1,0:T(8,128)(2,1)} %bases.1, bf16[16,64,64]{2,1,0:T(8,128)(2,1)} %transfers.1, s32[1,16]{1,0:T(1,128)} %bitcast.15, s32[2,128]{1,0:T(2,128)} %bitcast.10, bf16[64,64,128]{2,1,0:T(8,128)(2,1)} %bitcast.8, s32[2,32]{1,0:T(2,128)} %bitcast.13, ...), custom_call_target="tpu_custom_call" | custom-call | flops 40000000 | bytes 10000000 | tf_op jit(solution)/shard_map/upward/pallas_call | solution.py:376
  6.2 0.0 collective-permute-done.earlier.following
  6.2 0.0 copy-start
  6.3 0.0 copy-start.1
  6.3 0.0 copy-start.2
  6.3 0.0 copy-start.3
  6.3 0.0 copy-start.5
  6.3 0.0 copy-start.6
  6.3 0.0 copy-start.7
  6.3 8.3 %all-to-all-start = ((bf16[16,8,1920]{2,1,0:T(8,128)(2,1)}), bf16[16,8,1920]{2,1,0:T(8,128)(2,1)S(1)}, u32[]{:S(2)}, u32[]{:S(2)}) async-start(bf16[16,8,1920]{2,1,0:T(8,128)(2,1)} %bitcast.18), calls=%async_computation | async-start | bytes 983040 | tf_op jit(solution)/shard_map/all_to_all | solution.py:403
  14.6 0.0 copy-done.4
  14.6 0.0 copy-done.8
  14.6 5.0 %near.1 = (f32[16,8,256]{2,1,0:T(8,128)S(1)}, bf16[16,8,256]{2,1,0:T(8,128)(2,1)S(1)}) custom-call(s32[2,32]{1,0:T(2,128)S(1)} %bitcast.17, bf16[16,8,256]{2,1,0:T(8,128)(2,1)S(1)} %copy-done.4, bf16[16,8,256]{2,1,0:T(8,128)(2,1)S(1)} %collective-permute-done.earlier.following, bf16[16,256,256]{2,1,0:T(8,128)(2,1)} %self_blocks.1, ...), custom_call_target="tpu_custom_call" | custom-call | flops 80000000 | bytes 20000000 | tf_op jit(solution)/shard_map/near/pallas_call | solution.py:407
  19.6 2.3 %collective-permute-start.1 = (bf16[16,8,256]{2,1,0:T(8,128)(2,1)S(1)}, bf16[16,8,256]{2,1,0:T(8,128)(2,1)S(1)}, u32[]{:S(2)}, u32[]{:S(2)}) collective-permute-start(bf16[16,8,256]{2,1,0:T(8,128)(2,1)S(1)} %get-tuple-element.7), channel_id=1, source_target_pairs={{0,1},{1,2},{2,3},{3,4},{4,5},{5,6},{6,7},{7,8},{8,9},{9,10},{10,1... | collective-permute-start | bytes 196616 | tf_op jit(solution)/shard_map/ppermute | solution.py:332
  22.0 0.9 %collective-permute-done.1.earlier.near_back = bf16[16,8,256]{2,1,0:T(8,128)(2,1)S(1)} collective-permute-done((bf16[16,8,256]{2,1,0:T(8,128)(2,1)S(1)}, bf16[16,8,256]{2,1,0:T(8,128)(2,1)S(1)}, u32[]{:S(2)}, u32[]{:S(2)}) %collective-permute-start.1) | collective-permute-done | bytes 65568 | tf_op jit(solution)/shard_map/ppermute | solution.py:332
  22.8 5.5 %all-to-all-done = bf16[16,8,1920]{2,1,0:T(8,128)(2,1)S(1)} async-done(((bf16[16,8,1920]{2,1,0:T(8,128)(2,1)}), bf16[16,8,1920]{2,1,0:T(8,128)(2,1)S(1)}, u32[]{:S(2)}, u32[]{:S(2)}) %all-to-all-start) | async-done | bytes 491552 | tf_op jit(solution)/shard_map/all_to_all | solution.py:403
  28.4 0.2 collective-permute-start.2
  28.6 1.3 %collective-permute-done.2.mom2 = bf16[128,768]{1,0:T(8,128)(2,1)S(1)} collective-permute-done((bf16[128,768]{1,0:T(8,128)(2,1)S(1)}, bf16[128,768]{1,0:T(8,128)(2,1)S(1)}, u32[]{:S(2)}, u32[]{:S(2)}) %collective-permute-start.2) | collective-permute-done | bytes 196640 | tf_op jit(solution)/shard_map/ppermute | solution.py:433
  29.9 0.0 copy-done
  29.9 0.0 copy-done.1
  29.9 0.0 copy-done.2
  29.9 0.0 copy-done.3
  29.9 0.0 copy-done.5
  29.9 0.0 copy-done.6
  29.9 0.0 copy-done.7
  29.9 3.5 %downward.1 = f32[16,8,256]{2,1,0:T(8,128)} custom-call(s32[2,128]{1,0:T(2,128)S(1)} %bitcast.11, bf16[128,768]{1,0:T(8,128)(2,1)S(1)} %collective-permute-done.2.mom2, bf16[128,1920]{1,0:T(8,128)(2,1)S(1)} %after.3.got, bf16[16,64,256]{2,1,0:T(8,128)(2,1)S(1)} %copy-done.1, bf16[16,64,64]{2,1,0:T(8,128)(2,1)S(1)} %copy-done.3, s32[1,16]{1,0:T(1,128)S(1)} %bitcast.16, ...), custom_call_target="tpu_custom_call" | custom-call | tf_op jit(solution)/shard_map/downward/pallas_call | solution.py:437
  (3 shorter events, 0.0 us)
Async XLA Ops:
  0.0 14.6 %copy-start.4 = (bf16[16,8,256]{2,1,0:T(8,128)(2,1)S(1)}, bf16[16,8,256]{2,1,0:T(8,128)(2,1)}, u32[]{:S(2)}) copy-start(bf16[16,8,256]{2,1,0:T(8,128)(2,1)} %charges.1) | copy-start | bytes 196612
  0.0 14.6 %copy-start.8 = (s32[32,2]{0,1:T(2,128)S(1)}, s32[32,2]{0,1:T(2,128)}, u32[]{:S(2)}) copy-start(s32[32,2]{0,1:T(2,128)} %param.14) | copy-start | bytes 772
  0.0 6.2 %collective-permute-start = (bf16[16,8,256]{2,1,0:T(8,128)(2,1)}, bf16[16,8,256]{2,1,0:T(8,128)(2,1)S(1)}, u32[]{:S(2)}, u32[]{:S(2)}) collective-permute-start(bf16[16,8,256]{2,1,0:T(8,128)(2,1)} %charges.1), channel_id=1, source_target_pairs={{1,0},{2,1},{3,2},{4,3},{5,4},{6,5},{7,6},{8,7},{9,8},{10,9},{11,1... | collective-permute-start | bytes 196616 | tf_op jit(solution)/shard_map/ppermute | solution.py:332
  6.2 23.7 %copy-start = (bf16[128,64,64]{0,2,1:T(8,128)(2,1)S(1)}, bf16[128,64,64]{0,2,1:T(8,128)(2,1)}, u32[]{:S(2)}) copy-start(bf16[128,64,64]{0,2,1:T(8,128)(2,1)} %param.19) | copy-start | bytes 3145732
  6.3 23.6 %copy-start.1 = (bf16[16,64,256]{2,1,0:T(8,128)(2,1)S(1)}, bf16[16,64,256]{2,1,0:T(8,128)(2,1)}, u32[]{:S(2)}) copy-start(bf16[16,64,256]{2,1,0:T(8,128)(2,1)} %bases.1) | copy-start | bytes 1572868
  6.3 23.6 %copy-start.2 = (bf16[32,64,64]{2,1,0:T(8,128)(2,1)S(1)}, bf16[32,64,64]{2,1,0:T(8,128)(2,1)}, u32[]{:S(2)}) copy-start(bf16[32,64,64]{2,1,0:T(8,128)(2,1)} %par_c.1) | copy-start | bytes 786436
  6.3 23.6 %copy-start.3 = (bf16[16,64,64]{2,1,0:T(8,128)(2,1)S(1)}, bf16[16,64,64]{2,1,0:T(8,128)(2,1)}, u32[]{:S(2)}) copy-start(bf16[16,64,64]{2,1,0:T(8,128)(2,1)} %transfers.1) | copy-start | bytes 393220
  6.3 23.6 %copy-start.5 = (s32[128,2]{0,1:T(2,128)S(1)}, s32[128,2]{0,1:T(2,128)}, u32[]{:S(2)}) copy-start(s32[128,2]{0,1:T(2,128)} %param.18) | copy-start | bytes 3076
  6.3 23.6 %copy-start.6 = (s32[32,2]{0,1:T(2,128)S(1)}, s32[32,2]{0,1:T(2,128)}, u32[]{:S(2)}) copy-start(s32[32,2]{0,1:T(2,128)} %param.20) | copy-start | bytes 772
  6.3 23.6 %copy-start.7 = (s32[16]{0:T(128)S(1)}, s32[16]{0:T(128)}, u32[]{:S(2)}) copy-start(s32[16]{0:T(128)} %param.17) | copy-start | bytes 196
  6.3 22.0 %all-to-all-start = ((bf16[16,8,1920]{2,1,0:T(8,128)(2,1)}), bf16[16,8,1920]{2,1,0:T(8,128)(2,1)S(1)}, u32[]{:S(2)}, u32[]{:S(2)}) async-start(bf16[16,8,1920]{2,1,0:T(8,128)(2,1)} %bitcast.18), calls=%async_computation | async-start | bytes 983040 | tf_op jit(solution)/shard_map/all_to_all | solution.py:403
  19.6 3.2 %collective-permute-start.1 = (bf16[16,8,256]{2,1,0:T(8,128)(2,1)S(1)}, bf16[16,8,256]{2,1,0:T(8,128)(2,1)S(1)}, u32[]{:S(2)}, u32[]{:S(2)}) collective-permute-start(bf16[16,8,256]{2,1,0:T(8,128)(2,1)S(1)} %get-tuple-element.7), channel_id=1, source_target_pairs={{0,1},{1,2},{2,3},{3,4},{4,5},{5,6},{6,7},{7,8},{8,9},{9,10},{10,1... | collective-permute-start | bytes 196616 | tf_op jit(solution)/shard_map/ppermute | solution.py:332
  28.4 1.5 %collective-permute-start.2 = (bf16[128,768]{1,0:T(8,128)(2,1)S(1)}, bf16[128,768]{1,0:T(8,128)(2,1)S(1)}, u32[]{:S(2)}, u32[]{:S(2)}) collective-permute-start(bf16[128,768]{1,0:T(8,128)(2,1)S(1)} %slice.4), channel_id=1, source_target_pairs={{0,1},{1,0},{2,3},{3,2},{4,5},{5,4},{6,7},{7,6},{8,9},{9,8},{10,11... | collective-permute-start | bytes 589832 | tf_op jit(solution)/shard_map/ppermute | solution.py:433

commit v13 on v12

--- a/solution.py
+++ b/solution.py
@@ -100,6 +100,7 @@
     pm3,
     pb,
     a_ref,
+    e_ref,
 ):
     leaves, rhs, _ = charges.shape
     rank = bases.shape[1]
@@ -110,18 +111,19 @@
     rows = send.shape[0]
     copies = fetch(
         [
+            (far_pairs_h, far_pairs),
             (charges_h, charges),
             (bases_h, bases),
+            (far_c_h, far_c),
             (transfers_h, transfers),
             (parent_of_h, parent_of),
-            (far_pairs_h, far_pairs),
             (par_pairs_h, par_pairs),
             (par_pairs_h, par_smem),
-            (far_c_h, far_c),
             (par_c_h, par_c),
         ],
         sems,
     )
+
     def own_blocks(big):
         lane_leaf = iota((rank, leaves * rhs), 1) // rhs
         kept = big[0:rank]
@@ -129,16 +131,30 @@
             kept = jnp.where(lane_leaf == l, big[l * rank : (l + 1) * rank], kept)
         return kept
 
-    for copy in copies[:2]:
+    copies[0].wait()
+    owner_row = far_pairs[0:1, :] % leaves * rhs
+    row = iota((leaves * rhs, slots), 0)
+    for r in range(rhs):
+        e_ref[:, r * slots : (r + 1) * slots] = one_hot(row == owner_row + r)
+    partner = far_pairs[1:2, :]
+    local = jnp.where(partner >= 0, partner % leaves, -1).astype(F32)
+    unit = one_hot(iota((LANES, LANES), 0) == iota((LANES, LANES), 1))
+    for sb in range(slots // LANES):
+        lanes = slice(sb * LANES, (sb + 1) * LANES)
+        index = jnp.broadcast_to(local[:, lanes], (LANES, LANES)).astype(BF16)
+        send[lanes, width : width + LANES] = dot_nt(unit, index).astype(BF16)
+
+    for copy in copies[1:3]:
         copy.wait()
     panels = charges.shape[2]
     flat = charges[...].astype(F32).reshape(leaves * rhs, panels).astype(BF16)
     mt = own_blocks(dot_nt(bases[...].reshape(leaves * rank, panels), flat)).astype(BF16)
-    mo[...] = mt.astype(F32).T
-    copies[2].wait()
-    ch[...] = own_blocks(dot_nn(transfers[...].reshape(leaves * rank, rank), mt)).T
+    for r in range(rhs):
+        a_ref[r * rank : (r + 1) * rank, :] = dot_nn(mt, e_ref[:, r * slots : (r + 1) * slots])
     for copy in copies[3:]:
         copy.wait()
+    mo[...] = mt.astype(F32).T
+    ch[...] = own_blocks(dot_nn(transfers[...].reshape(leaves * rank, rank), mt)).T
     m2 = rows_to_lanes(mo, leaves, rhs)
     high, low = split2(rows_to_lanes(ch, leaves, rhs))
     par_hot = one_hot(parent_of[...] % parents == iota((parents, leaves), 0))
@@ -151,15 +167,10 @@
     for p in range(rows // (2 * parents)):
         send[p * 2 * parents : (p + 1) * 2 * parents, at : at + half] = shared
 
-    owner_hot = one_hot(far_pairs[0:1, :] % leaves == iota((leaves, slots), 0))
-    a_ref[...] = dot_tn(m2.astype(BF16), owner_hot)
     for s in range(pairs):
         q = par_smem[0, s] % parents
         x = pm3[pl.ds(pl.multiple_of(q * rhs, rhs), rhs), :].astype(BF16)
         pb[s * rhs : (s + 1) * rhs, :] = dot_nn(x, par_c[s])
-    partner = far_pairs[1:2, :]
-    local = jnp.where(partner >= 0, partner % leaves, -1).astype(F32)
-    unit = one_hot(iota((LANES, LANES), 0) == iota((LANES, LANES), 1))
     some = rhs // 2
     for sb in range(slots // LANES):
         lanes = slice(sb * LANES, (sb + 1) * LANES)
@@ -180,8 +191,6 @@
             part = jnp.concatenate(acc, axis=0).astype(BF16)
             at = rh * some * rank
             send[lanes, at : at + some * rank] = dot_nt(unit, part).astype(BF16)
-        index = jnp.broadcast_to(local[:, lanes], (LANES, LANES)).astype(BF16)
-        send[lanes, width : width + LANES] = dot_nt(unit, index).astype(BF16)
 
     high, low = split2(rows_to_lanes(pb, pairs, rhs))
     hot = one_hot(par_pairs[1:2, :] == iota((rows, pairs), 0))
@@ -394,6 +403,7 @@
             pltpu.VMEM((parents * rhs, rank), F32),
             pltpu.VMEM((pairs * rhs, rank), F32),
             pltpu.VMEM((width, slots), F32),
+            pltpu.VMEM((leaves * rhs, rhs * slots), BF16),
         ],
         compiler_params=params,
         cost_estimate=cost(10_000_000),

time: 33.8 us -> 34.1 us (level)
  transfers between devices with their start and end apart: 4 -> 4, of which waited for: 3 -> 3; matrix products, arithmetic and copies ran while one was open for 0% -> 0% of each run, Pallas kernels for 29% -> 30%
where the time goes in v13:
time: 34.1 us; the launch traced here: 33.7 us
  Pallas kernels  13.6 us (40%)
  starting transfers between devices  12.2 us (36%)
  waiting for transfers between devices  7.74 us (23%)
    all_to_all x1, starting transfers between devices, on_device(): got = lax.all_to_all(send, 'sfc', split_axis=0, concat_axis=0, tiled=True)  8.26 us
    all_to_all x1, waiting for transfers between devices, on_device(): got = lax.all_to_all(send, 'sfc', split_axis=0, concat_axis=0, tiled=True)  5.53 us
    pallas_call x1, Pallas kernels, on_device(): pl.pallas_call(near_kernel, grid=(steps,), out_shape=[jax.ShapeDtypeStruc...  5.02 us
    pallas_call x1, Pallas kernels, on_device(): pl.pallas_call(pre_kernel, out_shape=jax.ShapeDtypeStruct((rows, columns)...  5.02 us
    ppermute x2, starting transfers between devices, passed_along(): lax.ppermute(value, axis, [(source, source + steps) for source in range(l...  3.72 us
    pallas_call x1, Pallas kernels, on_device(): pl.pallas_call(post_kernel, out_shape=jax.ShapeDtypeStruct((leaves, rhs,...  3.53 us
    ppermute x1, waiting for transfers between devices, on_device(): lax.ppermute(got[:, 2 * width + LANES:], 'sfc', [(i, i ^ 1) for i in rang...  1.33 us
    ppermute x2, waiting for transfers between devices, passed_along(): lax.ppermute(value, axis, [(source, source + steps) for source in range(l...  0.88 us
  transfers between devices with their start and end apart: 4, of which 3 were waited for; matrix products, arithmetic and copies ran while one was open for 0% of the time, Pallas kernels for 30%

profile of v13, /device:TPU:0, one launch (start us, length us, event | category | flops | bytes accessed | tf_op | source)
XLA Modules:
  0.0 33.7 jit_solution(9970778666672950334)
XLA Ops:
  0.0 0.0 copy-start.4
  0.0 0.0 copy-start.8
  0.0 1.4 %collective-permute-start = (bf16[16,8,256]{2,1,0:T(8,128)(2,1)}, bf16[16,8,256]{2,1,0:T(8,128)(2,1)S(1)}, u32[]{:S(2)}, u32[]{:S(2)}) collective-permute-start(bf16[16,8,256]{2,1,0:T(8,128)(2,1)} %charges.1), channel_id=1, source_target_pairs={{1,0},{2,1},{3,2},{4,3},{5,4},{6,5},{7,6},{8,7},{9,8},{10,9},{11,1... | collective-permute-start | bytes 196616 | tf_op jit(solution)/shard_map/ppermute | solution.py:341
  1.4 5.0 %upward.1.value = bf16[128,1920]{1,0:T(8,128)(2,1)} custom-call(bf16[16,8,256]{2,1,0:T(8,128)(2,1)} %charges.1, bf16[16,64,256]{2,1,0:T(8,128)(2,1)} %bases.1, bf16[16,64,64]{2,1,0:T(8,128)(2,1)} %transfers.1, s32[1,16]{1,0:T(1,128)} %bitcast.15, s32[2,128]{1,0:T(2,128)} %bitcast.10, bf16[64,64,128]{2,1,0:T(8,128)(2,1)} %bitcast.8, s32[2,32]{1,0:T(2,128)} %bitcast.13, ...), custom_call_target="tpu_custom_call" | custom-call | flops 40000000 | bytes 10000000 | tf_op jit(solution)/shard_map/upward/pallas_call | solution.py:385
  6.5 0.0 collective-permute-done.earlier.following
  6.5 0.0 copy-start
  6.5 0.0 copy-start.1
  6.5 0.0 copy-start.2
  6.5 0.0 copy-start.3
  6.5 0.0 copy-start.5
  6.5 0.0 copy-start.6
  6.5 0.0 copy-start.7
  6.6 8.3 %all-to-all-start = ((bf16[16,8,1920]{2,1,0:T(8,128)(2,1)}), bf16[16,8,1920]{2,1,0:T(8,128)(2,1)S(1)}, u32[]{:S(2)}, u32[]{:S(2)}) async-start(bf16[16,8,1920]{2,1,0:T(8,128)(2,1)} %bitcast.18), calls=%async_computation | async-start | bytes 983040 | tf_op jit(solution)/shard_map/all_to_all | solution.py:413
  14.8 0.0 copy-done.4
  14.8 0.0 copy-done.8
  14.8 5.0 %near.1 = (f32[16,8,256]{2,1,0:T(8,128)S(1)}, bf16[16,8,256]{2,1,0:T(8,128)(2,1)S(1)}) custom-call(s32[2,32]{1,0:T(2,128)S(1)} %bitcast.17, bf16[16,8,256]{2,1,0:T(8,128)(2,1)S(1)} %copy-done.4, bf16[16,8,256]{2,1,0:T(8,128)(2,1)S(1)} %collective-permute-done.earlier.following, bf16[16,256,256]{2,1,0:T(8,128)(2,1)} %self_blocks.1, ...), custom_call_target="tpu_custom_call" | custom-call | flops 80000000 | bytes 20000000 | tf_op jit(solution)/shard_map/near/pallas_call | solution.py:417
  19.9 2.3 %collective-permute-start.1 = (bf16[16,8,256]{2,1,0:T(8,128)(2,1)S(1)}, bf16[16,8,256]{2,1,0:T(8,128)(2,1)S(1)}, u32[]{:S(2)}, u32[]{:S(2)}) collective-permute-start(bf16[16,8,256]{2,1,0:T(8,128)(2,1)S(1)} %get-tuple-element.7), channel_id=1, source_target_pairs={{0,1},{1,2},{2,3},{3,4},{4,5},{5,6},{6,7},{7,8},{8,9},{9,10},{10,1... | collective-permute-start | bytes 196616 | tf_op jit(solution)/shard_map/ppermute | solution.py:341
  22.2 0.9 %collective-permute-done.1.earlier.near_back = bf16[16,8,256]{2,1,0:T(8,128)(2,1)S(1)} collective-permute-done((bf16[16,8,256]{2,1,0:T(8,128)(2,1)S(1)}, bf16[16,8,256]{2,1,0:T(8,128)(2,1)S(1)}, u32[]{:S(2)}, u32[]{:S(2)}) %collective-permute-start.1) | collective-permute-done | bytes 65568 | tf_op jit(solution)/shard_map/ppermute | solution.py:341
  23.1 5.5 %all-to-all-done = bf16[16,8,1920]{2,1,0:T(8,128)(2,1)S(1)} async-done(((bf16[16,8,1920]{2,1,0:T(8,128)(2,1)}), bf16[16,8,1920]{2,1,0:T(8,128)(2,1)S(1)}, u32[]{:S(2)}, u32[]{:S(2)}) %all-to-all-start) | async-done | bytes 491552 | tf_op jit(solution)/shard_map/all_to_all | solution.py:413
  28.6 0.2 collective-permute-start.2
  28.8 1.3 %collective-permute-done.2.mom2 = bf16[128,768]{1,0:T(8,128)(2,1)S(1)} collective-permute-done((bf16[128,768]{1,0:T(8,128)(2,1)S(1)}, bf16[128,768]{1,0:T(8,128)(2,1)S(1)}, u32[]{:S(2)}, u32[]{:S(2)}) %collective-permute-start.2) | collective-permute-done | bytes 196640 | tf_op jit(solution)/shard_map/ppermute | solution.py:443
  30.1 0.0 copy-done
  30.1 0.0 copy-done.1
  30.1 0.0 copy-done.2
  30.1 0.0 copy-done.3
  30.1 0.0 copy-done.5
  30.2 0.0 copy-done.6
  30.2 0.0 copy-done.7
  30.2 3.5 %downward.1 = f32[16,8,256]{2,1,0:T(8,128)} custom-call(s32[2,128]{1,0:T(2,128)S(1)} %bitcast.11, bf16[128,768]{1,0:T(8,128)(2,1)S(1)} %collective-permute-done.2.mom2, bf16[128,1920]{1,0:T(8,128)(2,1)S(1)} %after.3.got, bf16[16,64,256]{2,1,0:T(8,128)(2,1)S(1)} %copy-done.1, bf16[16,64,64]{2,1,0:T(8,128)(2,1)S(1)} %copy-done.3, s32[1,16]{1,0:T(1,128)S(1)} %bitcast.16, ...), custom_call_target="tpu_custom_call" | custom-call | tf_op jit(solution)/shard_map/downward/pallas_call | solution.py:447
  (3 shorter events, 0.0 us)
Async XLA Ops:
  0.0 14.8 %copy-start.4 = (bf16[16,8,256]{2,1,0:T(8,128)(2,1)S(1)}, bf16[16,8,256]{2,1,0:T(8,128)(2,1)}, u32[]{:S(2)}) copy-start(bf16[16,8,256]{2,1,0:T(8,128)(2,1)} %charges.1) | copy-start | bytes 196612
  0.0 14.8 %copy-start.8 = (s32[32,2]{0,1:T(2,128)S(1)}, s32[32,2]{0,1:T(2,128)}, u32[]{:S(2)}) copy-start(s32[32,2]{0,1:T(2,128)} %param.14) | copy-start | bytes 772
  0.0 6.4 %collective-permute-start = (bf16[16,8,256]{2,1,0:T(8,128)(2,1)}, bf16[16,8,256]{2,1,0:T(8,128)(2,1)S(1)}, u32[]{:S(2)}, u32[]{:S(2)}) collective-permute-start(bf16[16,8,256]{2,1,0:T(8,128)(2,1)} %charges.1), channel_id=1, source_target_pairs={{1,0},{2,1},{3,2},{4,3},{5,4},{6,5},{7,6},{8,7},{9,8},{10,9},{11,1... | collective-permute-start | bytes 196616 | tf_op jit(solution)/shard_map/ppermute | solution.py:341
  6.5 23.7 %copy-start = (bf16[128,64,64]{0,2,1:T(8,128)(2,1)S(1)}, bf16[128,64,64]{0,2,1:T(8,128)(2,1)}, u32[]{:S(2)}) copy-start(bf16[128,64,64]{0,2,1:T(8,128)(2,1)} %param.19) | copy-start | bytes 3145732
  6.5 23.7 %copy-start.1 = (bf16[16,64,256]{2,1,0:T(8,128)(2,1)S(1)}, bf16[16,64,256]{2,1,0:T(8,128)(2,1)}, u32[]{:S(2)}) copy-start(bf16[16,64,256]{2,1,0:T(8,128)(2,1)} %bases.1) | copy-start | bytes 1572868
  6.5 23.6 %copy-start.2 = (bf16[32,64,64]{2,1,0:T(8,128)(2,1)S(1)}, bf16[32,64,64]{2,1,0:T(8,128)(2,1)}, u32[]{:S(2)}) copy-start(bf16[32,64,64]{2,1,0:T(8,128)(2,1)} %par_c.1) | copy-start | bytes 786436
  6.5 23.6 %copy-start.3 = (bf16[16,64,64]{2,1,0:T(8,128)(2,1)S(1)}, bf16[16,64,64]{2,1,0:T(8,128)(2,1)}, u32[]{:S(2)}) copy-start(bf16[16,64,64]{2,1,0:T(8,128)(2,1)} %transfers.1) | copy-start | bytes 393220
  6.5 23.6 %copy-start.5 = (s32[128,2]{0,1:T(2,128)S(1)}, s32[128,2]{0,1:T(2,128)}, u32[]{:S(2)}) copy-start(s32[128,2]{0,1:T(2,128)} %param.18) | copy-start | bytes 3076
  6.5 23.6 %copy-start.6 = (s32[32,2]{0,1:T(2,128)S(1)}, s32[32,2]{0,1:T(2,128)}, u32[]{:S(2)}) copy-start(s32[32,2]{0,1:T(2,128)} %param.20) | copy-start | bytes 772
  6.5 23.6 %copy-start.7 = (s32[16]{0:T(128)S(1)}, s32[16]{0:T(128)}, u32[]{:S(2)}) copy-start(s32[16]{0:T(128)} %param.17) | copy-start | bytes 196
  6.6 22.0 %all-to-all-start = ((bf16[16,8,1920]{2,1,0:T(8,128)(2,1)}), bf16[16,8,1920]{2,1,0:T(8,128)(2,1)S(1)}, u32[]{:S(2)}, u32[]{:S(2)}) async-start(bf16[16,8,1920]{2,1,0:T(8,128)(2,1)} %bitcast.18), calls=%async_computation | async-start | bytes 983040 | tf_op jit(solution)/shard_map/all_to_all | solution.py:413
  19.9 3.2 %collective-permute-start.1 = (bf16[16,8,256]{2,1,0:T(8,128)(2,1)S(1)}, bf16[16,8,256]{2,1,0:T(8,128)(2,1)S(1)}, u32[]{:S(2)}, u32[]{:S(2)}) collective-permute-start(bf16[16,8,256]{2,1,0:T(8,128)(2,1)S(1)} %get-tuple-element.7), channel_id=1, source_target_pairs={{0,1},{1,2},{2,3},{3,4},{4,5},{5,6},{6,7},{7,8},{8,9},{9,10},{10,1... | collective-permute-start | bytes 196616 | tf_op jit(solution)/shard_map/ppermute | solution.py:341
  28.6 1.5 %collective-permute-start.2 = (bf16[128,768]{1,0:T(8,128)(2,1)S(1)}, bf16[128,768]{1,0:T(8,128)(2,1)S(1)}, u32[]{:S(2)}, u32[]{:S(2)}) collective-permute-start(bf16[128,768]{1,0:T(8,128)(2,1)S(1)} %slice.4), channel_id=1, source_target_pairs={{0,1},{1,0},{2,3},{3,2},{4,5},{5,4},{6,7},{7,6},{8,9},{9,8},{10,11... | collective-permute-start | bytes 589832 | tf_op jit(solution)/shard_map/ppermute | solution.py:443

commit v14 on v10

--- a/solution.py
+++ b/solution.py
@@ -137,9 +137,12 @@
     par_hot = one_hot(parent_of[...] % parents == iota((parents, leaves), 0))
     pm = (dot_nn(par_hot, high) + dot_nn(par_hot, low)).astype(BF16).astype(F32)
     lanes_to_rows(pm3, pm, rhs)
-    shared = jnp.concatenate([m2[:parents], m2[parents:], pm], axis=1)
     half = 3 * width // 2
-    shared = jnp.concatenate([shared[:, :half], shared[:, half:]], axis=0).astype(BF16)
+    shared = [
+        jnp.concatenate([x[:, c * width // 2 : (c + 1) * width // 2] for x in (m2[:parents], m2[parents:], pm)], axis=1)
+        for c in range(2)
+    ]
+    shared = jnp.concatenate(shared, axis=0).astype(BF16)
     at = 2 * width + LANES
     for p in range(rows // (2 * parents)):
         send[p * 2 * parents : (p + 1) * 2 * parents, at : at + half] = shared
@@ -211,8 +214,57 @@
         away[...] = out[leaves:].astype(BF16)
 
 
+def far_half(mom, far_pairs, far_c, b_ref, fw, leaves, parents):
+    rows, slots = mom.shape[0], far_c.shape[2]
+    rank = far_c.shape[0]
+    wide = mom.shape[1] // 3
+    some = wide // rank
+    row_id = iota((rows, slots), 0)
+    base_leaf = row_id // parents * leaves + row_id % parents
+    partner = far_pairs[1:2, :]
+    total = None
+    for h in range(2):
+        hot = one_hot(partner == base_leaf + h * parents)
+        part = dot_tn(mom[:, h * wide : (h + 1) * wide], hot)
+        total = part if total is None else total + part
+    b_ref[...] = total
+
+    for sb in range(slots // LANES):
+        lanes = slice(sb * LANES, (sb + 1) * LANES)
+
+        def body(k8, carry):
+            parts = [[] for _ in range(some)]
+            for i in range(8):
+                c = far_c[k8 * 8 + i, :, lanes].astype(F32)
+                for r in range(some):
+                    prod = c * b_ref[r * rank : (r + 1) * rank, lanes]
+                    parts[r].append(sum(prod[j * 8 : (j + 1) * 8] for j in range(rank // 8)))
+            for r in range(some):
+                fw[pl.ds(pl.multiple_of(r * rank + k8 * 8, 8), 8), lanes] = row_sums(parts[r])
+            return carry
+
+        lax.fori_loop(0, rank // 8, body, 0, unroll=8)
+
+    hot = one_hot(far_pairs[0:1, :] % leaves == iota((leaves, slots), 0))
+    high, low = split2(fw[...])
+    return dot_nt(hot, high) + dot_nt(hot, low)
+
+
+def far_kernel(got, far_pairs, far_c, half, back, b_ref, fw):
+    leaves, width = back.shape
+    parents = leaves // 2
+    rows = got.shape[0]
+    index = got[:, width : width + LANES].astype(F32)[:, :leaves].astype(jnp.int32)
+    hot = one_hot(index == iota((rows, leaves), 1))
+    back[...] = dot_tn(hot, got[:, 0:width])
+    mom = got[:, 2 * width + LANES :]
+    half[...] = far_half(mom, far_pairs, far_c, b_ref, fw, leaves, parents)
+
+
 def post_kernel(
     core_smem,
+    half,
+    back,
     mom2,
     got,
     bases,
@@ -234,73 +286,38 @@
     dn,
 ):
     leaves, rank, _ = bases.shape
-    slots = far_c.shape[2]
+    width = back.shape[1]
+    rhs = width // rank
     pairs = par_c.shape[0]
     parents = leaves // 2
     rows = got.shape[0]
-    rhs = b_ref.shape[0] // rank
-    width = rhs * rank
-    at_par = width + LANES
-    at_mom = at_par + width
     core = core_smem[0, 0] // leaves % 2
-    mom = got[:, at_mom:]
-    shared = jnp.concatenate(
-        [jnp.where(core == 0, mom, mom2[...]), jnp.where(core == 0, mom2[...], mom)], axis=1
-    )
-    row_id = iota((rows, slots), 0)
-    base_leaf = row_id // parents * leaves + row_id % parents
-    partner = far_pairs[1:2, :]
-    total = None
-    for h in range(2):
-        hot = one_hot(partner == base_leaf + h * parents)
-        part = dot_tn(shared[:, h * width : (h + 1) * width], hot)
-        total = part if total is None else total + part
-    b_ref[...] = total
-
+
+    def in_order(mine, other):
+        return jnp.concatenate(
+            [jnp.where(core == 0, mine, other), jnp.where(core == 0, other, mine)], axis=1
+        )
+
+    wide = mom2.shape[1] // 3
+    shared = in_order(got[:, got.shape[1] - wide :], mom2[:, 2 * wide :])
     hot = one_hot(par_pairs[1:2, :] == iota((rows, pairs), 0))
-    lanes_to_rows(g_ref, dot_tn(hot, shared[:, 2 * width :]), rhs)
-
-    def couple(k8, sb):
-        lanes = slice(sb * LANES, (sb + 1) * LANES)
-        parts = [[] for _ in range(rhs)]
-        for i in range(8):
-            c = far_c[k8 * 8 + i, :, lanes].astype(F32)
-            for r in range(rhs):
-                prod = c * b_ref[r * rank : (r + 1) * rank, lanes]
-                parts[r].append(sum(prod[j * 8 : (j + 1) * 8] for j in range(rank // 8)))
-        for r in range(rhs):
-            fw[pl.ds(pl.multiple_of(r * rank + k8 * 8, 8), 8), lanes] = row_sums(parts[r])
-
+    lanes_to_rows(g_ref, dot_tn(hot, shared), rhs)
     for s in range(pairs):
         at = slice(s * rhs, (s + 1) * rhs)
         pf[at, :] = dot_nt(g_ref[at, :].astype(BF16), par_c[s])
     high, low = split2(rows_to_lanes(pf, pairs, rhs))
     hot = one_hot(par_pairs[0:1, :] % parents == iota((parents, pairs), 0))
     fold = one_hot(iota((parents, rows), 1) % parents == iota((parents, rows), 0))
-    locals_p = dot_nn(hot, high) + dot_nn(hot, low) + dot_nn(fold, got[:, at_par : at_par + width])
+    at = width + LANES
+    locals_p = dot_nn(hot, high) + dot_nn(hot, low) + dot_nn(fold, got[:, at : at + width])
     hot = one_hot(parent_of[...] % parents == iota((parents, leaves), 0))
     lanes_to_rows(pg, dot_tn(hot, locals_p.astype(BF16)), rhs)
-
     for l in range(leaves):
         at = slice(l * rhs, (l + 1) * rhs)
         dn[at, :] = dot_nn(pg[at, :].astype(BF16), transfers[l])
 
-    for sb in range(slots // LANES):
-
-        def body(k8, carry):
-            couple(k8, sb)
-            return carry
-
-        lax.fori_loop(0, rank // 8, body, 0, unroll=4)
-
-    hot = one_hot(far_pairs[0:1, :] % leaves == iota((leaves, slots), 0))
-    high, low = split2(fw[...])
-    leaf = dot_nt(hot, high) + dot_nt(hot, low)
-    index = got[:, width : width + LANES].astype(F32)[:, :leaves].astype(jnp.int32)
-    hot = one_hot(index == iota((rows, leaves), 1))
-    leaf = leaf + dot_tn(hot, got[:, 0:width])
-    lanes_to_rows(lf, leaf, rhs)
-
+    other = far_half(mom2[...], far_pairs, far_c, b_ref, fw, leaves, parents)
+    lanes_to_rows(lf, back[...] + in_order(half[...], other), rhs)
     for l in range(leaves):
         at = slice(l * rhs, (l + 1) * rhs)
         mine = (lf[at, :] + dn[at, :]).astype(BF16)
@@ -430,14 +447,28 @@
         got[:, 2 * width + LANES :], "sfc", [(i, i ^ 1) for i in range(devices)]
     )
 
+    half, back = pl.pallas_call(
+        far_kernel,
+        out_shape=[
+            jax.ShapeDtypeStruct((leaves, width // 2), F32),
+            jax.ShapeDtypeStruct((leaves, width), F32),
+        ],
+        in_specs=[vmem] * 3,
+        out_specs=[vmem] * 2,
+        scratch_shapes=[pltpu.VMEM((width // 2, slots), F32)] * 2,
+        compiler_params=late,
+        cost_estimate=cost(8_000_000),
+        name="far",
+    )(got, far_pairs, far_c)
+
     return pl.pallas_call(
         post_kernel,
         out_shape=jax.ShapeDtypeStruct((leaves, rhs, panels), F32),
-        in_specs=[smem] + [vmem] * 11,
+        in_specs=[smem] + [vmem] * 13,
         out_specs=vmem,
         scratch_shapes=[
-            pltpu.VMEM((width, slots), F32),
-            pltpu.VMEM((width, slots), F32),
+            pltpu.VMEM((width // 2, slots), F32),
+            pltpu.VMEM((width // 2, slots), F32),
             pltpu.VMEM((pairs * rhs, rank), F32),
             pltpu.VMEM((pairs * rhs, rank), F32),
             pltpu.VMEM((leaves * rhs, rank), F32),
@@ -448,6 +479,8 @@
         name="downward",
     )(
         far_pairs,
+        half,
+        back,
         mom2,
         got,
         bases,

time: 34.6 us -> 33.7 us (0.974)
  waiting for transfers between devices: 7.74 us -> 6.51 us
    ppermute x1, waiting for transfers between devices: 1.33 us -> 0.25 us  [on_device(): lax.ppermute(got[:, 2 * width + LANES:], 'sfc', [(i, i ^ 1) for i in rang...]
    pallas_call x0 -> x1, Pallas kernels: none -> 1.07 us  [on_device(): pl.pallas_call(far_kernel, out_shape=[jax.ShapeDtypeStruct((leaves, width...]
    pallas_call x1, Pallas kernels: 4.41 us -> 3.62 us  [on_device(): pl.pallas_call(post_kernel, out_shape=jax.ShapeDtypeStruct((leaves, rhs,...]
  transfers between devices with their start and end apart: 4 -> 4, of which waited for: 3 -> 3; matrix products, arithmetic and copies ran while one was open for 0% -> 0% of each run, Pallas kernels for 28% -> 32%
where the time goes in v14:
time: 33.7 us; the launch traced here: 33.3 us
  Pallas kernels  14.4 us (43%)
  starting transfers between devices  12.2 us (36%)
  waiting for transfers between devices  6.51 us (19%)
    all_to_all x1, starting transfers between devices, on_device(): got = lax.all_to_all(send, 'sfc', split_axis=0, concat_axis=0, tiled=True)  8.26 us
    all_to_all x1, waiting for transfers between devices, on_device(): got = lax.all_to_all(send, 'sfc', split_axis=0, concat_axis=0, tiled=True)  5.38 us
    pallas_call x1, Pallas kernels, on_device(): pl.pallas_call(near_kernel, grid=(steps,), out_shape=[jax.ShapeDtypeStruc...  5.11 us
    pallas_call x1, Pallas kernels, on_device(): pl.pallas_call(pre_kernel, out_shape=jax.ShapeDtypeStruct((rows, columns)...  4.63 us
    ppermute x2, starting transfers between devices, passed_along(): lax.ppermute(value, axis, [(source, source + steps) for source in range(l...  3.72 us
    pallas_call x1, Pallas kernels, on_device(): pl.pallas_call(post_kernel, out_shape=jax.ShapeDtypeStruct((leaves, rhs,...  3.62 us
    pallas_call x1, Pallas kernels, on_device(): pl.pallas_call(far_kernel, out_shape=[jax.ShapeDtypeStruct((leaves, width...  1.07 us
    ppermute x2, waiting for transfers between devices, passed_along(): lax.ppermute(value, axis, [(source, source + steps) for source in range(l...  0.88 us
  transfers between devices with their start and end apart: 4, of which 3 were waited for; matrix products, arithmetic and copies ran while one was open for 0% of the time, Pallas kernels for 32%

profile of v14, /device:TPU:0, one launch (start us, length us, event | category | flops | bytes accessed | tf_op | source)
XLA Modules:
  0.0 33.3 jit_solution(833284033213708983)
XLA Ops:
  0.0 0.0 copy-start.4
  0.0 0.0 copy-start.8
  0.0 1.4 %collective-permute-start = (bf16[16,8,256]{2,1,0:T(8,128)(2,1)}, bf16[16,8,256]{2,1,0:T(8,128)(2,1)S(1)}, u32[]{:S(2)}, u32[]{:S(2)}) collective-permute-start(bf16[16,8,256]{2,1,0:T(8,128)(2,1)} %charges.1), channel_id=1, source_target_pairs={{1,0},{2,1},{3,2},{4,3},{5,4},{6,5},{7,6},{8,7},{9,8},{10,9},{11,1... | collective-permute-start | bytes 196616 | tf_op jit(solution)/shard_map/ppermute | solution.py:344
  1.4 4.6 %upward.1.value = bf16[128,1920]{1,0:T(8,128)(2,1)} custom-call(bf16[16,8,256]{2,1,0:T(8,128)(2,1)} %charges.1, bf16[16,64,256]{2,1,0:T(8,128)(2,1)} %bases.1, bf16[16,64,64]{2,1,0:T(8,128)(2,1)} %transfers.1, s32[1,16]{1,0:T(1,128)} %bitcast.17, s32[2,128]{1,0:T(2,128)} %bitcast.11, bf16[64,64,128]{2,1,0:T(8,128)(2,1)} %bitcast.8, s32[2,32]{1,0:T(2,128)} %bitcast.15, ...), custom_call_target="tpu_custom_call" | custom-call | flops 40000000 | bytes 10000000 | tf_op jit(solution)/shard_map/upward/pallas_call | solution.py:388
  6.1 0.0 collective-permute-done.earlier.following
  6.1 0.0 copy-start
  6.1 0.0 copy-start.5
  6.1 8.3 %all-to-all-start = ((bf16[16,8,1920]{2,1,0:T(8,128)(2,1)}), bf16[16,8,1920]{2,1,0:T(8,128)(2,1)S(1)}, u32[]{:S(2)}, u32[]{:S(2)}) async-start(bf16[16,8,1920]{2,1,0:T(8,128)(2,1)} %bitcast.20), calls=%async_computation | async-start | bytes 983040 | tf_op jit(solution)/shard_map/all_to_all | solution.py:416
  14.4 0.0 copy-done.4
  14.4 0.0 copy-done.8
  14.4 0.0 copy-start.1
  14.4 0.0 copy-start.2
  14.4 0.0 copy-start.3
  14.4 0.0 copy-start.6
  14.4 0.0 copy-start.7
  14.5 5.1 %near.1 = (f32[16,8,256]{2,1,0:T(8,128)S(1)}, bf16[16,8,256]{2,1,0:T(8,128)(2,1)S(1)}) custom-call(s32[2,32]{1,0:T(2,128)S(1)} %bitcast.19, bf16[16,8,256]{2,1,0:T(8,128)(2,1)S(1)} %copy-done.4, bf16[16,8,256]{2,1,0:T(8,128)(2,1)S(1)} %collective-permute-done.earlier.following, bf16[16,256,256]{2,1,0:T(8,128)(2,1)} %self_blocks.1, ...), custom_call_target="tpu_custom_call" | custom-call | flops 80000000 | bytes 20000000 | tf_op jit(solution)/shard_map/near/pallas_call | solution.py:420
  19.6 2.3 %collective-permute-start.1 = (bf16[16,8,256]{2,1,0:T(8,128)(2,1)S(1)}, bf16[16,8,256]{2,1,0:T(8,128)(2,1)S(1)}, u32[]{:S(2)}, u32[]{:S(2)}) collective-permute-start(bf16[16,8,256]{2,1,0:T(8,128)(2,1)S(1)} %get-tuple-element.9), channel_id=1, source_target_pairs={{0,1},{1,2},{2,3},{3,4},{4,5},{5,6},{6,7},{7,8},{8,9},{9,10},{10,1... | collective-permute-start | bytes 196616 | tf_op jit(solution)/shard_map/ppermute | solution.py:344
  21.9 0.9 %collective-permute-done.1.earlier.near_back = bf16[16,8,256]{2,1,0:T(8,128)(2,1)S(1)} collective-permute-done((bf16[16,8,256]{2,1,0:T(8,128)(2,1)S(1)}, bf16[16,8,256]{2,1,0:T(8,128)(2,1)S(1)}, u32[]{:S(2)}, u32[]{:S(2)}) %collective-permute-start.1) | collective-permute-done | bytes 65568 | tf_op jit(solution)/shard_map/ppermute | solution.py:344
  22.8 5.4 %all-to-all-done = bf16[16,8,1920]{2,1,0:T(8,128)(2,1)S(1)} async-done(((bf16[16,8,1920]{2,1,0:T(8,128)(2,1)}), bf16[16,8,1920]{2,1,0:T(8,128)(2,1)S(1)}, u32[]{:S(2)}, u32[]{:S(2)}) %all-to-all-start) | async-done | bytes 491552 | tf_op jit(solution)/shard_map/all_to_all | solution.py:416
  28.2 0.2 collective-permute-start.2
  28.4 0.0 copy-done
  28.4 0.0 copy-done.5
  28.4 1.1 %far.1 = (f32[16,256]{1,0:T(8,128)S(1)}, f32[16,512]{1,0:T(8,128)S(1)}) custom-call(bf16[128,1920]{1,0:T(8,128)(2,1)S(1)} %after.3.got, s32[2,128]{1,0:T(2,128)S(1)} %bitcast.12, bf16[64,64,128]{2,1,0:T(8,128)(2,1)S(1)} %bitcast.9), custom_call_target="tpu_custom_call" | custom-call | flops 32000000 | bytes 8000000 | tf_op jit(solution)/shard_map/far/pallas_call | solution.py:450
  29.4 0.2 collective-permute-done.2.mom2
  29.7 0.0 copy-done.1
  29.7 0.0 copy-done.2
  29.7 0.0 copy-done.3
  29.7 0.0 copy-done.6
  29.7 0.0 copy-done.7
  29.7 3.6 %downward.1 = f32[16,8,256]{2,1,0:T(8,128)} custom-call(s32[2,128]{1,0:T(2,128)S(1)} %bitcast.13, f32[16,256]{1,0:T(8,128)S(1)} %get-tuple-element.10.half, f32[16,512]{1,0:T(8,128)S(1)} %get-tuple-element.11.back, bf16[128,768]{1,0:T(8,128)(2,1)S(1)} %collective-permute-done.2.mom2, bf16[128,1920]{1,0:T(8,128)(2,1)S(1)} %after.3.got, ...), custom_call_target="tpu_custom_call" | custom-call | tf_op jit(solution)/shard_map/downward/pallas_call | solution.py:464
  (3 shorter events, 0.0 us)
Async XLA Ops:
  0.0 14.4 %copy-start.4 = (bf16[16,8,256]{2,1,0:T(8,128)(2,1)S(1)}, bf16[16,8,256]{2,1,0:T(8,128)(2,1)}, u32[]{:S(2)}) copy-start(bf16[16,8,256]{2,1,0:T(8,128)(2,1)} %charges.1) | copy-start | bytes 196612
  0.0 14.4 %copy-start.8 = (s32[32,2]{0,1:T(2,128)S(1)}, s32[32,2]{0,1:T(2,128)}, u32[]{:S(2)}) copy-start(s32[32,2]{0,1:T(2,128)} %param.14) | copy-start | bytes 772
  0.0 6.1 %collective-permute-start = (bf16[16,8,256]{2,1,0:T(8,128)(2,1)}, bf16[16,8,256]{2,1,0:T(8,128)(2,1)S(1)}, u32[]{:S(2)}, u32[]{:S(2)}) collective-permute-start(bf16[16,8,256]{2,1,0:T(8,128)(2,1)} %charges.1), channel_id=1, source_target_pairs={{1,0},{2,1},{3,2},{4,3},{5,4},{6,5},{7,6},{8,7},{9,8},{10,9},{11,1... | collective-permute-start | bytes 196616 | tf_op jit(solution)/shard_map/ppermute | solution.py:344
  6.1 22.3 %copy-start = (bf16[128,64,64]{0,2,1:T(8,128)(2,1)S(1)}, bf16[128,64,64]{0,2,1:T(8,128)(2,1)}, u32[]{:S(2)}) copy-start(bf16[128,64,64]{0,2,1:T(8,128)(2,1)} %param.19) | copy-start | bytes 3145732
  6.1 22.3 %copy-start.5 = (s32[128,2]{0,1:T(2,128)S(1)}, s32[128,2]{0,1:T(2,128)}, u32[]{:S(2)}) copy-start(s32[128,2]{0,1:T(2,128)} %param.18) | copy-start | bytes 3076
  6.1 22.0 %all-to-all-start = ((bf16[16,8,1920]{2,1,0:T(8,128)(2,1)}), bf16[16,8,1920]{2,1,0:T(8,128)(2,1)S(1)}, u32[]{:S(2)}, u32[]{:S(2)}) async-start(bf16[16,8,1920]{2,1,0:T(8,128)(2,1)} %bitcast.20), calls=%async_computation | async-start | bytes 983040 | tf_op jit(solution)/shard_map/all_to_all | solution.py:416
  14.4 15.3 %copy-start.1 = (bf16[16,64,256]{2,1,0:T(8,128)(2,1)S(1)}, bf16[16,64,256]{2,1,0:T(8,128)(2,1)}, u32[]{:S(2)}) copy-start(bf16[16,64,256]{2,1,0:T(8,128)(2,1)} %bases.1) | copy-start | bytes 1572868
  14.4 15.3 %copy-start.2 = (bf16[32,64,64]{2,1,0:T(8,128)(2,1)S(1)}, bf16[32,64,64]{2,1,0:T(8,128)(2,1)}, u32[]{:S(2)}) copy-start(bf16[32,64,64]{2,1,0:T(8,128)(2,1)} %par_c.1) | copy-start | bytes 786436
  14.4 15.3 %copy-start.3 = (bf16[16,64,64]{2,1,0:T(8,128)(2,1)S(1)}, bf16[16,64,64]{2,1,0:T(8,128)(2,1)}, u32[]{:S(2)}) copy-start(bf16[16,64,64]{2,1,0:T(8,128)(2,1)} %transfers.1) | copy-start | bytes 393220
  14.4 15.3 %copy-start.6 = (s32[32,2]{0,1:T(2,128)S(1)}, s32[32,2]{0,1:T(2,128)}, u32[]{:S(2)}) copy-start(s32[32,2]{0,1:T(2,128)} %param.20) | copy-start | bytes 772
  14.4 15.3 %copy-start.7 = (s32[16]{0:T(128)S(1)}, s32[16]{0:T(128)}, u32[]{:S(2)}) copy-start(s32[16]{0:T(128)} %param.17) | copy-start | bytes 196
  19.6 3.2 %collective-permute-start.1 = (bf16[16,8,256]{2,1,0:T(8,128)(2,1)S(1)}, bf16[16,8,256]{2,1,0:T(8,128)(2,1)S(1)}, u32[]{:S(2)}, u32[]{:S(2)}) collective-permute-start(bf16[16,8,256]{2,1,0:T(8,128)(2,1)S(1)} %get-tuple-element.9), channel_id=1, source_target_pairs={{0,1},{1,2},{2,3},{3,4},{4,5},{5,6},{6,7},{7,8},{8,9},{9,10},{10,1... | collective-permute-start | bytes 196616 | tf_op jit(solution)/shard_map/ppermute | solution.py:344
  28.2 1.5 %collective-permute-start.2 = (bf16[128,768]{1,0:T(8,128)(2,1)S(1)}, bf16[128,768]{1,0:T(8,128)(2,1)S(1)}, u32[]{:S(2)}, u32[]{:S(2)}) collective-permute-start(bf16[128,768]{1,0:T(8,128)(2,1)S(1)} %slice.4), channel_id=1, source_target_pairs={{0,1},{1,0},{2,3},{3,2},{4,5},{5,4},{6,7},{7,6},{8,9},{9,8},{10,11... | collective-permute-start | bytes 589832 | tf_op jit(solution)/shard_map/ppermute | solution.py:446

commit v15 on v14

--- a/solution.py
+++ b/solution.py
@@ -261,6 +261,34 @@
     half[...] = far_half(mom, far_pairs, far_c, b_ref, fw, leaves, parents)
 
 
+def repeated(values, times):
+    count = values.shape[1]
+    spread = one_hot(iota((count, count * times), 1) // times == iota((count, count * times), 0))
+    rows = jnp.broadcast_to(values.astype(F32), (8, count)).astype(BF16)
+    return dot_nn(rows, spread)[0:1].astype(jnp.int32)
+
+
+def prepare_kernel(earlier, par_pairs, parent_of, par_c, par_t, pick, to_owner, to_leaf):
+    pairs = par_c.shape[0]
+    rows = pick.shape[1]
+    leaves = parent_of.shape[1]
+    parents = leaves // 2
+    rhs = to_owner.shape[0] // parents
+    for s in range(pairs):
+        par_t[s] = par_c[s].astype(F32).T.astype(BF16)
+    hot = jnp.where(par_pairs[1:2, :] == iota((rows, pairs), 0), 1.0, 0.0)
+    pick[...] = hot.T.astype(BF16)
+
+    def by_rows(targets):
+        shape = (parents * rhs, targets.shape[1] * rhs)
+        row, column = iota(shape, 0), iota(shape, 1)
+        same = (repeated(targets % parents, rhs) == row // rhs) & (row % rhs == column % rhs)
+        return jnp.where(same, 1.0, 0.0)
+
+    to_owner[...] = by_rows(par_pairs[0:1, :]).astype(BF16)
+    to_leaf[...] = by_rows(parent_of[...]).T.astype(BF16)
+
+
 def post_kernel(
     core_smem,
     half,
@@ -269,11 +297,12 @@
     got,
     bases,
     transfers,
-    parent_of,
     far_pairs,
     far_c,
-    par_pairs,
-    par_c,
+    par_t,
+    pick,
+    to_owner,
+    to_leaf,
     near_own,
     near_back,
     out,
@@ -282,13 +311,13 @@
     g_ref,
     pf,
     lf,
-    pg,
+    pb,
     dn,
 ):
     leaves, rank, _ = bases.shape
     width = back.shape[1]
     rhs = width // rank
-    pairs = par_c.shape[0]
+    pairs = par_t.shape[0]
     parents = leaves // 2
     rows = got.shape[0]
     core = core_smem[0, 0] // leaves % 2
@@ -300,21 +329,19 @@
 
     wide = mom2.shape[1] // 3
     shared = in_order(got[:, got.shape[1] - wide :], mom2[:, 2 * wide :])
-    hot = one_hot(par_pairs[1:2, :] == iota((rows, pairs), 0))
-    lanes_to_rows(g_ref, dot_tn(hot, shared), rhs)
+    fold = one_hot(iota((parents, rows), 1) % parents == iota((parents, rows), 0))
+    at = width + LANES
+    lanes_to_rows(pb, dot_nn(fold, got[:, at : at + width]), rhs)
+    lanes_to_rows(g_ref, dot_nn(pick[...], shared), rhs)
     for s in range(pairs):
         at = slice(s * rhs, (s + 1) * rhs)
-        pf[at, :] = dot_nt(g_ref[at, :].astype(BF16), par_c[s])
-    high, low = split2(rows_to_lanes(pf, pairs, rhs))
-    hot = one_hot(par_pairs[0:1, :] % parents == iota((parents, pairs), 0))
-    fold = one_hot(iota((parents, rows), 1) % parents == iota((parents, rows), 0))
-    at = width + LANES
-    locals_p = dot_nn(hot, high) + dot_nn(hot, low) + dot_nn(fold, got[:, at : at + width])
-    hot = one_hot(parent_of[...] % parents == iota((parents, leaves), 0))
-    lanes_to_rows(pg, dot_tn(hot, locals_p.astype(BF16)), rhs)
+        pf[at, :] = dot_nn(g_ref[at, :].astype(BF16), par_t[s])
+    high, low = split2(pf[...])
+    locals_p = dot_nn(to_owner[...], high) + dot_nn(to_owner[...], low) + pb[...]
+    picked = dot_nn(to_leaf[...], locals_p.astype(BF16)).astype(BF16)
     for l in range(leaves):
         at = slice(l * rhs, (l + 1) * rhs)
-        dn[at, :] = dot_nn(pg[at, :].astype(BF16), transfers[l])
+        dn[at, :] = dot_nn(picked[at, :], transfers[l])
 
     other = far_half(mom2[...], far_pairs, far_c, b_ref, fw, leaves, parents)
     lanes_to_rows(lf, back[...] + in_order(half[...], other), rhs)
@@ -328,14 +355,14 @@
 def after(value, earlier, vmem_limit):
     anywhere = pl.BlockSpec(memory_space=pl.ANY)
     return pl.pallas_call(
-        lambda value, earlier, same: None,
+        lambda *refs: None,
         out_shape=jax.ShapeDtypeStruct(value.shape, value.dtype),
-        in_specs=[anywhere] * 2,
+        in_specs=[anywhere] * (1 + len(earlier)),
         out_specs=anywhere,
         input_output_aliases={0: 0},
         compiler_params=pltpu.CompilerParams(vmem_limit_bytes=vmem_limit),
         name="after",
-    )(value, earlier)
+    )(value, *earlier)
 
 
 def passed_along(value, axis, steps):
@@ -412,7 +439,7 @@
         cost_estimate=cost(10_000_000),
         name="upward",
     )(charges, bases, transfers, parent_of, far_pairs, far_c, par_pairs, par_coupling)
-    send = after(send, following, 107 << 19)
+    send = after(send, [following], 107 << 19)
     got = lax.all_to_all(send, "sfc", split_axis=0, concat_axis=0, tiled=True)
     steps = 4
     selves, nears = leaves // steps, near_blocks.shape[0] // steps
@@ -442,7 +469,25 @@
     )(near_pairs, charges, following, self_blocks, near_blocks)
     near_back = passed_along(near_away, "sfc", 1)
 
-    got = after(got, near_back, 1 << 20)
+    prepared = pl.pallas_call(
+        prepare_kernel,
+        out_shape=[
+            jax.ShapeDtypeStruct(shape, BF16)
+            for shape in (
+                par_coupling.shape,
+                (pairs, rows),
+                (parents * rhs, pairs * rhs),
+                (leaves * rhs, parents * rhs),
+            )
+        ],
+        in_specs=[pl.BlockSpec(memory_space=pl.ANY)] + [vmem] * 3,
+        out_specs=[vmem] * 4,
+        compiler_params=late,
+        cost_estimate=cost(4_000_000),
+        name="prepare",
+    )(near_away, par_pairs, parent_of, par_coupling)
+
+    got = after(got, [near_back, *prepared], 1 << 20)
     mom2 = lax.ppermute(
         got[:, 2 * width + LANES :], "sfc", [(i, i ^ 1) for i in range(devices)]
     )
@@ -464,7 +509,7 @@
     return pl.pallas_call(
         post_kernel,
         out_shape=jax.ShapeDtypeStruct((leaves, rhs, panels), F32),
-        in_specs=[smem] + [vmem] * 13,
+        in_specs=[smem] + [vmem] * 14,
         out_specs=vmem,
         scratch_shapes=[
             pltpu.VMEM((width // 2, slots), F32),
@@ -472,7 +517,7 @@
             pltpu.VMEM((pairs * rhs, rank), F32),
             pltpu.VMEM((pairs * rhs, rank), F32),
             pltpu.VMEM((leaves * rhs, rank), F32),
-            pltpu.VMEM((leaves * rhs, rank), F32),
+            pltpu.VMEM((parents * rhs, rank), F32),
             pltpu.VMEM((leaves * rhs, rank), F32),
         ],
         compiler_params=late,
@@ -485,11 +530,9 @@
         got,
         bases,
         transfers,
-        parent_of,
         far_pairs,
         far_c,
-        par_pairs,
-        par_coupling,
+        *prepared,
         near_own,
         near_back,
     )

time: 33.7 us -> 34.3 us (1.018)
  local copies, waits for them, and re-layouts: 0.07 us -> 0.98 us
    unnamed x18 -> x22, local copies, waits for them, and re-layouts: 0.05 us -> 0.96 us
  transfers between devices with their start and end apart: 4 -> 4, of which waited for: 3 -> 3; matrix products, arithmetic and copies ran while one was open for 0% -> 0% of each run, Pallas kernels for 32% -> 33%
where the time goes in v15:
time: 34.3 us; the launch traced here: 33.9 us
  Pallas kernels  14.4 us (42%)
  starting transfers between devices  12.2 us (36%)
  waiting for transfers between devices  6.2 us (18%)
  local copies, waits for them, and re-layouts  0.98 us (3%)
    all_to_all x1, starting transfers between devices, on_device(): got = lax.all_to_all(send, 'sfc', split_axis=0, concat_axis=0, tiled=True)  8.26 us
    all_to_all x1, waiting for transfers between devices, on_device(): got = lax.all_to_all(send, 'sfc', split_axis=0, concat_axis=0, tiled=True)  5.35 us
    pallas_call x1, Pallas kernels, on_device(): pl.pallas_call(near_kernel, grid=(steps,), out_shape=[jax.ShapeDtypeStruc...  5.14 us
    pallas_call x1, Pallas kernels, on_device(): pl.pallas_call(pre_kernel, out_shape=jax.ShapeDtypeStruct((rows, columns)...  4.64 us
    ppermute x2, starting transfers between devices, passed_along(): lax.ppermute(value, axis, [(source, source + steps) for source in range(l...  3.72 us
    pallas_call x1, Pallas kernels, on_device(): pl.pallas_call(post_kernel, out_shape=jax.ShapeDtypeStruct((leaves, rhs,...  3.31 us
    pallas_call x1, Pallas kernels, on_device(): pl.pallas_call(far_kernel, out_shape=[jax.ShapeDtypeStruct((leaves, width...  1.07 us
    unnamed x22, local copies, waits for them, and re-layouts  0.96 us
  transfers between devices with their start and end apart: 4, of which 3 were waited for; matrix products, arithmetic and copies ran while one was open for 0% of the time, Pallas kernels for 33%

profile of v15, /device:TPU:0, one launch (start us, length us, event | category | flops | bytes accessed | tf_op | source)
XLA Modules:
  0.0 33.9 jit_solution(6002891940981526597)
XLA Ops:
  0.0 0.0 copy-start.4
  0.0 0.0 copy-start.10
  0.0 1.4 %collective-permute-start = (bf16[16,8,256]{2,1,0:T(8,128)(2,1)}, bf16[16,8,256]{2,1,0:T(8,128)(2,1)S(1)}, u32[]{:S(2)}, u32[]{:S(2)}) collective-permute-start(bf16[16,8,256]{2,1,0:T(8,128)(2,1)} %charges.1), channel_id=1, source_target_pairs={{1,0},{2,1},{3,2},{4,3},{5,4},{6,5},{7,6},{8,7},{9,8},{10,9},{11,1... | collective-permute-start | bytes 196616 | tf_op jit(solution)/shard_map/ppermute | solution.py:371
  1.4 4.6 %upward.1.refs_0_ = bf16[128,1920]{1,0:T(8,128)(2,1)} custom-call(bf16[16,8,256]{2,1,0:T(8,128)(2,1)} %charges.1, bf16[16,64,256]{2,1,0:T(8,128)(2,1)} %bases.1, bf16[16,64,64]{2,1,0:T(8,128)(2,1)} %transfers.1, s32[1,16]{1,0:T(1,128)} %bitcast.17, s32[2,128]{1,0:T(2,128)} %bitcast.11, bf16[64,64,128]{2,1,0:T(8,128)(2,1)} %bitcast.8, s32[2,32]{1,0:T(2,128)} %bitcast.15, ...), custom_call_target="tpu_custom_call" | custom-call | flops 40000000 | bytes 10000000 | tf_op jit(solution)/shard_map/upward/pallas_call | solution.py:415
  6.1 0.0 copy-start.1
  6.1 0.0 copy-start.8
  6.1 0.0 copy-start.9
  6.1 0.0 collective-permute-done.refs_1_.following
  6.1 8.3 %all-to-all-start = ((bf16[16,8,1920]{2,1,0:T(8,128)(2,1)}), bf16[16,8,1920]{2,1,0:T(8,128)(2,1)S(1)}, u32[]{:S(2)}, u32[]{:S(2)}) async-start(bf16[16,8,1920]{2,1,0:T(8,128)(2,1)} %bitcast.20), calls=%async_computation | async-start | bytes 983040 | tf_op jit(solution)/shard_map/all_to_all | solution.py:443
  14.4 0.0 copy-done.4
  14.4 0.0 copy-done.10
  14.4 0.0 copy-start
  14.4 0.0 copy-start.7
  14.4 0.0 copy-start.2
  14.5 0.0 copy-start.3
  14.5 5.1 %near.1 = (f32[16,8,256]{2,1,0:T(8,128)S(1)}, bf16[16,8,256]{2,1,0:T(8,128)(2,1)S(1)}) custom-call(s32[2,32]{1,0:T(2,128)S(1)} %bitcast.19, bf16[16,8,256]{2,1,0:T(8,128)(2,1)S(1)} %copy-done.4, bf16[16,8,256]{2,1,0:T(8,128)(2,1)S(1)} %collective-permute-done.refs_1_.following, bf16[16,256,256]{2,1,0:T(8,128)(2,1)} %self_blocks.1, ...), custom_call_target="tpu_custom_call" | custom-call | flops 80000000 | bytes 20000000 | tf_op jit(solution)/shard_map/near/pallas_call | solution.py:447
  19.6 0.0 copy-start.5
  19.6 2.3 %collective-permute-start.1 = (bf16[16,8,256]{2,1,0:T(8,128)(2,1)S(1)}, bf16[16,8,256]{2,1,0:T(8,128)(2,1)S(1)}, u32[]{:S(2)}, u32[]{:S(2)}) collective-permute-start(bf16[16,8,256]{2,1,0:T(8,128)(2,1)S(1)} %get-tuple-element.13.earlier), channel_id=1, source_target_pairs={{0,1},{1,2},{2,3},{3,4},{4,5},{5,6},{6,7},{7,8},{8,9},{9,10},{10,1... | collective-permute-start | bytes 196616 | tf_op jit(solution)/shard_map/ppermute | solution.py:371
  21.9 0.0 copy-done.1
  21.9 0.0 copy-done.8
  22.0 0.0 copy-done.9
  22.0 0.2 prepare.1
  22.2 0.0 copy-done.5
  22.2 0.6 %collective-permute-done.1.refs_1_.near_back = bf16[16,8,256]{2,1,0:T(8,128)(2,1)S(1)} collective-permute-done((bf16[16,8,256]{2,1,0:T(8,128)(2,1)S(1)}, bf16[16,8,256]{2,1,0:T(8,128)(2,1)S(1)}, u32[]{:S(2)}, u32[]{:S(2)}) %collective-permute-start.1) | collective-permute-done | bytes 65568 | tf_op jit(solution)/shard_map/ppermute | solution.py:371
  22.8 5.4 %all-to-all-done = bf16[16,8,1920]{2,1,0:T(8,128)(2,1)S(1)} async-done(((bf16[16,8,1920]{2,1,0:T(8,128)(2,1)}), bf16[16,8,1920]{2,1,0:T(8,128)(2,1)S(1)}, u32[]{:S(2)}, u32[]{:S(2)}) %all-to-all-start) | async-done | bytes 491552 | tf_op jit(solution)/shard_map/all_to_all | solution.py:443
  28.2 0.2 collective-permute-start.2
  28.4 0.0 copy-done
  28.4 0.0 copy-done.7
  28.4 1.1 %far.1 = (f32[16,256]{1,0:T(8,128)S(1)}, f32[16,512]{1,0:T(8,128)S(1)}) custom-call(bf16[128,1920]{1,0:T(8,128)(2,1)S(1)} %after.3.got, s32[2,128]{1,0:T(2,128)S(1)} %bitcast.12, bf16[64,64,128]{2,1,0:T(8,128)(2,1)S(1)} %bitcast.9), custom_call_target="tpu_custom_call" | custom-call | flops 32000000 | bytes 8000000 | tf_op jit(solution)/shard_map/far/pallas_call | solution.py:495
  29.4 0.2 collective-permute-done.2.mom2
  29.7 0.0 copy-done.2
  29.7 0.0 copy-done.3
  29.7 0.0 copy-start.6
  29.7 0.9 %copy-done.6 = f32[16,8,256]{2,1,0:T(8,128)S(1)} copy-done((f32[16,8,256]{2,1,0:T(8,128)S(1)}, f32[16,8,256]{2,1,0:T(8,128)}, u32[]{:S(2)}) %copy-start.6) | copy-done | bytes 131096
  30.6 3.3 %downward.1 = f32[16,8,256]{2,1,0:T(8,128)} custom-call(s32[2,128]{1,0:T(2,128)S(1)} %bitcast.13, f32[16,256]{1,0:T(8,128)S(1)} %get-tuple-element.18.half, f32[16,512]{1,0:T(8,128)S(1)} %get-tuple-element.19.back, bf16[128,768]{1,0:T(8,128)(2,1)S(1)} %collective-permute-done.2.mom2, bf16[128,1920]{1,0:T(8,128)(2,1)S(1)} %after.3.got, ...), custom_call_target="tpu_custom_call" | custom-call | tf_op jit(solution)/shard_map/downward/pallas_call | solution.py:509
  (3 shorter events, 0.0 us)
Async XLA Ops:
  0.0 14.4 %copy-start.4 = (bf16[16,8,256]{2,1,0:T(8,128)(2,1)S(1)}, bf16[16,8,256]{2,1,0:T(8,128)(2,1)}, u32[]{:S(2)}) copy-start(bf16[16,8,256]{2,1,0:T(8,128)(2,1)} %charges.1) | copy-start | bytes 196612
  0.0 14.4 %copy-start.10 = (s32[32,2]{0,1:T(2,128)S(1)}, s32[32,2]{0,1:T(2,128)}, u32[]{:S(2)}) copy-start(s32[32,2]{0,1:T(2,128)} %param.14) | copy-start | bytes 772
  0.0 6.1 %collective-permute-start = (bf16[16,8,256]{2,1,0:T(8,128)(2,1)}, bf16[16,8,256]{2,1,0:T(8,128)(2,1)S(1)}, u32[]{:S(2)}, u32[]{:S(2)}) collective-permute-start(bf16[16,8,256]{2,1,0:T(8,128)(2,1)} %charges.1), channel_id=1, source_target_pairs={{1,0},{2,1},{3,2},{4,3},{5,4},{6,5},{7,6},{8,7},{9,8},{10,9},{11,1... | collective-permute-start | bytes 196616 | tf_op jit(solution)/shard_map/ppermute | solution.py:371
  6.1 15.9 %copy-start.1 = (bf16[32,64,64]{2,1,0:T(8,128)(2,1)S(1)}, bf16[32,64,64]{2,1,0:T(8,128)(2,1)}, u32[]{:S(2)}) copy-start(bf16[32,64,64]{2,1,0:T(8,128)(2,1)} %par_c.1) | copy-start | bytes 786436
  6.1 15.9 %copy-start.8 = (s32[32,2]{0,1:T(2,128)S(1)}, s32[32,2]{0,1:T(2,128)}, u32[]{:S(2)}) copy-start(s32[32,2]{0,1:T(2,128)} %param.20) | copy-start | bytes 772
  6.1 15.9 %copy-start.9 = (s32[16]{0:T(128)S(1)}, s32[16]{0:T(128)}, u32[]{:S(2)}) copy-start(s32[16]{0:T(128)} %param.17) | copy-start | bytes 196
  6.1 22.0 %all-to-all-start = ((bf16[16,8,1920]{2,1,0:T(8,128)(2,1)}), bf16[16,8,1920]{2,1,0:T(8,128)(2,1)S(1)}, u32[]{:S(2)}, u32[]{:S(2)}) async-start(bf16[16,8,1920]{2,1,0:T(8,128)(2,1)} %bitcast.20), calls=%async_computation | async-start | bytes 983040 | tf_op jit(solution)/shard_map/all_to_all | solution.py:443
  14.4 14.0 %copy-start = (bf16[128,64,64]{0,2,1:T(8,128)(2,1)S(1)}, bf16[128,64,64]{0,2,1:T(8,128)(2,1)}, u32[]{:S(2)}) copy-start(bf16[128,64,64]{0,2,1:T(8,128)(2,1)} %param.19) | copy-start | bytes 3145732
  14.4 13.9 %copy-start.7 = (s32[128,2]{0,1:T(2,128)S(1)}, s32[128,2]{0,1:T(2,128)}, u32[]{:S(2)}) copy-start(s32[128,2]{0,1:T(2,128)} %param.18) | copy-start | bytes 3076
  14.4 15.3 %copy-start.2 = (bf16[16,64,256]{2,1,0:T(8,128)(2,1)S(1)}, bf16[16,64,256]{2,1,0:T(8,128)(2,1)}, u32[]{:S(2)}) copy-start(bf16[16,64,256]{2,1,0:T(8,128)(2,1)} %bases.1) | copy-start | bytes 1572868
  14.5 15.3 %copy-start.3 = (bf16[16,64,64]{2,1,0:T(8,128)(2,1)S(1)}, bf16[16,64,64]{2,1,0:T(8,128)(2,1)}, u32[]{:S(2)}) copy-start(bf16[16,64,64]{2,1,0:T(8,128)(2,1)} %transfers.1) | copy-start | bytes 393220
  19.6 2.6 %copy-start.5 = (f32[16,8,256]{2,1,0:T(8,128)}, f32[16,8,256]{2,1,0:T(8,128)S(1)}, u32[]{:S(2)}) copy-start(f32[16,8,256]{2,1,0:T(8,128)S(1)} %get-tuple-element.20.near_own) | copy-start | bytes 393220
  19.6 3.2 %collective-permute-start.1 = (bf16[16,8,256]{2,1,0:T(8,128)(2,1)S(1)}, bf16[16,8,256]{2,1,0:T(8,128)(2,1)S(1)}, u32[]{:S(2)}, u32[]{:S(2)}) collective-permute-start(bf16[16,8,256]{2,1,0:T(8,128)(2,1)S(1)} %get-tuple-element.13.earlier), channel_id=1, source_target_pairs={{0,1},{1,2},{2,3},{3,4},{4,5},{5,6},{6,7},{7,8},{8,9},{9,10},{10,1... | collective-permute-start | bytes 196616 | tf_op jit(solution)/shard_map/ppermute | solution.py:371
  28.2 1.5 %collective-permute-start.2 = (bf16[128,768]{1,0:T(8,128)(2,1)S(1)}, bf16[128,768]{1,0:T(8,128)(2,1)S(1)}, u32[]{:S(2)}, u32[]{:S(2)}) collective-permute-start(bf16[128,768]{1,0:T(8,128)(2,1)S(1)} %slice.4), channel_id=1, source_target_pairs={{0,1},{1,0},{2,3},{3,2},{4,5},{5,4},{6,7},{7,6},{8,9},{9,8},{10,11... | collective-permute-start | bytes 589832 | tf_op jit(solution)/shard_map/ppermute | solution.py:491
  29.7 0.9 %copy-start.6 = (f32[16,8,256]{2,1,0:T(8,128)S(1)}, f32[16,8,256]{2,1,0:T(8,128)}, u32[]{:S(2)}) copy-start(f32[16,8,256]{2,1,0:T(8,128)} %copy-done.5) | copy-start | bytes 393220

commit v16 on v15

--- a/solution.py
+++ b/solution.py
@@ -153,26 +153,19 @@
         q = par_smem[0, s] % parents
         x = pm3[pl.ds(pl.multiple_of(q * rhs, rhs), rhs), :].astype(BF16)
         pb[s * rhs : (s + 1) * rhs, :] = dot_nn(x, par_c[s])
-    half = rank // 2
+    some = rank // 4
     for sb in range(slots // LANES):
         lanes = slice(sb * LANES, (sb + 1) * LANES)
-        for jh in range(2):
-
-            def body(k8, acc):
-                rows_a = [
-                    a_ref[pl.ds(pl.multiple_of(r * rank + k8 * 8, 8), 8), lanes]
-                    for r in range(rhs)
-                ]
-                for i in range(8):
-                    c = far_c[k8 * 8 + i, jh * half : (jh + 1) * half, lanes].astype(F32)
-                    acc = tuple(acc[r] + c * rows_a[r][i : i + 1, :] for r in range(rhs))
-                return acc
-
-            acc = tuple(jnp.zeros((half, LANES), F32) for _ in range(rhs))
-            acc = lax.fori_loop(0, rank // 8, body, acc, unroll=4)
+        for first in range(0, rank, some):
+            acc = [None] * rhs
+            for k in range(rank):
+                c = far_c[k, first : first + some, lanes].astype(F32)
+                for r in range(rhs):
+                    term = c * a_ref[r * rank + k : r * rank + k + 1, lanes]
+                    acc[r] = term if k == 0 else acc[r] + term
             for r in range(rhs):
-                first = r * rank + jh * half
-                ob[first : first + half, lanes] = acc[r].astype(BF16)
+                at = r * rank + first
+                ob[at : at + some, lanes] = acc[r].astype(BF16)
     partner = far_pairs[1:2, :]
     local = jnp.where(partner >= 0, partner % leaves, -1).astype(F32)
     ob[width : width + LANES, :] = jnp.broadcast_to(local, (LANES, slots)).astype(BF16)
@@ -397,7 +390,7 @@
     smem = pl.BlockSpec(memory_space=pltpu.SMEM)
     hbm = pl.BlockSpec(memory_space=pltpu.HBM)
     params = pltpu.CompilerParams(vmem_limit_bytes=60 * 1024 * 1024)
-    late = pltpu.CompilerParams(vmem_limit_bytes=48 * 1024 * 1024)
+    late = pltpu.CompilerParams(vmem_limit_bytes=32 * 1024 * 1024)
 
     def cost(moved):
         return pl.CostEstimate(flops=4 * moved, bytes_accessed=moved, transcendentals=0)

time: 34.3 us -> 34.2 us (level)
  transfers between devices with their start and end apart: 4 -> 4, of which waited for: 3 -> 3; matrix products, arithmetic and copies ran while one was open for 0% -> 0% of each run, Pallas kernels for 33% -> 32%
where the time goes in v16:
time: 34.2 us; the launch traced here: 33.8 us
  Pallas kernels  14.3 us (42%)
  starting transfers between devices  12.2 us (36%)
  waiting for transfers between devices  6.2 us (18%)
  local copies, waits for them, and re-layouts  0.98 us (3%)
    all_to_all x1, starting transfers between devices, on_device(): got = lax.all_to_all(send, 'sfc', split_axis=0, concat_axis=0, tiled=True)  8.26 us
    all_to_all x1, waiting for transfers between devices, on_device(): got = lax.all_to_all(send, 'sfc', split_axis=0, concat_axis=0, tiled=True)  5.35 us
    pallas_call x1, Pallas kernels, on_device(): pl.pallas_call(near_kernel, grid=(steps,), out_shape=[jax.ShapeDtypeStruc...  5.14 us
    pallas_call x1, Pallas kernels, on_device(): pl.pallas_call(pre_kernel, out_shape=jax.ShapeDtypeStruct((rows, columns)...  4.5 us
    ppermute x2, starting transfers between devices, passed_along(): lax.ppermute(value, axis, [(source, source + steps) for source in range(l...  3.72 us
    pallas_call x1, Pallas kernels, on_device(): pl.pallas_call(post_kernel, out_shape=jax.ShapeDtypeStruct((leaves, rhs,...  3.31 us
    pallas_call x1, Pallas kernels, on_device(): pl.pallas_call(far_kernel, out_shape=[jax.ShapeDtypeStruct((leaves, width...  1.07 us
    unnamed x22, local copies, waits for them, and re-layouts  0.96 us
  transfers between devices with their start and end apart: 4, of which 3 were waited for; matrix products, arithmetic and copies ran while one was open for 0% of the time, Pallas kernels for 32%

profile of v16, /device:TPU:0, one launch (start us, length us, event | category | flops | bytes accessed | tf_op | source)
XLA Modules:
  0.0 33.8 jit_solution(8118267279085020768)
XLA Ops:
  0.0 0.0 copy-start.4
  0.0 0.0 copy-start.10
  0.0 1.4 %collective-permute-start = (bf16[16,8,256]{2,1,0:T(8,128)(2,1)}, bf16[16,8,256]{2,1,0:T(8,128)(2,1)S(1)}, u32[]{:S(2)}, u32[]{:S(2)}) collective-permute-start(bf16[16,8,256]{2,1,0:T(8,128)(2,1)} %charges.1), channel_id=1, source_target_pairs={{1,0},{2,1},{3,2},{4,3},{5,4},{6,5},{7,6},{8,7},{9,8},{10,9},{11,1... | collective-permute-start | bytes 196616 | tf_op jit(solution)/shard_map/ppermute | solution.py:364
  1.4 4.5 %upward.1.refs_0_ = bf16[128,1920]{1,0:T(8,128)(2,1)} custom-call(bf16[16,8,256]{2,1,0:T(8,128)(2,1)} %charges.1, bf16[16,64,256]{2,1,0:T(8,128)(2,1)} %bases.1, bf16[16,64,64]{2,1,0:T(8,128)(2,1)} %transfers.1, s32[1,16]{1,0:T(1,128)} %bitcast.17, s32[2,128]{1,0:T(2,128)} %bitcast.11, bf16[64,64,128]{2,1,0:T(8,128)(2,1)} %bitcast.8, s32[2,32]{1,0:T(2,128)} %bitcast.15, ...), custom_call_target="tpu_custom_call" | custom-call | flops 40000000 | bytes 10000000 | tf_op jit(solution)/shard_map/upward/pallas_call | solution.py:408
  5.9 0.0 copy-start.1
  5.9 0.0 copy-start.8
  6.0 0.0 copy-start.9
  6.0 0.0 collective-permute-done.refs_1_.following
  6.0 8.3 %all-to-all-start = ((bf16[16,8,1920]{2,1,0:T(8,128)(2,1)}), bf16[16,8,1920]{2,1,0:T(8,128)(2,1)S(1)}, u32[]{:S(2)}, u32[]{:S(2)}) async-start(bf16[16,8,1920]{2,1,0:T(8,128)(2,1)} %bitcast.20), calls=%async_computation | async-start | bytes 983040 | tf_op jit(solution)/shard_map/all_to_all | solution.py:436
  14.3 0.0 copy-done.4
  14.3 0.0 copy-done.10
  14.3 0.0 copy-start
  14.3 0.0 copy-start.7
  14.3 0.0 copy-start.2
  14.3 0.0 copy-start.3
  14.3 5.1 %near.1 = (f32[16,8,256]{2,1,0:T(8,128)S(1)}, bf16[16,8,256]{2,1,0:T(8,128)(2,1)S(1)}) custom-call(s32[2,32]{1,0:T(2,128)S(1)} %bitcast.19, bf16[16,8,256]{2,1,0:T(8,128)(2,1)S(1)} %copy-done.4, bf16[16,8,256]{2,1,0:T(8,128)(2,1)S(1)} %collective-permute-done.refs_1_.following, bf16[16,256,256]{2,1,0:T(8,128)(2,1)} %self_blocks.1, ...), custom_call_target="tpu_custom_call" | custom-call | flops 80000000 | bytes 20000000 | tf_op jit(solution)/shard_map/near/pallas_call | solution.py:440
  19.5 0.0 copy-start.5
  19.5 2.3 %collective-permute-start.1 = (bf16[16,8,256]{2,1,0:T(8,128)(2,1)S(1)}, bf16[16,8,256]{2,1,0:T(8,128)(2,1)S(1)}, u32[]{:S(2)}, u32[]{:S(2)}) collective-permute-start(bf16[16,8,256]{2,1,0:T(8,128)(2,1)S(1)} %get-tuple-element.13.earlier), channel_id=1, source_target_pairs={{0,1},{1,2},{2,3},{3,4},{4,5},{5,6},{6,7},{7,8},{8,9},{9,10},{10,1... | collective-permute-start | bytes 196616 | tf_op jit(solution)/shard_map/ppermute | solution.py:364
  21.8 0.0 copy-done.1
  21.8 0.0 copy-done.8
  21.8 0.0 copy-done.9
  21.8 0.2 prepare.1
  22.1 0.0 copy-done.5
  22.1 0.6 %collective-permute-done.1.refs_1_.near_back = bf16[16,8,256]{2,1,0:T(8,128)(2,1)S(1)} collective-permute-done((bf16[16,8,256]{2,1,0:T(8,128)(2,1)S(1)}, bf16[16,8,256]{2,1,0:T(8,128)(2,1)S(1)}, u32[]{:S(2)}, u32[]{:S(2)}) %collective-permute-start.1) | collective-permute-done | bytes 65568 | tf_op jit(solution)/shard_map/ppermute | solution.py:364
  22.7 5.3 %all-to-all-done = bf16[16,8,1920]{2,1,0:T(8,128)(2,1)S(1)} async-done(((bf16[16,8,1920]{2,1,0:T(8,128)(2,1)}), bf16[16,8,1920]{2,1,0:T(8,128)(2,1)S(1)}, u32[]{:S(2)}, u32[]{:S(2)}) %all-to-all-start) | async-done | bytes 491552 | tf_op jit(solution)/shard_map/all_to_all | solution.py:436
  28.1 0.2 collective-permute-start.2
  28.2 0.0 copy-done
  28.2 0.0 copy-done.7
  28.2 1.1 %far.1 = (f32[16,256]{1,0:T(8,128)S(1)}, f32[16,512]{1,0:T(8,128)S(1)}) custom-call(bf16[128,1920]{1,0:T(8,128)(2,1)S(1)} %after.3.got, s32[2,128]{1,0:T(2,128)S(1)} %bitcast.12, bf16[64,64,128]{2,1,0:T(8,128)(2,1)S(1)} %bitcast.9), custom_call_target="tpu_custom_call" | custom-call | flops 32000000 | bytes 8000000 | tf_op jit(solution)/shard_map/far/pallas_call | solution.py:488
  29.3 0.2 collective-permute-done.2.mom2
  29.6 0.0 copy-done.2
  29.6 0.0 copy-done.3
  29.6 0.0 copy-start.6
  29.6 0.9 %copy-done.6 = f32[16,8,256]{2,1,0:T(8,128)S(1)} copy-done((f32[16,8,256]{2,1,0:T(8,128)S(1)}, f32[16,8,256]{2,1,0:T(8,128)}, u32[]{:S(2)}) %copy-start.6) | copy-done | bytes 131096
  30.5 3.3 %downward.1 = f32[16,8,256]{2,1,0:T(8,128)} custom-call(s32[2,128]{1,0:T(2,128)S(1)} %bitcast.13, f32[16,256]{1,0:T(8,128)S(1)} %get-tuple-element.18.half, f32[16,512]{1,0:T(8,128)S(1)} %get-tuple-element.19.back, bf16[128,768]{1,0:T(8,128)(2,1)S(1)} %collective-permute-done.2.mom2, bf16[128,1920]{1,0:T(8,128)(2,1)S(1)} %after.3.got, ...), custom_call_target="tpu_custom_call" | custom-call | tf_op jit(solution)/shard_map/downward/pallas_call | solution.py:502
  (3 shorter events, 0.0 us)
Async XLA Ops:
  0.0 14.3 %copy-start.4 = (bf16[16,8,256]{2,1,0:T(8,128)(2,1)S(1)}, bf16[16,8,256]{2,1,0:T(8,128)(2,1)}, u32[]{:S(2)}) copy-start(bf16[16,8,256]{2,1,0:T(8,128)(2,1)} %charges.1) | copy-start | bytes 196612
  0.0 14.3 %copy-start.10 = (s32[32,2]{0,1:T(2,128)S(1)}, s32[32,2]{0,1:T(2,128)}, u32[]{:S(2)}) copy-start(s32[32,2]{0,1:T(2,128)} %param.14) | copy-start | bytes 772
  0.0 6.0 %collective-permute-start = (bf16[16,8,256]{2,1,0:T(8,128)(2,1)}, bf16[16,8,256]{2,1,0:T(8,128)(2,1)S(1)}, u32[]{:S(2)}, u32[]{:S(2)}) collective-permute-start(bf16[16,8,256]{2,1,0:T(8,128)(2,1)} %charges.1), channel_id=1, source_target_pairs={{1,0},{2,1},{3,2},{4,3},{5,4},{6,5},{7,6},{8,7},{9,8},{10,9},{11,1... | collective-permute-start | bytes 196616 | tf_op jit(solution)/shard_map/ppermute | solution.py:364
  5.9 15.9 %copy-start.1 = (bf16[32,64,64]{2,1,0:T(8,128)(2,1)S(1)}, bf16[32,64,64]{2,1,0:T(8,128)(2,1)}, u32[]{:S(2)}) copy-start(bf16[32,64,64]{2,1,0:T(8,128)(2,1)} %par_c.1) | copy-start | bytes 786436
  5.9 15.9 %copy-start.8 = (s32[32,2]{0,1:T(2,128)S(1)}, s32[32,2]{0,1:T(2,128)}, u32[]{:S(2)}) copy-start(s32[32,2]{0,1:T(2,128)} %param.20) | copy-start | bytes 772
  6.0 15.9 %copy-start.9 = (s32[16]{0:T(128)S(1)}, s32[16]{0:T(128)}, u32[]{:S(2)}) copy-start(s32[16]{0:T(128)} %param.17) | copy-start | bytes 196
  6.0 22.0 %all-to-all-start = ((bf16[16,8,1920]{2,1,0:T(8,128)(2,1)}), bf16[16,8,1920]{2,1,0:T(8,128)(2,1)S(1)}, u32[]{:S(2)}, u32[]{:S(2)}) async-start(bf16[16,8,1920]{2,1,0:T(8,128)(2,1)} %bitcast.20), calls=%async_computation | async-start | bytes 983040 | tf_op jit(solution)/shard_map/all_to_all | solution.py:436
  14.3 14.0 %copy-start = (bf16[128,64,64]{0,2,1:T(8,128)(2,1)S(1)}, bf16[128,64,64]{0,2,1:T(8,128)(2,1)}, u32[]{:S(2)}) copy-start(bf16[128,64,64]{0,2,1:T(8,128)(2,1)} %param.19) | copy-start | bytes 3145732
  14.3 13.9 %copy-start.7 = (s32[128,2]{0,1:T(2,128)S(1)}, s32[128,2]{0,1:T(2,128)}, u32[]{:S(2)}) copy-start(s32[128,2]{0,1:T(2,128)} %param.18) | copy-start | bytes 3076
  14.3 15.3 %copy-start.2 = (bf16[16,64,256]{2,1,0:T(8,128)(2,1)S(1)}, bf16[16,64,256]{2,1,0:T(8,128)(2,1)}, u32[]{:S(2)}) copy-start(bf16[16,64,256]{2,1,0:T(8,128)(2,1)} %bases.1) | copy-start | bytes 1572868
  14.3 15.3 %copy-start.3 = (bf16[16,64,64]{2,1,0:T(8,128)(2,1)S(1)}, bf16[16,64,64]{2,1,0:T(8,128)(2,1)}, u32[]{:S(2)}) copy-start(bf16[16,64,64]{2,1,0:T(8,128)(2,1)} %transfers.1) | copy-start | bytes 393220
  19.5 2.6 %copy-start.5 = (f32[16,8,256]{2,1,0:T(8,128)}, f32[16,8,256]{2,1,0:T(8,128)S(1)}, u32[]{:S(2)}) copy-start(f32[16,8,256]{2,1,0:T(8,128)S(1)} %get-tuple-element.20.near_own) | copy-start | bytes 393220
  19.5 3.2 %collective-permute-start.1 = (bf16[16,8,256]{2,1,0:T(8,128)(2,1)S(1)}, bf16[16,8,256]{2,1,0:T(8,128)(2,1)S(1)}, u32[]{:S(2)}, u32[]{:S(2)}) collective-permute-start(bf16[16,8,256]{2,1,0:T(8,128)(2,1)S(1)} %get-tuple-element.13.earlier), channel_id=1, source_target_pairs={{0,1},{1,2},{2,3},{3,4},{4,5},{5,6},{6,7},{7,8},{8,9},{9,10},{10,1... | collective-permute-start | bytes 196616 | tf_op jit(solution)/shard_map/ppermute | solution.py:364
  28.1 1.5 %collective-permute-start.2 = (bf16[128,768]{1,0:T(8,128)(2,1)S(1)}, bf16[128,768]{1,0:T(8,128)(2,1)S(1)}, u32[]{:S(2)}, u32[]{:S(2)}) collective-permute-start(bf16[128,768]{1,0:T(8,128)(2,1)S(1)} %slice.4), channel_id=1, source_target_pairs={{0,1},{1,0},{2,3},{3,2},{4,5},{5,4},{6,7},{7,6},{8,9},{9,8},{10,11... | collective-permute-start | bytes 589832 | tf_op jit(solution)/shard_map/ppermute | solution.py:484
  29.6 0.9 %copy-start.6 = (f32[16,8,256]{2,1,0:T(8,128)S(1)}, f32[16,8,256]{2,1,0:T(8,128)}, u32[]{:S(2)}) copy-start(f32[16,8,256]{2,1,0:T(8,128)} %copy-done.5) | copy-start | bytes 393220

commit v17 on v16

--- a/solution.py
+++ b/solution.py
@@ -46,6 +46,20 @@
     rank = width // rhs
     for r in range(rhs):
         ref[pl.ds(r, count, stride=rhs), :] = value[:, r * rank : (r + 1) * rank]
+
+
+def repeated(values, times):
+    count = values.shape[1]
+    spread = one_hot(iota((count, count * times), 1) // times == iota((count, count * times), 0))
+    rows = jnp.broadcast_to(values.astype(F32), (8, count)).astype(BF16)
+    return dot_nn(rows, spread)[0:1].astype(jnp.int32)
+
+
+def by_rows(targets, parents, rhs):
+    shape = (parents * rhs, targets.shape[1] * rhs)
+    row, column = iota(shape, 0), iota(shape, 1)
+    same = (repeated(targets % parents, rhs) == row // rhs) & (row % rhs == column % rhs)
+    return jnp.where(same, 1.0, 0.0)
 
 
 def row_sums(parts):
@@ -111,10 +125,10 @@
     rows = send.shape[0]
     copies = fetch(
         [
+            (parent_of_h, parent_of),
             (charges_h, charges),
             (bases_h, bases),
             (transfers_h, transfers),
-            (parent_of_h, parent_of),
             (far_pairs_h, far_pairs),
             (par_pairs_h, par_pairs),
             (par_pairs_h, par_smem),
@@ -123,20 +137,21 @@
         ],
         sems,
     )
-    for copy in copies[:3]:
+    copies[0].wait()
+    to_parent = by_rows(parent_of[...], parents, rhs).astype(BF16)
+    for copy in copies[1:4]:
         copy.wait()
 
     for l in range(leaves):
         m = dot_nt(charges[l], bases[l]).astype(BF16)
         mo[l * rhs : (l + 1) * rhs, :] = m.astype(F32)
         ch[l * rhs : (l + 1) * rhs, :] = dot_nt(m, transfers[l])
-    for copy in copies[3:]:
+    for copy in copies[4:]:
         copy.wait()
+    high, low = split2(ch[...])
+    pm3[...] = (dot_nn(to_parent, high) + dot_nn(to_parent, low)).astype(BF16).astype(F32)
     m2 = rows_to_lanes(mo, leaves, rhs)
-    high, low = split2(rows_to_lanes(ch, leaves, rhs))
-    par_hot = one_hot(parent_of[...] % parents == iota((parents, leaves), 0))
-    pm = (dot_nn(par_hot, high) + dot_nn(par_hot, low)).astype(BF16).astype(F32)
-    lanes_to_rows(pm3, pm, rhs)
+    pm = rows_to_lanes(pm3, parents, rhs)
     half = 3 * width // 2
     shared = [
         jnp.concatenate([x[:, c * width // 2 : (c + 1) * width // 2] for x in (m2[:parents], m2[parents:], pm)], axis=1)
@@ -254,32 +269,22 @@
     half[...] = far_half(mom, far_pairs, far_c, b_ref, fw, leaves, parents)
 
 
-def repeated(values, times):
-    count = values.shape[1]
-    spread = one_hot(iota((count, count * times), 1) // times == iota((count, count * times), 0))
-    rows = jnp.broadcast_to(values.astype(F32), (8, count)).astype(BF16)
-    return dot_nn(rows, spread)[0:1].astype(jnp.int32)
-
-
-def prepare_kernel(earlier, par_pairs, parent_of, par_c, par_t, pick, to_owner, to_leaf):
+def prepare_kernel(
+    near_own, near_back, par_pairs, parent_of, par_c, near, par_t, pick, to_owner, to_leaf
+):
     pairs = par_c.shape[0]
     rows = pick.shape[1]
     leaves = parent_of.shape[1]
     parents = leaves // 2
     rhs = to_owner.shape[0] // parents
+    near[...] = near_own[...] + near_back[...].astype(F32)
     for s in range(pairs):
         par_t[s] = par_c[s].astype(F32).T.astype(BF16)
     hot = jnp.where(par_pairs[1:2, :] == iota((rows, pairs), 0), 1.0, 0.0)
     pick[...] = hot.T.astype(BF16)
 
-    def by_rows(targets):
-        shape = (parents * rhs, targets.shape[1] * rhs)
-        row, column = iota(shape, 0), iota(shape, 1)
-        same = (repeated(targets % parents, rhs) == row // rhs) & (row % rhs == column % rhs)
-        return jnp.where(same, 1.0, 0.0)
-
-    to_owner[...] = by_rows(par_pairs[0:1, :]).astype(BF16)
-    to_leaf[...] = by_rows(parent_of[...]).T.astype(BF16)
+    to_owner[...] = by_rows(par_pairs[0:1, :], parents, rhs).astype(BF16)
+    to_leaf[...] = by_rows(parent_of[...], parents, rhs).T.astype(BF16)
 
 
 def post_kernel(
@@ -296,8 +301,7 @@
     pick,
     to_owner,
     to_leaf,
-    near_own,
-    near_back,
+    near,
     out,
     b_ref,
     fw,
@@ -341,8 +345,7 @@
     for l in range(leaves):
         at = slice(l * rhs, (l + 1) * rhs)
         mine = (lf[at, :] + dn[at, :]).astype(BF16)
-        near = near_own[l] + near_back[l].astype(F32)
-        out[l] = dot_nn(mine, bases[l]) + near
+        out[l] = dot_nn(mine, bases[l]) + near[l]
 
 
 def after(value, earlier, vmem_limit):
@@ -462,9 +465,10 @@
     )(near_pairs, charges, following, self_blocks, near_blocks)
     near_back = passed_along(near_away, "sfc", 1)
 
-    prepared = pl.pallas_call(
+    near, *prepared = pl.pallas_call(
         prepare_kernel,
-        out_shape=[
+        out_shape=[jax.ShapeDtypeStruct(near_own.shape, F32)]
+        + [
             jax.ShapeDtypeStruct(shape, BF16)
             for shape in (
                 par_coupling.shape,
@@ -473,14 +477,14 @@
                 (leaves * rhs, parents * rhs),
             )
         ],
-        in_specs=[pl.BlockSpec(memory_space=pl.ANY)] + [vmem] * 3,
-        out_specs=[vmem] * 4,
+        in_specs=[vmem] * 5,
+        out_specs=[vmem] * 5,
         compiler_params=late,
         cost_estimate=cost(4_000_000),
         name="prepare",
-    )(near_away, par_pairs, parent_of, par_coupling)
-
-    got = after(got, [near_back, *prepared], 1 << 20)
+    )(near_own, near_back, par_pairs, parent_of, par_coupling)
+
+    got = after(got, [near, *prepared], 1 << 20)
     mom2 = lax.ppermute(
         got[:, 2 * width + LANES :], "sfc", [(i, i ^ 1) for i in range(devices)]
     )
@@ -502,7 +506,7 @@
     return pl.pallas_call(
         post_kernel,
         out_shape=jax.ShapeDtypeStruct((leaves, rhs, panels), F32),
-        in_specs=[smem] + [vmem] * 14,
+        in_specs=[smem] + [vmem] * 13,
         out_specs=vmem,
         scratch_shapes=[
             pltpu.VMEM((width // 2, slots), F32),
@@ -526,8 +530,7 @@
         far_pairs,
         far_c,
         *prepared,
-        near_own,
-        near_back,
+        near,
     )
 
 

time: 34.2 us -> 34.7 us (1.015)
  the two profiles are of different devices: /device:TPU:0 before, /device:TPU:19 now
where the time goes in v17:
time: 34.7 us; the launch traced here: 34.3 us
  starting transfers between devices  15.5 us (45%)
  Pallas kernels  14.1 us (41%)
  waiting for transfers between devices  2.43 us (7%)
  local copies, waits for them, and re-layouts  2.11 us (6%)
    all_to_all x1, starting transfers between devices, on_device(): got = lax.all_to_all(send, 'sfc', split_axis=0, concat_axis=0, tiled=True)  6.08 us
    ppermute x2, starting transfers between devices, passed_along(): lax.ppermute(value, axis, [(source, source + steps) for source in range(l...  6.04 us
    pallas_call x1, Pallas kernels, on_device(): pl.pallas_call(near_kernel, grid=(steps,), out_shape=[jax.ShapeDtypeStruc...  5.14 us
    pallas_call x1, Pallas kernels, on_device(): pl.pallas_call(pre_kernel, out_shape=jax.ShapeDtypeStruct((rows, columns)...  4.33 us
    ppermute x1, starting transfers between devices, on_device(): lax.ppermute(got[:, 2 * width + LANES:], 'sfc', [(i, i ^ 1) for i in rang...  3.35 us
    pallas_call x1, Pallas kernels, on_device(): pl.pallas_call(post_kernel, out_shape=jax.ShapeDtypeStruct((leaves, rhs,...  3.32 us
    ppermute x2, waiting for transfers between devices, passed_along(): lax.ppermute(value, axis, [(source, source + steps) for source in range(l...  2.1 us
    unnamed x22, local copies, waits for them, and re-layouts  2.1 us
  transfers between devices with their start and end apart: 4, of which 2 were waited for; matrix products, arithmetic and copies ran while one was open for 0% of the time, Pallas kernels for 31%

profile of v17, /device:TPU:19, one launch (start us, length us, event | category | flops | bytes accessed | tf_op | source)
XLA Modules:
  0.0 34.3 jit_solution(9365914617221313195)
XLA Ops:
  0.0 0.0 copy-start.4
  0.0 0.0 copy-start.10
  0.0 2.7 %collective-permute-start = (bf16[16,8,256]{2,1,0:T(8,128)(2,1)}, bf16[16,8,256]{2,1,0:T(8,128)(2,1)S(1)}, u32[]{:S(2)}, u32[]{:S(2)}) collective-permute-start(bf16[16,8,256]{2,1,0:T(8,128)(2,1)} %charges.1), channel_id=1, source_target_pairs={{1,0},{2,1},{3,2},{4,3},{5,4},{6,5},{7,6},{8,7},{9,8},{10,9},{11,1... | collective-permute-start | bytes 196616 | tf_op jit(solution)/shard_map/ppermute | solution.py:367
  2.7 4.3 %upward.1.refs_0_ = bf16[128,1920]{1,0:T(8,128)(2,1)} custom-call(bf16[16,8,256]{2,1,0:T(8,128)(2,1)} %charges.1, bf16[16,64,256]{2,1,0:T(8,128)(2,1)} %bases.1, bf16[16,64,64]{2,1,0:T(8,128)(2,1)} %transfers.1, s32[1,16]{1,0:T(1,128)} %bitcast.17, s32[2,128]{1,0:T(2,128)} %bitcast.11, bf16[64,64,128]{2,1,0:T(8,128)(2,1)} %bitcast.8, s32[2,32]{1,0:T(2,128)} %bitcast.15, ...), custom_call_target="tpu_custom_call" | custom-call | flops 40000000 | bytes 10000000 | tf_op jit(solution)/shard_map/upward/pallas_call | solution.py:411
  7.1 0.0 copy-start.1
  7.1 0.0 copy-start.8
  7.1 0.0 collective-permute-done.refs_1_.following
  7.1 6.1 %all-to-all-start = ((bf16[16,8,1920]{2,1,0:T(8,128)(2,1)}), bf16[16,8,1920]{2,1,0:T(8,128)(2,1)S(1)}, u32[]{:S(2)}, u32[]{:S(2)}) async-start(bf16[16,8,1920]{2,1,0:T(8,128)(2,1)} %bitcast.20), calls=%async_computation | async-start | bytes 983040 | tf_op jit(solution)/shard_map/all_to_all | solution.py:439
  13.2 0.0 copy-done.4
  13.2 0.0 copy-done.10
  13.2 0.0 copy-start
  13.2 0.0 copy-start.7
  13.2 0.0 copy-start.2
  13.2 0.0 copy-start.3
  13.2 5.1 %near.1 = (f32[16,8,256]{2,1,0:T(8,128)S(1)}, bf16[16,8,256]{2,1,0:T(8,128)(2,1)S(1)}) custom-call(s32[2,32]{1,0:T(2,128)S(1)} %bitcast.19, bf16[16,8,256]{2,1,0:T(8,128)(2,1)S(1)} %copy-done.4, bf16[16,8,256]{2,1,0:T(8,128)(2,1)S(1)} %collective-permute-done.refs_1_.following, bf16[16,256,256]{2,1,0:T(8,128)(2,1)} %self_blocks.1, ...), custom_call_target="tpu_custom_call" | custom-call | flops 80000000 | bytes 20000000 | tf_op jit(solution)/shard_map/near/pallas_call | solution.py:443
  18.4 3.3 %collective-permute-start.1 = (bf16[16,8,256]{2,1,0:T(8,128)(2,1)S(1)}, bf16[16,8,256]{2,1,0:T(8,128)(2,1)S(1)}, u32[]{:S(2)}, u32[]{:S(2)}) collective-permute-start(bf16[16,8,256]{2,1,0:T(8,128)(2,1)S(1)} %get-tuple-element.15), channel_id=1, source_target_pairs={{0,1},{1,2},{2,3},{3,4},{4,5},{5,6},{6,7},{7,8},{8,9},{9,10},{10,1... | collective-permute-start | bytes 196616 | tf_op jit(solution)/shard_map/ppermute | solution.py:367
  21.7 2.1 %collective-permute-done.1.near_back = bf16[16,8,256]{2,1,0:T(8,128)(2,1)S(1)} collective-permute-done((bf16[16,8,256]{2,1,0:T(8,128)(2,1)S(1)}, bf16[16,8,256]{2,1,0:T(8,128)(2,1)S(1)}, u32[]{:S(2)}, u32[]{:S(2)}) %collective-permute-start.1) | collective-permute-done | bytes 65568 | tf_op jit(solution)/shard_map/ppermute | solution.py:367
  23.8 0.0 copy-done.1
  23.8 0.0 copy-done.8
  23.8 0.0 copy-start.9
  23.8 0.7 %copy-done.9 = s32[16]{0:T(128)S(1)} copy-done((s32[16]{0:T(128)S(1)}, s32[16]{0:T(128)}, u32[]{:S(2)}) %copy-start.9) | copy-done | bytes 88
  24.5 0.2 prepare.1
  24.7 0.0 copy-start.5
  24.7 0.6 %copy-done.5 = bf16[128,64]{1,0:T(8,128)(2,1)} copy-done((bf16[128,64]{1,0:T(8,128)(2,1)}, bf16[128,64]{1,0:T(8,128)(2,1)S(1)}, u32[]{:S(2)}) %copy-start.5) | copy-done | bytes 16408
  25.4 0.3 all-to-all-done
  25.7 0.0 copy-start.6
  25.7 0.8 %copy-done.6 = bf16[128,64]{1,0:T(8,128)(2,1)S(1)} copy-done((bf16[128,64]{1,0:T(8,128)(2,1)S(1)}, bf16[128,64]{1,0:T(8,128)(2,1)}, u32[]{:S(2)}) %copy-start.6) | copy-done | bytes 16408
  26.5 3.3 %collective-permute-start.2 = (bf16[128,768]{1,0:T(8,128)(2,1)S(1)}, bf16[128,768]{1,0:T(8,128)(2,1)S(1)}, u32[]{:S(2)}, u32[]{:S(2)}) collective-permute-start(bf16[128,768]{1,0:T(8,128)(2,1)S(1)} %slice.4), channel_id=1, source_target_pairs={{0,1},{1,0},{2,3},{3,2},{4,5},{5,4},{6,7},{7,6},{8,9},{9,8},{10,11... | collective-permute-start | bytes 589832 | tf_op jit(solution)/shard_map/ppermute | solution.py:488
  29.8 0.0 copy-done
  29.8 0.0 copy-done.7
  29.8 1.1 %far.1 = (f32[16,256]{1,0:T(8,128)S(1)}, f32[16,512]{1,0:T(8,128)S(1)}) custom-call(bf16[128,1920]{1,0:T(8,128)(2,1)S(1)} %after.3.got, s32[2,128]{1,0:T(2,128)S(1)} %bitcast.12, bf16[64,64,128]{2,1,0:T(8,128)(2,1)S(1)} %bitcast.9), custom_call_target="tpu_custom_call" | custom-call | flops 32000000 | bytes 8000000 | tf_op jit(solution)/shard_map/far/pallas_call | solution.py:492
  30.9 0.0 collective-permute-done.2.mom2
  30.9 0.0 copy-done.2
  30.9 0.0 copy-done.3
  30.9 3.3 %downward.1 = f32[16,8,256]{2,1,0:T(8,128)} custom-call(s32[2,128]{1,0:T(2,128)S(1)} %bitcast.13, f32[16,256]{1,0:T(8,128)S(1)} %get-tuple-element.21.half, f32[16,512]{1,0:T(8,128)S(1)} %get-tuple-element.22.back, bf16[128,768]{1,0:T(8,128)(2,1)S(1)} %collective-permute-done.2.mom2, bf16[128,1920]{1,0:T(8,128)(2,1)S(1)} %after.3.got, ...), custom_call_target="tpu_custom_call" | custom-call | tf_op jit(solution)/shard_map/downward/pallas_call | solution.py:506
  (3 shorter events, 0.0 us)
Async XLA Ops:
  0.0 13.2 %copy-start.4 = (bf16[16,8,256]{2,1,0:T(8,128)(2,1)S(1)}, bf16[16,8,256]{2,1,0:T(8,128)(2,1)}, u32[]{:S(2)}) copy-start(bf16[16,8,256]{2,1,0:T(8,128)(2,1)} %charges.1) | copy-start | bytes 196612
  0.0 13.2 %copy-start.10 = (s32[32,2]{0,1:T(2,128)S(1)}, s32[32,2]{0,1:T(2,128)}, u32[]{:S(2)}) copy-start(s32[32,2]{0,1:T(2,128)} %param.14) | copy-start | bytes 772
  0.0 7.1 %collective-permute-start = (bf16[16,8,256]{2,1,0:T(8,128)(2,1)}, bf16[16,8,256]{2,1,0:T(8,128)(2,1)S(1)}, u32[]{:S(2)}, u32[]{:S(2)}) collective-permute-start(bf16[16,8,256]{2,1,0:T(8,128)(2,1)} %charges.1), channel_id=1, source_target_pairs={{1,0},{2,1},{3,2},{4,3},{5,4},{6,5},{7,6},{8,7},{9,8},{10,9},{11,1... | collective-permute-start | bytes 196616 | tf_op jit(solution)/shard_map/ppermute | solution.py:367
  7.1 16.8 %copy-start.1 = (bf16[32,64,64]{2,1,0:T(8,128)(2,1)S(1)}, bf16[32,64,64]{2,1,0:T(8,128)(2,1)}, u32[]{:S(2)}) copy-start(bf16[32,64,64]{2,1,0:T(8,128)(2,1)} %par_c.1) | copy-start | bytes 786436
  7.1 16.8 %copy-start.8 = (s32[32,2]{0,1:T(2,128)S(1)}, s32[32,2]{0,1:T(2,128)}, u32[]{:S(2)}) copy-start(s32[32,2]{0,1:T(2,128)} %param.20) | copy-start | bytes 772
  7.1 18.6 %all-to-all-start = ((bf16[16,8,1920]{2,1,0:T(8,128)(2,1)}), bf16[16,8,1920]{2,1,0:T(8,128)(2,1)S(1)}, u32[]{:S(2)}, u32[]{:S(2)}) async-start(bf16[16,8,1920]{2,1,0:T(8,128)(2,1)} %bitcast.20), calls=%async_computation | async-start | bytes 983040 | tf_op jit(solution)/shard_map/all_to_all | solution.py:439
  13.2 16.6 %copy-start = (bf16[128,64,64]{0,2,1:T(8,128)(2,1)S(1)}, bf16[128,64,64]{0,2,1:T(8,128)(2,1)}, u32[]{:S(2)}) copy-start(bf16[128,64,64]{0,2,1:T(8,128)(2,1)} %param.19) | copy-start | bytes 3145732
  13.2 16.6 %copy-start.7 = (s32[128,2]{0,1:T(2,128)S(1)}, s32[128,2]{0,1:T(2,128)}, u32[]{:S(2)}) copy-start(s32[128,2]{0,1:T(2,128)} %param.18) | copy-start | bytes 3076
  13.2 17.7 %copy-start.2 = (bf16[16,64,256]{2,1,0:T(8,128)(2,1)S(1)}, bf16[16,64,256]{2,1,0:T(8,128)(2,1)}, u32[]{:S(2)}) copy-start(bf16[16,64,256]{2,1,0:T(8,128)(2,1)} %bases.1) | copy-start | bytes 1572868
  13.2 17.7 %copy-start.3 = (bf16[16,64,64]{2,1,0:T(8,128)(2,1)S(1)}, bf16[16,64,64]{2,1,0:T(8,128)(2,1)}, u32[]{:S(2)}) copy-start(bf16[16,64,64]{2,1,0:T(8,128)(2,1)} %transfers.1) | copy-start | bytes 393220
  18.4 5.4 %collective-permute-start.1 = (bf16[16,8,256]{2,1,0:T(8,128)(2,1)S(1)}, bf16[16,8,256]{2,1,0:T(8,128)(2,1)S(1)}, u32[]{:S(2)}, u32[]{:S(2)}) collective-permute-start(bf16[16,8,256]{2,1,0:T(8,128)(2,1)S(1)} %get-tuple-element.15), channel_id=1, source_target_pairs={{0,1},{1,2},{2,3},{3,4},{4,5},{5,6},{6,7},{7,8},{8,9},{9,10},{10,1... | collective-permute-start | bytes 196616 | tf_op jit(solution)/shard_map/ppermute | solution.py:367
  23.8 0.7 %copy-start.9 = (s32[16]{0:T(128)S(1)}, s32[16]{0:T(128)}, u32[]{:S(2)}) copy-start(s32[16]{0:T(128)} %param.17) | copy-start | bytes 196
  24.7 0.6 %copy-start.5 = (bf16[128,64]{1,0:T(8,128)(2,1)}, bf16[128,64]{1,0:T(8,128)(2,1)S(1)}, u32[]{:S(2)}) copy-start(bf16[128,64]{1,0:T(8,128)(2,1)S(1)} %get-tuple-element.20.refs_5_.to_leaf) | copy-start | bytes 49156
  25.7 0.8 %copy-start.6 = (bf16[128,64]{1,0:T(8,128)(2,1)S(1)}, bf16[128,64]{1,0:T(8,128)(2,1)}, u32[]{:S(2)}) copy-start(bf16[128,64]{1,0:T(8,128)(2,1)} %copy-done.5) | copy-start | bytes 49156
  26.5 4.4 %collective-permute-start.2 = (bf16[128,768]{1,0:T(8,128)(2,1)S(1)}, bf16[128,768]{1,0:T(8,128)(2,1)S(1)}, u32[]{:S(2)}, u32[]{:S(2)}) collective-permute-start(bf16[128,768]{1,0:T(8,128)(2,1)S(1)} %slice.4), channel_id=1, source_target_pairs={{0,1},{1,0},{2,3},{3,2},{4,5},{5,4},{6,7},{7,6},{8,9},{9,8},{10,11... | collective-permute-start | bytes 589832 | tf_op jit(solution)/shard_map/ppermute | solution.py:488

commit v18 on v17

--- a/solution.py
+++ b/solution.py
@@ -258,7 +258,22 @@
     return dot_nt(hot, high) + dot_nt(hot, low)
 
 
-def far_kernel(got, far_pairs, far_c, half, back, b_ref, fw):
+def far_kernel(
+    got,
+    far_pairs,
+    far_c,
+    par_pairs,
+    parent_of,
+    par_c,
+    half,
+    back,
+    par_t,
+    pick,
+    to_owner,
+    to_leaf,
+    b_ref,
+    fw,
+):
     leaves, width = back.shape
     parents = leaves // 2
     rows = got.shape[0]
@@ -268,21 +283,12 @@
     mom = got[:, 2 * width + LANES :]
     half[...] = far_half(mom, far_pairs, far_c, b_ref, fw, leaves, parents)
 
-
-def prepare_kernel(
-    near_own, near_back, par_pairs, parent_of, par_c, near, par_t, pick, to_owner, to_leaf
-):
     pairs = par_c.shape[0]
-    rows = pick.shape[1]
-    leaves = parent_of.shape[1]
-    parents = leaves // 2
     rhs = to_owner.shape[0] // parents
-    near[...] = near_own[...] + near_back[...].astype(F32)
     for s in range(pairs):
         par_t[s] = par_c[s].astype(F32).T.astype(BF16)
     hot = jnp.where(par_pairs[1:2, :] == iota((rows, pairs), 0), 1.0, 0.0)
     pick[...] = hot.T.astype(BF16)
-
     to_owner[...] = by_rows(par_pairs[0:1, :], parents, rhs).astype(BF16)
     to_leaf[...] = by_rows(parent_of[...], parents, rhs).T.astype(BF16)
 
@@ -301,7 +307,8 @@
     pick,
     to_owner,
     to_leaf,
-    near,
+    near_own,
+    near_back,
     out,
     b_ref,
     fw,
@@ -345,7 +352,8 @@
     for l in range(leaves):
         at = slice(l * rhs, (l + 1) * rhs)
         mine = (lf[at, :] + dn[at, :]).astype(BF16)
-        out[l] = dot_nn(mine, bases[l]) + near[l]
+        near = near_own[l] + near_back[l].astype(F32)
+        out[l] = dot_nn(mine, bases[l]) + near
 
 
 def after(value, earlier, vmem_limit):
@@ -393,7 +401,7 @@
     smem = pl.BlockSpec(memory_space=pltpu.SMEM)
     hbm = pl.BlockSpec(memory_space=pltpu.HBM)
     params = pltpu.CompilerParams(vmem_limit_bytes=60 * 1024 * 1024)
-    late = pltpu.CompilerParams(vmem_limit_bytes=32 * 1024 * 1024)
+    late = pltpu.CompilerParams(vmem_limit_bytes=48 * 1024 * 1024)
 
     def cost(moved):
         return pl.CostEstimate(flops=4 * moved, bytes_accessed=moved, transcendentals=0)
@@ -465,48 +473,33 @@
     )(near_pairs, charges, following, self_blocks, near_blocks)
     near_back = passed_along(near_away, "sfc", 1)
 
-    near, *prepared = pl.pallas_call(
-        prepare_kernel,
-        out_shape=[jax.ShapeDtypeStruct(near_own.shape, F32)]
-        + [
-            jax.ShapeDtypeStruct(shape, BF16)
-            for shape in (
-                par_coupling.shape,
-                (pairs, rows),
-                (parents * rhs, pairs * rhs),
-                (leaves * rhs, parents * rhs),
-            )
-        ],
-        in_specs=[vmem] * 5,
-        out_specs=[vmem] * 5,
-        compiler_params=late,
-        cost_estimate=cost(4_000_000),
-        name="prepare",
-    )(near_own, near_back, par_pairs, parent_of, par_coupling)
-
-    got = after(got, [near, *prepared], 1 << 20)
+    got = after(got, [near_back], 1 << 20)
     mom2 = lax.ppermute(
         got[:, 2 * width + LANES :], "sfc", [(i, i ^ 1) for i in range(devices)]
     )
 
-    half, back = pl.pallas_call(
+    half, back, *prepared = pl.pallas_call(
         far_kernel,
         out_shape=[
             jax.ShapeDtypeStruct((leaves, width // 2), F32),
             jax.ShapeDtypeStruct((leaves, width), F32),
-        ],
-        in_specs=[vmem] * 3,
-        out_specs=[vmem] * 2,
+            jax.ShapeDtypeStruct(par_coupling.shape, BF16),
+            jax.ShapeDtypeStruct((pairs, rows), BF16),
+            jax.ShapeDtypeStruct((parents * rhs, pairs * rhs), BF16),
+            jax.ShapeDtypeStruct((leaves * rhs, parents * rhs), BF16),
+        ],
+        in_specs=[vmem] * 6,
+        out_specs=[vmem] * 6,
         scratch_shapes=[pltpu.VMEM((width // 2, slots), F32)] * 2,
         compiler_params=late,
         cost_estimate=cost(8_000_000),
         name="far",
-    )(got, far_pairs, far_c)
+    )(got, far_pairs, far_c, par_pairs, parent_of, par_coupling)
 
     return pl.pallas_call(
         post_kernel,
         out_shape=jax.ShapeDtypeStruct((leaves, rhs, panels), F32),
-        in_specs=[smem] + [vmem] * 13,
+        in_specs=[smem] + [vmem] * 14,
         out_specs=vmem,
         scratch_shapes=[
             pltpu.VMEM((width // 2, slots), F32),
@@ -530,7 +523,8 @@
         far_pairs,
         far_c,
         *prepared,
-        near,
+        near_own,
+        near_back,
     )
 
 

time: 34.7 us -> 33.1 us (0.954)
  the two profiles are of different devices: /device:TPU:19 before, /device:TPU:0 now
where the time goes in v18:
time: 33.1 us; the launch traced here: 32.7 us
  Pallas kernels  13.9 us (42%)
  starting transfers between devices  12.2 us (37%)
  waiting for transfers between devices  6.4 us (19%)
    all_to_all x1, starting transfers between devices, on_device(): got = lax.all_to_all(send, 'sfc', split_axis=0, concat_axis=0, tiled=True)  8.26 us
    all_to_all x1, waiting for transfers between devices, on_device(): got = lax.all_to_all(send, 'sfc', split_axis=0, concat_axis=0, tiled=True)  5.44 us
    pallas_call x1, Pallas kernels, on_device(): pl.pallas_call(near_kernel, grid=(steps,), out_shape=[jax.ShapeDtypeStruc...  5.08 us
    pallas_call x1, Pallas kernels, on_device(): pl.pallas_call(pre_kernel, out_shape=jax.ShapeDtypeStruct((rows, columns)...  4.32 us
    ppermute x2, starting transfers between devices, passed_along(): lax.ppermute(value, axis, [(source, source + steps) for source in range(l...  3.73 us
    pallas_call x1, Pallas kernels, on_device(): pl.pallas_call(post_kernel, out_shape=jax.ShapeDtypeStruct((leaves, rhs,...  3.32 us
    pallas_call x1, Pallas kernels, on_device(): pl.pallas_call(far_kernel, out_shape=[jax.ShapeDtypeStruct((leaves, width...  1.22 us
    ppermute x2, waiting for transfers between devices, passed_along(): lax.ppermute(value, axis, [(source, source + steps) for source in range(l...  0.88 us
  transfers between devices with their start and end apart: 4, of which 3 were waited for; matrix products, arithmetic and copies ran while one was open for 0% of the time, Pallas kernels for 32%

profile of v18, /device:TPU:0, one launch (start us, length us, event | category | flops | bytes accessed | tf_op | source)
XLA Modules:
  0.0 32.7 jit_solution(13091463495165001779)
XLA Ops:
  0.0 0.0 copy-start.4
  0.0 0.0 copy-start.8
  0.0 1.4 %collective-permute-start = (bf16[16,8,256]{2,1,0:T(8,128)(2,1)}, bf16[16,8,256]{2,1,0:T(8,128)(2,1)S(1)}, u32[]{:S(2)}, u32[]{:S(2)}) collective-permute-start(bf16[16,8,256]{2,1,0:T(8,128)(2,1)} %charges.1), channel_id=1, source_target_pairs={{1,0},{2,1},{3,2},{4,3},{5,4},{6,5},{7,6},{8,7},{9,8},{10,9},{11,1... | collective-permute-start | bytes 196616 | tf_op jit(solution)/shard_map/ppermute | solution.py:375
  1.4 4.3 %upward.1.refs_0_ = bf16[128,1920]{1,0:T(8,128)(2,1)} custom-call(bf16[16,8,256]{2,1,0:T(8,128)(2,1)} %charges.1, bf16[16,64,256]{2,1,0:T(8,128)(2,1)} %bases.1, bf16[16,64,64]{2,1,0:T(8,128)(2,1)} %transfers.1, s32[1,16]{1,0:T(1,128)} %bitcast.17, s32[2,128]{1,0:T(2,128)} %bitcast.11, bf16[64,64,128]{2,1,0:T(8,128)(2,1)} %bitcast.8, s32[2,32]{1,0:T(2,128)} %bitcast.15, ...), custom_call_target="tpu_custom_call" | custom-call | flops 40000000 | bytes 10000000 | tf_op jit(solution)/shard_map/upward/pallas_call | solution.py:419
  5.8 0.0 collective-permute-done.refs_1_.following
  5.8 0.0 copy-start
  5.8 0.0 copy-start.1
  5.8 0.0 copy-start.5
  5.8 0.0 copy-start.6
  5.8 0.0 copy-start.7
  5.8 8.3 %all-to-all-start = ((bf16[16,8,1920]{2,1,0:T(8,128)(2,1)}), bf16[16,8,1920]{2,1,0:T(8,128)(2,1)S(1)}, u32[]{:S(2)}, u32[]{:S(2)}) async-start(bf16[16,8,1920]{2,1,0:T(8,128)(2,1)} %bitcast.20), calls=%async_computation | async-start | bytes 983040 | tf_op jit(solution)/shard_map/all_to_all | solution.py:447
  14.1 0.0 copy-done.4
  14.1 0.0 copy-done.8
  14.1 0.0 copy-start.2
  14.1 0.0 copy-start.3
  14.2 5.1 %near.1 = (f32[16,8,256]{2,1,0:T(8,128)S(1)}, bf16[16,8,256]{2,1,0:T(8,128)(2,1)S(1)}) custom-call(s32[2,32]{1,0:T(2,128)S(1)} %bitcast.19, bf16[16,8,256]{2,1,0:T(8,128)(2,1)S(1)} %copy-done.4, bf16[16,8,256]{2,1,0:T(8,128)(2,1)S(1)} %collective-permute-done.refs_1_.following, bf16[16,256,256]{2,1,0:T(8,128)(2,1)} %self_blocks.1, ...), custom_call_target="tpu_custom_call" | custom-call | flops 80000000 | bytes 20000000 | tf_op jit(solution)/shard_map/near/pallas_call | solution.py:451
  19.2 2.3 %collective-permute-start.1 = (bf16[16,8,256]{2,1,0:T(8,128)(2,1)S(1)}, bf16[16,8,256]{2,1,0:T(8,128)(2,1)S(1)}, u32[]{:S(2)}, u32[]{:S(2)}) collective-permute-start(bf16[16,8,256]{2,1,0:T(8,128)(2,1)S(1)} %get-tuple-element.13), channel_id=1, source_target_pairs={{0,1},{1,2},{2,3},{3,4},{4,5},{5,6},{6,7},{7,8},{8,9},{9,10},{10,1... | collective-permute-start | bytes 196616 | tf_op jit(solution)/shard_map/ppermute | solution.py:375
  21.6 0.9 %collective-permute-done.1.refs_1_.near_back = bf16[16,8,256]{2,1,0:T(8,128)(2,1)S(1)} collective-permute-done((bf16[16,8,256]{2,1,0:T(8,128)(2,1)S(1)}, bf16[16,8,256]{2,1,0:T(8,128)(2,1)S(1)}, u32[]{:S(2)}, u32[]{:S(2)}) %collective-permute-start.1) | collective-permute-done | bytes 65568 | tf_op jit(solution)/shard_map/ppermute | solution.py:375
  22.4 5.4 %all-to-all-done = bf16[16,8,1920]{2,1,0:T(8,128)(2,1)S(1)} async-done(((bf16[16,8,1920]{2,1,0:T(8,128)(2,1)}), bf16[16,8,1920]{2,1,0:T(8,128)(2,1)S(1)}, u32[]{:S(2)}, u32[]{:S(2)}) %all-to-all-start) | async-done | bytes 491552 | tf_op jit(solution)/shard_map/all_to_all | solution.py:447
  27.9 0.2 collective-permute-start.2
  28.1 0.0 copy-done
  28.1 0.0 copy-done.1
  28.1 0.0 copy-done.5
  28.1 0.0 copy-done.6
  28.1 0.0 copy-done.7
  28.1 1.2 %far.1 = (f32[16,256]{1,0:T(8,128)S(1)}, f32[16,512]{1,0:T(8,128)S(1)}, bf16[32,64,64]{2,1,0:T(8,128)(2,1)S(1)}, bf16[32,128]{1,0:T(8,128)(2,1)S(1)}, bf16[64,25...) custom-call(bf16[128,1920]{1,0:T(8,128)(2,1)S(1)} %after.3.got, s32[2,128]{1,0:T(2,128)S(1)} %bitcast.12, ...), custom_call_target="tpu_custom_call" | custom-call | flops 32000000 | bytes 8000000 | tf_op jit(solution)/shard_map/far/pallas_call | solution.py:481
  29.3 0.1 collective-permute-done.2.mom2
  29.4 0.0 copy-done.2
  29.4 0.0 copy-done.3
  29.4 3.3 %downward.1 = f32[16,8,256]{2,1,0:T(8,128)} custom-call(s32[2,128]{1,0:T(2,128)S(1)} %bitcast.13, f32[16,256]{1,0:T(8,128)S(1)} %get-tuple-element.14.half, f32[16,512]{1,0:T(8,128)S(1)} %get-tuple-element.15.back, bf16[128,768]{1,0:T(8,128)(2,1)S(1)} %collective-permute-done.2.mom2, bf16[128,1920]{1,0:T(8,128)(2,1)S(1)} %after.3.got, ...), custom_call_target="tpu_custom_call" | custom-call | tf_op jit(solution)/shard_map/downward/pallas_call | solution.py:499
  (3 shorter events, 0.0 us)
Async XLA Ops:
  0.0 14.1 %copy-start.4 = (bf16[16,8,256]{2,1,0:T(8,128)(2,1)S(1)}, bf16[16,8,256]{2,1,0:T(8,128)(2,1)}, u32[]{:S(2)}) copy-start(bf16[16,8,256]{2,1,0:T(8,128)(2,1)} %charges.1) | copy-start | bytes 196612
  0.0 14.1 %copy-start.8 = (s32[32,2]{0,1:T(2,128)S(1)}, s32[32,2]{0,1:T(2,128)}, u32[]{:S(2)}) copy-start(s32[32,2]{0,1:T(2,128)} %param.14) | copy-start | bytes 772
  0.0 5.8 %collective-permute-start = (bf16[16,8,256]{2,1,0:T(8,128)(2,1)}, bf16[16,8,256]{2,1,0:T(8,128)(2,1)S(1)}, u32[]{:S(2)}, u32[]{:S(2)}) collective-permute-start(bf16[16,8,256]{2,1,0:T(8,128)(2,1)} %charges.1), channel_id=1, source_target_pairs={{1,0},{2,1},{3,2},{4,3},{5,4},{6,5},{7,6},{8,7},{9,8},{10,9},{11,1... | collective-permute-start | bytes 196616 | tf_op jit(solution)/shard_map/ppermute | solution.py:375
  5.8 22.3 %copy-start = (bf16[128,64,64]{0,2,1:T(8,128)(2,1)S(1)}, bf16[128,64,64]{0,2,1:T(8,128)(2,1)}, u32[]{:S(2)}) copy-start(bf16[128,64,64]{0,2,1:T(8,128)(2,1)} %param.19) | copy-start | bytes 3145732
  5.8 22.3 %copy-start.1 = (bf16[32,64,64]{2,1,0:T(8,128)(2,1)S(1)}, bf16[32,64,64]{2,1,0:T(8,128)(2,1)}, u32[]{:S(2)}) copy-start(bf16[32,64,64]{2,1,0:T(8,128)(2,1)} %par_c.1) | copy-start | bytes 786436
  5.8 22.3 %copy-start.5 = (s32[128,2]{0,1:T(2,128)S(1)}, s32[128,2]{0,1:T(2,128)}, u32[]{:S(2)}) copy-start(s32[128,2]{0,1:T(2,128)} %param.18) | copy-start | bytes 3076
  5.8 22.3 %copy-start.6 = (s32[32,2]{0,1:T(2,128)S(1)}, s32[32,2]{0,1:T(2,128)}, u32[]{:S(2)}) copy-start(s32[32,2]{0,1:T(2,128)} %param.20) | copy-start | bytes 772
  5.8 22.3 %copy-start.7 = (s32[16]{0:T(128)S(1)}, s32[16]{0:T(128)}, u32[]{:S(2)}) copy-start(s32[16]{0:T(128)} %param.17) | copy-start | bytes 196
  5.8 22.0 %all-to-all-start = ((bf16[16,8,1920]{2,1,0:T(8,128)(2,1)}), bf16[16,8,1920]{2,1,0:T(8,128)(2,1)S(1)}, u32[]{:S(2)}, u32[]{:S(2)}) async-start(bf16[16,8,1920]{2,1,0:T(8,128)(2,1)} %bitcast.20), calls=%async_computation | async-start | bytes 983040 | tf_op jit(solution)/shard_map/all_to_all | solution.py:447
  14.1 15.3 %copy-start.2 = (bf16[16,64,256]{2,1,0:T(8,128)(2,1)S(1)}, bf16[16,64,256]{2,1,0:T(8,128)(2,1)}, u32[]{:S(2)}) copy-start(bf16[16,64,256]{2,1,0:T(8,128)(2,1)} %bases.1) | copy-start | bytes 1572868
  14.1 15.3 %copy-start.3 = (bf16[16,64,64]{2,1,0:T(8,128)(2,1)S(1)}, bf16[16,64,64]{2,1,0:T(8,128)(2,1)}, u32[]{:S(2)}) copy-start(bf16[16,64,64]{2,1,0:T(8,128)(2,1)} %transfers.1) | copy-start | bytes 393220
  19.2 3.2 %collective-permute-start.1 = (bf16[16,8,256]{2,1,0:T(8,128)(2,1)S(1)}, bf16[16,8,256]{2,1,0:T(8,128)(2,1)S(1)}, u32[]{:S(2)}, u32[]{:S(2)}) collective-permute-start(bf16[16,8,256]{2,1,0:T(8,128)(2,1)S(1)} %get-tuple-element.13), channel_id=1, source_target_pairs={{0,1},{1,2},{2,3},{3,4},{4,5},{5,6},{6,7},{7,8},{8,9},{9,10},{10,1... | collective-permute-start | bytes 196616 | tf_op jit(solution)/shard_map/ppermute | solution.py:375
  27.9 1.5 %collective-permute-start.2 = (bf16[128,768]{1,0:T(8,128)(2,1)S(1)}, bf16[128,768]{1,0:T(8,128)(2,1)S(1)}, u32[]{:S(2)}, u32[]{:S(2)}) collective-permute-start(bf16[128,768]{1,0:T(8,128)(2,1)S(1)} %slice.4), channel_id=1, source_target_pairs={{0,1},{1,0},{2,3},{3,2},{4,5},{5,4},{6,7},{7,6},{8,9},{9,8},{10,11... | collective-permute-start | bytes 589832 | tf_op jit(solution)/shard_map/ppermute | solution.py:477

commit v19 on v18

--- a/solution.py
+++ b/solution.py
@@ -164,14 +164,18 @@
 
     owner_hot = one_hot(far_pairs[0:1, :] % leaves == iota((leaves, slots), 0))
     a_ref[...] = dot_tn(m2.astype(BF16), owner_hot)
-    for s in range(pairs):
-        q = par_smem[0, s] % parents
-        x = pm3[pl.ds(pl.multiple_of(q * rhs, rhs), rhs), :].astype(BF16)
-        pb[s * rhs : (s + 1) * rhs, :] = dot_nn(x, par_c[s])
+    def parent_products(first, last):
+        for s in range(first, last):
+            q = par_smem[0, s] % parents
+            x = pm3[pl.ds(pl.multiple_of(q * rhs, rhs), rhs), :].astype(BF16)
+            pb[s * rhs : (s + 1) * rhs, :] = dot_nn(x, par_c[s])
+
     some = rank // 4
+    parent_products(0, pairs // 4)
     for sb in range(slots // LANES):
         lanes = slice(sb * LANES, (sb + 1) * LANES)
-        for first in range(0, rank, some):
+        for part in range(4):
+            first = part * some
             acc = [None] * rhs
             for k in range(rank):
                 c = far_c[k, first : first + some, lanes].astype(F32)
@@ -181,6 +185,14 @@
             for r in range(rhs):
                 at = r * rank + first
                 ob[at : at + some, lanes] = acc[r].astype(BF16)
+            if sb == 0 and part < 2:
+                parent_products(pairs // 4 * (part + 1), pairs // 4 * (part + 2))
+            if sb == 0 and part == 2:
+                parent_products(pairs // 4 * 3, pairs)
+                high, low = split2(rows_to_lanes(pb, pairs, rhs))
+                hot = one_hot(par_pairs[1:2, :] == iota((rows, pairs), 0))
+                at = width + LANES
+                send[:, at : at + width] = (dot_nn(hot, high) + dot_nn(hot, low)).astype(BF16)
     partner = far_pairs[1:2, :]
     local = jnp.where(partner >= 0, partner % leaves, -1).astype(F32)
     ob[width : width + LANES, :] = jnp.broadcast_to(local, (LANES, slots)).astype(BF16)
@@ -188,11 +200,6 @@
     for sb in range(slots // LANES):
         lanes = slice(sb * LANES, (sb + 1) * LANES)
         send[lanes, 0 : width + LANES] = dot_nt(unit, ob[:, lanes]).astype(BF16)
-
-    high, low = split2(rows_to_lanes(pb, pairs, rhs))
-    hot = one_hot(par_pairs[1:2, :] == iota((rows, pairs), 0))
-    at = width + LANES
-    send[:, at : at + width] = (dot_nn(hot, high) + dot_nn(hot, low)).astype(BF16)
 
 
 def near_kernel(pairs, charges, following, self_blocks, near_blocks, own, away, ext, out):
@@ -222,11 +229,9 @@
         away[...] = out[leaves:].astype(BF16)
 
 
-def far_half(mom, far_pairs, far_c, b_ref, fw, leaves, parents):
-    rows, slots = mom.shape[0], far_c.shape[2]
-    rank = far_c.shape[0]
+def far_gather(mom, far_pairs, b_ref, leaves, parents):
+    rows, slots = mom.shape[0], b_ref.shape[1]
     wide = mom.shape[1] // 3
-    some = wide // rank
     row_id = iota((rows, slots), 0)
     base_leaf = row_id // parents * leaves + row_id % parents
     partner = far_pairs[1:2, :]
@@ -237,23 +242,30 @@
         total = part if total is None else total + part
     b_ref[...] = total
 
-    for sb in range(slots // LANES):
+
+def far_chunks(far_c, b_ref, fw):
+    rank, slots = far_c.shape[0], far_c.shape[2]
+    some = b_ref.shape[0] // rank
+
+    def chunk(sb, k8):
         lanes = slice(sb * LANES, (sb + 1) * LANES)
-
-        def body(k8, carry):
-            parts = [[] for _ in range(some)]
-            for i in range(8):
-                c = far_c[k8 * 8 + i, :, lanes].astype(F32)
-                for r in range(some):
-                    prod = c * b_ref[r * rank : (r + 1) * rank, lanes]
-                    parts[r].append(sum(prod[j * 8 : (j + 1) * 8] for j in range(rank // 8)))
+        parts = [[] for _ in range(some)]
+        for i in range(8):
+            c = far_c[k8 * 8 + i, :, lanes].astype(F32)
             for r in range(some):
-                fw[pl.ds(pl.multiple_of(r * rank + k8 * 8, 8), 8), lanes] = row_sums(parts[r])
-            return carry
-
-        lax.fori_loop(0, rank // 8, body, 0, unroll=8)
-
-    hot = one_hot(far_pairs[0:1, :] % leaves == iota((leaves, slots), 0))
+                prod = c * b_ref[r * rank : (r + 1) * rank, lanes]
+                parts[r].append(sum(prod[j * 8 : (j + 1) * 8] for j in range(rank // 8)))
+        for r in range(some):
+            first = r * rank + k8 * 8
+            fw[first : first + 8, lanes] = row_sums(parts[r])
+
+    return [
+        functools.partial(chunk, sb, k8) for sb in range(slots // LANES) for k8 in range(rank // 8)
+    ]
+
+
+def far_scatter(far_pairs, fw, leaves):
+    hot = one_hot(far_pairs[0:1, :] % leaves == iota((leaves, fw.shape[1]), 0))
     high, low = split2(fw[...])
     return dot_nt(hot, high) + dot_nt(hot, low)
 
@@ -281,7 +293,10 @@
     hot = one_hot(index == iota((rows, leaves), 1))
     back[...] = dot_tn(hot, got[:, 0:width])
     mom = got[:, 2 * width + LANES :]
-    half[...] = far_half(mom, far_pairs, far_c, b_ref, fw, leaves, parents)
+    far_gather(mom, far_pairs, b_ref, leaves, parents)
+    for chunk in far_chunks(far_c, b_ref, fw):
+        chunk()
+    half[...] = far_scatter(far_pairs, fw, leaves)
 
     pairs = par_c.shape[0]
     rhs = to_owner.shape[0] // parents
@@ -337,17 +352,25 @@
     at = width + LANES
     lanes_to_rows(pb, dot_nn(fold, got[:, at : at + width]), rhs)
     lanes_to_rows(g_ref, dot_nn(pick[...], shared), rhs)
+    far_gather(mom2[...], far_pairs, b_ref, leaves, parents)
+    chunks = far_chunks(far_c, b_ref, fw)
+    each = -(-len(chunks) // 8)
     for s in range(pairs):
         at = slice(s * rhs, (s + 1) * rhs)
         pf[at, :] = dot_nn(g_ref[at, :].astype(BF16), par_t[s])
+        if s % 4 == 3:
+            for chunk in chunks[s // 4 * each : (s // 4 + 1) * each]:
+                chunk()
+    for chunk in chunks[pairs // 4 * each :]:
+        chunk()
     high, low = split2(pf[...])
     locals_p = dot_nn(to_owner[...], high) + dot_nn(to_owner[...], low) + pb[...]
-    picked = dot_nn(to_leaf[...], locals_p.astype(BF16)).astype(BF16)
+    picked = dot_nn(to_leaf[...], locals_p.astype(BF16))
     for l in range(leaves):
         at = slice(l * rhs, (l + 1) * rhs)
-        dn[at, :] = dot_nn(picked[at, :], transfers[l])
-
-    other = far_half(mom2[...], far_pairs, far_c, b_ref, fw, leaves, parents)
+        dn[at, :] = dot_nn(picked[at, :].astype(BF16), transfers[l])
+
+    other = far_scatter(far_pairs, fw, leaves)
     lanes_to_rows(lf, back[...] + in_order(half[...], other), rhs)
     for l in range(leaves):
         at = slice(l * rhs, (l + 1) * rhs)

time: 33.1 us -> 32.6 us (0.985)
  Pallas kernels: 13.9 us -> 13.5 us
    pallas_call x1, Pallas kernels: 3.32 us -> 2.86 us  [on_device(): pl.pallas_call(post_kernel, out_shape=jax.ShapeDtypeStruct((leaves, rhs,...]
  transfers between devices with their start and end apart: 4 -> 4, of which waited for: 3 -> 3; matrix products, arithmetic and copies ran while one was open for 0% -> 0% of each run, Pallas kernels for 32% -> 33%
where the time goes in v19:
time: 32.6 us; the launch traced here: 32.2 us
  Pallas kernels  13.5 us (41%)
  starting transfers between devices  12.2 us (37%)
  waiting for transfers between devices  6.4 us (20%)
    all_to_all x1, starting transfers between devices, on_device(): got = lax.all_to_all(send, 'sfc', split_axis=0, concat_axis=0, tiled=True)  8.26 us
    all_to_all x1, waiting for transfers between devices, on_device(): got = lax.all_to_all(send, 'sfc', split_axis=0, concat_axis=0, tiled=True)  5.44 us
    pallas_call x1, Pallas kernels, on_device(): pl.pallas_call(near_kernel, grid=(steps,), out_shape=[jax.ShapeDtypeStruc...  5.08 us
    pallas_call x1, Pallas kernels, on_device(): pl.pallas_call(pre_kernel, out_shape=jax.ShapeDtypeStruct((rows, columns)...  4.29 us
    ppermute x2, starting transfers between devices, passed_along(): lax.ppermute(value, axis, [(source, source + steps) for source in range(l...  3.72 us
    pallas_call x1, Pallas kernels, on_device(): pl.pallas_call(post_kernel, out_shape=jax.ShapeDtypeStruct((leaves, rhs,...  2.86 us
    pallas_call x1, Pallas kernels, on_device(): pl.pallas_call(far_kernel, out_shape=[jax.ShapeDtypeStruct((leaves, width...  1.22 us
    ppermute x2, waiting for transfers between devices, passed_along(): lax.ppermute(value, axis, [(source, source + steps) for source in range(l...  0.88 us
  transfers between devices with their start and end apart: 4, of which 3 were waited for; matrix products, arithmetic and copies ran while one was open for 0% of the time, Pallas kernels for 33%

profile of v19, /device:TPU:0, one launch (start us, length us, event | category | flops | bytes accessed | tf_op | source)
XLA Modules:
  0.0 32.2 jit_solution(2995376165850574087)
XLA Ops:
  0.0 0.0 copy-start.4
  0.0 0.0 copy-start.8
  0.0 1.4 %collective-permute-start = (bf16[16,8,256]{2,1,0:T(8,128)(2,1)}, bf16[16,8,256]{2,1,0:T(8,128)(2,1)S(1)}, u32[]{:S(2)}, u32[]{:S(2)}) collective-permute-start(bf16[16,8,256]{2,1,0:T(8,128)(2,1)} %charges.1), channel_id=1, source_target_pairs={{1,0},{2,1},{3,2},{4,3},{5,4},{6,5},{7,6},{8,7},{9,8},{10,9},{11,1... | collective-permute-start | bytes 196616 | tf_op jit(solution)/shard_map/ppermute | solution.py:398
  1.4 4.3 %upward.1.refs_0_ = bf16[128,1920]{1,0:T(8,128)(2,1)} custom-call(bf16[16,8,256]{2,1,0:T(8,128)(2,1)} %charges.1, bf16[16,64,256]{2,1,0:T(8,128)(2,1)} %bases.1, bf16[16,64,64]{2,1,0:T(8,128)(2,1)} %transfers.1, s32[1,16]{1,0:T(1,128)} %bitcast.17, s32[2,128]{1,0:T(2,128)} %bitcast.11, bf16[64,64,128]{2,1,0:T(8,128)(2,1)} %bitcast.8, s32[2,32]{1,0:T(2,128)} %bitcast.15, ...), custom_call_target="tpu_custom_call" | custom-call | flops 40000000 | bytes 10000000 | tf_op jit(solution)/shard_map/upward/pallas_call | solution.py:442
  5.7 0.0 collective-permute-done.refs_1_.following
  5.7 0.0 copy-start
  5.8 0.0 copy-start.1
  5.8 0.0 copy-start.5
  5.8 0.0 copy-start.6
  5.8 0.0 copy-start.7
  5.8 8.3 %all-to-all-start = ((bf16[16,8,1920]{2,1,0:T(8,128)(2,1)}), bf16[16,8,1920]{2,1,0:T(8,128)(2,1)S(1)}, u32[]{:S(2)}, u32[]{:S(2)}) async-start(bf16[16,8,1920]{2,1,0:T(8,128)(2,1)} %bitcast.20), calls=%async_computation | async-start | bytes 983040 | tf_op jit(solution)/shard_map/all_to_all | solution.py:470
  14.1 0.0 copy-done.4
  14.1 0.0 copy-done.8
  14.1 0.0 copy-start.2
  14.1 0.0 copy-start.3
  14.1 5.1 %near.1 = (f32[16,8,256]{2,1,0:T(8,128)S(1)}, bf16[16,8,256]{2,1,0:T(8,128)(2,1)S(1)}) custom-call(s32[2,32]{1,0:T(2,128)S(1)} %bitcast.19, bf16[16,8,256]{2,1,0:T(8,128)(2,1)S(1)} %copy-done.4, bf16[16,8,256]{2,1,0:T(8,128)(2,1)S(1)} %collective-permute-done.refs_1_.following, bf16[16,256,256]{2,1,0:T(8,128)(2,1)} %self_blocks.1, ...), custom_call_target="tpu_custom_call" | custom-call | flops 80000000 | bytes 20000000 | tf_op jit(solution)/shard_map/near/pallas_call | solution.py:474
  19.2 2.3 %collective-permute-start.1 = (bf16[16,8,256]{2,1,0:T(8,128)(2,1)S(1)}, bf16[16,8,256]{2,1,0:T(8,128)(2,1)S(1)}, u32[]{:S(2)}, u32[]{:S(2)}) collective-permute-start(bf16[16,8,256]{2,1,0:T(8,128)(2,1)S(1)} %get-tuple-element.13), channel_id=1, source_target_pairs={{0,1},{1,2},{2,3},{3,4},{4,5},{5,6},{6,7},{7,8},{8,9},{9,10},{10,1... | collective-permute-start | bytes 196616 | tf_op jit(solution)/shard_map/ppermute | solution.py:398
  21.5 0.9 %collective-permute-done.1.refs_1_.near_back = bf16[16,8,256]{2,1,0:T(8,128)(2,1)S(1)} collective-permute-done((bf16[16,8,256]{2,1,0:T(8,128)(2,1)S(1)}, bf16[16,8,256]{2,1,0:T(8,128)(2,1)S(1)}, u32[]{:S(2)}, u32[]{:S(2)}) %collective-permute-start.1) | collective-permute-done | bytes 65568 | tf_op jit(solution)/shard_map/ppermute | solution.py:398
  22.4 5.4 %all-to-all-done = bf16[16,8,1920]{2,1,0:T(8,128)(2,1)S(1)} async-done(((bf16[16,8,1920]{2,1,0:T(8,128)(2,1)}), bf16[16,8,1920]{2,1,0:T(8,128)(2,1)S(1)}, u32[]{:S(2)}, u32[]{:S(2)}) %all-to-all-start) | async-done | bytes 491552 | tf_op jit(solution)/shard_map/all_to_all | solution.py:470
  27.9 0.2 collective-permute-start.2
  28.0 0.0 copy-done
  28.1 0.0 copy-done.1
  28.1 0.0 copy-done.5
  28.1 0.0 copy-done.6
  28.1 0.0 copy-done.7
  28.1 1.2 %far.1 = (f32[16,256]{1,0:T(8,128)S(1)}, f32[16,512]{1,0:T(8,128)S(1)}, bf16[32,64,64]{2,1,0:T(8,128)(2,1)S(1)}, bf16[32,128]{1,0:T(8,128)(2,1)S(1)}, bf16[64,25...) custom-call(bf16[128,1920]{1,0:T(8,128)(2,1)S(1)} %after.3.got, s32[2,128]{1,0:T(2,128)S(1)} %bitcast.12, ...), custom_call_target="tpu_custom_call" | custom-call | flops 32000000 | bytes 8000000 | tf_op jit(solution)/shard_map/far/pallas_call | solution.py:504
  29.3 0.1 collective-permute-done.2.mom2
  29.4 0.0 copy-done.2
  29.4 0.0 copy-done.3
  29.4 2.9 %downward.1 = f32[16,8,256]{2,1,0:T(8,128)} custom-call(s32[2,128]{1,0:T(2,128)S(1)} %bitcast.13, f32[16,256]{1,0:T(8,128)S(1)} %get-tuple-element.14.half, f32[16,512]{1,0:T(8,128)S(1)} %get-tuple-element.15.back, bf16[128,768]{1,0:T(8,128)(2,1)S(1)} %collective-permute-done.2.mom2, bf16[128,1920]{1,0:T(8,128)(2,1)S(1)} %after.3.got, ...), custom_call_target="tpu_custom_call" | custom-call | tf_op jit(solution)/shard_map/downward/pallas_call | solution.py:522
  (3 shorter events, 0.0 us)
Async XLA Ops:
  0.0 14.1 %copy-start.4 = (bf16[16,8,256]{2,1,0:T(8,128)(2,1)S(1)}, bf16[16,8,256]{2,1,0:T(8,128)(2,1)}, u32[]{:S(2)}) copy-start(bf16[16,8,256]{2,1,0:T(8,128)(2,1)} %charges.1) | copy-start | bytes 196612
  0.0 14.1 %copy-start.8 = (s32[32,2]{0,1:T(2,128)S(1)}, s32[32,2]{0,1:T(2,128)}, u32[]{:S(2)}) copy-start(s32[32,2]{0,1:T(2,128)} %param.14) | copy-start | bytes 772
  0.0 5.7 %collective-permute-start = (bf16[16,8,256]{2,1,0:T(8,128)(2,1)}, bf16[16,8,256]{2,1,0:T(8,128)(2,1)S(1)}, u32[]{:S(2)}, u32[]{:S(2)}) collective-permute-start(bf16[16,8,256]{2,1,0:T(8,128)(2,1)} %charges.1), channel_id=1, source_target_pairs={{1,0},{2,1},{3,2},{4,3},{5,4},{6,5},{7,6},{8,7},{9,8},{10,9},{11,1... | collective-permute-start | bytes 196616 | tf_op jit(solution)/shard_map/ppermute | solution.py:398
  5.7 22.3 %copy-start = (bf16[128,64,64]{0,2,1:T(8,128)(2,1)S(1)}, bf16[128,64,64]{0,2,1:T(8,128)(2,1)}, u32[]{:S(2)}) copy-start(bf16[128,64,64]{0,2,1:T(8,128)(2,1)} %param.19) | copy-start | bytes 3145732
  5.8 22.3 %copy-start.1 = (bf16[32,64,64]{2,1,0:T(8,128)(2,1)S(1)}, bf16[32,64,64]{2,1,0:T(8,128)(2,1)}, u32[]{:S(2)}) copy-start(bf16[32,64,64]{2,1,0:T(8,128)(2,1)} %par_c.1) | copy-start | bytes 786436
  5.8 22.3 %copy-start.5 = (s32[128,2]{0,1:T(2,128)S(1)}, s32[128,2]{0,1:T(2,128)}, u32[]{:S(2)}) copy-start(s32[128,2]{0,1:T(2,128)} %param.18) | copy-start | bytes 3076
  5.8 22.3 %copy-start.6 = (s32[32,2]{0,1:T(2,128)S(1)}, s32[32,2]{0,1:T(2,128)}, u32[]{:S(2)}) copy-start(s32[32,2]{0,1:T(2,128)} %param.20) | copy-start | bytes 772
  5.8 22.3 %copy-start.7 = (s32[16]{0:T(128)S(1)}, s32[16]{0:T(128)}, u32[]{:S(2)}) copy-start(s32[16]{0:T(128)} %param.17) | copy-start | bytes 196
  5.8 22.0 %all-to-all-start = ((bf16[16,8,1920]{2,1,0:T(8,128)(2,1)}), bf16[16,8,1920]{2,1,0:T(8,128)(2,1)S(1)}, u32[]{:S(2)}, u32[]{:S(2)}) async-start(bf16[16,8,1920]{2,1,0:T(8,128)(2,1)} %bitcast.20), calls=%async_computation | async-start | bytes 983040 | tf_op jit(solution)/shard_map/all_to_all | solution.py:470
  14.1 15.3 %copy-start.2 = (bf16[16,64,256]{2,1,0:T(8,128)(2,1)S(1)}, bf16[16,64,256]{2,1,0:T(8,128)(2,1)}, u32[]{:S(2)}) copy-start(bf16[16,64,256]{2,1,0:T(8,128)(2,1)} %bases.1) | copy-start | bytes 1572868
  14.1 15.3 %copy-start.3 = (bf16[16,64,64]{2,1,0:T(8,128)(2,1)S(1)}, bf16[16,64,64]{2,1,0:T(8,128)(2,1)}, u32[]{:S(2)}) copy-start(bf16[16,64,64]{2,1,0:T(8,128)(2,1)} %transfers.1) | copy-start | bytes 393220
  19.2 3.2 %collective-permute-start.1 = (bf16[16,8,256]{2,1,0:T(8,128)(2,1)S(1)}, bf16[16,8,256]{2,1,0:T(8,128)(2,1)S(1)}, u32[]{:S(2)}, u32[]{:S(2)}) collective-permute-start(bf16[16,8,256]{2,1,0:T(8,128)(2,1)S(1)} %get-tuple-element.13), channel_id=1, source_target_pairs={{0,1},{1,2},{2,3},{3,4},{4,5},{5,6},{6,7},{7,8},{8,9},{9,10},{10,1... | collective-permute-start | bytes 196616 | tf_op jit(solution)/shard_map/ppermute | solution.py:398
  27.9 1.5 %collective-permute-start.2 = (bf16[128,768]{1,0:T(8,128)(2,1)S(1)}, bf16[128,768]{1,0:T(8,128)(2,1)S(1)}, u32[]{:S(2)}, u32[]{:S(2)}) collective-permute-start(bf16[128,768]{1,0:T(8,128)(2,1)S(1)} %slice.4), channel_id=1, source_target_pairs={{0,1},{1,0},{2,3},{3,2},{4,5},{5,4},{6,7},{7,6},{8,9},{9,8},{10,11... | collective-permute-start | bytes 589832 | tf_op jit(solution)/shard_map/ppermute | solution.py:500

commit v20 on v19

--- a/solution.py
+++ b/solution.py
@@ -126,31 +126,41 @@
     copies = fetch(
         [
             (parent_of_h, parent_of),
+            (far_pairs_h, far_pairs),
+            (par_pairs_h, par_pairs),
             (charges_h, charges),
             (bases_h, bases),
             (transfers_h, transfers),
-            (far_pairs_h, far_pairs),
-            (par_pairs_h, par_pairs),
             (par_pairs_h, par_smem),
             (far_c_h, far_c),
             (par_c_h, par_c),
         ],
         sems,
     )
-    copies[0].wait()
+    for copy in copies[:3]:
+        copy.wait()
     to_parent = by_rows(parent_of[...], parents, rhs).astype(BF16)
-    for copy in copies[1:4]:
+    owner_hot = one_hot(far_pairs[0:1, :] % leaves == iota((leaves, slots), 0))
+    partner_hot = one_hot(par_pairs[1:2, :] == iota((rows, pairs), 0))
+    partner = far_pairs[1:2, :]
+    local = jnp.where(partner >= 0, partner % leaves, -1).astype(F32)
+    ob[width : width + LANES, :] = jnp.broadcast_to(local, (LANES, slots)).astype(BF16)
+    unit = one_hot(iota((LANES, LANES), 0) == iota((LANES, LANES), 1))
+
+    for copy in copies[3:5]:
         copy.wait()
-
+    ms = [dot_nt(charges[l], bases[l]).astype(BF16) for l in range(leaves)]
     for l in range(leaves):
-        m = dot_nt(charges[l], bases[l]).astype(BF16)
-        mo[l * rhs : (l + 1) * rhs, :] = m.astype(F32)
-        ch[l * rhs : (l + 1) * rhs, :] = dot_nt(m, transfers[l])
-    for copy in copies[4:]:
-        copy.wait()
+        mo[l * rhs : (l + 1) * rhs, :] = ms[l].astype(F32)
+    copies[5].wait()
+    for l in range(leaves):
+        ch[l * rhs : (l + 1) * rhs, :] = dot_nt(ms[l], transfers[l])
+    m2 = rows_to_lanes(mo, leaves, rhs)
+    a_ref[...] = dot_tn(m2.astype(BF16), owner_hot)
     high, low = split2(ch[...])
     pm3[...] = (dot_nn(to_parent, high) + dot_nn(to_parent, low)).astype(BF16).astype(F32)
-    m2 = rows_to_lanes(mo, leaves, rhs)
+    for copy in copies[6:]:
+        copy.wait()
     pm = rows_to_lanes(pm3, parents, rhs)
     half = 3 * width // 2
     shared = [
@@ -162,8 +172,6 @@
     for p in range(rows // (2 * parents)):
         send[p * 2 * parents : (p + 1) * 2 * parents, at : at + half] = shared
 
-    owner_hot = one_hot(far_pairs[0:1, :] % leaves == iota((leaves, slots), 0))
-    a_ref[...] = dot_tn(m2.astype(BF16), owner_hot)
     def parent_products(first, last):
         for s in range(first, last):
             q = par_smem[0, s] % parents
@@ -190,13 +198,9 @@
             if sb == 0 and part == 2:
                 parent_products(pairs // 4 * 3, pairs)
                 high, low = split2(rows_to_lanes(pb, pairs, rhs))
-                hot = one_hot(par_pairs[1:2, :] == iota((rows, pairs), 0))
                 at = width + LANES
-                send[:, at : at + width] = (dot_nn(hot, high) + dot_nn(hot, low)).astype(BF16)
-    partner = far_pairs[1:2, :]
-    local = jnp.where(partner >= 0, partner % leaves, -1).astype(F32)
-    ob[width : width + LANES, :] = jnp.broadcast_to(local, (LANES, slots)).astype(BF16)
-    unit = one_hot(iota((LANES, LANES), 0) == iota((LANES, LANES), 1))
+                sums = dot_nn(partner_hot, high) + dot_nn(partner_hot, low)
+                send[:, at : at + width] = sums.astype(BF16)
     for sb in range(slots // LANES):
         lanes = slice(sb * LANES, (sb + 1) * LANES)
         send[lanes, 0 : width + LANES] = dot_nt(unit, ob[:, lanes]).astype(BF16)
@@ -351,21 +355,28 @@
     fold = one_hot(iota((parents, rows), 1) % parents == iota((parents, rows), 0))
     at = width + LANES
     lanes_to_rows(pb, dot_nn(fold, got[:, at : at + width]), rhs)
-    lanes_to_rows(g_ref, dot_nn(pick[...], shared), rhs)
     far_gather(mom2[...], far_pairs, b_ref, leaves, parents)
     chunks = far_chunks(far_c, b_ref, fw)
-    each = -(-len(chunks) // 8)
+    each = len(chunks) // 8
+
+    def some_chunks(group):
+        for chunk in chunks[group * each : (group + 1) * each]:
+            chunk()
+
+    picked = dot_nn(pick[...], shared)
+    some_chunks(0)
+    lanes_to_rows(g_ref, picked, rhs)
     for s in range(pairs):
         at = slice(s * rhs, (s + 1) * rhs)
         pf[at, :] = dot_nn(g_ref[at, :].astype(BF16), par_t[s])
-        if s % 4 == 3:
-            for chunk in chunks[s // 4 * each : (s // 4 + 1) * each]:
-                chunk()
-    for chunk in chunks[pairs // 4 * each :]:
-        chunk()
+        if s % (pairs // 4) == pairs // 4 - 1:
+            some_chunks(1 + s // (pairs // 4))
     high, low = split2(pf[...])
     locals_p = dot_nn(to_owner[...], high) + dot_nn(to_owner[...], low) + pb[...]
+    some_chunks(5)
     picked = dot_nn(to_leaf[...], locals_p.astype(BF16))
+    some_chunks(6)
+    some_chunks(7)
     for l in range(leaves):
         at = slice(l * rhs, (l + 1) * rhs)
         dn[at, :] = dot_nn(picked[at, :].astype(BF16), transfers[l])

time: 32.6 us -> 32.6 us (level)
  no operation moved by 1% of the time
where the time goes in v20:
time: 32.6 us; the launch traced here: 32.3 us
  Pallas kernels  13.5 us (41%)
  starting transfers between devices  12.2 us (37%)
  waiting for transfers between devices  6.4 us (20%)
    all_to_all x1, starting transfers between devices, on_device(): got = lax.all_to_all(send, 'sfc', split_axis=0, concat_axis=0, tiled=True)  8.26 us
    all_to_all x1, waiting for transfers between devices, on_device(): got = lax.all_to_all(send, 'sfc', split_axis=0, concat_axis=0, tiled=True)  5.44 us
    pallas_call x1, Pallas kernels, on_device(): pl.pallas_call(near_kernel, grid=(steps,), out_shape=[jax.ShapeDtypeStruc...  5.08 us
    pallas_call x1, Pallas kernels, on_device(): pl.pallas_call(pre_kernel, out_shape=jax.ShapeDtypeStruct((rows, columns)...  4.32 us
    ppermute x2, starting transfers between devices, passed_along(): lax.ppermute(value, axis, [(source, source + steps) for source in range(l...  3.72 us
    pallas_call x1, Pallas kernels, on_device(): pl.pallas_call(post_kernel, out_shape=jax.ShapeDtypeStruct((leaves, rhs,...  2.86 us
    pallas_call x1, Pallas kernels, on_device(): pl.pallas_call(far_kernel, out_shape=[jax.ShapeDtypeStruct((leaves, width...  1.22 us
    ppermute x2, waiting for transfers between devices, passed_along(): lax.ppermute(value, axis, [(source, source + steps) for source in range(l...  0.88 us
  transfers between devices with their start and end apart: 4, of which 3 were waited for; matrix products, arithmetic and copies ran while one was open for 0% of the time, Pallas kernels for 33%

profile of v20, /device:TPU:0, one launch (start us, length us, event | category | flops | bytes accessed | tf_op | source)
XLA Modules:
  0.0 32.3 jit_solution(15881846976027805595)
XLA Ops:
  0.0 0.0 copy-start.4
  0.0 0.0 copy-start.8
  0.0 1.4 %collective-permute-start = (bf16[16,8,256]{2,1,0:T(8,128)(2,1)}, bf16[16,8,256]{2,1,0:T(8,128)(2,1)S(1)}, u32[]{:S(2)}, u32[]{:S(2)}) collective-permute-start(bf16[16,8,256]{2,1,0:T(8,128)(2,1)} %charges.1), channel_id=1, source_target_pairs={{1,0},{2,1},{3,2},{4,3},{5,4},{6,5},{7,6},{8,7},{9,8},{10,9},{11,1... | collective-permute-start | bytes 196616 | tf_op jit(solution)/shard_map/ppermute | solution.py:409
  1.4 4.3 %upward.1.refs_0_ = bf16[128,1920]{1,0:T(8,128)(2,1)} custom-call(bf16[16,8,256]{2,1,0:T(8,128)(2,1)} %charges.1, bf16[16,64,256]{2,1,0:T(8,128)(2,1)} %bases.1, bf16[16,64,64]{2,1,0:T(8,128)(2,1)} %transfers.1, s32[1,16]{1,0:T(1,128)} %bitcast.17, s32[2,128]{1,0:T(2,128)} %bitcast.11, bf16[64,64,128]{2,1,0:T(8,128)(2,1)} %bitcast.8, s32[2,32]{1,0:T(2,128)} %bitcast.15, ...), custom_call_target="tpu_custom_call" | custom-call | flops 40000000 | bytes 10000000 | tf_op jit(solution)/shard_map/upward/pallas_call | solution.py:453
  5.8 0.0 collective-permute-done.refs_1_.following
  5.8 0.0 copy-start
  5.8 0.0 copy-start.1
  5.8 0.0 copy-start.5
  5.8 0.0 copy-start.6
  5.8 0.0 copy-start.7
  5.8 8.3 %all-to-all-start = ((bf16[16,8,1920]{2,1,0:T(8,128)(2,1)}), bf16[16,8,1920]{2,1,0:T(8,128)(2,1)S(1)}, u32[]{:S(2)}, u32[]{:S(2)}) async-start(bf16[16,8,1920]{2,1,0:T(8,128)(2,1)} %bitcast.20), calls=%async_computation | async-start | bytes 983040 | tf_op jit(solution)/shard_map/all_to_all | solution.py:481
  14.1 0.0 copy-done.4
  14.1 0.0 copy-done.8
  14.1 0.0 copy-start.2
  14.1 0.0 copy-start.3
  14.1 5.1 %near.1 = (f32[16,8,256]{2,1,0:T(8,128)S(1)}, bf16[16,8,256]{2,1,0:T(8,128)(2,1)S(1)}) custom-call(s32[2,32]{1,0:T(2,128)S(1)} %bitcast.19, bf16[16,8,256]{2,1,0:T(8,128)(2,1)S(1)} %copy-done.4, bf16[16,8,256]{2,1,0:T(8,128)(2,1)S(1)} %collective-permute-done.refs_1_.following, bf16[16,256,256]{2,1,0:T(8,128)(2,1)} %self_blocks.1, ...), custom_call_target="tpu_custom_call" | custom-call | flops 80000000 | bytes 20000000 | tf_op jit(solution)/shard_map/near/pallas_call | solution.py:485
  19.2 2.3 %collective-permute-start.1 = (bf16[16,8,256]{2,1,0:T(8,128)(2,1)S(1)}, bf16[16,8,256]{2,1,0:T(8,128)(2,1)S(1)}, u32[]{:S(2)}, u32[]{:S(2)}) collective-permute-start(bf16[16,8,256]{2,1,0:T(8,128)(2,1)S(1)} %get-tuple-element.13), channel_id=1, source_target_pairs={{0,1},{1,2},{2,3},{3,4},{4,5},{5,6},{6,7},{7,8},{8,9},{9,10},{10,1... | collective-permute-start | bytes 196616 | tf_op jit(solution)/shard_map/ppermute | solution.py:409
  21.6 0.9 %collective-permute-done.1.refs_1_.near_back = bf16[16,8,256]{2,1,0:T(8,128)(2,1)S(1)} collective-permute-done((bf16[16,8,256]{2,1,0:T(8,128)(2,1)S(1)}, bf16[16,8,256]{2,1,0:T(8,128)(2,1)S(1)}, u32[]{:S(2)}, u32[]{:S(2)}) %collective-permute-start.1) | collective-permute-done | bytes 65568 | tf_op jit(solution)/shard_map/ppermute | solution.py:409
  22.4 5.4 %all-to-all-done = bf16[16,8,1920]{2,1,0:T(8,128)(2,1)S(1)} async-done(((bf16[16,8,1920]{2,1,0:T(8,128)(2,1)}), bf16[16,8,1920]{2,1,0:T(8,128)(2,1)S(1)}, u32[]{:S(2)}, u32[]{:S(2)}) %all-to-all-start) | async-done | bytes 491552 | tf_op jit(solution)/shard_map/all_to_all | solution.py:481
  27.9 0.2 collective-permute-start.2
  28.1 0.0 copy-done
  28.1 0.0 copy-done.1
  28.1 0.0 copy-done.5
  28.1 0.0 copy-done.6
  28.1 0.0 copy-done.7
  28.1 1.2 %far.1 = (f32[16,256]{1,0:T(8,128)S(1)}, f32[16,512]{1,0:T(8,128)S(1)}, bf16[32,64,64]{2,1,0:T(8,128)(2,1)S(1)}, bf16[32,128]{1,0:T(8,128)(2,1)S(1)}, bf16[64,25...) custom-call(bf16[128,1920]{1,0:T(8,128)(2,1)S(1)} %after.3.got, s32[2,128]{1,0:T(2,128)S(1)} %bitcast.12, ...), custom_call_target="tpu_custom_call" | custom-call | flops 32000000 | bytes 8000000 | tf_op jit(solution)/shard_map/far/pallas_call | solution.py:515
  29.3 0.1 collective-permute-done.2.mom2
  29.4 0.0 copy-done.2
  29.4 0.0 copy-done.3
  29.4 2.9 %downward.1 = f32[16,8,256]{2,1,0:T(8,128)} custom-call(s32[2,128]{1,0:T(2,128)S(1)} %bitcast.13, f32[16,256]{1,0:T(8,128)S(1)} %get-tuple-element.14.half, f32[16,512]{1,0:T(8,128)S(1)} %get-tuple-element.15.back, bf16[128,768]{1,0:T(8,128)(2,1)S(1)} %collective-permute-done.2.mom2, bf16[128,1920]{1,0:T(8,128)(2,1)S(1)} %after.3.got, ...), custom_call_target="tpu_custom_call" | custom-call | tf_op jit(solution)/shard_map/downward/pallas_call | solution.py:533
  (3 shorter events, 0.0 us)
Async XLA Ops:
  0.0 14.1 %copy-start.4 = (bf16[16,8,256]{2,1,0:T(8,128)(2,1)S(1)}, bf16[16,8,256]{2,1,0:T(8,128)(2,1)}, u32[]{:S(2)}) copy-start(bf16[16,8,256]{2,1,0:T(8,128)(2,1)} %charges.1) | copy-start | bytes 196612
  0.0 14.1 %copy-start.8 = (s32[32,2]{0,1:T(2,128)S(1)}, s32[32,2]{0,1:T(2,128)}, u32[]{:S(2)}) copy-start(s32[32,2]{0,1:T(2,128)} %param.14) | copy-start | bytes 772
  0.0 5.8 %collective-permute-start = (bf16[16,8,256]{2,1,0:T(8,128)(2,1)}, bf16[16,8,256]{2,1,0:T(8,128)(2,1)S(1)}, u32[]{:S(2)}, u32[]{:S(2)}) collective-permute-start(bf16[16,8,256]{2,1,0:T(8,128)(2,1)} %charges.1), channel_id=1, source_target_pairs={{1,0},{2,1},{3,2},{4,3},{5,4},{6,5},{7,6},{8,7},{9,8},{10,9},{11,1... | collective-permute-start | bytes 196616 | tf_op jit(solution)/shard_map/ppermute | solution.py:409
  5.8 22.3 %copy-start = (bf16[128,64,64]{0,2,1:T(8,128)(2,1)S(1)}, bf16[128,64,64]{0,2,1:T(8,128)(2,1)}, u32[]{:S(2)}) copy-start(bf16[128,64,64]{0,2,1:T(8,128)(2,1)} %param.19) | copy-start | bytes 3145732
  5.8 22.3 %copy-start.1 = (bf16[32,64,64]{2,1,0:T(8,128)(2,1)S(1)}, bf16[32,64,64]{2,1,0:T(8,128)(2,1)}, u32[]{:S(2)}) copy-start(bf16[32,64,64]{2,1,0:T(8,128)(2,1)} %par_c.1) | copy-start | bytes 786436
  5.8 22.3 %copy-start.5 = (s32[128,2]{0,1:T(2,128)S(1)}, s32[128,2]{0,1:T(2,128)}, u32[]{:S(2)}) copy-start(s32[128,2]{0,1:T(2,128)} %param.18) | copy-start | bytes 3076
  5.8 22.3 %copy-start.6 = (s32[32,2]{0,1:T(2,128)S(1)}, s32[32,2]{0,1:T(2,128)}, u32[]{:S(2)}) copy-start(s32[32,2]{0,1:T(2,128)} %param.20) | copy-start | bytes 772
  5.8 22.3 %copy-start.7 = (s32[16]{0:T(128)S(1)}, s32[16]{0:T(128)}, u32[]{:S(2)}) copy-start(s32[16]{0:T(128)} %param.17) | copy-start | bytes 196
  5.8 22.0 %all-to-all-start = ((bf16[16,8,1920]{2,1,0:T(8,128)(2,1)}), bf16[16,8,1920]{2,1,0:T(8,128)(2,1)S(1)}, u32[]{:S(2)}, u32[]{:S(2)}) async-start(bf16[16,8,1920]{2,1,0:T(8,128)(2,1)} %bitcast.20), calls=%async_computation | async-start | bytes 983040 | tf_op jit(solution)/shard_map/all_to_all | solution.py:481
  14.1 15.3 %copy-start.2 = (bf16[16,64,256]{2,1,0:T(8,128)(2,1)S(1)}, bf16[16,64,256]{2,1,0:T(8,128)(2,1)}, u32[]{:S(2)}) copy-start(bf16[16,64,256]{2,1,0:T(8,128)(2,1)} %bases.1) | copy-start | bytes 1572868
  14.1 15.3 %copy-start.3 = (bf16[16,64,64]{2,1,0:T(8,128)(2,1)S(1)}, bf16[16,64,64]{2,1,0:T(8,128)(2,1)}, u32[]{:S(2)}) copy-start(bf16[16,64,64]{2,1,0:T(8,128)(2,1)} %transfers.1) | copy-start | bytes 393220
  19.2 3.2 %collective-permute-start.1 = (bf16[16,8,256]{2,1,0:T(8,128)(2,1)S(1)}, bf16[16,8,256]{2,1,0:T(8,128)(2,1)S(1)}, u32[]{:S(2)}, u32[]{:S(2)}) collective-permute-start(bf16[16,8,256]{2,1,0:T(8,128)(2,1)S(1)} %get-tuple-element.13), channel_id=1, source_target_pairs={{0,1},{1,2},{2,3},{3,4},{4,5},{5,6},{6,7},{7,8},{8,9},{9,10},{10,1... | collective-permute-start | bytes 196616 | tf_op jit(solution)/shard_map/ppermute | solution.py:409
  27.9 1.5 %collective-permute-start.2 = (bf16[128,768]{1,0:T(8,128)(2,1)S(1)}, bf16[128,768]{1,0:T(8,128)(2,1)S(1)}, u32[]{:S(2)}, u32[]{:S(2)}) collective-permute-start(bf16[128,768]{1,0:T(8,128)(2,1)S(1)} %slice.4), channel_id=1, source_target_pairs={{0,1},{1,0},{2,3},{3,2},{4,5},{5,4},{6,7},{7,6},{8,9},{9,8},{10,11... | collective-permute-start | bytes 589832 | tf_op jit(solution)/shard_map/ppermute | solution.py:511
